TPU v7x, 128 devices: a whole 4x4x4 slice. The times are simulated.
128 devices in a mesh: row: 16 (over x, y), col: 8 (over z, core).
Axes of the slice: x: 4, y: 4, z: 4, core: 2. Of those that a mesh axis runs over, the one named last changes fastest.
Arguments:
- basis_in: bfloat16 [131072, 128], P(('row', 'col')), may hold values from -6 to 6
- tiles: bfloat16 [20480, 256, 256], P(('row', 'col'))
- tile_coords: int32 [20480, 2], P(('row', 'col')), may hold values from 0 to 511, as said below
- tile_count: int32 [128], P(('row', 'col')), may hold values from 40 to 160, as said below
Outputs:
- basis_out: float32 [131072, 128], P(('row', 'col'))
- factor: float32 [128, 128], replicated
Inputs may be any that keep to these rules, and one draw needn't show every extreme that they name: `tile_coords`: slots d*160 to (d+1)*160 - 1 belong to device d of the row+col order (d = row index * 8 + col index). Pairs are distinct within a device; the block row lies in [r*8*4, (r+1)*8*4) for the device's row index r; the block column b satisfies (b // 4) mod 8 == the device's col index. Unused slots hold pairs of the same kind. `tile_count`: used slots are the leading ones of each device; 160 is reached by some devices in every draw.
All inputs are finite; a program needn't handle non-finite values.
Results may differ from a plain program's by a relative error of at most 0.0019.
Values may be sent and summed in bfloat16 or wider, within the bound.
No kernel may reach another device: no remote copies, remote signals or barrier semaphores. Data moves between devices by JAX's collectives and lax.ppermute only.
A program may use at most 192 MiB of HBM per device.

v0:
```python
import jax
import jax.numpy as jnp
from jax import lax
from jax.sharding import PartitionSpec as P


def gram_total(local_gram):
    return lax.psum(local_gram, ("row", "col"))


def shards(basis_in, tiles, tile_coords, tile_count):
    row_index = lax.axis_index("row")
    row_size = lax.axis_size("row")
    col_size = lax.axis_size("col")
    tile_side = tiles.shape[1]
    width = basis_in.shape[1]
    per_device = basis_in.shape[0] // tile_side
    slot_total = tiles.shape[0]
    used = jnp.arange(slot_total, dtype=jnp.int32) < tile_count[0]
    local_row = tile_coords[:, 0] - row_index * (col_size * per_device)
    block_col = tile_coords[:, 1]
    local_col = block_col // (col_size * per_device) * per_device + block_col % per_device
    gathered = lax.all_gather(basis_in, "row", axis=0, tiled=True)
    gathered = gathered.reshape(row_size * per_device, tile_side, width)
    chosen = gathered[local_col]
    product = jnp.einsum("tab,tbk->tak", tiles, chosen, preferred_element_type=jnp.float32)
    flat_product = product.reshape(slot_total, tile_side * width)
    row_hot = (
        (local_row[None, :] == jnp.arange(col_size * per_device, dtype=jnp.int32)[:, None])
        & used[None, :]
    ).astype(jnp.float32)
    summed = jnp.dot(row_hot, flat_product, precision=lax.Precision.HIGH)
    inner_mine = lax.psum_scatter(
        summed.reshape(per_device * tile_side * lax.axis_size("col"), width),
        "col",
        scatter_dimension=0,
        tiled=True,
    ).astype(jnp.bfloat16)
    inner_group = lax.all_gather(inner_mine, "col", axis=0, tiled=True)
    inner_blocks = inner_group.reshape(col_size * per_device, tile_side, width)
    picked = inner_blocks[local_row]
    transposed = jnp.einsum("tab,tak->tbk", tiles, picked, preferred_element_type=jnp.float32)
    flat_transposed = transposed.reshape(slot_total, tile_side * width)
    col_hot = (
        (local_col[None, :] == jnp.arange(row_size * per_device, dtype=jnp.int32)[:, None])
        & used[None, :]
    ).astype(jnp.float32)
    summed = jnp.dot(col_hot, flat_transposed, precision=lax.Precision.HIGH)
    outer = lax.psum_scatter(
        summed.reshape(per_device * tile_side * lax.axis_size("row"), width),
        "row",
        scatter_dimension=0,
        tiled=True,
    )
    gram_one = gram_total(jnp.dot(outer.T, outer, precision=lax.Precision.HIGHEST))
    lower_one = jnp.linalg.cholesky(gram_one)
    first = jax.scipy.linalg.solve_triangular(lower_one, outer.T, lower=True).T
    entities = per_device * tile_side * row_size * col_size
    scale = jnp.sqrt(jnp.float32(entities))
    factor = lower_one.T / scale
    return (first * scale, factor)


def solution(mesh):
    placed = (
        P(("row", "col"), None),
        P(("row", "col"), None, None),
        P(("row", "col"), None),
        P(("row", "col")),
    )
    return jax.shard_map(
        shards,
        mesh=mesh,
        in_specs=placed,
        out_specs=(P(("row", "col"), None), P()),
        check_vma=False,
    )
```

profile of v0, /device:TPU:0, one launch (start us, length us, event | category | flops | bytes accessed | tf_op | source)
XLA Modules:
  0.0 566.2 jit_solution(14515275755911802990)
XLA Ops:
  7.2 0.0 all-gather.3.cloned.1.call-start
  7.2 0.7 all-gather.3.cloned.1.call-update
  7.9 0.0 reduce-scatter.3.cloned.1.call-start
  8.6 0.8 fusion.18
  9.4 54.6 %all-gather.3.cloned.1.call-done = bf16[16384,128]{1,0:T(8,128)(2,1)} async-done(((bf16[1024,128]{1,0:T(8,128)(2,1)}), bf16[16384,128]{1,0:T(8,128)(2,1)}) %all-gather.3.cloned.1.call-update) | async-done | bytes 4194320 | tf_op jit(solution)/shard_map/all_gather | solution.py:23
  64.0 9.8 %gather_fusion = bf16[160,256,128]{2,1,0:T(8,128)(2,1)} fusion(bf16[64,256,128]{2,1,0:T(8,128)(2,1)} %bitcast.41, s32[1024]{0:T(1024)S(1)} %pad_clamp_fusion.1), kind=kCustom, calls=%fused_computation | custom fusion | bytes 20972160 | tf_op jit(solution)/shard_map/gather | solution.py:25
  73.9 20.9 %convolution_bitcast_fusion.1 = f32[160,256,128]{1,2,0:T(8,128)} fusion(bf16[160,256,128]{2,1,0:T(8,128)(2,1)} %gather_fusion, bf16[160,256,256]{2,1,0:T(8,128)(2,1)} %param.5), kind=kOutput, calls=%fused_computation.9 | convolution fusion | flops 2684354560 | bytes 52428800 | tf_op jit(solution)/shard_map/tab,tbk->tak/dot_general | solution.py:26
  94.8 21.5 %copy.10 = f32[160,256,128]{2,1,0:T(8,128)} copy(f32[160,256,128]{1,2,0:T(8,128)} %convolution_bitcast_fusion.1) | data formatting | bytes 41943040 | tf_op jit(solution)/shard_map/tab,tbk->tak/dot_general | solution.py:26
  116.3 35.7 %fusion.3 = f32[32,32768]{1,0:T(8,128)} fusion(f32[20,8,256,128]{3,2,1,0:T(8,128)} %bitcast.39, s32[160]{0:T(256)S(1)} %bitcast.42, pred[160]{0:T(512)(128)(4,1)S(1)} %iota_compare_fusion.4), kind=kOutput, calls=%fused_computation.5 | convolution fusion | flops 1006643200 | bytes 25166624 | tf_op jit(solution)/shard_map/dot_general | solution.py:32
  152.0 4.9 reshape.95
  156.9 0.0 reduce-scatter.3.cloned.1.call-update
  156.9 0.0 all-gather.5.cloned.1.call-start
  157.0 37.9 %reduce-scatter.3.cloned.1.call-done = f32[1024,128]{1,0:T(8,128)} async-done(((f32[8192,128]{1,0:T(8,128)}), f32[1024,128]{1,0:T(8,128)}) %reduce-scatter.3.cloned.1.call-update) | async-done | bytes 524304 | tf_op jit(solution)/shard_map/reduce_scatter | solution.py:33
  194.9 1.8 convert_element_type.2
  196.7 0.0 all-gather.5.cloned.1.call-update
  196.7 0.0 reduce-scatter.5.cloned.1.call-start
  196.8 24.7 %all-gather.5.cloned.1.call-done = bf16[8192,128]{1,0:T(8,128)(2,1)} async-done(((bf16[1024,128]{1,0:T(8,128)(2,1)}), bf16[8192,128]{1,0:T(8,128)(2,1)}) %all-gather.5.cloned.1.call-update) | async-done | bytes 2097168 | tf_op jit(solution)/shard_map/all_gather | solution.py:39
  221.4 9.2 %gather_fusion.1 = bf16[160,256,128]{2,1,0:T(8,128)(2,1)} fusion(bf16[32,256,128]{2,1,0:T(8,128)(2,1)} %bitcast.40, s32[1024]{0:T(1024)S(1)} %pad_clamp_fusion), kind=kCustom, calls=%fused_computation.1 | custom fusion | bytes 20972160 | tf_op jit(solution)/shard_map/gather | solution.py:41
  230.7 19.2 %convolution_bitcast_fusion = f32[160,256,128]{1,2,0:T(8,128)} fusion(bf16[160,256,128]{2,1,0:T(8,128)(2,1)} %gather_fusion.1, bf16[160,256,256]{2,1,0:T(8,128)(2,1)} %param.5), kind=kOutput, calls=%fused_computation.8 | convolution fusion | flops 2684354560 | bytes 52428800 | tf_op jit(solution)/shard_map/tab,tak->tbk/dot_general | solution.py:42
  249.8 21.1 %copy.12 = f32[160,256,128]{2,1,0:T(8,128)} copy(f32[160,256,128]{1,2,0:T(8,128)} %convolution_bitcast_fusion) | data formatting | bytes 41943040 | tf_op jit(solution)/shard_map/tab,tak->tbk/dot_general | solution.py:42
  271.0 25.8 %fusion = f32[64,32768]{1,0:T(8,128)} fusion(f32[20,8,256,128]{3,2,1,0:T(8,128)} %bitcast.38, s32[160]{0:T(256)S(1)} %fusion.17, pred[160]{0:T(512)(128)(4,1)S(1)} %iota_compare_fusion.4), kind=kOutput, calls=%fused_computation.2 | convolution fusion | flops 2013286400 | bytes 29360928 | tf_op jit(solution)/shard_map/dot_general | solution.py:48
  296.8 9.3 %reshape.98 = f32[16384,128]{1,0:T(8,128)} reshape(f32[64,32768]{1,0:T(8,128)} %fusion) | data formatting | bytes 16777216 | tf_op jit(solution)/shard_map/reshape | solution.py:50
  306.0 0.0 reduce-scatter.5.cloned.1.call-update
  306.1 0.0 all-reduce.2.cloned.1.call-start
  306.1 85.5 %reduce-scatter.5.cloned.1.call-done = f32[1024,128]{1,0:T(8,128)} async-done(((f32[16384,128]{1,0:T(8,128)}), f32[1024,128]{1,0:T(8,128)}) %reduce-scatter.5.cloned.1.call-update) | async-done | bytes 524304 | tf_op jit(solution)/shard_map/reduce_scatter | solution.py:49
  391.6 2.8 fusion.19
  394.5 0.0 all-reduce.2.cloned.1.call-update
  394.5 137.2 %all-reduce.2.cloned.1.call-done = f32[128,128]{0,1:T(8,128)} async-done(((f32[128,128]{0,1:T(8,128)}), f32[128,128]{0,1:T(8,128)}) %all-reduce.2.cloned.1.call-update) | async-done | bytes 65552 | tf_op jit(solution)/shard_map/psum | solution.py:8
  531.7 0.9 copy.14
  532.6 0.9 fusion.7
  533.5 11.7 %cholesky.16 = f32[128,128]{1,0:T(8,128)S(1)} custom-call(f32[128,128]{1,0:T(8,128)S(1)} %fusion.7), custom_call_target="Cholesky" | custom-call | tf_op jit(solution)/shard_map/jit(cholesky)/cholesky | solution.py:56
  545.2 0.6 compare_reduce_fusion
  545.8 0.7 multiply_bitcast_fusion
  546.5 9.8 %custom-call.7 = f32[1,128,128]{1,2,0:T(8,128)S(1)} custom-call(f32[1,128,128]{2,1,0:T(8,128)S(1)} %get-tuple-element.9), custom_call_target="InvertDiagBlocksLowerTriangular" | custom-call | tf_op jit(solution)/shard_map/jit(_solve_triangular)/triangular_solve | solution.py:57
  556.3 0.7 copy.15
  557.1 2.4 convolution_multiply_fusion
  (5 shorter events, 0.1 us)
Async XLA Ops:
  7.2 56.9 %all-gather.3.cloned.1.call-start = ((), (), s32[]{:S(2)}) async-start(), calls=%async_computation.2 | async-start | bytes 4456448 | tf_op jit(solution)/shard_map/all_gather | solution.py:23
  7.9 187.0 %reduce-scatter.3.cloned.1.call-start = ((), (), s32[]{:S(2)}) async-start(), calls=%async_computation.3 | async-start | bytes 4718592 | tf_op jit(solution)/shard_map/reduce_scatter | solution.py:33
  156.9 64.5 %all-gather.5.cloned.1.call-start = ((), (), s32[]{:S(2)}) async-start(), calls=%async_computation.4 | async-start | bytes 2359296 | tf_op jit(solution)/shard_map/all_gather | solution.py:39
  196.7 195.0 %reduce-scatter.5.cloned.1.call-start = ((), (), s32[]{:S(2)}) async-start(), calls=%async_computation.5 | async-start | bytes 8912896 | tf_op jit(solution)/shard_map/reduce_scatter | solution.py:49
  306.1 225.6 %all-reduce.2.cloned.1.call-start = ((), (), s32[]{:S(2)}) async-start(), calls=%async_computation.6 | async-start | bytes 131072 | tf_op jit(solution)/shard_map/psum | solution.py:8
Sparse Core Ops, SparseCore 0:
  10.1 53.8 all-gather.2
  157.0 37.7 reduce-scatter.2
  197.2 24.2 all-gather.4
  306.2 85.3 reduce-scatter.4
  396.8 134.8 all-reduce.1
where the time goes:
time: 575 us; the launch traced here: 566 us
  waiting for transfers between devices  341 us (59%)
  matrix products  107 us (19%)
  local copies, waits for them, and re-layouts  77.6 us (13%)
  other arithmetic  26.3 us (5%)
  between operations  14.7 us (3%)
    psum x1, waiting for transfers between devices, gram_total(): return lax.psum(local_gram, ('row', 'col'))  137 us
    reduce_scatter x1, waiting for transfers between devices, shards(): lax.psum_scatter(summed.reshape(per_device * tile_side * lax.axis_size('r...  85.5 us
    all_gather x1, waiting for transfers between devices, shards(): gathered = lax.all_gather(basis_in, 'row', axis=0, tiled=True)  54.6 us
    reduce_scatter x1, waiting for transfers between devices, shards(): lax.psum_scatter(summed.reshape(per_device * tile_side * lax.axis_size('c...  37.9 us
    dot_general x1, matrix products, shards(): summed = jnp.dot(row_hot, flat_product, precision=lax.Precision.HIGH)  35.7 us
    dot_general x1, matrix products, shards(): summed = jnp.dot(col_hot, flat_transposed, precision=lax.Precision.HIGH)  25.8 us
    all_gather x1, waiting for transfers between devices, shards(): inner_group = lax.all_gather(inner_mine, 'col', axis=0, tiled=True)  24.7 us
    dot_general x1, local copies, waits for them, and re-layouts, shards(): jnp.einsum('tab,tbk->tak', tiles, chosen, preferred_element_type=jnp.floa...  21.5 us
  transfers between devices with their start and end apart: 5, of which 5 were waited for; matrix products, arithmetic and copies ran while one was open for 0% of the time, Pallas kernels for 0%

commit v1 on v0

v1 whole, which is shorter than its diff:
```python
import jax
import jax.numpy as jnp
from jax import lax
from jax.experimental import pallas as pl
from jax.experimental.pallas import tpu as pltpu
from jax.sharding import Mesh, PartitionSpec as P

AXES = ("x", "y", "z", "core")
SIZES = {"x": 4, "y": 4, "z": 4, "core": 2}
SIDE = 256
RANK = 128
CHUNK = 8
F32 = jnp.float32
BF16 = jnp.bfloat16


def send(array, axis, step):
    size = SIZES[axis]
    return lax.ppermute(array, axis, [(i, (i + step) % size) for i in range(size)])


def limits(mib):
    return pltpu.CompilerParams(vmem_limit_bytes=mib * 1024 * 1024)


def whole(count):
    return [pl.BlockSpec(memory_space=pltpu.VMEM)] * count


def load_pieces(pieces, held, sems):
    copies = []
    at = 0
    for i, piece in enumerate(pieces):
        rows = piece.shape[0]
        copies.append(pltpu.make_async_copy(piece, held.at[pl.ds(at, rows)], sems.at[i]))
        at += rows
    for copy in copies:
        copy.start()
    return copies


def forward_kernel(count, row_at, col_at, tiles, *rest):
    pieces, (keep, away, held, total, sems, out_sems) = rest[:8], rest[8:]
    step = pl.program_id(0)

    @pl.when(step == 0)
    def _():
        copies = load_pieces(pieces, held, sems)
        total[...] = jnp.zeros_like(total)
        for copy in copies:
            copy.wait()

    @pl.when(step * CHUNK < count[0])
    def _():
        for k in range(CHUNK):
            slot = step * CHUNK + k
            row = row_at[slot]
            col = col_at[slot]
            total[row] += jnp.dot(tiles[k], held[col], preferred_element_type=F32)

    @pl.when(step == pl.num_programs(0) - 1)
    def _():
        half = keep.shape[0]
        one = pltpu.make_async_copy(total.at[pl.ds(half, half)], away, out_sems.at[0])
        two = pltpu.make_async_copy(total.at[pl.ds(0, half)], keep, out_sems.at[1])
        one.start()
        two.start()
        one.wait()
        two.wait()


def tile_spec():
    def index(step, count, row_at, col_at):
        return (jnp.minimum(step, (count[0] - 1) // CHUNK), 0, 0)

    return pl.BlockSpec((CHUNK, SIDE, SIDE), index)


def forward(count, row_at, col_at, tiles, pieces):
    slots = tiles.shape[0]
    any_spec = pl.BlockSpec(memory_space=pl.ANY)
    half = jax.ShapeDtypeStruct((16, SIDE, RANK), F32)
    return pl.pallas_call(
        forward_kernel,
        out_shape=(half, half),
        grid_spec=pltpu.PrefetchScalarGridSpec(
            num_scalar_prefetch=3,
            grid=(slots // CHUNK,),
            in_specs=[tile_spec()] + [any_spec] * 8,
            out_specs=(any_spec, any_spec),
            scratch_shapes=[
                pltpu.VMEM((64, SIDE, RANK), BF16),
                pltpu.VMEM((33, SIDE, RANK), F32),
                pltpu.SemaphoreType.DMA((8,)),
                pltpu.SemaphoreType.DMA((2,)),
            ],
        ),
        compiler_params=limits(32),
        name="forward",
    )(count, row_at, col_at, tiles, *pieces)


def backward_kernel(count, row_at, col_at, tiles, *rest):
    pieces, keep, aways, (held, total, sems) = rest[:8], rest[8], rest[9:15], rest[15:]
    step = pl.program_id(0)

    @pl.when(step == 0)
    def _():
        copies = load_pieces(pieces, held, sems)
        total[...] = jnp.zeros_like(total)
        for copy in copies:
            copy.wait()

    @pl.when(step * CHUNK < count[0])
    def _():
        for k in range(CHUNK):
            slot = step * CHUNK + k
            row = row_at[slot]
            col = col_at[slot]
            total[col] += jnp.dot(held[row], tiles[k], preferred_element_type=F32)

    @pl.when(step == pl.num_programs(0) - 1)
    def _():
        for h in range(2):
            keep[h] = total[pl.ds(32 * h, 8)]
            for d in range(3):
                aways[3 * h + d][...] = total[pl.ds(32 * h + 8 * (d + 1), 8)].astype(BF16)


def backward(count, row_at, col_at, tiles, pieces):
    slots = tiles.shape[0]
    any_spec = pl.BlockSpec(memory_space=pl.ANY)
    part = jax.ShapeDtypeStruct((8, RANK, SIDE), BF16)
    return pl.pallas_call(
        backward_kernel,
        out_shape=(jax.ShapeDtypeStruct((2, 8, RANK, SIDE), F32),) + (part,) * 6,
        grid_spec=pltpu.PrefetchScalarGridSpec(
            num_scalar_prefetch=3,
            grid=(slots // CHUNK,),
            in_specs=[tile_spec()] + [any_spec] * 8,
            out_specs=tuple(whole(7)),
            scratch_shapes=[
                pltpu.VMEM((32, RANK, SIDE), BF16),
                pltpu.VMEM((65, RANK, SIDE), F32),
                pltpu.SemaphoreType.DMA((8,)),
            ],
        ),
        compiler_params=limits(40),
        name="backward",
    )(count, row_at, col_at, tiles, *pieces)


def core_sum_kernel(keep, came, *outs):
    for d in range(4):
        at = pl.ds(4 * d, 4)
        outs[d][...] = keep[at] + came[at]


def core_sum(keep, came):
    part = jax.ShapeDtypeStruct((4, SIDE, RANK), F32)
    return pl.pallas_call(
        core_sum_kernel,
        out_shape=(part,) * 4,
        in_specs=whole(2),
        out_specs=tuple(whole(4)),
        compiler_params=limits(16),
        name="core_sum",
    )(keep, came)


def inner_kernel(a, b, c, d, out):
    for i in range(out.shape[0]):
        summed = (a[i] + b[i]) + (c[i] + d[i])
        out[i] = summed.T.astype(BF16)


def inner_sum(parts):
    return pl.pallas_call(
        inner_kernel,
        out_shape=jax.ShapeDtypeStruct((4, RANK, SIDE), BF16),
        in_specs=whole(4),
        out_specs=whole(1)[0],
        compiler_params=limits(16),
        name="inner_sum",
    )(*parts)


def middle_kernel(keep, *rest):
    came, next_keep, aways = rest[:6], rest[6], rest[7:]
    for h in range(2):
        for d in range(4):
            at = pl.ds(2 * d, 2)
            total = keep[h, at]
            for one in came[3 * h : 3 * h + 3]:
                total += one[at].astype(F32)
            if d == 0:
                next_keep[h] = total
            else:
                aways[3 * h + d - 1][...] = total.astype(BF16)


def middle_sum(keep, came):
    part = jax.ShapeDtypeStruct((2, RANK, SIDE), BF16)
    return pl.pallas_call(
        middle_kernel,
        out_shape=(jax.ShapeDtypeStruct((2, 2, RANK, SIDE), F32),) + (part,) * 6,
        in_specs=whole(7),
        out_specs=tuple(whole(7)),
        compiler_params=limits(16),
        name="middle_sum",
    )(keep, *came)


def exact_dot(a, b, dims):
    return lax.dot_general(
        a, b, (dims, ((), ())), precision=lax.Precision.HIGHEST, preferred_element_type=F32
    )


def outer_kernel(keep, *rest):
    came, outer, gram = rest[:6], rest[6], rest[7]
    gram_total = jnp.zeros((RANK, RANK), F32)
    for h in range(2):
        for b in range(2):
            total = keep[h, b]
            for one in came[3 * h : 3 * h + 3]:
                total += one[b].astype(F32)
            outer[2 * h + b] = total
            gram_total += exact_dot(total, total, ((1,), (1,)))
    gram[...] = gram_total


def outer_sum(keep, came):
    return pl.pallas_call(
        outer_kernel,
        out_shape=(
            jax.ShapeDtypeStruct((4, RANK, SIDE), F32),
            jax.ShapeDtypeStruct((RANK, RANK), F32),
        ),
        in_specs=whole(7),
        out_specs=tuple(whole(2)),
        compiler_params=limits(16),
        name="outer_sum",
    )(keep, *came)


def finish_kernel(scale, gram, outer, basis, factor, work):
    rows = lax.broadcasted_iota(jnp.int32, (RANK, RANK), 0)
    cols = lax.broadcasted_iota(jnp.int32, (RANK, RANK), 1)
    work[:, :RANK] = gram[...]
    work[:, RANK:] = jnp.where(rows == cols, 1.0, 0.0)
    sub = lax.broadcasted_iota(jnp.int32, (8, 2 * RANK), 0)
    for j in range(0, RANK, 8):
        panel = work[j : j + 8, :]
        for i in range(8):
            column = panel[:, j + i : j + i + 1]
            pivot = panel[i : i + 1, j + i : j + i + 1]
            root = lax.rsqrt(pivot)
            root = root * (1.5 - 0.5 * pivot * root * root)
            row = panel[i : i + 1, :] * root
            panel = jnp.where(
                sub == i, row, jnp.where(sub > i, panel - (column * root) * row, panel)
            )
        work[j : j + 8, :] = panel
        if j + 8 < RANK:
            lower = panel[:, :RANK]
            update = exact_dot(lower, panel, ((0,), (0,)))
            work[j + 8 :, :] -= update[j + 8 :, :]
    factor[...] = jnp.where(cols >= rows, work[:, :RANK], 0.0) * (1.0 / scale)
    inverse = work[:, RANK:] * scale
    for b in range(outer.shape[0]):
        basis[pl.ds(b * SIDE, SIDE), :] = exact_dot(outer[b], inverse, ((0,), (1,)))


def finish(gram, outer, entities):
    scale = float(entities) ** 0.5

    def kernel(*refs):
        finish_kernel(scale, *refs)

    return pl.pallas_call(
        kernel,
        out_shape=(
            jax.ShapeDtypeStruct((4 * SIDE, RANK), F32),
            jax.ShapeDtypeStruct((RANK, RANK), F32),
        ),
        in_specs=whole(2),
        out_specs=tuple(whole(2)),
        scratch_shapes=[pltpu.VMEM((RANK, 2 * RANK), F32)],
        compiler_params=limits(16),
        name="finish",
    )(gram, outer)


def shards(basis_in, tiles, tile_coords, tile_count):
    x, y, z, core = (lax.axis_index(name) for name in AXES)
    slots = tiles.shape[0]
    used = jnp.arange(slots, dtype=jnp.int32) < tile_count[0]
    local_row = tile_coords[:, 0] - (x * 4 + y) * 32
    dz = (local_row // 8 - z) % 4
    dc = (local_row // 4 - core) % 2
    row_at = dc * 16 + dz * 4 + local_row % 4
    row_group = tile_coords[:, 1] // 32
    b = tile_coords[:, 1] % 4
    dx = (row_group // 4 - x) % 4
    dy = (row_group % 4 - y) % 4
    col_at = jnp.where(b < 2, dy * 8 + dx * 2 + b, 32 + dx * 8 + dy * 2 + b - 2)

    with jax.named_scope("gather_basis"):
        halves = (basis_in[: 2 * SIDE], basis_in[2 * SIDE :])
        orders = (("x", "y"), ("y", "x"))
        firsts = [
            jnp.concatenate([half] + [send(half, order[0], -d) for d in (1, 2, 3)], axis=0)
            for half, order in zip(halves, orders)
        ]
        pieces = []
        for first, order in zip(firsts, orders):
            pieces += [first] + [send(first, order[1], -d) for d in (1, 2, 3)]
        pieces = [piece.reshape(8, SIDE, RANK) for piece in pieces]

    keep, away = forward(tile_count, jnp.where(used, row_at, 32), col_at, tiles, pieces)

    with jax.named_scope("reduce_inner"):
        came = send(away, "core", 1)
        sums = core_sum(keep, came)
        inner = inner_sum([sums[0]] + [send(sums[d], "z", d) for d in (1, 2, 3)])

    with jax.named_scope("gather_inner"):
        mine = [inner] + [send(inner, "z", -d) for d in (1, 2, 3)]
        theirs = [send(one, "core", 1) for one in mine]

    keep, *aways = backward(
        tile_count, row_at, jnp.where(used, col_at, 64), tiles, mine + theirs
    )

    with jax.named_scope("reduce_outer"):
        back = ("y",) * 3 + ("x",) * 3
        steps = (1, 2, 3) * 2
        came = [send(a, axis, d) for a, axis, d in zip(aways, back, steps)]
        keep, *aways = middle_sum(keep, came)
        forth = ("x",) * 3 + ("y",) * 3
        came = [send(a, axis, d) for a, axis, d in zip(aways, forth, steps)]
        outer, gram = outer_sum(keep, came)

    with jax.named_scope("reduce_gram"):
        gram = gram + send(gram, "core", 1)
        for axis in ("z", "y", "x"):
            parts = [send(gram, axis, d) for d in (1, 2, 3)]
            gram = (gram + parts[1]) + (parts[0] + parts[2])

    entities = basis_in.shape[0] * 128
    return finish(gram, outer, entities)


def solution(mesh):
    split = Mesh(mesh.devices.reshape(4, 4, 4, 2), AXES)
    placed = (P(AXES, None), P(AXES, None, None), P(AXES, None), P(AXES))
    return jax.shard_map(
        shards,
        mesh=split,
        in_specs=placed,
        out_specs=(P(AXES, None), P()),
        check_vma=False,
    )
```

time: 575 us -> 237 us (0.41); the launches traced: 566 us -> 238 us
  waiting for transfers between devices: 341 us -> 103 us
  matrix products: 107 us -> 0 us
  starting transfers between devices: 0.2 us -> 98.6 us
  local copies, waits for them, and re-layouts: 77.6 us -> 1 us
  Pallas kernels: 0 us -> 34 us
  other arithmetic: 26.3 us -> 0.17 us
  between operations: 14.7 us -> 1.43 us
    psum x1 -> x0, waiting for transfers between devices: 137 us -> none  [gram_total(): return lax.psum(local_gram, ('row', 'col'))]
    reduce_scatter x2 -> x0, waiting for transfers between devices: 123 us -> none  [the longest x1 85.5 us: shards(): lax.psum_scatter(summed.reshape(per_device * tile_side * lax.axis_size('r...]
    dot_general x5 -> x0, matrix products: 104 us -> none  [the longest x1 35.7 us: shards(): summed = jnp.dot(row_hot, flat_product, precision=lax.Precision.HIGH)]
    ppermute x0 -> x45, waiting for transfers between devices: none -> 103 us  [send(): lax.ppermute(array, axis, [(i, (i + step) % size) for i in range(size)])]
    ppermute x0 -> x45, starting transfers between devices: none -> 98.6 us  [send(): lax.ppermute(array, axis, [(i, (i + step) % size) for i in range(size)])]
    all_gather x2 -> x0, waiting for transfers between devices: 79.3 us -> none  [the longest x1 54.6 us: shards(): gathered = lax.all_gather(basis_in, 'row', axis=0, tiled=True)]
    dot_general x2 -> x0, local copies, waits for them, and re-layouts: 42.7 us -> none  [the longest x1 21.5 us: shards(): jnp.einsum('tab,tbk->tak', tiles, chosen, preferred_element_type=jnp.floa...]
    pallas_call x0 -> x7, Pallas kernels: none -> 34 us  [the longest x1 17.4 us: finish(): pl.pallas_call(kernel, out_shape=(jax.ShapeDtypeStruct((4 * SIDE, RANK),...]
  transfers between devices with their start and end apart: 5 -> 45, of which waited for: 5 -> 29; matrix products, arithmetic and copies ran while one was open for 0% -> 0% of each run, Pallas kernels for 0% -> 0%
where the time goes in v1:
time: 237 us; the launch traced here: 238 us
  waiting for transfers between devices  103 us (43%)
  starting transfers between devices  98.6 us (42%)
  Pallas kernels  34 us (14%)
    ppermute x45, waiting for transfers between devices, send(): lax.ppermute(array, axis, [(i, (i + step) % size) for i in range(size)])  103 us
    ppermute x45, starting transfers between devices, send(): lax.ppermute(array, axis, [(i, (i + step) % size) for i in range(size)])  98.6 us
    pallas_call x1, Pallas kernels, finish(): pl.pallas_call(kernel, out_shape=(jax.ShapeDtypeStruct((4 * SIDE, RANK),...  17.4 us
    pallas_call x1, Pallas kernels, forward(): pl.pallas_call(forward_kernel, out_shape=(half, half), grid_spec=pltpu.Pr...  8 us
    pallas_call x1, Pallas kernels, backward(): pl.pallas_call(backward_kernel, out_shape=(jax.ShapeDtypeStruct((2, 8, RA...  7.09 us
  transfers between devices with their start and end apart: 45, of which 29 were waited for; matrix products, arithmetic and copies ran while one was open for 0% of the time, Pallas kernels for 0%

profile of v1, /device:TPU:0, one launch (start us, length us, event | category | flops | bytes accessed | tf_op | source)
XLA Modules:
  0.0 237.9 jit_solution(14128494193906583456)
XLA Ops:
  0.6 1.0 fusion.12
  1.6 1.6 collective-permute-start.2
  3.3 2.7 %collective-permute-start.1 = (bf16[512,128]{1,0:T(8,128)(2,1)S(1)}, bf16[512,128]{1,0:T(8,128)(2,1)S(1)}, u32[]{:S(2)}, u32[]{:S(2)}) collective-permute-start(bf16[512,128]{1,0:T(8,128)(2,1)S(1)} %get-tuple-element.51), channel_id=1, source_target_pairs={{0,64},{32,96},{64,0},{96,32},{1,65},{33,97},{65,1},{97,33},{2,66}... | collective-permute-start | bytes 393224 | tf_op jit(solution)/shard_map/gather_basis/ppermute | solution.py:19
  6.0 1.4 collective-permute-start
  8.0 4.0 %collective-permute-done.1 = bf16[512,128]{1,0:T(8,128)(2,1)S(1)} collective-permute-done((bf16[512,128]{1,0:T(8,128)(2,1)S(1)}, bf16[512,128]{1,0:T(8,128)(2,1)S(1)}, u32[]{:S(2)}, u32[]{:S(2)}) %collective-permute-start.1) | collective-permute-done | bytes 131104 | tf_op jit(solution)/shard_map/gather_basis/ppermute | solution.py:19
  12.1 1.6 collective-permute-start.5
  13.7 1.6 collective-permute-start.8
  15.3 1.5 collective-permute-start.7
  16.8 2.4 %collective-permute-start.6 = (bf16[512,128]{1,0:T(8,128)(2,1)S(1)}, bf16[512,128]{1,0:T(8,128)(2,1)S(1)}, u32[]{:S(2)}, u32[]{:S(2)}) collective-permute-start(bf16[512,128]{1,0:T(8,128)(2,1)S(1)} %get-tuple-element.50), channel_id=1, source_target_pairs={{0,24},{8,0},{16,8},{24,16},{1,25},{9,1},{17,9},{25,17},{2,26},{10... | collective-permute-start | bytes 393224 | tf_op jit(solution)/shard_map/gather_basis/ppermute | solution.py:19
  19.2 0.6 collective-permute-start.4
  19.9 10.0 %collective-permute-done.8 = bf16[512,128]{1,0:T(8,128)(2,1)S(1)} collective-permute-done((bf16[512,128]{1,0:T(8,128)(2,1)S(1)}, bf16[512,128]{1,0:T(8,128)(2,1)S(1)}, u32[]{:S(2)}, u32[]{:S(2)}) %collective-permute-start.8) | collective-permute-done | bytes 131104 | tf_op jit(solution)/shard_map/gather_basis/ppermute | solution.py:19
  29.9 2.9 %collective-permute-start.3 = (bf16[2048,128]{1,0:T(8,128)(2,1)S(1)}, bf16[2048,128]{1,0:T(8,128)(2,1)S(1)}, u32[]{:S(2)}, u32[]{:S(2)}) collective-permute-start(bf16[2048,128]{1,0:T(8,128)(2,1)S(1)} %pad_maximum_fusion), channel_id=1, source_target_pairs={{0,24},{8,0},{16,8},{24,16},{1,25},{9,1},{17,9},{25,17},{2,26},{10... | collective-permute-start | bytes 1572872 | tf_op jit(solution)/shard_map/gather_basis/ppermute | solution.py:19
  32.8 2.2 collective-permute-done.7
  35.1 1.4 collective-permute-start.11
  36.5 2.4 %collective-permute-start.10 = (bf16[2048,128]{1,0:T(8,128)(2,1)S(1)}, bf16[2048,128]{1,0:T(8,128)(2,1)}, u32[]{:S(2)}, u32[]{:S(2)}) collective-permute-start(bf16[2048,128]{1,0:T(8,128)(2,1)S(1)} %pad_maximum_fusion.1), channel_id=1, source_target_pairs={{0,64},{32,96},{64,0},{96,32},{1,65},{33,97},{65,1},{97,33},{2,66}... | collective-permute-start | bytes 1572872 | tf_op jit(solution)/shard_map/gather_basis/ppermute | solution.py:19
  38.9 1.6 collective-permute-start.9
  41.2 3.0 %collective-permute-done.4 = bf16[2048,128]{1,0:T(8,128)(2,1)S(1)} collective-permute-done((bf16[2048,128]{1,0:T(8,128)(2,1)S(1)}, bf16[2048,128]{1,0:T(8,128)(2,1)S(1)}, u32[]{:S(2)}, u32[]{:S(2)}) %collective-permute-start.4) | collective-permute-done | bytes 524320 | tf_op jit(solution)/shard_map/gather_basis/ppermute | solution.py:19
  44.2 0.7 collective-permute-done.3
  44.9 5.0 %collective-permute-done.11 = bf16[2048,128]{1,0:T(8,128)(2,1)S(1)} collective-permute-done((bf16[2048,128]{1,0:T(8,128)(2,1)S(1)}, bf16[2048,128]{1,0:T(8,128)(2,1)S(1)}, u32[]{:S(2)}, u32[]{:S(2)}) %collective-permute-start.11) | collective-permute-done | bytes 524320 | tf_op jit(solution)/shard_map/gather_basis/ppermute | solution.py:19
  49.9 8.3 %collective-permute-done.10 = bf16[2048,128]{1,0:T(8,128)(2,1)} collective-permute-done((bf16[2048,128]{1,0:T(8,128)(2,1)S(1)}, bf16[2048,128]{1,0:T(8,128)(2,1)}, u32[]{:S(2)}, u32[]{:S(2)}) %collective-permute-start.10) | collective-permute-done | bytes 524320 | tf_op jit(solution)/shard_map/gather_basis/ppermute | solution.py:19
  58.2 8.0 %forward.1 = (f32[16,256,128]{2,1,0:T(8,128)S(1)}, f32[16,256,128]{2,1,0:T(8,128)S(1)}) custom-call(s32[1]{0:T(128)} %copy.6.count, s32[160]{0:T(256)S(1)} %get-tuple-element.46.row_at, s32[160]{0:T(256)S(1)} %get-tuple-element.55.col_at, bf16[160,256,256]{2,1,0:T(8,128)(2,1)} %tiles.3, bf16[8,256,128]{2,1,0:T(8,128)(2,1)S(1)} %bitcast.12, ...), custom_call_target="tpu_custom_call" | custom-call | tf_op jit(solution)/shard_map/forward/pallas_call | solution.py:83
  66.2 1.1 collective-permute-start.12
  67.2 3.8 %collective-permute-done.12.came = f32[16,256,128]{2,1,0:T(8,128)S(1)} collective-permute-done((f32[16,256,128]{2,1,0:T(8,128)S(1)}, f32[16,256,128]{2,1,0:T(8,128)S(1)}, u32[]{:S(2)}, u32[]{:S(2)}) %collective-permute-start.12) | collective-permute-done | bytes 2097184 | tf_op jit(solution)/shard_map/reduce_inner/ppermute | solution.py:19
  71.3 3.6 %collective-permute-start.13 = (f32[4,256,128]{2,1,0:T(8,128)S(1)}, f32[4,256,128]{2,1,0:T(8,128)S(1)}, u32[]{:S(2)}, u32[]{:S(2)}) collective-permute-start(f32[4,256,128]{2,1,0:T(8,128)S(1)} %get-tuple-element.27), channel_id=1, source_target_pairs={{0,2},{2,4},{4,6},{6,0},{1,3},{3,5},{5,7},{7,1},{8,10},{10,12},{12... | collective-permute-start | bytes 1572872 | tf_op jit(solution)/shard_map/reduce_inner/ppermute | solution.py:19
  74.9 5.3 %collective-permute-start.14 = (f32[4,256,128]{2,1,0:T(8,128)S(1)}, f32[4,256,128]{2,1,0:T(8,128)S(1)}, u32[]{:S(2)}, u32[]{:S(2)}) collective-permute-start(f32[4,256,128]{2,1,0:T(8,128)S(1)} %get-tuple-element.28), channel_id=1, source_target_pairs={{0,4},{2,6},{4,0},{6,2},{1,5},{3,7},{5,1},{7,3},{8,12},{10,14},{12... | collective-permute-start | bytes 1572872 | tf_op jit(solution)/shard_map/reduce_inner/ppermute | solution.py:19
  80.6 10.4 %collective-permute-done.13.b = f32[4,256,128]{2,1,0:T(8,128)S(1)} collective-permute-done((f32[4,256,128]{2,1,0:T(8,128)S(1)}, f32[4,256,128]{2,1,0:T(8,128)S(1)}, u32[]{:S(2)}, u32[]{:S(2)}) %collective-permute-start.13) | collective-permute-done | bytes 524320 | tf_op jit(solution)/shard_map/reduce_inner/ppermute | solution.py:19
  90.9 12.4 %collective-permute-done.14.c = f32[4,256,128]{2,1,0:T(8,128)S(1)} collective-permute-done((f32[4,256,128]{2,1,0:T(8,128)S(1)}, f32[4,256,128]{2,1,0:T(8,128)S(1)}, u32[]{:S(2)}, u32[]{:S(2)}) %collective-permute-start.14) | collective-permute-done | bytes 524320 | tf_op jit(solution)/shard_map/reduce_inner/ppermute | solution.py:19
  103.5 1.0 collective-permute-start.18
  104.5 2.7 %collective-permute-start.17 = (bf16[4,128,256]{2,1,0:T(8,128)(2,1)S(1)}, bf16[4,128,256]{2,1,0:T(8,128)(2,1)S(1)}, u32[]{:S(2)}, u32[]{:S(2)}) collective-permute-start(bf16[4,128,256]{2,1,0:T(8,128)(2,1)S(1)} %inner_sum.1.rest_0_), channel_id=1, source_target_pairs={{0,4},{2,6},{4,0},{6,2},{1,5},{3,7},{5,1},{7,3},{8,12},{10,14},{12... | collective-permute-start | bytes 786440 | tf_op jit(solution)/shard_map/gather_inner/ppermute | solution.py:19
  107.8 4.5 %collective-permute-done.18.rest_3_ = bf16[4,128,256]{2,1,0:T(8,128)(2,1)S(1)} collective-permute-done((bf16[4,128,256]{2,1,0:T(8,128)(2,1)S(1)}, bf16[4,128,256]{2,1,0:T(8,128)(2,1)S(1)}, u32[]{:S(2)}, u32[]{:S(2)}) %collective-permute-start.18) | collective-permute-done | bytes 262176 | tf_op jit(solution)/shard_map/gather_inner/ppermute | solution.py:19
  112.3 6.7 %collective-permute-done.17.rest_2_ = bf16[4,128,256]{2,1,0:T(8,128)(2,1)S(1)} collective-permute-done((bf16[4,128,256]{2,1,0:T(8,128)(2,1)S(1)}, bf16[4,128,256]{2,1,0:T(8,128)(2,1)S(1)}, u32[]{:S(2)}, u32[]{:S(2)}) %collective-permute-start.17) | collective-permute-done | bytes 262176 | tf_op jit(solution)/shard_map/gather_inner/ppermute | solution.py:19
  119.6 1.0 collective-permute-done.21.rest_6_
  121.0 7.1 %backward.1 = (f32[2,8,128,256]{3,2,1,0:T(8,128)S(1)}, bf16[8,128,256]{2,1,0:T(8,128)(2,1)S(1)}, bf16[8,128,256]{2,1,0:T(8,128)(2,1)S(1)}, bf16[8,128,256]{2,1,0...) custom-call(s32[1]{0:T(128)} %copy.6.count, ...), custom_call_target="tpu_custom_call" | custom-call | tf_op jit(solution)/shard_map/backward/pallas_call | solution.py:134
  128.1 6.4 %collective-permute-start.24 = (bf16[8,128,256]{2,1,0:T(8,128)(2,1)S(1)}, bf16[8,128,256]{2,1,0:T(8,128)(2,1)S(1)}, u32[]{:S(2)}, u32[]{:S(2)}) collective-permute-start(bf16[8,128,256]{2,1,0:T(8,128)(2,1)S(1)} %get-tuple-element.32), channel_id=1, source_target_pairs={{0,16},{8,24},{16,0},{24,8},{1,17},{9,25},{17,1},{25,9},{2,18},{10... | collective-permute-start | bytes 1572872 | tf_op jit(solution)/shard_map/reduce_outer/ppermute | solution.py:19
  134.6 2.6 %collective-permute-start.25 = (bf16[8,128,256]{2,1,0:T(8,128)(2,1)S(1)}, bf16[8,128,256]{2,1,0:T(8,128)(2,1)S(1)}, u32[]{:S(2)}, u32[]{:S(2)}) collective-permute-start(bf16[8,128,256]{2,1,0:T(8,128)(2,1)S(1)} %get-tuple-element.33), channel_id=1, source_target_pairs={{0,24},{8,0},{16,8},{24,16},{1,25},{9,1},{17,9},{25,17},{2,26},{10... | collective-permute-start | bytes 1572872 | tf_op jit(solution)/shard_map/reduce_outer/ppermute | solution.py:19
  137.1 9.8 %collective-permute-start.26 = (bf16[8,128,256]{2,1,0:T(8,128)(2,1)S(1)}, bf16[8,128,256]{2,1,0:T(8,128)(2,1)S(1)}, u32[]{:S(2)}, u32[]{:S(2)}) collective-permute-start(bf16[8,128,256]{2,1,0:T(8,128)(2,1)S(1)} %get-tuple-element.34), channel_id=1, source_target_pairs={{0,32},{32,64},{64,96},{96,0},{1,33},{33,65},{65,97},{97,1},{2,34}... | collective-permute-start | bytes 1572872 | tf_op jit(solution)/shard_map/reduce_outer/ppermute | solution.py:19
  147.0 7.9 %collective-permute-start.28 = (bf16[8,128,256]{2,1,0:T(8,128)(2,1)S(1)}, bf16[8,128,256]{2,1,0:T(8,128)(2,1)S(1)}, u32[]{:S(2)}, u32[]{:S(2)}) collective-permute-start(bf16[8,128,256]{2,1,0:T(8,128)(2,1)S(1)} %get-tuple-element.36), channel_id=1, source_target_pairs={{0,96},{32,0},{64,32},{96,64},{1,97},{33,1},{65,33},{97,65},{2,98}... | collective-permute-start | bytes 1572872 | tf_op jit(solution)/shard_map/reduce_outer/ppermute | solution.py:19
  154.9 3.4 %collective-permute-done.24.rest_1_ = bf16[8,128,256]{2,1,0:T(8,128)(2,1)S(1)} collective-permute-done((bf16[8,128,256]{2,1,0:T(8,128)(2,1)S(1)}, bf16[8,128,256]{2,1,0:T(8,128)(2,1)S(1)}, u32[]{:S(2)}, u32[]{:S(2)}) %collective-permute-start.24) | collective-permute-done | bytes 524320 | tf_op jit(solution)/shard_map/reduce_outer/ppermute | solution.py:19
  158.4 1.0 collective-permute-done.26.rest_3_
  159.3 7.9 %collective-permute-done.27.rest_4_ = bf16[8,128,256]{2,1,0:T(8,128)(2,1)S(1)} collective-permute-done((bf16[8,128,256]{2,1,0:T(8,128)(2,1)S(1)}, bf16[8,128,256]{2,1,0:T(8,128)(2,1)S(1)}, u32[]{:S(2)}, u32[]{:S(2)}) %collective-permute-start.27) | collective-permute-done | bytes 524320 | tf_op jit(solution)/shard_map/reduce_outer/ppermute | solution.py:19
  167.3 0.7 collective-permute-done.28.rest_5_
  168.5 3.3 %collective-permute-start.29 = (bf16[2,128,256]{2,1,0:T(8,128)(2,1)S(1)}, bf16[2,128,256]{2,1,0:T(8,128)(2,1)S(1)}, u32[]{:S(2)}, u32[]{:S(2)}) collective-permute-start(bf16[2,128,256]{2,1,0:T(8,128)(2,1)S(1)} %get-tuple-element.38), channel_id=1, source_target_pairs={{0,32},{32,64},{64,96},{96,0},{1,33},{33,65},{65,97},{97,1},{2,34}... | collective-permute-start | bytes 393224 | tf_op jit(solution)/shard_map/reduce_outer/ppermute | solution.py:19
  171.8 0.9 collective-permute-start.30
  172.7 2.4 %collective-permute-start.31 = (bf16[2,128,256]{2,1,0:T(8,128)(2,1)S(1)}, bf16[2,128,256]{2,1,0:T(8,128)(2,1)S(1)}, u32[]{:S(2)}, u32[]{:S(2)}) collective-permute-start(bf16[2,128,256]{2,1,0:T(8,128)(2,1)S(1)} %get-tuple-element.40), channel_id=1, source_target_pairs={{0,96},{32,0},{64,32},{96,64},{1,97},{33,1},{65,33},{97,65},{2,98}... | collective-permute-start | bytes 393224 | tf_op jit(solution)/shard_map/reduce_outer/ppermute | solution.py:19
  175.1 5.2 %collective-permute-start.32 = (bf16[2,128,256]{2,1,0:T(8,128)(2,1)S(1)}, bf16[2,128,256]{2,1,0:T(8,128)(2,1)S(1)}, u32[]{:S(2)}, u32[]{:S(2)}) collective-permute-start(bf16[2,128,256]{2,1,0:T(8,128)(2,1)S(1)} %get-tuple-element.41), channel_id=1, source_target_pairs={{0,8},{8,16},{16,24},{24,0},{1,9},{9,17},{17,25},{25,1},{2,10},{10... | collective-permute-start | bytes 393224 | tf_op jit(solution)/shard_map/reduce_outer/ppermute | solution.py:19
  180.3 2.5 %collective-permute-start.33 = (bf16[2,128,256]{2,1,0:T(8,128)(2,1)S(1)}, bf16[2,128,256]{2,1,0:T(8,128)(2,1)S(1)}, u32[]{:S(2)}, u32[]{:S(2)}) collective-permute-start(bf16[2,128,256]{2,1,0:T(8,128)(2,1)S(1)} %get-tuple-element.42), channel_id=1, source_target_pairs={{0,16},{8,24},{16,0},{24,8},{1,17},{9,25},{17,1},{25,9},{2,18},{10... | collective-permute-start | bytes 393224 | tf_op jit(solution)/shard_map/reduce_outer/ppermute | solution.py:19
  182.8 2.6 %collective-permute-start.34 = (bf16[2,128,256]{2,1,0:T(8,128)(2,1)S(1)}, bf16[2,128,256]{2,1,0:T(8,128)(2,1)S(1)}, u32[]{:S(2)}, u32[]{:S(2)}) collective-permute-start(bf16[2,128,256]{2,1,0:T(8,128)(2,1)S(1)} %get-tuple-element.43), channel_id=1, source_target_pairs={{0,24},{8,0},{16,8},{24,16},{1,25},{9,1},{17,9},{25,17},{2,26},{10... | collective-permute-start | bytes 393224 | tf_op jit(solution)/shard_map/reduce_outer/ppermute | solution.py:19
  185.4 1.7 collective-permute-done.33.rest_4_
  187.1 0.8 collective-permute-done.34.rest_5_
  188.6 1.2 collective-permute-done.35
  189.9 4.7 %collective-permute-start.38 = (f32[128,128]{1,0:T(8,128)S(1)}, f32[128,128]{1,0:T(8,128)S(1)}, u32[]{:S(2)}, u32[]{:S(2)}) collective-permute-start(f32[128,128]{1,0:T(8,128)S(1)} %add.105), channel_id=1, source_target_pairs={{0,6},{2,0},{4,2},{6,4},{1,7},{3,1},{5,3},{7,5},{8,14},{10,8},{12,... | collective-permute-start | bytes 196616 | tf_op jit(solution)/shard_map/reduce_gram/ppermute | solution.py:19
  194.6 4.7 %collective-permute-start.36 = (f32[128,128]{1,0:T(8,128)S(1)}, f32[128,128]{1,0:T(8,128)S(1)}, u32[]{:S(2)}, u32[]{:S(2)}) collective-permute-start(f32[128,128]{1,0:T(8,128)S(1)} %add.105), channel_id=1, source_target_pairs={{0,4},{2,6},{4,0},{6,2},{1,5},{3,7},{5,1},{7,3},{8,12},{10,14},{12... | collective-permute-start | bytes 196616 | tf_op jit(solution)/shard_map/reduce_gram/ppermute | solution.py:19
  199.4 0.8 collective-permute-done.37
  200.1 2.5 %collective-permute-done.36 = f32[128,128]{1,0:T(8,128)S(1)} collective-permute-done((f32[128,128]{1,0:T(8,128)S(1)}, f32[128,128]{1,0:T(8,128)S(1)}, u32[]{:S(2)}, u32[]{:S(2)}) %collective-permute-start.36) | collective-permute-done | bytes 65568 | tf_op jit(solution)/shard_map/reduce_gram/ppermute | solution.py:19
  202.6 3.7 %collective-permute-start.41 = (f32[128,128]{1,0:T(8,128)S(1)}, f32[128,128]{1,0:T(8,128)S(1)}, u32[]{:S(2)}, u32[]{:S(2)}) collective-permute-start(f32[128,128]{1,0:T(8,128)S(1)} %add_add_fusion.2), channel_id=1, source_target_pairs={{0,24},{8,0},{16,8},{24,16},{1,25},{9,1},{17,9},{25,17},{2,26},{10... | collective-permute-start | bytes 196616 | tf_op jit(solution)/shard_map/reduce_gram/ppermute | solution.py:19
  206.4 1.6 collective-permute-start.39
  208.3 4.3 %collective-permute-done.40 = f32[128,128]{1,0:T(8,128)S(1)} collective-permute-done((f32[128,128]{1,0:T(8,128)S(1)}, f32[128,128]{1,0:T(8,128)S(1)}, u32[]{:S(2)}, u32[]{:S(2)}) %collective-permute-start.40) | collective-permute-done | bytes 65568 | tf_op jit(solution)/shard_map/reduce_gram/ppermute | solution.py:19
  212.6 1.4 collective-permute-start.44
  214.0 0.7 collective-permute-start.43
  214.7 0.8 collective-permute-start.42
  215.5 1.4 collective-permute-done.44
  216.9 2.5 %collective-permute-done.43 = f32[128,128]{1,0:T(8,128)S(1)} collective-permute-done((f32[128,128]{1,0:T(8,128)S(1)}, f32[128,128]{1,0:T(8,128)S(1)}, u32[]{:S(2)}, u32[]{:S(2)}) %collective-permute-start.43) | collective-permute-done | bytes 65568 | tf_op jit(solution)/shard_map/reduce_gram/ppermute | solution.py:19
  219.4 1.0 collective-permute-done.42
  220.4 17.4 %finish.1 = (f32[1024,128]{1,0:T(8,128)}, f32[128,128]{1,0:T(8,128)}) custom-call(f32[128,128]{1,0:T(8,128)S(1)} %add_add_fusion.refs_0_, f32[4,128,256]{2,1,0:T(8,128)S(1)} %get-tuple-element.45.refs_1_), custom_call_target="tpu_custom_call" | custom-call | tf_op jit(solution)/shard_map/finish/pallas_call | solution.py:281
  (44 shorter events, 4.7 us)
Async XLA Ops:
  0.6 40.5 %copy-start = (s32[160,2]{0,1:T(2,128)S(1)}, s32[160,2]{0,1:T(2,128)}, u32[]{:S(2)}) copy-start(s32[160,2]{0,1:T(2,128)} %param.6) | copy-start | bytes 3844
  1.6 6.4 %collective-permute-start.2 = (bf16[512,128]{1,0:T(8,128)(2,1)S(1)}, bf16[512,128]{1,0:T(8,128)(2,1)S(1)}, u32[]{:S(2)}, u32[]{:S(2)}) collective-permute-start(bf16[512,128]{1,0:T(8,128)(2,1)S(1)} %get-tuple-element.51), channel_id=1, source_target_pairs={{0,32},{32,64},{64,96},{96,0},{1,33},{33,65},{65,97},{97,1},{2,34}... | collective-permute-start | bytes 393224 | tf_op jit(solution)/shard_map/gather_basis/ppermute | solution.py:19
  3.3 8.7 %collective-permute-start.1 = (bf16[512,128]{1,0:T(8,128)(2,1)S(1)}, bf16[512,128]{1,0:T(8,128)(2,1)S(1)}, u32[]{:S(2)}, u32[]{:S(2)}) collective-permute-start(bf16[512,128]{1,0:T(8,128)(2,1)S(1)} %get-tuple-element.51), channel_id=1, source_target_pairs={{0,64},{32,96},{64,0},{96,32},{1,65},{33,97},{65,1},{97,33},{2,66}... | collective-permute-start | bytes 393224 | tf_op jit(solution)/shard_map/gather_basis/ppermute | solution.py:19
  6.0 6.0 %collective-permute-start = (bf16[512,128]{1,0:T(8,128)(2,1)S(1)}, bf16[512,128]{1,0:T(8,128)(2,1)S(1)}, u32[]{:S(2)}, u32[]{:S(2)}) collective-permute-start(bf16[512,128]{1,0:T(8,128)(2,1)S(1)} %get-tuple-element.51), channel_id=1, source_target_pairs={{0,96},{32,0},{64,32},{96,64},{1,97},{33,1},{65,33},{97,65},{2,98}... | collective-permute-start | bytes 393224 | tf_op jit(solution)/shard_map/gather_basis/ppermute | solution.py:19
  12.1 26.8 %collective-permute-start.5 = (bf16[2048,128]{1,0:T(8,128)(2,1)S(1)}, bf16[2048,128]{1,0:T(8,128)(2,1)S(1)}, u32[]{:S(2)}, u32[]{:S(2)}) collective-permute-start(bf16[2048,128]{1,0:T(8,128)(2,1)S(1)} %pad_maximum_fusion), channel_id=1, source_target_pairs={{0,8},{8,16},{16,24},{24,0},{1,9},{9,17},{17,25},{25,1},{2,10},{10... | collective-permute-start | bytes 1572872 | tf_op jit(solution)/shard_map/gather_basis/ppermute | solution.py:19
  13.7 16.2 %collective-permute-start.8 = (bf16[512,128]{1,0:T(8,128)(2,1)S(1)}, bf16[512,128]{1,0:T(8,128)(2,1)S(1)}, u32[]{:S(2)}, u32[]{:S(2)}) collective-permute-start(bf16[512,128]{1,0:T(8,128)(2,1)S(1)} %get-tuple-element.50), channel_id=1, source_target_pairs={{0,8},{8,16},{16,24},{24,0},{1,9},{9,17},{17,25},{25,1},{2,10},{10... | collective-permute-start | bytes 393224 | tf_op jit(solution)/shard_map/gather_basis/ppermute | solution.py:19
  15.3 19.8 %collective-permute-start.7 = (bf16[512,128]{1,0:T(8,128)(2,1)S(1)}, bf16[512,128]{1,0:T(8,128)(2,1)S(1)}, u32[]{:S(2)}, u32[]{:S(2)}) collective-permute-start(bf16[512,128]{1,0:T(8,128)(2,1)S(1)} %get-tuple-element.50), channel_id=1, source_target_pairs={{0,16},{8,24},{16,0},{24,8},{1,17},{9,25},{17,1},{25,9},{2,18},{10... | collective-permute-start | bytes 393224 | tf_op jit(solution)/shard_map/gather_basis/ppermute | solution.py:19
  16.8 18.2 %collective-permute-start.6 = (bf16[512,128]{1,0:T(8,128)(2,1)S(1)}, bf16[512,128]{1,0:T(8,128)(2,1)S(1)}, u32[]{:S(2)}, u32[]{:S(2)}) collective-permute-start(bf16[512,128]{1,0:T(8,128)(2,1)S(1)} %get-tuple-element.50), channel_id=1, source_target_pairs={{0,24},{8,0},{16,8},{24,16},{1,25},{9,1},{17,9},{25,17},{2,26},{10... | collective-permute-start | bytes 393224 | tf_op jit(solution)/shard_map/gather_basis/ppermute | solution.py:19
  19.2 25.0 %collective-permute-start.4 = (bf16[2048,128]{1,0:T(8,128)(2,1)S(1)}, bf16[2048,128]{1,0:T(8,128)(2,1)S(1)}, u32[]{:S(2)}, u32[]{:S(2)}) collective-permute-start(bf16[2048,128]{1,0:T(8,128)(2,1)S(1)} %pad_maximum_fusion), channel_id=1, source_target_pairs={{0,16},{8,24},{16,0},{24,8},{1,17},{9,25},{17,1},{25,9},{2,18},{10... | collective-permute-start | bytes 1572872 | tf_op jit(solution)/shard_map/gather_basis/ppermute | solution.py:19
  29.9 15.0 %collective-permute-start.3 = (bf16[2048,128]{1,0:T(8,128)(2,1)S(1)}, bf16[2048,128]{1,0:T(8,128)(2,1)S(1)}, u32[]{:S(2)}, u32[]{:S(2)}) collective-permute-start(bf16[2048,128]{1,0:T(8,128)(2,1)S(1)} %pad_maximum_fusion), channel_id=1, source_target_pairs={{0,24},{8,0},{16,8},{24,16},{1,25},{9,1},{17,9},{25,17},{2,26},{10... | collective-permute-start | bytes 1572872 | tf_op jit(solution)/shard_map/gather_basis/ppermute | solution.py:19
  35.1 14.8 %collective-permute-start.11 = (bf16[2048,128]{1,0:T(8,128)(2,1)S(1)}, bf16[2048,128]{1,0:T(8,128)(2,1)S(1)}, u32[]{:S(2)}, u32[]{:S(2)}) collective-permute-start(bf16[2048,128]{1,0:T(8,128)(2,1)S(1)} %pad_maximum_fusion.1), channel_id=1, source_target_pairs={{0,32},{32,64},{64,96},{96,0},{1,33},{33,65},{65,97},{97,1},{2,34}... | collective-permute-start | bytes 1572872 | tf_op jit(solution)/shard_map/gather_basis/ppermute | solution.py:19
  36.5 21.6 %collective-permute-start.10 = (bf16[2048,128]{1,0:T(8,128)(2,1)S(1)}, bf16[2048,128]{1,0:T(8,128)(2,1)}, u32[]{:S(2)}, u32[]{:S(2)}) collective-permute-start(bf16[2048,128]{1,0:T(8,128)(2,1)S(1)} %pad_maximum_fusion.1), channel_id=1, source_target_pairs={{0,64},{32,96},{64,0},{96,32},{1,65},{33,97},{65,1},{97,33},{2,66}... | collective-permute-start | bytes 1572872 | tf_op jit(solution)/shard_map/gather_basis/ppermute | solution.py:19
  38.9 19.2 %collective-permute-start.9 = (bf16[2048,128]{1,0:T(8,128)(2,1)S(1)}, bf16[2048,128]{1,0:T(8,128)(2,1)}, u32[]{:S(2)}, u32[]{:S(2)}) collective-permute-start(bf16[2048,128]{1,0:T(8,128)(2,1)S(1)} %pad_maximum_fusion.1), channel_id=1, source_target_pairs={{0,96},{32,0},{64,32},{96,64},{1,97},{33,1},{65,33},{97,65},{2,98}... | collective-permute-start | bytes 1572872 | tf_op jit(solution)/shard_map/gather_basis/ppermute | solution.py:19
  66.2 4.9 %collective-permute-start.12 = (f32[16,256,128]{2,1,0:T(8,128)S(1)}, f32[16,256,128]{2,1,0:T(8,128)S(1)}, u32[]{:S(2)}, u32[]{:S(2)}) collective-permute-start(f32[16,256,128]{2,1,0:T(8,128)S(1)} %get-tuple-element.25), channel_id=1, source_target_pairs={{0,1},{1,0},{2,3},{3,2},{4,5},{5,4},{6,7},{7,6},{8,9},{9,8},{10,11... | collective-permute-start | bytes 6291464 | tf_op jit(solution)/shard_map/reduce_inner/ppermute | solution.py:19
  71.3 19.6 %collective-permute-start.13 = (f32[4,256,128]{2,1,0:T(8,128)S(1)}, f32[4,256,128]{2,1,0:T(8,128)S(1)}, u32[]{:S(2)}, u32[]{:S(2)}) collective-permute-start(f32[4,256,128]{2,1,0:T(8,128)S(1)} %get-tuple-element.27), channel_id=1, source_target_pairs={{0,2},{2,4},{4,6},{6,0},{1,3},{3,5},{5,7},{7,1},{8,10},{10,12},{12... | collective-permute-start | bytes 1572872 | tf_op jit(solution)/shard_map/reduce_inner/ppermute | solution.py:19
  74.9 28.4 %collective-permute-start.14 = (f32[4,256,128]{2,1,0:T(8,128)S(1)}, f32[4,256,128]{2,1,0:T(8,128)S(1)}, u32[]{:S(2)}, u32[]{:S(2)}) collective-permute-start(f32[4,256,128]{2,1,0:T(8,128)S(1)} %get-tuple-element.28), channel_id=1, source_target_pairs={{0,4},{2,6},{4,0},{6,2},{1,5},{3,7},{5,1},{7,3},{8,12},{10,14},{12... | collective-permute-start | bytes 1572872 | tf_op jit(solution)/shard_map/reduce_inner/ppermute | solution.py:19
  80.2 23.2 %collective-permute-start.15 = (f32[4,256,128]{2,1,0:T(8,128)S(1)}, f32[4,256,128]{2,1,0:T(8,128)S(1)}, u32[]{:S(2)}, u32[]{:S(2)}) collective-permute-start(f32[4,256,128]{2,1,0:T(8,128)S(1)} %get-tuple-element.29), channel_id=1, source_target_pairs={{0,6},{2,0},{4,2},{6,4},{1,7},{3,1},{5,3},{7,5},{8,14},{10,8},{12,... | collective-permute-start | bytes 1572872 | tf_op jit(solution)/shard_map/reduce_inner/ppermute | solution.py:19
  103.5 8.8 %collective-permute-start.18 = (bf16[4,128,256]{2,1,0:T(8,128)(2,1)S(1)}, bf16[4,128,256]{2,1,0:T(8,128)(2,1)S(1)}, u32[]{:S(2)}, u32[]{:S(2)}) collective-permute-start(bf16[4,128,256]{2,1,0:T(8,128)(2,1)S(1)} %inner_sum.1.rest_0_), channel_id=1, source_target_pairs={{0,2},{2,4},{4,6},{6,0},{1,3},{3,5},{5,7},{7,1},{8,10},{10,12},{12... | collective-permute-start | bytes 786440 | tf_op jit(solution)/shard_map/gather_inner/ppermute | solution.py:19
  104.5 14.5 %collective-permute-start.17 = (bf16[4,128,256]{2,1,0:T(8,128)(2,1)S(1)}, bf16[4,128,256]{2,1,0:T(8,128)(2,1)S(1)}, u32[]{:S(2)}, u32[]{:S(2)}) collective-permute-start(bf16[4,128,256]{2,1,0:T(8,128)(2,1)S(1)} %inner_sum.1.rest_0_), channel_id=1, source_target_pairs={{0,4},{2,6},{4,0},{6,2},{1,5},{3,7},{5,1},{7,3},{8,12},{10,14},{12... | collective-permute-start | bytes 786440 | tf_op jit(solution)/shard_map/gather_inner/ppermute | solution.py:19
  107.2 11.8 %collective-permute-start.16 = (bf16[4,128,256]{2,1,0:T(8,128)(2,1)S(1)}, bf16[4,128,256]{2,1,0:T(8,128)(2,1)S(1)}, u32[]{:S(2)}, u32[]{:S(2)}) collective-permute-start(bf16[4,128,256]{2,1,0:T(8,128)(2,1)S(1)} %inner_sum.1.rest_0_), channel_id=1, source_target_pairs={{0,6},{2,0},{4,2},{6,4},{1,7},{3,1},{5,3},{7,5},{8,14},{10,8},{12,... | collective-permute-start | bytes 786440 | tf_op jit(solution)/shard_map/gather_inner/ppermute | solution.py:19
  107.8 11.7 %collective-permute-start.19 = (bf16[4,128,256]{2,1,0:T(8,128)(2,1)S(1)}, bf16[4,128,256]{2,1,0:T(8,128)(2,1)S(1)}, u32[]{:S(2)}, u32[]{:S(2)}) collective-permute-start(bf16[4,128,256]{2,1,0:T(8,128)(2,1)S(1)} %inner_sum.1.rest_0_), channel_id=1, source_target_pairs={{0,1},{1,0},{2,3},{3,2},{4,5},{5,4},{6,7},{7,6},{8,9},{9,8},{10,11... | collective-permute-start | bytes 786440 | tf_op jit(solution)/shard_map/gather_inner/ppermute | solution.py:19
  112.3 7.2 %collective-permute-start.22 = (bf16[4,128,256]{2,1,0:T(8,128)(2,1)S(1)}, bf16[4,128,256]{2,1,0:T(8,128)(2,1)S(1)}, u32[]{:S(2)}, u32[]{:S(2)}) collective-permute-start(bf16[4,128,256]{2,1,0:T(8,128)(2,1)S(1)} %collective-permute-done.18.rest_3_), channel_id=1, source_target_pairs={{0,1},{1,0},{2,3},{3,2},{4,5},{5,4},{6,7},{7,6},{8,9},{9,8},{10,11... | collective-permute-start | bytes 786440 | tf_op jit(solution)/shard_map/gather_inner/ppermute | solution.py:19
  119.0 1.5 collective-permute-start.21
  119.0 1.9 collective-permute-start.20
  128.0 18.9 %collective-permute-start.23 = (bf16[8,128,256]{2,1,0:T(8,128)(2,1)S(1)}, bf16[8,128,256]{2,1,0:T(8,128)(2,1)S(1)}, u32[]{:S(2)}, u32[]{:S(2)}) collective-permute-start(bf16[8,128,256]{2,1,0:T(8,128)(2,1)S(1)} %get-tuple-element.31), channel_id=1, source_target_pairs={{0,8},{8,16},{16,24},{24,0},{1,9},{9,17},{17,25},{25,1},{2,10},{10... | collective-permute-start | bytes 1572872 | tf_op jit(solution)/shard_map/reduce_outer/ppermute | solution.py:19
  128.1 30.2 %collective-permute-start.24 = (bf16[8,128,256]{2,1,0:T(8,128)(2,1)S(1)}, bf16[8,128,256]{2,1,0:T(8,128)(2,1)S(1)}, u32[]{:S(2)}, u32[]{:S(2)}) collective-permute-start(bf16[8,128,256]{2,1,0:T(8,128)(2,1)S(1)} %get-tuple-element.32), channel_id=1, source_target_pairs={{0,16},{8,24},{16,0},{24,8},{1,17},{9,25},{17,1},{25,9},{2,18},{10... | collective-permute-start | bytes 1572872 | tf_op jit(solution)/shard_map/reduce_outer/ppermute | solution.py:19
  134.6 23.8 %collective-permute-start.25 = (bf16[8,128,256]{2,1,0:T(8,128)(2,1)S(1)}, bf16[8,128,256]{2,1,0:T(8,128)(2,1)S(1)}, u32[]{:S(2)}, u32[]{:S(2)}) collective-permute-start(bf16[8,128,256]{2,1,0:T(8,128)(2,1)S(1)} %get-tuple-element.33), channel_id=1, source_target_pairs={{0,24},{8,0},{16,8},{24,16},{1,25},{9,1},{17,9},{25,17},{2,26},{10... | collective-permute-start | bytes 1572872 | tf_op jit(solution)/shard_map/reduce_outer/ppermute | solution.py:19
  137.1 22.2 %collective-permute-start.26 = (bf16[8,128,256]{2,1,0:T(8,128)(2,1)S(1)}, bf16[8,128,256]{2,1,0:T(8,128)(2,1)S(1)}, u32[]{:S(2)}, u32[]{:S(2)}) collective-permute-start(bf16[8,128,256]{2,1,0:T(8,128)(2,1)S(1)} %get-tuple-element.34), channel_id=1, source_target_pairs={{0,32},{32,64},{64,96},{96,0},{1,33},{33,65},{65,97},{97,1},{2,34}... | collective-permute-start | bytes 1572872 | tf_op jit(solution)/shard_map/reduce_outer/ppermute | solution.py:19
  147.0 20.3 %collective-permute-start.27 = (bf16[8,128,256]{2,1,0:T(8,128)(2,1)S(1)}, bf16[8,128,256]{2,1,0:T(8,128)(2,1)S(1)}, u32[]{:S(2)}, u32[]{:S(2)}) collective-permute-start(bf16[8,128,256]{2,1,0:T(8,128)(2,1)S(1)} %get-tuple-element.35), channel_id=1, source_target_pairs={{0,64},{32,96},{64,0},{96,32},{1,65},{33,97},{65,1},{97,33},{2,66}... | collective-permute-start | bytes 1572872 | tf_op jit(solution)/shard_map/reduce_outer/ppermute | solution.py:19
  147.0 21.1 %collective-permute-start.28 = (bf16[8,128,256]{2,1,0:T(8,128)(2,1)S(1)}, bf16[8,128,256]{2,1,0:T(8,128)(2,1)S(1)}, u32[]{:S(2)}, u32[]{:S(2)}) collective-permute-start(bf16[8,128,256]{2,1,0:T(8,128)(2,1)S(1)} %get-tuple-element.36), channel_id=1, source_target_pairs={{0,96},{32,0},{64,32},{96,64},{1,97},{33,1},{65,33},{97,65},{2,98}... | collective-permute-start | bytes 1572872 | tf_op jit(solution)/shard_map/reduce_outer/ppermute | solution.py:19
  168.5 14.3 %collective-permute-start.29 = (bf16[2,128,256]{2,1,0:T(8,128)(2,1)S(1)}, bf16[2,128,256]{2,1,0:T(8,128)(2,1)S(1)}, u32[]{:S(2)}, u32[]{:S(2)}) collective-permute-start(bf16[2,128,256]{2,1,0:T(8,128)(2,1)S(1)} %get-tuple-element.38), channel_id=1, source_target_pairs={{0,32},{32,64},{64,96},{96,0},{1,33},{33,65},{65,97},{97,1},{2,34}... | collective-permute-start | bytes 393224 | tf_op jit(solution)/shard_map/reduce_outer/ppermute | solution.py:19
  171.8 13.6 %collective-permute-start.30 = (bf16[2,128,256]{2,1,0:T(8,128)(2,1)S(1)}, bf16[2,128,256]{2,1,0:T(8,128)(2,1)S(1)}, u32[]{:S(2)}, u32[]{:S(2)}) collective-permute-start(bf16[2,128,256]{2,1,0:T(8,128)(2,1)S(1)} %get-tuple-element.39), channel_id=1, source_target_pairs={{0,64},{32,96},{64,0},{96,32},{1,65},{33,97},{65,1},{97,33},{2,66}... | collective-permute-start | bytes 393224 | tf_op jit(solution)/shard_map/reduce_outer/ppermute | solution.py:19
  172.7 12.7 %collective-permute-start.31 = (bf16[2,128,256]{2,1,0:T(8,128)(2,1)S(1)}, bf16[2,128,256]{2,1,0:T(8,128)(2,1)S(1)}, u32[]{:S(2)}, u32[]{:S(2)}) collective-permute-start(bf16[2,128,256]{2,1,0:T(8,128)(2,1)S(1)} %get-tuple-element.40), channel_id=1, source_target_pairs={{0,96},{32,0},{64,32},{96,64},{1,97},{33,1},{65,33},{97,65},{2,98}... | collective-permute-start | bytes 393224 | tf_op jit(solution)/shard_map/reduce_outer/ppermute | solution.py:19
  175.1 10.3 %collective-permute-start.32 = (bf16[2,128,256]{2,1,0:T(8,128)(2,1)S(1)}, bf16[2,128,256]{2,1,0:T(8,128)(2,1)S(1)}, u32[]{:S(2)}, u32[]{:S(2)}) collective-permute-start(bf16[2,128,256]{2,1,0:T(8,128)(2,1)S(1)} %get-tuple-element.41), channel_id=1, source_target_pairs={{0,8},{8,16},{16,24},{24,0},{1,9},{9,17},{17,25},{25,1},{2,10},{10... | collective-permute-start | bytes 393224 | tf_op jit(solution)/shard_map/reduce_outer/ppermute | solution.py:19
  180.3 6.9 %collective-permute-start.33 = (bf16[2,128,256]{2,1,0:T(8,128)(2,1)S(1)}, bf16[2,128,256]{2,1,0:T(8,128)(2,1)S(1)}, u32[]{:S(2)}, u32[]{:S(2)}) collective-permute-start(bf16[2,128,256]{2,1,0:T(8,128)(2,1)S(1)} %get-tuple-element.42), channel_id=1, source_target_pairs={{0,16},{8,24},{16,0},{24,8},{1,17},{9,25},{17,1},{25,9},{2,18},{10... | collective-permute-start | bytes 393224 | tf_op jit(solution)/shard_map/reduce_outer/ppermute | solution.py:19
  182.8 5.2 %collective-permute-start.34 = (bf16[2,128,256]{2,1,0:T(8,128)(2,1)S(1)}, bf16[2,128,256]{2,1,0:T(8,128)(2,1)S(1)}, u32[]{:S(2)}, u32[]{:S(2)}) collective-permute-start(bf16[2,128,256]{2,1,0:T(8,128)(2,1)S(1)} %get-tuple-element.43), channel_id=1, source_target_pairs={{0,24},{8,0},{16,8},{24,16},{1,25},{9,1},{17,9},{25,17},{2,26},{10... | collective-permute-start | bytes 393224 | tf_op jit(solution)/shard_map/reduce_outer/ppermute | solution.py:19
  188.6 1.3 collective-permute-start.35
  189.9 9.5 %collective-permute-start.38 = (f32[128,128]{1,0:T(8,128)S(1)}, f32[128,128]{1,0:T(8,128)S(1)}, u32[]{:S(2)}, u32[]{:S(2)}) collective-permute-start(f32[128,128]{1,0:T(8,128)S(1)} %add.105), channel_id=1, source_target_pairs={{0,6},{2,0},{4,2},{6,4},{1,7},{3,1},{5,3},{7,5},{8,14},{10,8},{12,... | collective-permute-start | bytes 196616 | tf_op jit(solution)/shard_map/reduce_gram/ppermute | solution.py:19
  194.6 5.6 %collective-permute-start.37 = (f32[128,128]{1,0:T(8,128)S(1)}, f32[128,128]{1,0:T(8,128)S(1)}, u32[]{:S(2)}, u32[]{:S(2)}) collective-permute-start(f32[128,128]{1,0:T(8,128)S(1)} %add.105), channel_id=1, source_target_pairs={{0,2},{2,4},{4,6},{6,0},{1,3},{3,5},{5,7},{7,1},{8,10},{10,12},{12... | collective-permute-start | bytes 196616 | tf_op jit(solution)/shard_map/reduce_gram/ppermute | solution.py:19
  194.6 8.0 %collective-permute-start.36 = (f32[128,128]{1,0:T(8,128)S(1)}, f32[128,128]{1,0:T(8,128)S(1)}, u32[]{:S(2)}, u32[]{:S(2)}) collective-permute-start(f32[128,128]{1,0:T(8,128)S(1)} %add.105), channel_id=1, source_target_pairs={{0,4},{2,6},{4,0},{6,2},{1,5},{3,7},{5,1},{7,3},{8,12},{10,14},{12... | collective-permute-start | bytes 196616 | tf_op jit(solution)/shard_map/reduce_gram/ppermute | solution.py:19
  202.6 5.6 %collective-permute-start.41 = (f32[128,128]{1,0:T(8,128)S(1)}, f32[128,128]{1,0:T(8,128)S(1)}, u32[]{:S(2)}, u32[]{:S(2)}) collective-permute-start(f32[128,128]{1,0:T(8,128)S(1)} %add_add_fusion.2), channel_id=1, source_target_pairs={{0,24},{8,0},{16,8},{24,16},{1,25},{9,1},{17,9},{25,17},{2,26},{10... | collective-permute-start | bytes 196616 | tf_op jit(solution)/shard_map/reduce_gram/ppermute | solution.py:19
  206.4 6.2 %collective-permute-start.40 = (f32[128,128]{1,0:T(8,128)S(1)}, f32[128,128]{1,0:T(8,128)S(1)}, u32[]{:S(2)}, u32[]{:S(2)}) collective-permute-start(f32[128,128]{1,0:T(8,128)S(1)} %add_add_fusion.2), channel_id=1, source_target_pairs={{0,8},{8,16},{16,24},{24,0},{1,9},{9,17},{17,25},{25,1},{2,10},{10... | collective-permute-start | bytes 196616 | tf_op jit(solution)/shard_map/reduce_gram/ppermute | solution.py:19
  206.4 6.2 %collective-permute-start.39 = (f32[128,128]{1,0:T(8,128)S(1)}, f32[128,128]{1,0:T(8,128)S(1)}, u32[]{:S(2)}, u32[]{:S(2)}) collective-permute-start(f32[128,128]{1,0:T(8,128)S(1)} %add_add_fusion.2), channel_id=1, source_target_pairs={{0,16},{8,24},{16,0},{24,8},{1,17},{9,25},{17,1},{25,9},{2,18},{10... | collective-permute-start | bytes 196616 | tf_op jit(solution)/shard_map/reduce_gram/ppermute | solution.py:19
  212.6 4.3 %collective-permute-start.44 = (f32[128,128]{1,0:T(8,128)S(1)}, f32[128,128]{1,0:T(8,128)S(1)}, u32[]{:S(2)}, u32[]{:S(2)}) collective-permute-start(f32[128,128]{1,0:T(8,128)S(1)} %add_add_fusion.1), channel_id=1, source_target_pairs={{0,96},{32,0},{64,32},{96,64},{1,97},{33,1},{65,33},{97,65},{2,98}... | collective-permute-start | bytes 196616 | tf_op jit(solution)/shard_map/reduce_gram/ppermute | solution.py:19
  214.0 5.5 %collective-permute-start.43 = (f32[128,128]{1,0:T(8,128)S(1)}, f32[128,128]{1,0:T(8,128)S(1)}, u32[]{:S(2)}, u32[]{:S(2)}) collective-permute-start(f32[128,128]{1,0:T(8,128)S(1)} %add_add_fusion.1), channel_id=1, source_target_pairs={{0,32},{32,64},{64,96},{96,0},{1,33},{33,65},{65,97},{97,1},{2,34}... | collective-permute-start | bytes 196616 | tf_op jit(solution)/shard_map/reduce_gram/ppermute | solution.py:19
  214.7 5.8 %collective-permute-start.42 = (f32[128,128]{1,0:T(8,128)S(1)}, f32[128,128]{1,0:T(8,128)S(1)}, u32[]{:S(2)}, u32[]{:S(2)}) collective-permute-start(f32[128,128]{1,0:T(8,128)S(1)} %add_add_fusion.1), channel_id=1, source_target_pairs={{0,64},{32,96},{64,0},{96,32},{1,65},{33,97},{65,1},{97,33},{2,66}... | collective-permute-start | bytes 196616 | tf_op jit(solution)/shard_map/reduce_gram/ppermute | solution.py:19

commit v2 on v1

--- a/solution.py
+++ b/solution.py
@@ -9,7 +9,8 @@
 SIZES = {"x": 4, "y": 4, "z": 4, "core": 2}
 SIDE = 256
 RANK = 128
-CHUNK = 8
+CHUNK = 20
+WINDOW = 3
 F32 = jnp.float32
 BF16 = jnp.bfloat16
 
@@ -39,41 +40,49 @@
     return copies
 
 
+def tile_window(count, tiles, window, sems):
+    chunks = (count[0] + CHUNK - 1) // CHUNK
+
+    def copy(i):
+        at = pl.ds(i * CHUNK, CHUNK)
+        return pltpu.make_async_copy(tiles.at[at], window.at[at], sems.at[i])
+
+    def start(i):
+        @pl.when(i < chunks)
+        def _():
+            copy(i).start()
+
+    return chunks, copy, start
+
+
 def forward_kernel(count, row_at, col_at, tiles, *rest):
-    pieces, (keep, away, held, total, sems, out_sems) = rest[:8], rest[8:]
-    step = pl.program_id(0)
-
-    @pl.when(step == 0)
-    def _():
-        copies = load_pieces(pieces, held, sems)
-        total[...] = jnp.zeros_like(total)
-        for copy in copies:
-            copy.wait()
-
-    @pl.when(step * CHUNK < count[0])
-    def _():
+    pieces, (keep, away, held, total, window, sems, tile_sems) = rest[:8], rest[8:]
+    chunks, copy, start = tile_window(count, tiles, window, tile_sems)
+    copies = load_pieces(pieces, held, sems)
+    for i in range(WINDOW):
+        start(i)
+    total[...] = jnp.zeros_like(total)
+    for one in copies:
+        one.wait()
+
+    def body(i, _):
+        copy(i).wait()
+        start(i + WINDOW)
         for k in range(CHUNK):
-            slot = step * CHUNK + k
-            row = row_at[slot]
-            col = col_at[slot]
-            total[row] += jnp.dot(tiles[k], held[col], preferred_element_type=F32)
-
-    @pl.when(step == pl.num_programs(0) - 1)
-    def _():
-        half = keep.shape[0]
-        one = pltpu.make_async_copy(total.at[pl.ds(half, half)], away, out_sems.at[0])
-        two = pltpu.make_async_copy(total.at[pl.ds(0, half)], keep, out_sems.at[1])
-        one.start()
-        two.start()
-        one.wait()
-        two.wait()
-
-
-def tile_spec():
-    def index(step, count, row_at, col_at):
-        return (jnp.minimum(step, (count[0] - 1) // CHUNK), 0, 0)
-
-    return pl.BlockSpec((CHUNK, SIDE, SIDE), index)
+            slot = i * CHUNK + k
+            total[row_at[slot]] += jnp.dot(
+                window[slot], held[col_at[slot]], preferred_element_type=F32
+            )
+        return 0
+
+    lax.fori_loop(0, chunks, body, 0)
+    half = keep.shape[0]
+    one = pltpu.make_async_copy(total.at[pl.ds(half, half)], away, sems.at[0])
+    two = pltpu.make_async_copy(total.at[pl.ds(0, half)], keep, sems.at[1])
+    one.start()
+    two.start()
+    one.wait()
+    two.wait()
 
 
 def forward(count, row_at, col_at, tiles, pieces):
@@ -83,48 +92,46 @@
     return pl.pallas_call(
         forward_kernel,
         out_shape=(half, half),
-        grid_spec=pltpu.PrefetchScalarGridSpec(
-            num_scalar_prefetch=3,
-            grid=(slots // CHUNK,),
-            in_specs=[tile_spec()] + [any_spec] * 8,
-            out_specs=(any_spec, any_spec),
-            scratch_shapes=[
-                pltpu.VMEM((64, SIDE, RANK), BF16),
-                pltpu.VMEM((33, SIDE, RANK), F32),
-                pltpu.SemaphoreType.DMA((8,)),
-                pltpu.SemaphoreType.DMA((2,)),
-            ],
-        ),
-        compiler_params=limits(32),
+        in_specs=[pl.BlockSpec(memory_space=pltpu.SMEM)] * 3 + [any_spec] * 9,
+        out_specs=(any_spec, any_spec),
+        scratch_shapes=[
+            pltpu.VMEM((64, SIDE, RANK), BF16),
+            pltpu.VMEM((33, SIDE, RANK), F32),
+            pltpu.VMEM((slots, SIDE, SIDE), BF16),
+            pltpu.SemaphoreType.DMA((8,)),
+            pltpu.SemaphoreType.DMA((slots // CHUNK,)),
+        ],
+        compiler_params=limits(36),
         name="forward",
     )(count, row_at, col_at, tiles, *pieces)
 
 
 def backward_kernel(count, row_at, col_at, tiles, *rest):
-    pieces, keep, aways, (held, total, sems) = rest[:8], rest[8], rest[9:15], rest[15:]
-    step = pl.program_id(0)
-
-    @pl.when(step == 0)
-    def _():
-        copies = load_pieces(pieces, held, sems)
-        total[...] = jnp.zeros_like(total)
-        for copy in copies:
-            copy.wait()
-
-    @pl.when(step * CHUNK < count[0])
-    def _():
+    pieces, keep, aways = rest[:8], rest[8], rest[9:15]
+    held, total, window, sems, tile_sems = rest[15:]
+    chunks, copy, start = tile_window(count, tiles, window, tile_sems)
+    copies = load_pieces(pieces, held, sems)
+    for i in range(WINDOW):
+        start(i)
+    total[...] = jnp.zeros_like(total)
+    for one in copies:
+        one.wait()
+
+    def body(i, _):
+        copy(i).wait()
+        start(i + WINDOW)
         for k in range(CHUNK):
-            slot = step * CHUNK + k
-            row = row_at[slot]
-            col = col_at[slot]
-            total[col] += jnp.dot(held[row], tiles[k], preferred_element_type=F32)
-
-    @pl.when(step == pl.num_programs(0) - 1)
-    def _():
-        for h in range(2):
-            keep[h] = total[pl.ds(32 * h, 8)]
-            for d in range(3):
-                aways[3 * h + d][...] = total[pl.ds(32 * h + 8 * (d + 1), 8)].astype(BF16)
+            slot = i * CHUNK + k
+            total[col_at[slot]] += jnp.dot(
+                held[row_at[slot]], window[slot], preferred_element_type=F32
+            )
+        return 0
+
+    lax.fori_loop(0, chunks, body, 0)
+    for h in range(2):
+        keep[h] = total[pl.ds(32 * h, 8)]
+        for d in range(3):
+            aways[3 * h + d][...] = total[pl.ds(32 * h + 8 * (d + 1), 8)].astype(BF16)
 
 
 def backward(count, row_at, col_at, tiles, pieces):
@@ -134,18 +141,16 @@
     return pl.pallas_call(
         backward_kernel,
         out_shape=(jax.ShapeDtypeStruct((2, 8, RANK, SIDE), F32),) + (part,) * 6,
-        grid_spec=pltpu.PrefetchScalarGridSpec(
-            num_scalar_prefetch=3,
-            grid=(slots // CHUNK,),
-            in_specs=[tile_spec()] + [any_spec] * 8,
-            out_specs=tuple(whole(7)),
-            scratch_shapes=[
-                pltpu.VMEM((32, RANK, SIDE), BF16),
-                pltpu.VMEM((65, RANK, SIDE), F32),
-                pltpu.SemaphoreType.DMA((8,)),
-            ],
-        ),
-        compiler_params=limits(40),
+        in_specs=[pl.BlockSpec(memory_space=pltpu.SMEM)] * 3 + [any_spec] * 9,
+        out_specs=tuple(whole(7)),
+        scratch_shapes=[
+            pltpu.VMEM((32, RANK, SIDE), BF16),
+            pltpu.VMEM((65, RANK, SIDE), F32),
+            pltpu.VMEM((slots, SIDE, SIDE), BF16),
+            pltpu.SemaphoreType.DMA((8,)),
+            pltpu.SemaphoreType.DMA((slots // CHUNK,)),
+        ],
+        compiler_params=limits(44),
         name="backward",
     )(count, row_at, col_at, tiles, *pieces)
 
@@ -244,28 +249,53 @@
     )(keep, *came)
 
 
+def wide(value):
+    return jnp.broadcast_to(value, (8, RANK))
+
+
 def finish_kernel(scale, gram, outer, basis, factor, work):
     rows = lax.broadcasted_iota(jnp.int32, (RANK, RANK), 0)
     cols = lax.broadcasted_iota(jnp.int32, (RANK, RANK), 1)
+    sub = lax.broadcasted_iota(jnp.int32, (8, RANK), 0)
     work[:, :RANK] = gram[...]
     work[:, RANK:] = jnp.where(rows == cols, 1.0, 0.0)
-    sub = lax.broadcasted_iota(jnp.int32, (8, 2 * RANK), 0)
     for j in range(0, RANK, 8):
-        panel = work[j : j + 8, :]
+        halves = [work[j : j + 8, :RANK], work[j : j + 8, RANK:]]
+        diag = [
+            [wide(halves[0][r : r + 1, j + s : j + s + 1]) for s in range(r + 1)]
+            for r in range(8)
+        ]
+        upper = [[wide(half[r : r + 1, :]) for half in halves] for r in range(8)]
+        lower = [[None] * 8 for _ in range(8)]
+        root = [None] * 8
         for i in range(8):
-            column = panel[:, j + i : j + i + 1]
-            pivot = panel[i : i + 1, j + i : j + i + 1]
-            root = lax.rsqrt(pivot)
-            root = root * (1.5 - 0.5 * pivot * root * root)
-            row = panel[i : i + 1, :] * root
-            panel = jnp.where(
-                sub == i, row, jnp.where(sub > i, panel - (column * root) * row, panel)
-            )
-        work[j : j + 8, :] = panel
-        if j + 8 < RANK:
-            lower = panel[:, :RANK]
-            update = exact_dot(lower, panel, ((0,), (0,)))
-            work[j + 8 :, :] -= update[j + 8 :, :]
+            root[i] = lax.rsqrt(diag[i][i])
+            for r in range(i + 1, 8):
+                lower[r][i] = diag[r][i] * root[i]
+            for r in range(i + 1, 8):
+                for s in range(i + 1, r + 1):
+                    diag[r][s] = diag[r][s] - lower[r][i] * lower[s][i]
+            upper[i] = [one * root[i] for one in upper[i]]
+            for r in range(i + 1, 8):
+                upper[r] = [a - lower[r][i] * b for a, b in zip(upper[r], upper[i])]
+        for h in range(2):
+            panel = upper[0][h]
+            for r in range(1, 8):
+                panel = jnp.where(sub == r, upper[r][h], panel)
+            work[j : j + 8, h * RANK : (h + 1) * RANK] = panel
+        for g in range(j + 8, RANK, 8):
+            halves = [work[g : g + 8, :RANK], work[g : g + 8, RANK:]]
+            column = []
+            for k in range(8):
+                one = wide(halves[0][:, j + k : j + k + 1])
+                for i in range(k):
+                    one = one - column[i] * lower[k][i]
+                column.append(one * root[k])
+            for h in range(2):
+                block = halves[h]
+                for k in range(8):
+                    block = block - column[k] * upper[k][h]
+                work[g : g + 8, h * RANK : (h + 1) * RANK] = block
     factor[...] = jnp.where(cols >= rows, work[:, :RANK], 0.0) * (1.0 / scale)
     inverse = work[:, RANK:] * scale
     for b in range(outer.shape[0]):
@@ -309,10 +339,12 @@
     with jax.named_scope("gather_basis"):
         halves = (basis_in[: 2 * SIDE], basis_in[2 * SIDE :])
         orders = (("x", "y"), ("y", "x"))
-        firsts = [
-            jnp.concatenate([half] + [send(half, order[0], -d) for d in (1, 2, 3)], axis=0)
+        near = [
+            [half] + [send(half, order[0], -d) for d in (1, 2, 3)]
             for half, order in zip(halves, orders)
         ]
+        near = lax.optimization_barrier(near)
+        firsts = [jnp.concatenate(four, axis=0) for four in near]
         pieces = []
         for first, order in zip(firsts, orders):
             pieces += [first] + [send(first, order[1], -d) for d in (1, 2, 3)]

time: 237 us -> 202 us (0.85); the launches traced: 238 us -> 200 us
  starting transfers between devices: 98.6 us -> 70.2 us
  Pallas kernels: 34 us -> 18.4 us
  waiting for transfers between devices: 103 us -> 108 us
    ppermute x45, starting transfers between devices: 98.6 us -> 70.2 us  [send(): lax.ppermute(array, axis, [(i, (i + step) % size) for i in range(size)])]
    pallas_call x1, Pallas kernels: 17.4 us -> 5.91 us  [finish(): pl.pallas_call(kernel, out_shape=(jax.ShapeDtypeStruct((4 * SIDE, RANK),...]
    ppermute x45, waiting for transfers between devices: 103 us -> 108 us  [send(): lax.ppermute(array, axis, [(i, (i + step) % size) for i in range(size)])]
  transfers between devices with their start and end apart: 45 -> 45, of which waited for: 29 -> 30; matrix products, arithmetic and copies ran while one was open for 0% -> 0% of each run, Pallas kernels for 0% -> 0%
where the time goes in v2:
time: 202 us; the launch traced here: 200 us
  waiting for transfers between devices  108 us (53%)
  starting transfers between devices  70.2 us (35%)
  Pallas kernels  18.4 us (9%)
    ppermute x45, waiting for transfers between devices, send(): lax.ppermute(array, axis, [(i, (i + step) % size) for i in range(size)])  108 us
    ppermute x45, starting transfers between devices, send(): lax.ppermute(array, axis, [(i, (i + step) % size) for i in range(size)])  70.2 us
    pallas_call x1, Pallas kernels, finish(): pl.pallas_call(kernel, out_shape=(jax.ShapeDtypeStruct((4 * SIDE, RANK),...  5.91 us
    pallas_call x1, Pallas kernels, forward(): pl.pallas_call(forward_kernel, out_shape=(half, half), in_specs=[pl.Block...  5.71 us
    pallas_call x1, Pallas kernels, backward(): pl.pallas_call(backward_kernel, out_shape=(jax.ShapeDtypeStruct((2, 8, RA...  5.22 us
  transfers between devices with their start and end apart: 45, of which 30 were waited for; matrix products, arithmetic and copies ran while one was open for 0% of the time, Pallas kernels for 0%

profile of v2, /device:TPU:0, one launch (start us, length us, event | category | flops | bytes accessed | tf_op | source)
XLA Modules:
  0.0 199.7 jit_solution(7125434051257035399)
XLA Ops:
  0.6 1.0 fusion.12
  1.6 1.7 collective-permute-start.5
  3.4 2.9 %collective-permute-start.4 = (bf16[512,128]{1,0:T(8,128)(2,1)S(1)}, bf16[512,128]{1,0:T(8,128)(2,1)S(1)}, u32[]{:S(2)}, u32[]{:S(2)}) collective-permute-start(bf16[512,128]{1,0:T(8,128)(2,1)S(1)} %get-tuple-element.36), channel_id=1, source_target_pairs={{0,16},{8,24},{16,0},{24,8},{1,17},{9,25},{17,1},{25,9},{2,18},{10... | collective-permute-start | bytes 393224 | tf_op jit(solution)/shard_map/gather_basis/ppermute | solution.py:20
  6.3 1.3 collective-permute-start.3
  7.6 1.5 collective-permute-start.2
  9.1 2.7 %collective-permute-start.1 = (bf16[512,128]{1,0:T(8,128)(2,1)S(1)}, bf16[512,128]{1,0:T(8,128)(2,1)S(1)}, u32[]{:S(2)}, u32[]{:S(2)}) collective-permute-start(bf16[512,128]{1,0:T(8,128)(2,1)S(1)} %get-tuple-element.32), channel_id=1, source_target_pairs={{0,64},{32,96},{64,0},{96,32},{1,65},{33,97},{65,1},{97,33},{2,66}... | collective-permute-start | bytes 393224 | tf_op jit(solution)/shard_map/gather_basis/ppermute | solution.py:20
  11.8 1.4 collective-permute-start
  13.3 1.9 collective-permute-done.2
  15.2 1.8 collective-permute-done.1
  17.2 1.3 collective-permute-start.11
  18.5 2.9 %collective-permute-start.10 = (bf16[2048,128]{1,0:T(8,128)(2,1)S(1)}, bf16[2048,128]{1,0:T(8,128)(2,1)S(1)}, u32[]{:S(2)}, u32[]{:S(2)}) collective-permute-start(bf16[2048,128]{1,0:T(8,128)(2,1)S(1)} %constant_dynamic-update-slice_fusion.4), channel_id=1, source_target_pairs={{0,64},{32,96},{64,0},{96,32},{1,65},{33,97},{65,1},{97,33},{2,66}... | collective-permute-start | bytes 1572872 | tf_op jit(solution)/shard_map/gather_basis/ppermute | solution.py:20
  21.4 1.1 collective-permute-start.9
  22.6 0.7 collective-permute-start.8
  23.3 1.1 collective-permute-start.7
  24.4 7.8 %collective-permute-done.11 = bf16[2048,128]{1,0:T(8,128)(2,1)S(1)} collective-permute-done((bf16[2048,128]{1,0:T(8,128)(2,1)S(1)}, bf16[2048,128]{1,0:T(8,128)(2,1)S(1)}, u32[]{:S(2)}, u32[]{:S(2)}) %collective-permute-start.11) | collective-permute-done | bytes 524320 | tf_op jit(solution)/shard_map/gather_basis/ppermute | solution.py:20
  33.0 9.7 %collective-permute-done.10 = bf16[2048,128]{1,0:T(8,128)(2,1)S(1)} collective-permute-done((bf16[2048,128]{1,0:T(8,128)(2,1)S(1)}, bf16[2048,128]{1,0:T(8,128)(2,1)S(1)}, u32[]{:S(2)}, u32[]{:S(2)}) %collective-permute-start.10) | collective-permute-done | bytes 524320 | tf_op jit(solution)/shard_map/gather_basis/ppermute | solution.py:20
  42.8 3.1 %collective-permute-done.8 = bf16[2048,128]{1,0:T(8,128)(2,1)S(1)} collective-permute-done((bf16[2048,128]{1,0:T(8,128)(2,1)S(1)}, bf16[2048,128]{1,0:T(8,128)(2,1)S(1)}, u32[]{:S(2)}, u32[]{:S(2)}) %collective-permute-start.8) | collective-permute-done | bytes 524320 | tf_op jit(solution)/shard_map/gather_basis/ppermute | solution.py:20
  45.9 0.7 collective-permute-done.6
  46.6 5.7 %forward.1 = (f32[16,256,128]{2,1,0:T(8,128)S(1)}, f32[16,256,128]{2,1,0:T(8,128)S(1)}) custom-call(s32[1]{0:T(128)} %copy.12.count, s32[160]{0:T(256)S(1)} %get-tuple-element.62.row_at, s32[160]{0:T(256)S(1)} %get-tuple-element.71.col_at, bf16[160,256,256]{2,1,0:T(8,128)(2,1)} %tiles.3, bf16[8,256,128]{2,1,0:T(8,128)(2,1)S(1)} %bitcast.13, ...), custom_call_target="tpu_custom_call" | custom-call | tf_op jit(solution)/shard_map/forward/pallas_call | solution.py:92
  52.4 4.1 %collective-permute-done.12.came = f32[16,256,128]{2,1,0:T(8,128)S(1)} collective-permute-done((f32[16,256,128]{2,1,0:T(8,128)S(1)}, f32[16,256,128]{2,1,0:T(8,128)S(1)}, u32[]{:S(2)}, u32[]{:S(2)}) %collective-permute-start.12) | collective-permute-done | bytes 2097184 | tf_op jit(solution)/shard_map/reduce_inner/ppermute | solution.py:20
  56.8 2.8 %collective-permute-start.13 = (f32[4,256,128]{2,1,0:T(8,128)S(1)}, f32[4,256,128]{2,1,0:T(8,128)S(1)}, u32[]{:S(2)}, u32[]{:S(2)}) collective-permute-start(f32[4,256,128]{2,1,0:T(8,128)S(1)} %get-tuple-element.43), channel_id=1, source_target_pairs={{0,2},{2,4},{4,6},{6,0},{1,3},{3,5},{5,7},{7,1},{8,10},{10,12},{12... | collective-permute-start | bytes 1572872 | tf_op jit(solution)/shard_map/reduce_inner/ppermute | solution.py:20
  59.7 3.6 %collective-permute-start.14 = (f32[4,256,128]{2,1,0:T(8,128)S(1)}, f32[4,256,128]{2,1,0:T(8,128)S(1)}, u32[]{:S(2)}, u32[]{:S(2)}) collective-permute-start(f32[4,256,128]{2,1,0:T(8,128)S(1)} %get-tuple-element.44), channel_id=1, source_target_pairs={{0,4},{2,6},{4,0},{6,2},{1,5},{3,7},{5,1},{7,3},{8,12},{10,14},{12... | collective-permute-start | bytes 1572872 | tf_op jit(solution)/shard_map/reduce_inner/ppermute | solution.py:20
  63.2 1.0 collective-permute-start.15
  64.2 9.8 %collective-permute-done.13.b = f32[4,256,128]{2,1,0:T(8,128)S(1)} collective-permute-done((f32[4,256,128]{2,1,0:T(8,128)S(1)}, f32[4,256,128]{2,1,0:T(8,128)S(1)}, u32[]{:S(2)}, u32[]{:S(2)}) %collective-permute-start.13) | collective-permute-done | bytes 524320 | tf_op jit(solution)/shard_map/reduce_inner/ppermute | solution.py:20
  74.0 12.4 %collective-permute-done.14.c = f32[4,256,128]{2,1,0:T(8,128)S(1)} collective-permute-done((f32[4,256,128]{2,1,0:T(8,128)S(1)}, f32[4,256,128]{2,1,0:T(8,128)S(1)}, u32[]{:S(2)}, u32[]{:S(2)}) %collective-permute-start.14) | collective-permute-done | bytes 524320 | tf_op jit(solution)/shard_map/reduce_inner/ppermute | solution.py:20
  86.6 1.3 collective-permute-start.18
  87.9 2.4 %collective-permute-start.17 = (bf16[4,128,256]{2,1,0:T(8,128)(2,1)S(1)}, bf16[4,128,256]{2,1,0:T(8,128)(2,1)S(1)}, u32[]{:S(2)}, u32[]{:S(2)}) collective-permute-start(bf16[4,128,256]{2,1,0:T(8,128)(2,1)S(1)} %inner_sum.1.rest_0_), channel_id=1, source_target_pairs={{0,4},{2,6},{4,0},{6,2},{1,5},{3,7},{5,1},{7,3},{8,12},{10,14},{12... | collective-permute-start | bytes 786440 | tf_op jit(solution)/shard_map/gather_inner/ppermute | solution.py:20
  90.3 1.2 collective-permute-start.16
  91.5 3.9 %collective-permute-done.18.rest_3_ = bf16[4,128,256]{2,1,0:T(8,128)(2,1)S(1)} collective-permute-done((bf16[4,128,256]{2,1,0:T(8,128)(2,1)S(1)}, bf16[4,128,256]{2,1,0:T(8,128)(2,1)S(1)}, u32[]{:S(2)}, u32[]{:S(2)}) %collective-permute-start.18) | collective-permute-done | bytes 262176 | tf_op jit(solution)/shard_map/gather_inner/ppermute | solution.py:20
  95.4 6.7 %collective-permute-done.17.rest_2_ = bf16[4,128,256]{2,1,0:T(8,128)(2,1)S(1)} collective-permute-done((bf16[4,128,256]{2,1,0:T(8,128)(2,1)S(1)}, bf16[4,128,256]{2,1,0:T(8,128)(2,1)S(1)}, u32[]{:S(2)}, u32[]{:S(2)}) %collective-permute-start.17) | collective-permute-done | bytes 262176 | tf_op jit(solution)/shard_map/gather_inner/ppermute | solution.py:20
  102.1 0.5 collective-permute-start.20
  102.6 1.0 collective-permute-done.21.rest_6_
  104.0 5.2 %backward.1 = (f32[2,8,128,256]{3,2,1,0:T(8,128)S(1)}, bf16[8,128,256]{2,1,0:T(8,128)(2,1)S(1)}, bf16[8,128,256]{2,1,0:T(8,128)(2,1)S(1)}, bf16[8,128,256]{2,1,0...) custom-call(s32[1]{0:T(128)} %copy.12.count, ...), custom_call_target="tpu_custom_call" | custom-call | tf_op jit(solution)/shard_map/backward/pallas_call | solution.py:141
  109.2 6.1 %collective-permute-start.23 = (bf16[8,128,256]{2,1,0:T(8,128)(2,1)S(1)}, bf16[8,128,256]{2,1,0:T(8,128)(2,1)S(1)}, u32[]{:S(2)}, u32[]{:S(2)}) collective-permute-start(bf16[8,128,256]{2,1,0:T(8,128)(2,1)S(1)} %get-tuple-element.47), channel_id=1, source_target_pairs={{0,8},{8,16},{16,24},{24,0},{1,9},{9,17},{17,25},{25,1},{2,10},{10... | collective-permute-start | bytes 1572872 | tf_op jit(solution)/shard_map/reduce_outer/ppermute | solution.py:20
  115.4 2.9 %collective-permute-start.25 = (bf16[8,128,256]{2,1,0:T(8,128)(2,1)S(1)}, bf16[8,128,256]{2,1,0:T(8,128)(2,1)S(1)}, u32[]{:S(2)}, u32[]{:S(2)}) collective-permute-start(bf16[8,128,256]{2,1,0:T(8,128)(2,1)S(1)} %get-tuple-element.49), channel_id=1, source_target_pairs={{0,24},{8,0},{16,8},{24,16},{1,25},{9,1},{17,9},{25,17},{2,26},{10... | collective-permute-start | bytes 1572872 | tf_op jit(solution)/shard_map/reduce_outer/ppermute | solution.py:20
  118.4 9.4 %collective-permute-done.23.rest_0_ = bf16[8,128,256]{2,1,0:T(8,128)(2,1)S(1)} collective-permute-done((bf16[8,128,256]{2,1,0:T(8,128)(2,1)S(1)}, bf16[8,128,256]{2,1,0:T(8,128)(2,1)S(1)}, u32[]{:S(2)}, u32[]{:S(2)}) %collective-permute-start.23) | collective-permute-done | bytes 524320 | tf_op jit(solution)/shard_map/reduce_outer/ppermute | solution.py:20
  127.7 9.2 %collective-permute-done.24.rest_1_ = bf16[8,128,256]{2,1,0:T(8,128)(2,1)S(1)} collective-permute-done((bf16[8,128,256]{2,1,0:T(8,128)(2,1)S(1)}, bf16[8,128,256]{2,1,0:T(8,128)(2,1)S(1)}, u32[]{:S(2)}, u32[]{:S(2)}) %collective-permute-start.24) | collective-permute-done | bytes 524320 | tf_op jit(solution)/shard_map/reduce_outer/ppermute | solution.py:20
  137.3 4.5 %collective-permute-done.27.rest_4_ = bf16[8,128,256]{2,1,0:T(8,128)(2,1)S(1)} collective-permute-done((bf16[8,128,256]{2,1,0:T(8,128)(2,1)S(1)}, bf16[8,128,256]{2,1,0:T(8,128)(2,1)S(1)}, u32[]{:S(2)}, u32[]{:S(2)}) %collective-permute-start.27) | collective-permute-done | bytes 524320 | tf_op jit(solution)/shard_map/reduce_outer/ppermute | solution.py:20
  142.3 0.5 middle_sum.1
  142.7 11.8 %collective-permute-start.29 = (bf16[2,128,256]{2,1,0:T(8,128)(2,1)S(1)}, bf16[2,128,256]{2,1,0:T(8,128)(2,1)S(1)}, u32[]{:S(2)}, u32[]{:S(2)}) collective-permute-start(bf16[2,128,256]{2,1,0:T(8,128)(2,1)S(1)} %get-tuple-element.54), channel_id=1, source_target_pairs={{0,32},{32,64},{64,96},{96,0},{1,33},{33,65},{65,97},{97,1},{2,34}... | collective-permute-start | bytes 393224 | tf_op jit(solution)/shard_map/reduce_outer/ppermute | solution.py:20
  154.5 1.9 collective-permute-start.30
  156.4 2.5 %collective-permute-start.31 = (bf16[2,128,256]{2,1,0:T(8,128)(2,1)S(1)}, bf16[2,128,256]{2,1,0:T(8,128)(2,1)S(1)}, u32[]{:S(2)}, u32[]{:S(2)}) collective-permute-start(bf16[2,128,256]{2,1,0:T(8,128)(2,1)S(1)} %get-tuple-element.56), channel_id=1, source_target_pairs={{0,96},{32,0},{64,32},{96,64},{1,97},{33,1},{65,33},{97,65},{2,98}... | collective-permute-start | bytes 393224 | tf_op jit(solution)/shard_map/reduce_outer/ppermute | solution.py:20
  159.0 1.2 collective-permute-start.33
  160.2 2.0 %collective-permute-start.34 = (bf16[2,128,256]{2,1,0:T(8,128)(2,1)S(1)}, bf16[2,128,256]{2,1,0:T(8,128)(2,1)S(1)}, u32[]{:S(2)}, u32[]{:S(2)}) collective-permute-start(bf16[2,128,256]{2,1,0:T(8,128)(2,1)S(1)} %get-tuple-element.59), channel_id=1, source_target_pairs={{0,24},{8,0},{16,8},{24,16},{1,25},{9,1},{17,9},{25,17},{2,26},{10... | collective-permute-start | bytes 393224 | tf_op jit(solution)/shard_map/reduce_outer/ppermute | solution.py:20
  162.2 4.6 %collective-permute-done.32.rest_3_ = bf16[2,128,256]{2,1,0:T(8,128)(2,1)S(1)} collective-permute-done((bf16[2,128,256]{2,1,0:T(8,128)(2,1)S(1)}, bf16[2,128,256]{2,1,0:T(8,128)(2,1)S(1)}, u32[]{:S(2)}, u32[]{:S(2)}) %collective-permute-start.32) | collective-permute-done | bytes 131104 | tf_op jit(solution)/shard_map/reduce_outer/ppermute | solution.py:20
  166.8 0.7 collective-permute-done.34.rest_5_
  167.5 0.6 outer_sum.1
  168.2 1.2 collective-permute-done.35
  169.4 1.3 collective-permute-start.38
  170.7 0.8 collective-permute-start.37
  171.5 0.7 collective-permute-start.36
  172.3 1.5 collective-permute-done.38
  173.8 3.1 %collective-permute-done.37 = f32[128,128]{1,0:T(8,128)S(1)} collective-permute-done((f32[128,128]{1,0:T(8,128)S(1)}, f32[128,128]{1,0:T(8,128)S(1)}, u32[]{:S(2)}, u32[]{:S(2)}) %collective-permute-start.37) | collective-permute-done | bytes 65568 | tf_op jit(solution)/shard_map/reduce_gram/ppermute | solution.py:20
  176.9 0.5 collective-permute-done.36
  177.4 2.4 %collective-permute-start.41 = (f32[128,128]{1,0:T(8,128)S(1)}, f32[128,128]{1,0:T(8,128)S(1)}, u32[]{:S(2)}, u32[]{:S(2)}) collective-permute-start(f32[128,128]{1,0:T(8,128)S(1)} %add_add_fusion.2), channel_id=1, source_target_pairs={{0,24},{8,0},{16,8},{24,16},{1,25},{9,1},{17,9},{25,17},{2,26},{10... | collective-permute-start | bytes 196616 | tf_op jit(solution)/shard_map/reduce_gram/ppermute | solution.py:20
  179.7 1.5 collective-permute-start.39
  181.3 0.4 collective-permute-done.41
  181.7 4.2 %collective-permute-done.40 = f32[128,128]{1,0:T(8,128)S(1)} collective-permute-done((f32[128,128]{1,0:T(8,128)S(1)}, f32[128,128]{1,0:T(8,128)S(1)}, u32[]{:S(2)}, u32[]{:S(2)}) %collective-permute-start.40) | collective-permute-done | bytes 65568 | tf_op jit(solution)/shard_map/reduce_gram/ppermute | solution.py:20
  186.3 1.7 collective-permute-start.43
  188.0 0.8 collective-permute-start.42
  188.9 1.4 collective-permute-done.44
  190.3 1.5 collective-permute-done.43
  191.8 2.0 %collective-permute-done.42 = f32[128,128]{1,0:T(8,128)S(1)} collective-permute-done((f32[128,128]{1,0:T(8,128)S(1)}, f32[128,128]{1,0:T(8,128)S(1)}, u32[]{:S(2)}, u32[]{:S(2)}) %collective-permute-start.42) | collective-permute-done | bytes 65568 | tf_op jit(solution)/shard_map/reduce_gram/ppermute | solution.py:20
  193.8 5.9 %finish.1 = (f32[1024,128]{1,0:T(8,128)}, f32[128,128]{1,0:T(8,128)}) custom-call(f32[128,128]{1,0:T(8,128)S(1)} %add_add_fusion.refs_0_, f32[4,128,256]{2,1,0:T(8,128)S(1)} %get-tuple-element.61.refs_1_), custom_call_target="tpu_custom_call" | custom-call | tf_op jit(solution)/shard_map/finish/pallas_call | solution.py:311
  (50 shorter events, 2.7 us)
Async XLA Ops:
  0.6 32.3 %copy-start = (s32[160,2]{0,1:T(2,128)S(1)}, s32[160,2]{0,1:T(2,128)}, u32[]{:S(2)}) copy-start(s32[160,2]{0,1:T(2,128)} %param.6) | copy-start | bytes 3844
  1.6 10.2 %collective-permute-start.5 = (bf16[512,128]{1,0:T(8,128)(2,1)S(1)}, bf16[512,128]{1,0:T(8,128)(2,1)S(1)}, u32[]{:S(2)}, u32[]{:S(2)}) collective-permute-start(bf16[512,128]{1,0:T(8,128)(2,1)S(1)} %get-tuple-element.36), channel_id=1, source_target_pairs={{0,8},{8,16},{16,24},{24,0},{1,9},{9,17},{17,25},{25,1},{2,10},{10... | collective-permute-start | bytes 393224 | tf_op jit(solution)/shard_map/gather_basis/ppermute | solution.py:20
  3.4 9.9 %collective-permute-start.4 = (bf16[512,128]{1,0:T(8,128)(2,1)S(1)}, bf16[512,128]{1,0:T(8,128)(2,1)S(1)}, u32[]{:S(2)}, u32[]{:S(2)}) collective-permute-start(bf16[512,128]{1,0:T(8,128)(2,1)S(1)} %get-tuple-element.36), channel_id=1, source_target_pairs={{0,16},{8,24},{16,0},{24,8},{1,17},{9,25},{17,1},{25,9},{2,18},{10... | collective-permute-start | bytes 393224 | tf_op jit(solution)/shard_map/gather_basis/ppermute | solution.py:20
  6.3 7.0 %collective-permute-start.3 = (bf16[512,128]{1,0:T(8,128)(2,1)S(1)}, bf16[512,128]{1,0:T(8,128)(2,1)S(1)}, u32[]{:S(2)}, u32[]{:S(2)}) collective-permute-start(bf16[512,128]{1,0:T(8,128)(2,1)S(1)} %get-tuple-element.36), channel_id=1, source_target_pairs={{0,24},{8,0},{16,8},{24,16},{1,25},{9,1},{17,9},{25,17},{2,26},{10... | collective-permute-start | bytes 393224 | tf_op jit(solution)/shard_map/gather_basis/ppermute | solution.py:20
  7.6 7.6 %collective-permute-start.2 = (bf16[512,128]{1,0:T(8,128)(2,1)S(1)}, bf16[512,128]{1,0:T(8,128)(2,1)S(1)}, u32[]{:S(2)}, u32[]{:S(2)}) collective-permute-start(bf16[512,128]{1,0:T(8,128)(2,1)S(1)} %get-tuple-element.32), channel_id=1, source_target_pairs={{0,32},{32,64},{64,96},{96,0},{1,33},{33,65},{65,97},{97,1},{2,34}... | collective-permute-start | bytes 393224 | tf_op jit(solution)/shard_map/gather_basis/ppermute | solution.py:20
  9.1 7.9 %collective-permute-start.1 = (bf16[512,128]{1,0:T(8,128)(2,1)S(1)}, bf16[512,128]{1,0:T(8,128)(2,1)S(1)}, u32[]{:S(2)}, u32[]{:S(2)}) collective-permute-start(bf16[512,128]{1,0:T(8,128)(2,1)S(1)} %get-tuple-element.32), channel_id=1, source_target_pairs={{0,64},{32,96},{64,0},{96,32},{1,65},{33,97},{65,1},{97,33},{2,66}... | collective-permute-start | bytes 393224 | tf_op jit(solution)/shard_map/gather_basis/ppermute | solution.py:20
  11.8 5.2 %collective-permute-start = (bf16[512,128]{1,0:T(8,128)(2,1)S(1)}, bf16[512,128]{1,0:T(8,128)(2,1)S(1)}, u32[]{:S(2)}, u32[]{:S(2)}) collective-permute-start(bf16[512,128]{1,0:T(8,128)(2,1)S(1)} %get-tuple-element.32), channel_id=1, source_target_pairs={{0,96},{32,0},{64,32},{96,64},{1,97},{33,1},{65,33},{97,65},{2,98}... | collective-permute-start | bytes 393224 | tf_op jit(solution)/shard_map/gather_basis/ppermute | solution.py:20
  17.2 15.0 %collective-permute-start.11 = (bf16[2048,128]{1,0:T(8,128)(2,1)S(1)}, bf16[2048,128]{1,0:T(8,128)(2,1)S(1)}, u32[]{:S(2)}, u32[]{:S(2)}) collective-permute-start(bf16[2048,128]{1,0:T(8,128)(2,1)S(1)} %constant_dynamic-update-slice_fusion.4), channel_id=1, source_target_pairs={{0,32},{32,64},{64,96},{96,0},{1,33},{33,65},{65,97},{97,1},{2,34}... | collective-permute-start | bytes 1572872 | tf_op jit(solution)/shard_map/gather_basis/ppermute | solution.py:20
  18.5 24.3 %collective-permute-start.10 = (bf16[2048,128]{1,0:T(8,128)(2,1)S(1)}, bf16[2048,128]{1,0:T(8,128)(2,1)S(1)}, u32[]{:S(2)}, u32[]{:S(2)}) collective-permute-start(bf16[2048,128]{1,0:T(8,128)(2,1)S(1)} %constant_dynamic-update-slice_fusion.4), channel_id=1, source_target_pairs={{0,64},{32,96},{64,0},{96,32},{1,65},{33,97},{65,1},{97,33},{2,66}... | collective-permute-start | bytes 1572872 | tf_op jit(solution)/shard_map/gather_basis/ppermute | solution.py:20
  21.4 21.4 %collective-permute-start.9 = (bf16[2048,128]{1,0:T(8,128)(2,1)S(1)}, bf16[2048,128]{1,0:T(8,128)(2,1)S(1)}, u32[]{:S(2)}, u32[]{:S(2)}) collective-permute-start(bf16[2048,128]{1,0:T(8,128)(2,1)S(1)} %constant_dynamic-update-slice_fusion.4), channel_id=1, source_target_pairs={{0,96},{32,0},{64,32},{96,64},{1,97},{33,1},{65,33},{97,65},{2,98}... | collective-permute-start | bytes 1572872 | tf_op jit(solution)/shard_map/gather_basis/ppermute | solution.py:20
  22.6 23.3 %collective-permute-start.8 = (bf16[2048,128]{1,0:T(8,128)(2,1)S(1)}, bf16[2048,128]{1,0:T(8,128)(2,1)S(1)}, u32[]{:S(2)}, u32[]{:S(2)}) collective-permute-start(bf16[2048,128]{1,0:T(8,128)(2,1)S(1)} %constant_dynamic-update-slice_fusion), channel_id=1, source_target_pairs={{0,8},{8,16},{16,24},{24,0},{1,9},{9,17},{17,25},{25,1},{2,10},{10... | collective-permute-start | bytes 1572872 | tf_op jit(solution)/shard_map/gather_basis/ppermute | solution.py:20
  23.3 22.6 %collective-permute-start.7 = (bf16[2048,128]{1,0:T(8,128)(2,1)S(1)}, bf16[2048,128]{1,0:T(8,128)(2,1)}, u32[]{:S(2)}, u32[]{:S(2)}) collective-permute-start(bf16[2048,128]{1,0:T(8,128)(2,1)S(1)} %constant_dynamic-update-slice_fusion), channel_id=1, source_target_pairs={{0,16},{8,24},{16,0},{24,8},{1,17},{9,25},{17,1},{25,9},{2,18},{10... | collective-permute-start | bytes 1572872 | tf_op jit(solution)/shard_map/gather_basis/ppermute | solution.py:20
  32.1 14.4 %collective-permute-start.6 = (bf16[2048,128]{1,0:T(8,128)(2,1)S(1)}, bf16[2048,128]{1,0:T(8,128)(2,1)}, u32[]{:S(2)}, u32[]{:S(2)}) collective-permute-start(bf16[2048,128]{1,0:T(8,128)(2,1)S(1)} %constant_dynamic-update-slice_fusion), channel_id=1, source_target_pairs={{0,24},{8,0},{16,8},{24,16},{1,25},{9,1},{17,9},{25,17},{2,26},{10... | collective-permute-start | bytes 1572872 | tf_op jit(solution)/shard_map/gather_basis/ppermute | solution.py:20
  52.3 4.2 %collective-permute-start.12 = (f32[16,256,128]{2,1,0:T(8,128)S(1)}, f32[16,256,128]{2,1,0:T(8,128)S(1)}, u32[]{:S(2)}, u32[]{:S(2)}) collective-permute-start(f32[16,256,128]{2,1,0:T(8,128)S(1)} %get-tuple-element.41), channel_id=1, source_target_pairs={{0,1},{1,0},{2,3},{3,2},{4,5},{5,4},{6,7},{7,6},{8,9},{9,8},{10,11... | collective-permute-start | bytes 6291464 | tf_op jit(solution)/shard_map/reduce_inner/ppermute | solution.py:20
  56.8 17.2 %collective-permute-start.13 = (f32[4,256,128]{2,1,0:T(8,128)S(1)}, f32[4,256,128]{2,1,0:T(8,128)S(1)}, u32[]{:S(2)}, u32[]{:S(2)}) collective-permute-start(f32[4,256,128]{2,1,0:T(8,128)S(1)} %get-tuple-element.43), channel_id=1, source_target_pairs={{0,2},{2,4},{4,6},{6,0},{1,3},{3,5},{5,7},{7,1},{8,10},{10,12},{12... | collective-permute-start | bytes 1572872 | tf_op jit(solution)/shard_map/reduce_inner/ppermute | solution.py:20
  59.7 26.8 %collective-permute-start.14 = (f32[4,256,128]{2,1,0:T(8,128)S(1)}, f32[4,256,128]{2,1,0:T(8,128)S(1)}, u32[]{:S(2)}, u32[]{:S(2)}) collective-permute-start(f32[4,256,128]{2,1,0:T(8,128)S(1)} %get-tuple-element.44), channel_id=1, source_target_pairs={{0,4},{2,6},{4,0},{6,2},{1,5},{3,7},{5,1},{7,3},{8,12},{10,14},{12... | collective-permute-start | bytes 1572872 | tf_op jit(solution)/shard_map/reduce_inner/ppermute | solution.py:20
  63.2 23.2 %collective-permute-start.15 = (f32[4,256,128]{2,1,0:T(8,128)S(1)}, f32[4,256,128]{2,1,0:T(8,128)S(1)}, u32[]{:S(2)}, u32[]{:S(2)}) collective-permute-start(f32[4,256,128]{2,1,0:T(8,128)S(1)} %get-tuple-element.45), channel_id=1, source_target_pairs={{0,6},{2,0},{4,2},{6,4},{1,7},{3,1},{5,3},{7,5},{8,14},{10,8},{12,... | collective-permute-start | bytes 1572872 | tf_op jit(solution)/shard_map/reduce_inner/ppermute | solution.py:20
  86.6 8.8 %collective-permute-start.18 = (bf16[4,128,256]{2,1,0:T(8,128)(2,1)S(1)}, bf16[4,128,256]{2,1,0:T(8,128)(2,1)S(1)}, u32[]{:S(2)}, u32[]{:S(2)}) collective-permute-start(bf16[4,128,256]{2,1,0:T(8,128)(2,1)S(1)} %inner_sum.1.rest_0_), channel_id=1, source_target_pairs={{0,2},{2,4},{4,6},{6,0},{1,3},{3,5},{5,7},{7,1},{8,10},{10,12},{12... | collective-permute-start | bytes 786440 | tf_op jit(solution)/shard_map/gather_inner/ppermute | solution.py:20
  87.9 14.2 %collective-permute-start.17 = (bf16[4,128,256]{2,1,0:T(8,128)(2,1)S(1)}, bf16[4,128,256]{2,1,0:T(8,128)(2,1)S(1)}, u32[]{:S(2)}, u32[]{:S(2)}) collective-permute-start(bf16[4,128,256]{2,1,0:T(8,128)(2,1)S(1)} %inner_sum.1.rest_0_), channel_id=1, source_target_pairs={{0,4},{2,6},{4,0},{6,2},{1,5},{3,7},{5,1},{7,3},{8,12},{10,14},{12... | collective-permute-start | bytes 786440 | tf_op jit(solution)/shard_map/gather_inner/ppermute | solution.py:20
  90.3 11.8 %collective-permute-start.16 = (bf16[4,128,256]{2,1,0:T(8,128)(2,1)S(1)}, bf16[4,128,256]{2,1,0:T(8,128)(2,1)S(1)}, u32[]{:S(2)}, u32[]{:S(2)}) collective-permute-start(bf16[4,128,256]{2,1,0:T(8,128)(2,1)S(1)} %inner_sum.1.rest_0_), channel_id=1, source_target_pairs={{0,6},{2,0},{4,2},{6,4},{1,7},{3,1},{5,3},{7,5},{8,14},{10,8},{12,... | collective-permute-start | bytes 786440 | tf_op jit(solution)/shard_map/gather_inner/ppermute | solution.py:20
  91.5 11.1 %collective-permute-start.19 = (bf16[4,128,256]{2,1,0:T(8,128)(2,1)S(1)}, bf16[4,128,256]{2,1,0:T(8,128)(2,1)S(1)}, u32[]{:S(2)}, u32[]{:S(2)}) collective-permute-start(bf16[4,128,256]{2,1,0:T(8,128)(2,1)S(1)} %inner_sum.1.rest_0_), channel_id=1, source_target_pairs={{0,1},{1,0},{2,3},{3,2},{4,5},{5,4},{6,7},{7,6},{8,9},{9,8},{10,11... | collective-permute-start | bytes 786440 | tf_op jit(solution)/shard_map/gather_inner/ppermute | solution.py:20
  95.4 7.2 %collective-permute-start.22 = (bf16[4,128,256]{2,1,0:T(8,128)(2,1)S(1)}, bf16[4,128,256]{2,1,0:T(8,128)(2,1)S(1)}, u32[]{:S(2)}, u32[]{:S(2)}) collective-permute-start(bf16[4,128,256]{2,1,0:T(8,128)(2,1)S(1)} %collective-permute-done.18.rest_3_), channel_id=1, source_target_pairs={{0,1},{1,0},{2,3},{3,2},{4,5},{5,4},{6,7},{7,6},{8,9},{9,8},{10,11... | collective-permute-start | bytes 786440 | tf_op jit(solution)/shard_map/gather_inner/ppermute | solution.py:20
  102.1 1.5 collective-permute-start.21
  102.1 1.9 collective-permute-start.20
  109.2 18.5 %collective-permute-start.23 = (bf16[8,128,256]{2,1,0:T(8,128)(2,1)S(1)}, bf16[8,128,256]{2,1,0:T(8,128)(2,1)S(1)}, u32[]{:S(2)}, u32[]{:S(2)}) collective-permute-start(bf16[8,128,256]{2,1,0:T(8,128)(2,1)S(1)} %get-tuple-element.47), channel_id=1, source_target_pairs={{0,8},{8,16},{16,24},{24,0},{1,9},{9,17},{17,25},{25,1},{2,10},{10... | collective-permute-start | bytes 1572872 | tf_op jit(solution)/shard_map/reduce_outer/ppermute | solution.py:20
  115.4 21.6 %collective-permute-start.24 = (bf16[8,128,256]{2,1,0:T(8,128)(2,1)S(1)}, bf16[8,128,256]{2,1,0:T(8,128)(2,1)S(1)}, u32[]{:S(2)}, u32[]{:S(2)}) collective-permute-start(bf16[8,128,256]{2,1,0:T(8,128)(2,1)S(1)} %get-tuple-element.48), channel_id=1, source_target_pairs={{0,16},{8,24},{16,0},{24,8},{1,17},{9,25},{17,1},{25,9},{2,18},{10... | collective-permute-start | bytes 1572872 | tf_op jit(solution)/shard_map/reduce_outer/ppermute | solution.py:20
  115.4 21.9 %collective-permute-start.25 = (bf16[8,128,256]{2,1,0:T(8,128)(2,1)S(1)}, bf16[8,128,256]{2,1,0:T(8,128)(2,1)S(1)}, u32[]{:S(2)}, u32[]{:S(2)}) collective-permute-start(bf16[8,128,256]{2,1,0:T(8,128)(2,1)S(1)} %get-tuple-element.49), channel_id=1, source_target_pairs={{0,24},{8,0},{16,8},{24,16},{1,25},{9,1},{17,9},{25,17},{2,26},{10... | collective-permute-start | bytes 1572872 | tf_op jit(solution)/shard_map/reduce_outer/ppermute | solution.py:20
  118.3 19.0 %collective-permute-start.26 = (bf16[8,128,256]{2,1,0:T(8,128)(2,1)S(1)}, bf16[8,128,256]{2,1,0:T(8,128)(2,1)S(1)}, u32[]{:S(2)}, u32[]{:S(2)}) collective-permute-start(bf16[8,128,256]{2,1,0:T(8,128)(2,1)S(1)} %get-tuple-element.50), channel_id=1, source_target_pairs={{0,32},{32,64},{64,96},{96,0},{1,33},{33,65},{65,97},{97,1},{2,34}... | collective-permute-start | bytes 1572872 | tf_op jit(solution)/shard_map/reduce_outer/ppermute | solution.py:20
  118.3 23.5 %collective-permute-start.27 = (bf16[8,128,256]{2,1,0:T(8,128)(2,1)S(1)}, bf16[8,128,256]{2,1,0:T(8,128)(2,1)S(1)}, u32[]{:S(2)}, u32[]{:S(2)}) collective-permute-start(bf16[8,128,256]{2,1,0:T(8,128)(2,1)S(1)} %get-tuple-element.51), channel_id=1, source_target_pairs={{0,64},{32,96},{64,0},{96,32},{1,65},{33,97},{65,1},{97,33},{2,66}... | collective-permute-start | bytes 1572872 | tf_op jit(solution)/shard_map/reduce_outer/ppermute | solution.py:20
  127.7 14.5 %collective-permute-start.28 = (bf16[8,128,256]{2,1,0:T(8,128)(2,1)S(1)}, bf16[8,128,256]{2,1,0:T(8,128)(2,1)S(1)}, u32[]{:S(2)}, u32[]{:S(2)}) collective-permute-start(bf16[8,128,256]{2,1,0:T(8,128)(2,1)S(1)} %get-tuple-element.52), channel_id=1, source_target_pairs={{0,96},{32,0},{64,32},{96,64},{1,97},{33,1},{65,33},{97,65},{2,98}... | collective-permute-start | bytes 1572872 | tf_op jit(solution)/shard_map/reduce_outer/ppermute | solution.py:20
  142.7 17.4 %collective-permute-start.29 = (bf16[2,128,256]{2,1,0:T(8,128)(2,1)S(1)}, bf16[2,128,256]{2,1,0:T(8,128)(2,1)S(1)}, u32[]{:S(2)}, u32[]{:S(2)}) collective-permute-start(bf16[2,128,256]{2,1,0:T(8,128)(2,1)S(1)} %get-tuple-element.54), channel_id=1, source_target_pairs={{0,32},{32,64},{64,96},{96,0},{1,33},{33,65},{65,97},{97,1},{2,34}... | collective-permute-start | bytes 393224 | tf_op jit(solution)/shard_map/reduce_outer/ppermute | solution.py:20
  154.5 7.7 %collective-permute-start.30 = (bf16[2,128,256]{2,1,0:T(8,128)(2,1)S(1)}, bf16[2,128,256]{2,1,0:T(8,128)(2,1)S(1)}, u32[]{:S(2)}, u32[]{:S(2)}) collective-permute-start(bf16[2,128,256]{2,1,0:T(8,128)(2,1)S(1)} %get-tuple-element.55), channel_id=1, source_target_pairs={{0,64},{32,96},{64,0},{96,32},{1,65},{33,97},{65,1},{97,33},{2,66}... | collective-permute-start | bytes 393224 | tf_op jit(solution)/shard_map/reduce_outer/ppermute | solution.py:20
  156.4 5.8 %collective-permute-start.31 = (bf16[2,128,256]{2,1,0:T(8,128)(2,1)S(1)}, bf16[2,128,256]{2,1,0:T(8,128)(2,1)S(1)}, u32[]{:S(2)}, u32[]{:S(2)}) collective-permute-start(bf16[2,128,256]{2,1,0:T(8,128)(2,1)S(1)} %get-tuple-element.56), channel_id=1, source_target_pairs={{0,96},{32,0},{64,32},{96,64},{1,97},{33,1},{65,33},{97,65},{2,98}... | collective-permute-start | bytes 393224 | tf_op jit(solution)/shard_map/reduce_outer/ppermute | solution.py:20
  159.0 7.9 %collective-permute-start.32 = (bf16[2,128,256]{2,1,0:T(8,128)(2,1)S(1)}, bf16[2,128,256]{2,1,0:T(8,128)(2,1)S(1)}, u32[]{:S(2)}, u32[]{:S(2)}) collective-permute-start(bf16[2,128,256]{2,1,0:T(8,128)(2,1)S(1)} %get-tuple-element.57), channel_id=1, source_target_pairs={{0,8},{8,16},{16,24},{24,0},{1,9},{9,17},{17,25},{25,1},{2,10},{10... | collective-permute-start | bytes 393224 | tf_op jit(solution)/shard_map/reduce_outer/ppermute | solution.py:20
  159.0 7.9 %collective-permute-start.33 = (bf16[2,128,256]{2,1,0:T(8,128)(2,1)S(1)}, bf16[2,128,256]{2,1,0:T(8,128)(2,1)S(1)}, u32[]{:S(2)}, u32[]{:S(2)}) collective-permute-start(bf16[2,128,256]{2,1,0:T(8,128)(2,1)S(1)} %get-tuple-element.58), channel_id=1, source_target_pairs={{0,16},{8,24},{16,0},{24,8},{1,17},{9,25},{17,1},{25,9},{2,18},{10... | collective-permute-start | bytes 393224 | tf_op jit(solution)/shard_map/reduce_outer/ppermute | solution.py:20
  160.2 7.3 %collective-permute-start.34 = (bf16[2,128,256]{2,1,0:T(8,128)(2,1)S(1)}, bf16[2,128,256]{2,1,0:T(8,128)(2,1)S(1)}, u32[]{:S(2)}, u32[]{:S(2)}) collective-permute-start(bf16[2,128,256]{2,1,0:T(8,128)(2,1)S(1)} %get-tuple-element.59), channel_id=1, source_target_pairs={{0,24},{8,0},{16,8},{24,16},{1,25},{9,1},{17,9},{25,17},{2,26},{10... | collective-permute-start | bytes 393224 | tf_op jit(solution)/shard_map/reduce_outer/ppermute | solution.py:20
  168.1 1.3 collective-permute-start.35
  169.4 4.3 %collective-permute-start.38 = (f32[128,128]{1,0:T(8,128)S(1)}, f32[128,128]{1,0:T(8,128)S(1)}, u32[]{:S(2)}, u32[]{:S(2)}) collective-permute-start(f32[128,128]{1,0:T(8,128)S(1)} %add.105), channel_id=1, source_target_pairs={{0,6},{2,0},{4,2},{6,4},{1,7},{3,1},{5,3},{7,5},{8,14},{10,8},{12,... | collective-permute-start | bytes 196616 | tf_op jit(solution)/shard_map/reduce_gram/ppermute | solution.py:20
  170.7 6.2 %collective-permute-start.37 = (f32[128,128]{1,0:T(8,128)S(1)}, f32[128,128]{1,0:T(8,128)S(1)}, u32[]{:S(2)}, u32[]{:S(2)}) collective-permute-start(f32[128,128]{1,0:T(8,128)S(1)} %add.105), channel_id=1, source_target_pairs={{0,2},{2,4},{4,6},{6,0},{1,3},{3,5},{5,7},{7,1},{8,10},{10,12},{12... | collective-permute-start | bytes 196616 | tf_op jit(solution)/shard_map/reduce_gram/ppermute | solution.py:20
  171.5 5.8 %collective-permute-start.36 = (f32[128,128]{1,0:T(8,128)S(1)}, f32[128,128]{1,0:T(8,128)S(1)}, u32[]{:S(2)}, u32[]{:S(2)}) collective-permute-start(f32[128,128]{1,0:T(8,128)S(1)} %add.105), channel_id=1, source_target_pairs={{0,4},{2,6},{4,0},{6,2},{1,5},{3,7},{5,1},{7,3},{8,12},{10,14},{12... | collective-permute-start | bytes 196616 | tf_op jit(solution)/shard_map/reduce_gram/ppermute | solution.py:20
  177.4 4.3 %collective-permute-start.41 = (f32[128,128]{1,0:T(8,128)S(1)}, f32[128,128]{1,0:T(8,128)S(1)}, u32[]{:S(2)}, u32[]{:S(2)}) collective-permute-start(f32[128,128]{1,0:T(8,128)S(1)} %add_add_fusion.2), channel_id=1, source_target_pairs={{0,24},{8,0},{16,8},{24,16},{1,25},{9,1},{17,9},{25,17},{2,26},{10... | collective-permute-start | bytes 196616 | tf_op jit(solution)/shard_map/reduce_gram/ppermute | solution.py:20
  179.7 6.2 %collective-permute-start.40 = (f32[128,128]{1,0:T(8,128)S(1)}, f32[128,128]{1,0:T(8,128)S(1)}, u32[]{:S(2)}, u32[]{:S(2)}) collective-permute-start(f32[128,128]{1,0:T(8,128)S(1)} %add_add_fusion.2), channel_id=1, source_target_pairs={{0,8},{8,16},{16,24},{24,0},{1,9},{9,17},{17,25},{25,1},{2,10},{10... | collective-permute-start | bytes 196616 | tf_op jit(solution)/shard_map/reduce_gram/ppermute | solution.py:20
  179.7 6.2 %collective-permute-start.39 = (f32[128,128]{1,0:T(8,128)S(1)}, f32[128,128]{1,0:T(8,128)S(1)}, u32[]{:S(2)}, u32[]{:S(2)}) collective-permute-start(f32[128,128]{1,0:T(8,128)S(1)} %add_add_fusion.2), channel_id=1, source_target_pairs={{0,16},{8,24},{16,0},{24,8},{1,17},{9,25},{17,1},{25,9},{2,18},{10... | collective-permute-start | bytes 196616 | tf_op jit(solution)/shard_map/reduce_gram/ppermute | solution.py:20
  185.9 4.3 %collective-permute-start.44 = (f32[128,128]{1,0:T(8,128)S(1)}, f32[128,128]{1,0:T(8,128)S(1)}, u32[]{:S(2)}, u32[]{:S(2)}) collective-permute-start(f32[128,128]{1,0:T(8,128)S(1)} %add_add_fusion.1), channel_id=1, source_target_pairs={{0,96},{32,0},{64,32},{96,64},{1,97},{33,1},{65,33},{97,65},{2,98}... | collective-permute-start | bytes 196616 | tf_op jit(solution)/shard_map/reduce_gram/ppermute | solution.py:20
  186.3 5.5 %collective-permute-start.43 = (f32[128,128]{1,0:T(8,128)S(1)}, f32[128,128]{1,0:T(8,128)S(1)}, u32[]{:S(2)}, u32[]{:S(2)}) collective-permute-start(f32[128,128]{1,0:T(8,128)S(1)} %add_add_fusion.1), channel_id=1, source_target_pairs={{0,32},{32,64},{64,96},{96,0},{1,33},{33,65},{65,97},{97,1},{2,34}... | collective-permute-start | bytes 196616 | tf_op jit(solution)/shard_map/reduce_gram/ppermute | solution.py:20
  188.0 5.8 %collective-permute-start.42 = (f32[128,128]{1,0:T(8,128)S(1)}, f32[128,128]{1,0:T(8,128)S(1)}, u32[]{:S(2)}, u32[]{:S(2)}) collective-permute-start(f32[128,128]{1,0:T(8,128)S(1)} %add_add_fusion.1), channel_id=1, source_target_pairs={{0,64},{32,96},{64,0},{96,32},{1,65},{33,97},{65,1},{97,33},{2,66}... | collective-permute-start | bytes 196616 | tf_op jit(solution)/shard_map/reduce_gram/ppermute | solution.py:20

commit v3 on v2

--- a/solution.py
+++ b/solution.py
@@ -9,8 +9,8 @@
 SIZES = {"x": 4, "y": 4, "z": 4, "core": 2}
 SIDE = 256
 RANK = 128
-CHUNK = 20
-WINDOW = 3
+CHUNK = 32
+EXTRA = 16
 F32 = jnp.float32
 BF16 = jnp.bfloat16
 
@@ -40,38 +40,53 @@
     return copies
 
 
-def tile_window(count, tiles, window, sems):
+def hold_kernel(count, tiles, held, sems):
     chunks = (count[0] + CHUNK - 1) // CHUNK
 
     def copy(i):
         at = pl.ds(i * CHUNK, CHUNK)
-        return pltpu.make_async_copy(tiles.at[at], window.at[at], sems.at[i])
-
-    def start(i):
-        @pl.when(i < chunks)
-        def _():
-            copy(i).start()
-
-    return chunks, copy, start
+        return pltpu.make_async_copy(tiles.at[at], held.at[at], sems.at[i])
+
+    def start(i, _):
+        copy(i).start()
+        return 0
+
+    def wait(i, _):
+        copy(i).wait()
+        return 0
+
+    lax.fori_loop(0, chunks, start, 0)
+    lax.fori_loop(0, chunks, wait, 0)
+
+
+def hold_tiles(count, tiles):
+    return pl.pallas_call(
+        hold_kernel,
+        out_shape=jax.ShapeDtypeStruct(tiles.shape, tiles.dtype),
+        in_specs=[pl.BlockSpec(memory_space=pltpu.SMEM), pl.BlockSpec(memory_space=pl.ANY)],
+        out_specs=whole(1)[0],
+        scratch_shapes=[pltpu.SemaphoreType.DMA((tiles.shape[0] // CHUNK,))],
+        compiler_params=limits(27),
+        cost_estimate=pl.CostEstimate(
+            flops=0, bytes_accessed=2 * tiles.size * tiles.dtype.itemsize, transcendentals=0
+        ),
+        name="hold_tiles",
+    )(count, tiles)
 
 
 def forward_kernel(count, row_at, col_at, tiles, *rest):
-    pieces, (keep, away, held, total, window, sems, tile_sems) = rest[:8], rest[8:]
-    chunks, copy, start = tile_window(count, tiles, window, tile_sems)
+    pieces, (keep, away, held, total, sems) = rest[:8], rest[8:]
+    chunks = (count[0] + CHUNK - 1) // CHUNK
     copies = load_pieces(pieces, held, sems)
-    for i in range(WINDOW):
-        start(i)
     total[...] = jnp.zeros_like(total)
     for one in copies:
         one.wait()
 
     def body(i, _):
-        copy(i).wait()
-        start(i + WINDOW)
         for k in range(CHUNK):
             slot = i * CHUNK + k
             total[row_at[slot]] += jnp.dot(
-                window[slot], held[col_at[slot]], preferred_element_type=F32
+                tiles[slot], held[col_at[slot]], preferred_element_type=F32
             )
         return 0
 
@@ -86,134 +101,134 @@
 
 
 def forward(count, row_at, col_at, tiles, pieces):
-    slots = tiles.shape[0]
     any_spec = pl.BlockSpec(memory_space=pl.ANY)
     half = jax.ShapeDtypeStruct((16, SIDE, RANK), F32)
     return pl.pallas_call(
         forward_kernel,
         out_shape=(half, half),
-        in_specs=[pl.BlockSpec(memory_space=pltpu.SMEM)] * 3 + [any_spec] * 9,
+        in_specs=[pl.BlockSpec(memory_space=pltpu.SMEM)] * 3 + whole(1) + [any_spec] * 8,
         out_specs=(any_spec, any_spec),
         scratch_shapes=[
             pltpu.VMEM((64, SIDE, RANK), BF16),
             pltpu.VMEM((33, SIDE, RANK), F32),
-            pltpu.VMEM((slots, SIDE, SIDE), BF16),
             pltpu.SemaphoreType.DMA((8,)),
-            pltpu.SemaphoreType.DMA((slots // CHUNK,)),
         ],
-        compiler_params=limits(36),
+        compiler_params=limits(11),
         name="forward",
     )(count, row_at, col_at, tiles, *pieces)
 
 
 def backward_kernel(count, row_at, col_at, tiles, *rest):
-    pieces, keep, aways = rest[:8], rest[8], rest[9:15]
-    held, total, window, sems, tile_sems = rest[15:]
-    chunks, copy, start = tile_window(count, tiles, window, tile_sems)
+    pieces, keeps, aways = rest[:8], rest[8:10], rest[10:16]
+    held, total, sems = rest[16:]
+    chunks = (count[0] + CHUNK - 1) // CHUNK
     copies = load_pieces(pieces, held, sems)
-    for i in range(WINDOW):
-        start(i)
     total[...] = jnp.zeros_like(total)
     for one in copies:
         one.wait()
 
     def body(i, _):
-        copy(i).wait()
-        start(i + WINDOW)
         for k in range(CHUNK):
             slot = i * CHUNK + k
             total[col_at[slot]] += jnp.dot(
-                held[row_at[slot]], window[slot], preferred_element_type=F32
+                held[row_at[slot]], tiles[slot], preferred_element_type=F32
             )
         return 0
 
     lax.fori_loop(0, chunks, body, 0)
     for h in range(2):
-        keep[h] = total[pl.ds(32 * h, 8)]
+        keeps[h][...] = total[pl.ds(32 * h, 8)]
         for d in range(3):
             aways[3 * h + d][...] = total[pl.ds(32 * h + 8 * (d + 1), 8)].astype(BF16)
 
 
 def backward(count, row_at, col_at, tiles, pieces):
-    slots = tiles.shape[0]
     any_spec = pl.BlockSpec(memory_space=pl.ANY)
     part = jax.ShapeDtypeStruct((8, RANK, SIDE), BF16)
-    return pl.pallas_call(
+    keep = jax.ShapeDtypeStruct((8, RANK, SIDE), F32)
+    outs = pl.pallas_call(
         backward_kernel,
-        out_shape=(jax.ShapeDtypeStruct((2, 8, RANK, SIDE), F32),) + (part,) * 6,
-        in_specs=[pl.BlockSpec(memory_space=pltpu.SMEM)] * 3 + [any_spec] * 9,
-        out_specs=tuple(whole(7)),
+        out_shape=(keep,) * 2 + (part,) * 6,
+        in_specs=[pl.BlockSpec(memory_space=pltpu.SMEM)] * 3 + whole(1) + [any_spec] * 8,
+        out_specs=tuple(whole(8)),
         scratch_shapes=[
             pltpu.VMEM((32, RANK, SIDE), BF16),
             pltpu.VMEM((65, RANK, SIDE), F32),
-            pltpu.VMEM((slots, SIDE, SIDE), BF16),
             pltpu.SemaphoreType.DMA((8,)),
-            pltpu.SemaphoreType.DMA((slots // CHUNK,)),
         ],
-        compiler_params=limits(44),
+        compiler_params=limits(14),
         name="backward",
     )(count, row_at, col_at, tiles, *pieces)
-
-
-def core_sum_kernel(keep, came, *outs):
-    for d in range(4):
-        at = pl.ds(4 * d, 4)
-        outs[d][...] = keep[at] + came[at]
+    return outs[:2], (outs[2:5], outs[5:8])
+
+
+def core_sum_kernel(keep, came, kept, *outs):
+    kept[...] = keep[pl.ds(0, 4)] + came[pl.ds(0, 4)]
+    for d, out in enumerate(outs):
+        at = pl.ds(4 * (d + 1), 4)
+        total = keep[at] + came[at]
+        largest = jnp.max(jnp.abs(total), axis=0)
+        largest = jnp.max(jnp.max(largest, axis=0, keepdims=True), axis=1, keepdims=True)
+        power = jnp.floor(jnp.log2(jnp.maximum(largest, 1e-30))) - 13.0
+        scale = jnp.exp2(-power)
+        for i in range(4):
+            out[pl.ds(SIDE * i, SIDE), :] = total[i] * scale
+        out[pl.ds(4 * SIDE, EXTRA), :] = jnp.broadcast_to(power, (EXTRA, RANK))
 
 
 def core_sum(keep, came):
-    part = jax.ShapeDtypeStruct((4, SIDE, RANK), F32)
+    part = jax.ShapeDtypeStruct((4 * SIDE + EXTRA, RANK), F32)
     return pl.pallas_call(
         core_sum_kernel,
-        out_shape=(part,) * 4,
+        out_shape=(jax.ShapeDtypeStruct((4, SIDE, RANK), F32),) + (part,) * 3,
         in_specs=whole(2),
         out_specs=tuple(whole(4)),
-        compiler_params=limits(16),
+        compiler_params=limits(6),
         name="core_sum",
     )(keep, came)
 
 
-def inner_kernel(a, b, c, d, out):
+def inner_kernel(kept, a, b, c, out):
+    scales = [jnp.exp2(one[pl.ds(4 * SIDE, 1), :]) for one in (a, b, c)]
     for i in range(out.shape[0]):
-        summed = (a[i] + b[i]) + (c[i] + d[i])
+        summed = kept[i]
+        for one, scale in zip((a, b, c), scales):
+            summed += one[pl.ds(SIDE * i, SIDE), :] * scale
         out[i] = summed.T.astype(BF16)
 
 
-def inner_sum(parts):
+def inner_sum(kept, parts):
     return pl.pallas_call(
         inner_kernel,
         out_shape=jax.ShapeDtypeStruct((4, RANK, SIDE), BF16),
         in_specs=whole(4),
         out_specs=whole(1)[0],
-        compiler_params=limits(16),
+        compiler_params=limits(6),
         name="inner_sum",
-    )(*parts)
-
-
-def middle_kernel(keep, *rest):
-    came, next_keep, aways = rest[:6], rest[6], rest[7:]
-    for h in range(2):
-        for d in range(4):
-            at = pl.ds(2 * d, 2)
-            total = keep[h, at]
-            for one in came[3 * h : 3 * h + 3]:
-                total += one[at].astype(F32)
-            if d == 0:
-                next_keep[h] = total
-            else:
-                aways[3 * h + d - 1][...] = total.astype(BF16)
+    )(kept, *parts)
+
+
+def middle_kernel(keep, a, b, c, next_keep, *aways):
+    for d in range(4):
+        at = pl.ds(2 * d, 2)
+        total = (keep[at] + a[at].astype(F32)) + (b[at].astype(F32) + c[at].astype(F32))
+        if d == 0:
+            next_keep[...] = total
+        else:
+            aways[d - 1][...] = total.astype(BF16)
 
 
 def middle_sum(keep, came):
     part = jax.ShapeDtypeStruct((2, RANK, SIDE), BF16)
-    return pl.pallas_call(
+    keep, *aways = pl.pallas_call(
         middle_kernel,
-        out_shape=(jax.ShapeDtypeStruct((2, 2, RANK, SIDE), F32),) + (part,) * 6,
-        in_specs=whole(7),
-        out_specs=tuple(whole(7)),
-        compiler_params=limits(16),
+        out_shape=(jax.ShapeDtypeStruct((2, RANK, SIDE), F32),) + (part,) * 3,
+        in_specs=whole(4),
+        out_specs=tuple(whole(4)),
+        compiler_params=limits(6),
         name="middle_sum",
     )(keep, *came)
+    return keep, aways
 
 
 def exact_dot(a, b, dims):
@@ -222,12 +237,12 @@
     )
 
 
-def outer_kernel(keep, *rest):
-    came, outer, gram = rest[:6], rest[6], rest[7]
+def outer_kernel(*refs):
+    keeps, came, outer, gram = refs[:2], refs[2:8], refs[8], refs[9]
     gram_total = jnp.zeros((RANK, RANK), F32)
     for h in range(2):
         for b in range(2):
-            total = keep[h, b]
+            total = keeps[h][b]
             for one in came[3 * h : 3 * h + 3]:
                 total += one[b].astype(F32)
             outer[2 * h + b] = total
@@ -235,18 +250,18 @@
     gram[...] = gram_total
 
 
-def outer_sum(keep, came):
+def outer_sum(keeps, came):
     return pl.pallas_call(
         outer_kernel,
         out_shape=(
             jax.ShapeDtypeStruct((4, RANK, SIDE), F32),
             jax.ShapeDtypeStruct((RANK, RANK), F32),
         ),
-        in_specs=whole(7),
+        in_specs=whole(8),
         out_specs=tuple(whole(2)),
-        compiler_params=limits(16),
+        compiler_params=limits(6),
         name="outer_sum",
-    )(keep, *came)
+    )(*keeps, *came)
 
 
 def wide(value):
@@ -317,7 +332,7 @@
         in_specs=whole(2),
         out_specs=tuple(whole(2)),
         scratch_shapes=[pltpu.VMEM((RANK, 2 * RANK), F32)],
-        compiler_params=limits(16),
+        compiler_params=limits(6),
         name="finish",
     )(gram, outer)
 
@@ -343,36 +358,41 @@
             [half] + [send(half, order[0], -d) for d in (1, 2, 3)]
             for half, order in zip(halves, orders)
         ]
-        near = lax.optimization_barrier(near)
+        near, first_tiles = lax.optimization_barrier((near, tiles))
         firsts = [jnp.concatenate(four, axis=0) for four in near]
         pieces = []
         for first, order in zip(firsts, orders):
             pieces += [first] + [send(first, order[1], -d) for d in (1, 2, 3)]
         pieces = [piece.reshape(8, SIDE, RANK) for piece in pieces]
 
-    keep, away = forward(tile_count, jnp.where(used, row_at, 32), col_at, tiles, pieces)
+    held = hold_tiles(tile_count, first_tiles)
+    keep, away = forward(tile_count, jnp.where(used, row_at, 32), col_at, held, pieces)
 
     with jax.named_scope("reduce_inner"):
         came = send(away, "core", 1)
-        sums = core_sum(keep, came)
-        inner = inner_sum([sums[0]] + [send(sums[d], "z", d) for d in (1, 2, 3)])
+        kept, *sums = core_sum(keep, came)
+        sums, second_tiles = lax.optimization_barrier((sums, tiles))
+        held = hold_tiles(tile_count, second_tiles)
+        sums = [send(one.astype(jnp.float16), "z", d) for d, one in zip((1, 2, 3), sums)]
+        sums, held = lax.optimization_barrier((sums, held))
+        inner = inner_sum(kept, [one.astype(F32) for one in sums])
 
     with jax.named_scope("gather_inner"):
         mine = [inner] + [send(inner, "z", -d) for d in (1, 2, 3)]
         theirs = [send(one, "core", 1) for one in mine]
 
-    keep, *aways = backward(
-        tile_count, row_at, jnp.where(used, col_at, 64), tiles, mine + theirs
+    keeps, aways = backward(
+        tile_count, row_at, jnp.where(used, col_at, 64), held, mine + theirs
     )
 
     with jax.named_scope("reduce_outer"):
-        back = ("y",) * 3 + ("x",) * 3
-        steps = (1, 2, 3) * 2
-        came = [send(a, axis, d) for a, axis, d in zip(aways, back, steps)]
-        keep, *aways = middle_sum(keep, came)
-        forth = ("x",) * 3 + ("y",) * 3
-        came = [send(a, axis, d) for a, axis, d in zip(aways, forth, steps)]
-        outer, gram = outer_sum(keep, came)
+        last_keeps, last_came = [], []
+        for keep, away, (first, then) in zip(keeps, aways, (("y", "x"), ("x", "y"))):
+            came = [send(one, first, d) for d, one in zip((1, 2, 3), away)]
+            keep, away = middle_sum(keep, came)
+            last_keeps.append(keep)
+            last_came += [send(one, then, d) for d, one in zip((1, 2, 3), away)]
+        outer, gram = outer_sum(last_keeps, last_came)
 
     with jax.named_scope("reduce_gram"):
         gram = gram + send(gram, "core", 1)

time: 202 us -> 187 us (0.926); the launches traced: 200 us -> 187 us
  waiting for transfers between devices: 108 us -> 94.6 us
  Pallas kernels: 18.4 us -> 23.6 us
  starting transfers between devices: 70.2 us -> 65.5 us
    ppermute x45, waiting for transfers between devices: 108 us -> 94.6 us  [send(): lax.ppermute(array, axis, [(i, (i + step) % size) for i in range(size)])]
    pallas_call x3 -> x6, Pallas kernels: 5.96 us -> 11.9 us  [the longest x2 7.03 us: hold_tiles(): pl.pallas_call(hold_kernel, out_shape=jax.ShapeDtypeStruct(tiles.shape, t...]
    ppermute x45, starting transfers between devices: 70.2 us -> 65.5 us  [send(): lax.ppermute(array, axis, [(i, (i + step) % size) for i in range(size)])]
  transfers between devices with their start and end apart: 45 -> 45, of which waited for: 30 -> 28; matrix products, arithmetic and copies ran while one was open for 0% -> 0% of each run, Pallas kernels for 0% -> 4%
where the time goes in v3:
time: 187 us
  waiting for transfers between devices  94.6 us (51%)
  starting transfers between devices  65.5 us (35%)
  Pallas kernels  23.6 us (13%)
    ppermute x45, waiting for transfers between devices, send(): lax.ppermute(array, axis, [(i, (i + step) % size) for i in range(size)])  94.6 us
    ppermute x45, starting transfers between devices, send(): lax.ppermute(array, axis, [(i, (i + step) % size) for i in range(size)])  65.5 us
    pallas_call x2, Pallas kernels, hold_tiles(): pl.pallas_call(hold_kernel, out_shape=jax.ShapeDtypeStruct(tiles.shape, t...  7.03 us
    pallas_call x1, Pallas kernels, finish(): pl.pallas_call(kernel, out_shape=(jax.ShapeDtypeStruct((4 * SIDE, RANK),...  5.91 us
    pallas_call x1, Pallas kernels, forward(): pl.pallas_call(forward_kernel, out_shape=(half, half), in_specs=[pl.Block...  4.89 us
    pallas_call x1, Pallas kernels, backward(): pl.pallas_call(backward_kernel, out_shape=(keep,) * 2 + (part,) * 6, in_s...  3.87 us
  transfers between devices with their start and end apart: 45, of which 28 were waited for; matrix products, arithmetic and copies ran while one was open for 0% of the time, Pallas kernels for 4%

profile of v3, /device:TPU:0, one launch (start us, length us, event | category | flops | bytes accessed | tf_op | source)
XLA Modules:
  0.0 187.4 jit_solution(445843183894753990)
XLA Ops:
  0.6 1.0 fusion.12
  1.6 1.7 collective-permute-start.5
  3.3 2.9 %collective-permute-start.4 = (bf16[512,128]{1,0:T(8,128)(2,1)S(1)}, bf16[512,128]{1,0:T(8,128)(2,1)S(1)}, u32[]{:S(2)}, u32[]{:S(2)}) collective-permute-start(bf16[512,128]{1,0:T(8,128)(2,1)S(1)} %get-tuple-element.48), channel_id=1, source_target_pairs={{0,16},{8,24},{16,0},{24,8},{1,17},{9,25},{17,1},{25,9},{2,18},{10... | collective-permute-start | bytes 393224 | tf_op jit(solution)/shard_map/gather_basis/ppermute | solution.py:20
  6.2 1.3 collective-permute-start.3
  7.6 1.5 collective-permute-start.2
  9.1 2.7 %collective-permute-start.1 = (bf16[512,128]{1,0:T(8,128)(2,1)S(1)}, bf16[512,128]{1,0:T(8,128)(2,1)S(1)}, u32[]{:S(2)}, u32[]{:S(2)}) collective-permute-start(bf16[512,128]{1,0:T(8,128)(2,1)S(1)} %get-tuple-element.44), channel_id=1, source_target_pairs={{0,64},{32,96},{64,0},{96,32},{1,65},{33,97},{65,1},{97,33},{2,66}... | collective-permute-start | bytes 393224 | tf_op jit(solution)/shard_map/gather_basis/ppermute | solution.py:20
  11.8 1.4 collective-permute-start
  13.3 1.9 %collective-permute-done.2 = bf16[512,128]{1,0:T(8,128)(2,1)S(1)} collective-permute-done((bf16[512,128]{1,0:T(8,128)(2,1)S(1)}, bf16[512,128]{1,0:T(8,128)(2,1)S(1)}, u32[]{:S(2)}, u32[]{:S(2)}) %collective-permute-start.2) | collective-permute-done | bytes 131104 | tf_op jit(solution)/shard_map/gather_basis/ppermute | solution.py:20
  15.2 1.8 collective-permute-done.1
  17.2 1.3 collective-permute-start.11
  18.5 2.9 %collective-permute-start.10 = (bf16[2048,128]{1,0:T(8,128)(2,1)S(1)}, bf16[2048,128]{1,0:T(8,128)(2,1)S(1)}, u32[]{:S(2)}, u32[]{:S(2)}) collective-permute-start(bf16[2048,128]{1,0:T(8,128)(2,1)S(1)} %constant_dynamic-update-slice_fusion.4), channel_id=1, source_target_pairs={{0,64},{32,96},{64,0},{96,32},{1,65},{33,97},{65,1},{97,33},{2,66}... | collective-permute-start | bytes 1572872 | tf_op jit(solution)/shard_map/gather_basis/ppermute | solution.py:20
  21.4 1.1 collective-permute-start.9
  22.6 0.7 collective-permute-start.8
  23.3 1.1 collective-permute-start.7
  24.4 7.8 %collective-permute-done.11 = bf16[2048,128]{1,0:T(8,128)(2,1)S(1)} collective-permute-done((bf16[2048,128]{1,0:T(8,128)(2,1)S(1)}, bf16[2048,128]{1,0:T(8,128)(2,1)S(1)}, u32[]{:S(2)}, u32[]{:S(2)}) %collective-permute-start.11) | collective-permute-done | bytes 524320 | tf_op jit(solution)/shard_map/gather_basis/ppermute | solution.py:20
  33.0 0.8 fusion.13
  33.8 3.5 %hold_tiles.2.tiles = bf16[160,256,256]{2,1,0:T(8,128)(2,1)S(1)} custom-call(s32[1]{0:T(128)} %copy.12.count, bf16[160,256,256]{2,1,0:T(8,128)(2,1)} %tiles.1), custom_call_target="tpu_custom_call" | custom-call | bytes 41943040 | tf_op jit(solution)/shard_map/hold_tiles/pallas_call | solution.py:63
  37.3 5.5 %collective-permute-done.10 = bf16[2048,128]{1,0:T(8,128)(2,1)S(1)} collective-permute-done((bf16[2048,128]{1,0:T(8,128)(2,1)S(1)}, bf16[2048,128]{1,0:T(8,128)(2,1)S(1)}, u32[]{:S(2)}, u32[]{:S(2)}) %collective-permute-start.10) | collective-permute-done | bytes 524320 | tf_op jit(solution)/shard_map/gather_basis/ppermute | solution.py:20
  42.8 3.1 %collective-permute-done.8 = bf16[2048,128]{1,0:T(8,128)(2,1)S(1)} collective-permute-done((bf16[2048,128]{1,0:T(8,128)(2,1)S(1)}, bf16[2048,128]{1,0:T(8,128)(2,1)S(1)}, u32[]{:S(2)}, u32[]{:S(2)}) %collective-permute-start.8) | collective-permute-done | bytes 524320 | tf_op jit(solution)/shard_map/gather_basis/ppermute | solution.py:20
  45.9 0.7 collective-permute-done.6
  46.6 4.9 %forward.1 = (f32[16,256,128]{2,1,0:T(8,128)S(1)}, f32[16,256,128]{2,1,0:T(8,128)S(1)}) custom-call(s32[1]{0:T(128)} %copy.12.count, s32[160]{0:T(256)S(1)} %get-tuple-element.84.row_at, s32[160]{0:T(256)S(1)} %get-tuple-element.93.col_at, bf16[160,256,256]{2,1,0:T(8,128)(2,1)S(1)} %hold_tiles.2.tiles, bf16[8,256,128]{2,1,0:T(8,128)(2,1)S(1)} %bitcast.13, ...), custom_call_target="tpu_custom_call" | custom-call | tf_op jit(solution)/shard_map/forward/pallas_call | solution.py:106
  51.6 4.1 %collective-permute-done.12.came = f32[16,256,128]{2,1,0:T(8,128)S(1)} collective-permute-done((f32[16,256,128]{2,1,0:T(8,128)S(1)}, f32[16,256,128]{2,1,0:T(8,128)S(1)}, u32[]{:S(2)}, u32[]{:S(2)}) %collective-permute-start.12) | collective-permute-done | bytes 2097184 | tf_op jit(solution)/shard_map/reduce_inner/ppermute | solution.py:20
  55.7 0.5 core_sum.1
  56.4 5.5 %collective-permute-start.15 = (f16[1040,128]{1,0:T(8,128)(2,1)S(1)}, f16[1040,128]{1,0:T(8,128)(2,1)S(1)}, u32[]{:S(2)}, u32[]{:S(2)}) collective-permute-start(f16[1040,128]{1,0:T(8,128)(2,1)S(1)} %convert_element_type.20), channel_id=1, source_target_pairs={{0,6},{2,0},{4,2},{6,4},{1,7},{3,1},{5,3},{7,5},{8,14},{10,8},{12,... | collective-permute-start | bytes 798728 | tf_op jit(solution)/shard_map/reduce_inner/ppermute | solution.py:20
  61.8 1.3 collective-permute-start.13
  63.1 3.5 %hold_tiles.3.tiles = bf16[160,256,256]{2,1,0:T(8,128)(2,1)S(1)} custom-call(s32[1]{0:T(128)} %copy.12.count, bf16[160,256,256]{2,1,0:T(8,128)(2,1)} %tiles.1), custom_call_target="tpu_custom_call" | custom-call | bytes 41943040 | tf_op jit(solution)/shard_map/reduce_inner/hold_tiles/pallas_call | solution.py:63
  66.6 6.9 %collective-permute-done.15 = f16[1040,128]{1,0:T(8,128)(2,1)S(1)} collective-permute-done((f16[1040,128]{1,0:T(8,128)(2,1)S(1)}, f16[1040,128]{1,0:T(8,128)(2,1)S(1)}, u32[]{:S(2)}, u32[]{:S(2)}) %collective-permute-start.15) | collective-permute-done | bytes 266272 | tf_op jit(solution)/shard_map/reduce_inner/ppermute | solution.py:20
  73.5 3.4 %collective-permute-done.13 = f16[1040,128]{1,0:T(8,128)(2,1)S(1)} collective-permute-done((f16[1040,128]{1,0:T(8,128)(2,1)S(1)}, f16[1040,128]{1,0:T(8,128)(2,1)S(1)}, u32[]{:S(2)}, u32[]{:S(2)}) %collective-permute-start.13) | collective-permute-done | bytes 266272 | tf_op jit(solution)/shard_map/reduce_inner/ppermute | solution.py:20
  77.4 2.3 %collective-permute-start.17 = (bf16[4,128,256]{2,1,0:T(8,128)(2,1)S(1)}, bf16[4,128,256]{2,1,0:T(8,128)(2,1)S(1)}, u32[]{:S(2)}, u32[]{:S(2)}) collective-permute-start(bf16[4,128,256]{2,1,0:T(8,128)(2,1)S(1)} %inner_sum.1.rest_0_), channel_id=1, source_target_pairs={{0,4},{2,6},{4,0},{6,2},{1,5},{3,7},{5,1},{7,3},{8,12},{10,14},{12... | collective-permute-start | bytes 786440 | tf_op jit(solution)/shard_map/gather_inner/ppermute | solution.py:20
  79.7 0.9 collective-permute-start.16
  80.6 11.5 %collective-permute-done.18.rest_3_ = bf16[4,128,256]{2,1,0:T(8,128)(2,1)S(1)} collective-permute-done((bf16[4,128,256]{2,1,0:T(8,128)(2,1)S(1)}, bf16[4,128,256]{2,1,0:T(8,128)(2,1)S(1)}, u32[]{:S(2)}, u32[]{:S(2)}) %collective-permute-start.18) | collective-permute-done | bytes 262176 | tf_op jit(solution)/shard_map/gather_inner/ppermute | solution.py:20
  92.1 0.5 collective-permute-start.21
  92.7 0.9 collective-permute-done.22.rest_7_
  94.4 3.9 %backward.1 = (f32[8,128,256]{2,1,0:T(8,128)S(1)}, f32[8,128,256]{2,1,0:T(8,128)S(1)}, bf16[8,128,256]{2,1,0:T(8,128)(2,1)S(1)}, bf16[8,128,256]{2,1,0:T(8,128)(...) custom-call(s32[1]{0:T(128)} %copy.12.count, ...), custom_call_target="tpu_custom_call" | custom-call | tf_op jit(solution)/shard_map/backward/pallas_call | solution.py:149
  98.3 0.7 collective-permute-start.23
  99.0 2.1 %collective-permute-start.24 = (bf16[8,128,256]{2,1,0:T(8,128)(2,1)S(1)}, bf16[8,128,256]{2,1,0:T(8,128)(2,1)S(1)}, u32[]{:S(2)}, u32[]{:S(2)}) collective-permute-start(bf16[8,128,256]{2,1,0:T(8,128)(2,1)S(1)} %get-tuple-element.68), channel_id=1, source_target_pairs={{0,16},{8,24},{16,0},{24,8},{1,17},{9,25},{17,1},{25,9},{2,18},{10... | collective-permute-start | bytes 1572872 | tf_op jit(solution)/shard_map/reduce_outer/ppermute | solution.py:20
  101.1 0.6 collective-permute-start.25
  101.8 3.7 %collective-permute-start.26 = (bf16[8,128,256]{2,1,0:T(8,128)(2,1)S(1)}, bf16[8,128,256]{2,1,0:T(8,128)(2,1)S(1)}, u32[]{:S(2)}, u32[]{:S(2)}) collective-permute-start(bf16[8,128,256]{2,1,0:T(8,128)(2,1)S(1)} %get-tuple-element.72), channel_id=1, source_target_pairs={{0,32},{32,64},{64,96},{96,0},{1,33},{33,65},{65,97},{97,1},{2,34}... | collective-permute-start | bytes 1572872 | tf_op jit(solution)/shard_map/reduce_outer/ppermute | solution.py:20
  105.5 2.7 %collective-permute-start.27 = (bf16[8,128,256]{2,1,0:T(8,128)(2,1)S(1)}, bf16[8,128,256]{2,1,0:T(8,128)(2,1)S(1)}, u32[]{:S(2)}, u32[]{:S(2)}) collective-permute-start(bf16[8,128,256]{2,1,0:T(8,128)(2,1)S(1)} %get-tuple-element.73), channel_id=1, source_target_pairs={{0,64},{32,96},{64,0},{96,32},{1,65},{33,97},{65,1},{97,33},{2,66}... | collective-permute-start | bytes 1572872 | tf_op jit(solution)/shard_map/reduce_outer/ppermute | solution.py:20
  108.2 17.3 %collective-permute-done.23.a = bf16[8,128,256]{2,1,0:T(8,128)(2,1)S(1)} collective-permute-done((bf16[8,128,256]{2,1,0:T(8,128)(2,1)S(1)}, bf16[8,128,256]{2,1,0:T(8,128)(2,1)S(1)}, u32[]{:S(2)}, u32[]{:S(2)}) %collective-permute-start.23) | collective-permute-done | bytes 524320 | tf_op jit(solution)/shard_map/reduce_outer/ppermute | solution.py:20
  125.5 0.9 collective-permute-done.25.c
  126.6 1.6 collective-permute-start.29
  128.2 2.6 %collective-permute-start.30 = (bf16[2,128,256]{2,1,0:T(8,128)(2,1)S(1)}, bf16[2,128,256]{2,1,0:T(8,128)(2,1)S(1)}, u32[]{:S(2)}, u32[]{:S(2)}) collective-permute-start(bf16[2,128,256]{2,1,0:T(8,128)(2,1)S(1)} %get-tuple-element.77), channel_id=1, source_target_pairs={{0,64},{32,96},{64,0},{96,32},{1,65},{33,97},{65,1},{97,33},{2,66}... | collective-permute-start | bytes 393224 | tf_op jit(solution)/shard_map/reduce_outer/ppermute | solution.py:20
  130.9 2.5 %collective-permute-start.31 = (bf16[2,128,256]{2,1,0:T(8,128)(2,1)S(1)}, bf16[2,128,256]{2,1,0:T(8,128)(2,1)S(1)}, u32[]{:S(2)}, u32[]{:S(2)}) collective-permute-start(bf16[2,128,256]{2,1,0:T(8,128)(2,1)S(1)} %get-tuple-element.78), channel_id=1, source_target_pairs={{0,96},{32,0},{64,32},{96,64},{1,97},{33,1},{65,33},{97,65},{2,98}... | collective-permute-start | bytes 393224 | tf_op jit(solution)/shard_map/reduce_outer/ppermute | solution.py:20
  133.4 6.8 %collective-permute-done.28.c = bf16[8,128,256]{2,1,0:T(8,128)(2,1)S(1)} collective-permute-done((bf16[8,128,256]{2,1,0:T(8,128)(2,1)S(1)}, bf16[8,128,256]{2,1,0:T(8,128)(2,1)S(1)}, u32[]{:S(2)}, u32[]{:S(2)}) %collective-permute-start.28) | collective-permute-done | bytes 524320 | tf_op jit(solution)/shard_map/reduce_outer/ppermute | solution.py:20
  140.6 0.8 collective-permute-start.33
  141.4 2.4 %collective-permute-start.34 = (bf16[2,128,256]{2,1,0:T(8,128)(2,1)S(1)}, bf16[2,128,256]{2,1,0:T(8,128)(2,1)S(1)}, u32[]{:S(2)}, u32[]{:S(2)}) collective-permute-start(bf16[2,128,256]{2,1,0:T(8,128)(2,1)S(1)} %get-tuple-element.81), channel_id=1, source_target_pairs={{0,24},{8,0},{16,8},{24,16},{1,25},{9,1},{17,9},{25,17},{2,26},{10... | collective-permute-start | bytes 393224 | tf_op jit(solution)/shard_map/reduce_outer/ppermute | solution.py:20
  143.8 1.4 collective-permute-done.31.refs_4_
  145.2 3.5 %collective-permute-done.32.refs_5_ = bf16[2,128,256]{2,1,0:T(8,128)(2,1)S(1)} collective-permute-done((bf16[2,128,256]{2,1,0:T(8,128)(2,1)S(1)}, bf16[2,128,256]{2,1,0:T(8,128)(2,1)S(1)}, u32[]{:S(2)}, u32[]{:S(2)}) %collective-permute-start.32) | collective-permute-done | bytes 131104 | tf_op jit(solution)/shard_map/reduce_outer/ppermute | solution.py:20
  148.7 0.7 collective-permute-done.34.refs_7_
  149.4 0.6 outer_sum.1
  150.1 1.2 collective-permute-done.35
  151.4 5.0 %collective-permute-start.38 = (f32[128,128]{1,0:T(8,128)S(1)}, f32[128,128]{1,0:T(8,128)S(1)}, u32[]{:S(2)}, u32[]{:S(2)}) collective-permute-start(f32[128,128]{1,0:T(8,128)S(1)} %add.105), channel_id=1, source_target_pairs={{0,6},{2,0},{4,2},{6,4},{1,7},{3,1},{5,3},{7,5},{8,14},{10,8},{12,... | collective-permute-start | bytes 196616 | tf_op jit(solution)/shard_map/reduce_gram/ppermute | solution.py:20
  156.4 1.5 collective-permute-start.36
  158.3 4.6 %collective-permute-done.37 = f32[128,128]{1,0:T(8,128)S(1)} collective-permute-done((f32[128,128]{1,0:T(8,128)S(1)}, f32[128,128]{1,0:T(8,128)S(1)}, u32[]{:S(2)}, u32[]{:S(2)}) %collective-permute-start.37) | collective-permute-done | bytes 65568 | tf_op jit(solution)/shard_map/reduce_gram/ppermute | solution.py:20
  162.9 2.4 %collective-permute-start.41 = (f32[128,128]{1,0:T(8,128)S(1)}, f32[128,128]{1,0:T(8,128)S(1)}, u32[]{:S(2)}, u32[]{:S(2)}) collective-permute-start(f32[128,128]{1,0:T(8,128)S(1)} %add_add_fusion.2), channel_id=1, source_target_pairs={{0,24},{8,0},{16,8},{24,16},{1,25},{9,1},{17,9},{25,17},{2,26},{10... | collective-permute-start | bytes 196616 | tf_op jit(solution)/shard_map/reduce_gram/ppermute | solution.py:20
  165.3 1.5 collective-permute-start.39
  166.8 0.4 collective-permute-done.41
  167.2 4.3 %collective-permute-done.40 = f32[128,128]{1,0:T(8,128)S(1)} collective-permute-done((f32[128,128]{1,0:T(8,128)S(1)}, f32[128,128]{1,0:T(8,128)S(1)}, u32[]{:S(2)}, u32[]{:S(2)}) %collective-permute-start.40) | collective-permute-done | bytes 65568 | tf_op jit(solution)/shard_map/reduce_gram/ppermute | solution.py:20
  171.5 3.8 %collective-permute-start.44 = (f32[128,128]{1,0:T(8,128)S(1)}, f32[128,128]{1,0:T(8,128)S(1)}, u32[]{:S(2)}, u32[]{:S(2)}) collective-permute-start(f32[128,128]{1,0:T(8,128)S(1)} %add_add_fusion.1), channel_id=1, source_target_pairs={{0,96},{32,0},{64,32},{96,64},{1,97},{33,1},{65,33},{97,65},{2,98}... | collective-permute-start | bytes 196616 | tf_op jit(solution)/shard_map/reduce_gram/ppermute | solution.py:20
  175.3 1.5 collective-permute-start.42
  176.8 1.0 collective-permute-done.44
  177.8 3.7 %collective-permute-done.43 = f32[128,128]{1,0:T(8,128)S(1)} collective-permute-done((f32[128,128]{1,0:T(8,128)S(1)}, f32[128,128]{1,0:T(8,128)S(1)}, u32[]{:S(2)}, u32[]{:S(2)}) %collective-permute-start.43) | collective-permute-done | bytes 65568 | tf_op jit(solution)/shard_map/reduce_gram/ppermute | solution.py:20
  181.5 5.9 %finish.1 = (f32[1024,128]{1,0:T(8,128)}, f32[128,128]{1,0:T(8,128)}) custom-call(f32[128,128]{1,0:T(8,128)S(1)} %add_add_fusion.refs_0_, f32[4,128,256]{2,1,0:T(8,128)S(1)} %get-tuple-element.83.refs_1_), custom_call_target="tpu_custom_call" | custom-call | tf_op jit(solution)/shard_map/finish/pallas_call | solution.py:326
  (57 shorter events, 3.1 us)
Async XLA Ops:
  1.6 10.2 %collective-permute-start.5 = (bf16[512,128]{1,0:T(8,128)(2,1)S(1)}, bf16[512,128]{1,0:T(8,128)(2,1)S(1)}, u32[]{:S(2)}, u32[]{:S(2)}) collective-permute-start(bf16[512,128]{1,0:T(8,128)(2,1)S(1)} %get-tuple-element.48), channel_id=1, source_target_pairs={{0,8},{8,16},{16,24},{24,0},{1,9},{9,17},{17,25},{25,1},{2,10},{10... | collective-permute-start | bytes 393224 | tf_op jit(solution)/shard_map/gather_basis/ppermute | solution.py:20
  3.3 9.9 %collective-permute-start.4 = (bf16[512,128]{1,0:T(8,128)(2,1)S(1)}, bf16[512,128]{1,0:T(8,128)(2,1)S(1)}, u32[]{:S(2)}, u32[]{:S(2)}) collective-permute-start(bf16[512,128]{1,0:T(8,128)(2,1)S(1)} %get-tuple-element.48), channel_id=1, source_target_pairs={{0,16},{8,24},{16,0},{24,8},{1,17},{9,25},{17,1},{25,9},{2,18},{10... | collective-permute-start | bytes 393224 | tf_op jit(solution)/shard_map/gather_basis/ppermute | solution.py:20
  6.2 7.0 %collective-permute-start.3 = (bf16[512,128]{1,0:T(8,128)(2,1)S(1)}, bf16[512,128]{1,0:T(8,128)(2,1)S(1)}, u32[]{:S(2)}, u32[]{:S(2)}) collective-permute-start(bf16[512,128]{1,0:T(8,128)(2,1)S(1)} %get-tuple-element.48), channel_id=1, source_target_pairs={{0,24},{8,0},{16,8},{24,16},{1,25},{9,1},{17,9},{25,17},{2,26},{10... | collective-permute-start | bytes 393224 | tf_op jit(solution)/shard_map/gather_basis/ppermute | solution.py:20
  7.6 7.6 %collective-permute-start.2 = (bf16[512,128]{1,0:T(8,128)(2,1)S(1)}, bf16[512,128]{1,0:T(8,128)(2,1)S(1)}, u32[]{:S(2)}, u32[]{:S(2)}) collective-permute-start(bf16[512,128]{1,0:T(8,128)(2,1)S(1)} %get-tuple-element.44), channel_id=1, source_target_pairs={{0,32},{32,64},{64,96},{96,0},{1,33},{33,65},{65,97},{97,1},{2,34}... | collective-permute-start | bytes 393224 | tf_op jit(solution)/shard_map/gather_basis/ppermute | solution.py:20
  9.1 7.9 %collective-permute-start.1 = (bf16[512,128]{1,0:T(8,128)(2,1)S(1)}, bf16[512,128]{1,0:T(8,128)(2,1)S(1)}, u32[]{:S(2)}, u32[]{:S(2)}) collective-permute-start(bf16[512,128]{1,0:T(8,128)(2,1)S(1)} %get-tuple-element.44), channel_id=1, source_target_pairs={{0,64},{32,96},{64,0},{96,32},{1,65},{33,97},{65,1},{97,33},{2,66}... | collective-permute-start | bytes 393224 | tf_op jit(solution)/shard_map/gather_basis/ppermute | solution.py:20
  11.8 5.2 %collective-permute-start = (bf16[512,128]{1,0:T(8,128)(2,1)S(1)}, bf16[512,128]{1,0:T(8,128)(2,1)S(1)}, u32[]{:S(2)}, u32[]{:S(2)}) collective-permute-start(bf16[512,128]{1,0:T(8,128)(2,1)S(1)} %get-tuple-element.44), channel_id=1, source_target_pairs={{0,96},{32,0},{64,32},{96,64},{1,97},{33,1},{65,33},{97,65},{2,98}... | collective-permute-start | bytes 393224 | tf_op jit(solution)/shard_map/gather_basis/ppermute | solution.py:20
  17.2 15.0 %collective-permute-start.11 = (bf16[2048,128]{1,0:T(8,128)(2,1)S(1)}, bf16[2048,128]{1,0:T(8,128)(2,1)S(1)}, u32[]{:S(2)}, u32[]{:S(2)}) collective-permute-start(bf16[2048,128]{1,0:T(8,128)(2,1)S(1)} %constant_dynamic-update-slice_fusion.4), channel_id=1, source_target_pairs={{0,32},{32,64},{64,96},{96,0},{1,33},{33,65},{65,97},{97,1},{2,34}... | collective-permute-start | bytes 1572872 | tf_op jit(solution)/shard_map/gather_basis/ppermute | solution.py:20
  18.5 24.3 %collective-permute-start.10 = (bf16[2048,128]{1,0:T(8,128)(2,1)S(1)}, bf16[2048,128]{1,0:T(8,128)(2,1)S(1)}, u32[]{:S(2)}, u32[]{:S(2)}) collective-permute-start(bf16[2048,128]{1,0:T(8,128)(2,1)S(1)} %constant_dynamic-update-slice_fusion.4), channel_id=1, source_target_pairs={{0,64},{32,96},{64,0},{96,32},{1,65},{33,97},{65,1},{97,33},{2,66}... | collective-permute-start | bytes 1572872 | tf_op jit(solution)/shard_map/gather_basis/ppermute | solution.py:20
  21.4 21.4 %collective-permute-start.9 = (bf16[2048,128]{1,0:T(8,128)(2,1)S(1)}, bf16[2048,128]{1,0:T(8,128)(2,1)S(1)}, u32[]{:S(2)}, u32[]{:S(2)}) collective-permute-start(bf16[2048,128]{1,0:T(8,128)(2,1)S(1)} %constant_dynamic-update-slice_fusion.4), channel_id=1, source_target_pairs={{0,96},{32,0},{64,32},{96,64},{1,97},{33,1},{65,33},{97,65},{2,98}... | collective-permute-start | bytes 1572872 | tf_op jit(solution)/shard_map/gather_basis/ppermute | solution.py:20
  22.6 23.3 %collective-permute-start.8 = (bf16[2048,128]{1,0:T(8,128)(2,1)S(1)}, bf16[2048,128]{1,0:T(8,128)(2,1)S(1)}, u32[]{:S(2)}, u32[]{:S(2)}) collective-permute-start(bf16[2048,128]{1,0:T(8,128)(2,1)S(1)} %constant_dynamic-update-slice_fusion), channel_id=1, source_target_pairs={{0,8},{8,16},{16,24},{24,0},{1,9},{9,17},{17,25},{25,1},{2,10},{10... | collective-permute-start | bytes 1572872 | tf_op jit(solution)/shard_map/gather_basis/ppermute | solution.py:20
  23.3 22.6 %collective-permute-start.7 = (bf16[2048,128]{1,0:T(8,128)(2,1)S(1)}, bf16[2048,128]{1,0:T(8,128)(2,1)}, u32[]{:S(2)}, u32[]{:S(2)}) collective-permute-start(bf16[2048,128]{1,0:T(8,128)(2,1)S(1)} %constant_dynamic-update-slice_fusion), channel_id=1, source_target_pairs={{0,16},{8,24},{16,0},{24,8},{1,17},{9,25},{17,1},{25,9},{2,18},{10... | collective-permute-start | bytes 1572872 | tf_op jit(solution)/shard_map/gather_basis/ppermute | solution.py:20
  32.1 14.4 %collective-permute-start.6 = (bf16[2048,128]{1,0:T(8,128)(2,1)S(1)}, bf16[2048,128]{1,0:T(8,128)(2,1)}, u32[]{:S(2)}, u32[]{:S(2)}) collective-permute-start(bf16[2048,128]{1,0:T(8,128)(2,1)S(1)} %constant_dynamic-update-slice_fusion), channel_id=1, source_target_pairs={{0,24},{8,0},{16,8},{24,16},{1,25},{9,1},{17,9},{25,17},{2,26},{10... | collective-permute-start | bytes 1572872 | tf_op jit(solution)/shard_map/gather_basis/ppermute | solution.py:20
  51.5 4.2 %collective-permute-start.12 = (f32[16,256,128]{2,1,0:T(8,128)S(1)}, f32[16,256,128]{2,1,0:T(8,128)S(1)}, u32[]{:S(2)}, u32[]{:S(2)}) collective-permute-start(f32[16,256,128]{2,1,0:T(8,128)S(1)} %get-tuple-element.53), channel_id=1, source_target_pairs={{0,1},{1,0},{2,3},{3,2},{4,5},{5,4},{6,7},{7,6},{8,9},{9,8},{10,11... | collective-permute-start | bytes 6291464 | tf_op jit(solution)/shard_map/reduce_inner/ppermute | solution.py:20
  56.4 17.1 %collective-permute-start.15 = (f16[1040,128]{1,0:T(8,128)(2,1)S(1)}, f16[1040,128]{1,0:T(8,128)(2,1)S(1)}, u32[]{:S(2)}, u32[]{:S(2)}) collective-permute-start(f16[1040,128]{1,0:T(8,128)(2,1)S(1)} %convert_element_type.20), channel_id=1, source_target_pairs={{0,6},{2,0},{4,2},{6,4},{1,7},{3,1},{5,3},{7,5},{8,14},{10,8},{12,... | collective-permute-start | bytes 798728 | tf_op jit(solution)/shard_map/reduce_inner/ppermute | solution.py:20
  61.8 11.7 %collective-permute-start.14 = (f16[1040,128]{1,0:T(8,128)(2,1)S(1)}, f16[1040,128]{1,0:T(8,128)(2,1)S(1)}, u32[]{:S(2)}, u32[]{:S(2)}) collective-permute-start(f16[1040,128]{1,0:T(8,128)(2,1)S(1)} %convert_element_type.19), channel_id=1, source_target_pairs={{0,4},{2,6},{4,0},{6,2},{1,5},{3,7},{5,1},{7,3},{8,12},{10,14},{12... | collective-permute-start | bytes 798728 | tf_op jit(solution)/shard_map/reduce_inner/ppermute | solution.py:20
  61.8 15.1 %collective-permute-start.13 = (f16[1040,128]{1,0:T(8,128)(2,1)S(1)}, f16[1040,128]{1,0:T(8,128)(2,1)S(1)}, u32[]{:S(2)}, u32[]{:S(2)}) collective-permute-start(f16[1040,128]{1,0:T(8,128)(2,1)S(1)} %convert_element_type.18), channel_id=1, source_target_pairs={{0,2},{2,4},{4,6},{6,0},{1,3},{3,5},{5,7},{7,1},{8,10},{10,12},{12... | collective-permute-start | bytes 798728 | tf_op jit(solution)/shard_map/reduce_inner/ppermute | solution.py:20
  77.3 14.8 %collective-permute-start.18 = (bf16[4,128,256]{2,1,0:T(8,128)(2,1)S(1)}, bf16[4,128,256]{2,1,0:T(8,128)(2,1)S(1)}, u32[]{:S(2)}, u32[]{:S(2)}) collective-permute-start(bf16[4,128,256]{2,1,0:T(8,128)(2,1)S(1)} %inner_sum.1.rest_0_), channel_id=1, source_target_pairs={{0,2},{2,4},{4,6},{6,0},{1,3},{3,5},{5,7},{7,1},{8,10},{10,12},{12... | collective-permute-start | bytes 786440 | tf_op jit(solution)/shard_map/gather_inner/ppermute | solution.py:20
  77.4 14.7 %collective-permute-start.17 = (bf16[4,128,256]{2,1,0:T(8,128)(2,1)S(1)}, bf16[4,128,256]{2,1,0:T(8,128)(2,1)S(1)}, u32[]{:S(2)}, u32[]{:S(2)}) collective-permute-start(bf16[4,128,256]{2,1,0:T(8,128)(2,1)S(1)} %inner_sum.1.rest_0_), channel_id=1, source_target_pairs={{0,4},{2,6},{4,0},{6,2},{1,5},{3,7},{5,1},{7,3},{8,12},{10,14},{12... | collective-permute-start | bytes 786440 | tf_op jit(solution)/shard_map/gather_inner/ppermute | solution.py:20
  79.7 13.0 %collective-permute-start.16 = (bf16[4,128,256]{2,1,0:T(8,128)(2,1)S(1)}, bf16[4,128,256]{2,1,0:T(8,128)(2,1)S(1)}, u32[]{:S(2)}, u32[]{:S(2)}) collective-permute-start(bf16[4,128,256]{2,1,0:T(8,128)(2,1)S(1)} %inner_sum.1.rest_0_), channel_id=1, source_target_pairs={{0,6},{2,0},{4,2},{6,4},{1,7},{3,1},{5,3},{7,5},{8,14},{10,8},{12,... | collective-permute-start | bytes 786440 | tf_op jit(solution)/shard_map/gather_inner/ppermute | solution.py:20
  80.6 12.1 %collective-permute-start.19 = (bf16[4,128,256]{2,1,0:T(8,128)(2,1)S(1)}, bf16[4,128,256]{2,1,0:T(8,128)(2,1)S(1)}, u32[]{:S(2)}, u32[]{:S(2)}) collective-permute-start(bf16[4,128,256]{2,1,0:T(8,128)(2,1)S(1)} %inner_sum.1.rest_0_), channel_id=1, source_target_pairs={{0,1},{1,0},{2,3},{3,2},{4,5},{5,4},{6,7},{7,6},{8,9},{9,8},{10,11... | collective-permute-start | bytes 786440 | tf_op jit(solution)/shard_map/gather_inner/ppermute | solution.py:20
  92.1 1.5 collective-permute-start.22
  92.1 1.9 %collective-permute-start.21 = (bf16[4,128,256]{2,1,0:T(8,128)(2,1)S(1)}, bf16[4,128,256]{2,1,0:T(8,128)(2,1)S(1)}, u32[]{:S(2)}, u32[]{:S(2)}) collective-permute-start(bf16[4,128,256]{2,1,0:T(8,128)(2,1)S(1)} %collective-permute-done.17.rest_2_), channel_id=1, source_target_pairs={{0,1},{1,0},{2,3},{3,2},{4,5},{5,4},{6,7},{7,6},{8,9},{9,8},{10,11... | collective-permute-start | bytes 786440 | tf_op jit(solution)/shard_map/gather_inner/ppermute | solution.py:20
  92.7 1.7 collective-permute-start.20
  98.3 27.2 %collective-permute-start.23 = (bf16[8,128,256]{2,1,0:T(8,128)(2,1)S(1)}, bf16[8,128,256]{2,1,0:T(8,128)(2,1)S(1)}, u32[]{:S(2)}, u32[]{:S(2)}) collective-permute-start(bf16[8,128,256]{2,1,0:T(8,128)(2,1)S(1)} %get-tuple-element.67), channel_id=1, source_target_pairs={{0,8},{8,16},{16,24},{24,0},{1,9},{9,17},{17,25},{25,1},{2,10},{10... | collective-permute-start | bytes 1572872 | tf_op jit(solution)/shard_map/reduce_outer/ppermute | solution.py:20
  99.0 26.5 %collective-permute-start.24 = (bf16[8,128,256]{2,1,0:T(8,128)(2,1)S(1)}, bf16[8,128,256]{2,1,0:T(8,128)(2,1)S(1)}, u32[]{:S(2)}, u32[]{:S(2)}) collective-permute-start(bf16[8,128,256]{2,1,0:T(8,128)(2,1)S(1)} %get-tuple-element.68), channel_id=1, source_target_pairs={{0,16},{8,24},{16,0},{24,8},{1,17},{9,25},{17,1},{25,9},{2,18},{10... | collective-permute-start | bytes 1572872 | tf_op jit(solution)/shard_map/reduce_outer/ppermute | solution.py:20
  101.1 25.2 %collective-permute-start.25 = (bf16[8,128,256]{2,1,0:T(8,128)(2,1)S(1)}, bf16[8,128,256]{2,1,0:T(8,128)(2,1)S(1)}, u32[]{:S(2)}, u32[]{:S(2)}) collective-permute-start(bf16[8,128,256]{2,1,0:T(8,128)(2,1)S(1)} %get-tuple-element.69), channel_id=1, source_target_pairs={{0,24},{8,0},{16,8},{24,16},{1,25},{9,1},{17,9},{25,17},{2,26},{10... | collective-permute-start | bytes 1572872 | tf_op jit(solution)/shard_map/reduce_outer/ppermute | solution.py:20
  101.8 29.1 %collective-permute-start.26 = (bf16[8,128,256]{2,1,0:T(8,128)(2,1)S(1)}, bf16[8,128,256]{2,1,0:T(8,128)(2,1)S(1)}, u32[]{:S(2)}, u32[]{:S(2)}) collective-permute-start(bf16[8,128,256]{2,1,0:T(8,128)(2,1)S(1)} %get-tuple-element.72), channel_id=1, source_target_pairs={{0,32},{32,64},{64,96},{96,0},{1,33},{33,65},{65,97},{97,1},{2,34}... | collective-permute-start | bytes 1572872 | tf_op jit(solution)/shard_map/reduce_outer/ppermute | solution.py:20
  105.5 27.9 %collective-permute-start.27 = (bf16[8,128,256]{2,1,0:T(8,128)(2,1)S(1)}, bf16[8,128,256]{2,1,0:T(8,128)(2,1)S(1)}, u32[]{:S(2)}, u32[]{:S(2)}) collective-permute-start(bf16[8,128,256]{2,1,0:T(8,128)(2,1)S(1)} %get-tuple-element.73), channel_id=1, source_target_pairs={{0,64},{32,96},{64,0},{96,32},{1,65},{33,97},{65,1},{97,33},{2,66}... | collective-permute-start | bytes 1572872 | tf_op jit(solution)/shard_map/reduce_outer/ppermute | solution.py:20
  125.5 14.8 %collective-permute-start.28 = (bf16[8,128,256]{2,1,0:T(8,128)(2,1)S(1)}, bf16[8,128,256]{2,1,0:T(8,128)(2,1)S(1)}, u32[]{:S(2)}, u32[]{:S(2)}) collective-permute-start(bf16[8,128,256]{2,1,0:T(8,128)(2,1)S(1)} %get-tuple-element.74), channel_id=1, source_target_pairs={{0,96},{32,0},{64,32},{96,64},{1,97},{33,1},{65,33},{97,65},{2,98}... | collective-permute-start | bytes 1572872 | tf_op jit(solution)/shard_map/reduce_outer/ppermute | solution.py:20
  126.6 14.8 %collective-permute-start.29 = (bf16[2,128,256]{2,1,0:T(8,128)(2,1)S(1)}, bf16[2,128,256]{2,1,0:T(8,128)(2,1)S(1)}, u32[]{:S(2)}, u32[]{:S(2)}) collective-permute-start(bf16[2,128,256]{2,1,0:T(8,128)(2,1)S(1)} %get-tuple-element.76), channel_id=1, source_target_pairs={{0,32},{32,64},{64,96},{96,0},{1,33},{33,65},{65,97},{97,1},{2,34}... | collective-permute-start | bytes 393224 | tf_op jit(solution)/shard_map/reduce_outer/ppermute | solution.py:20
  128.2 15.6 %collective-permute-start.30 = (bf16[2,128,256]{2,1,0:T(8,128)(2,1)S(1)}, bf16[2,128,256]{2,1,0:T(8,128)(2,1)S(1)}, u32[]{:S(2)}, u32[]{:S(2)}) collective-permute-start(bf16[2,128,256]{2,1,0:T(8,128)(2,1)S(1)} %get-tuple-element.77), channel_id=1, source_target_pairs={{0,64},{32,96},{64,0},{96,32},{1,65},{33,97},{65,1},{97,33},{2,66}... | collective-permute-start | bytes 393224 | tf_op jit(solution)/shard_map/reduce_outer/ppermute | solution.py:20
  130.9 14.3 %collective-permute-start.31 = (bf16[2,128,256]{2,1,0:T(8,128)(2,1)S(1)}, bf16[2,128,256]{2,1,0:T(8,128)(2,1)S(1)}, u32[]{:S(2)}, u32[]{:S(2)}) collective-permute-start(bf16[2,128,256]{2,1,0:T(8,128)(2,1)S(1)} %get-tuple-element.78), channel_id=1, source_target_pairs={{0,96},{32,0},{64,32},{96,64},{1,97},{33,1},{65,33},{97,65},{2,98}... | collective-permute-start | bytes 393224 | tf_op jit(solution)/shard_map/reduce_outer/ppermute | solution.py:20
  140.5 8.2 %collective-permute-start.32 = (bf16[2,128,256]{2,1,0:T(8,128)(2,1)S(1)}, bf16[2,128,256]{2,1,0:T(8,128)(2,1)S(1)}, u32[]{:S(2)}, u32[]{:S(2)}) collective-permute-start(bf16[2,128,256]{2,1,0:T(8,128)(2,1)S(1)} %get-tuple-element.79), channel_id=1, source_target_pairs={{0,8},{8,16},{16,24},{24,0},{1,9},{9,17},{17,25},{25,1},{2,10},{10... | collective-permute-start | bytes 393224 | tf_op jit(solution)/shard_map/reduce_outer/ppermute | solution.py:20
  140.6 8.1 %collective-permute-start.33 = (bf16[2,128,256]{2,1,0:T(8,128)(2,1)S(1)}, bf16[2,128,256]{2,1,0:T(8,128)(2,1)S(1)}, u32[]{:S(2)}, u32[]{:S(2)}) collective-permute-start(bf16[2,128,256]{2,1,0:T(8,128)(2,1)S(1)} %get-tuple-element.80), channel_id=1, source_target_pairs={{0,16},{8,24},{16,0},{24,8},{1,17},{9,25},{17,1},{25,9},{2,18},{10... | collective-permute-start | bytes 393224 | tf_op jit(solution)/shard_map/reduce_outer/ppermute | solution.py:20
  141.4 8.0 %collective-permute-start.34 = (bf16[2,128,256]{2,1,0:T(8,128)(2,1)S(1)}, bf16[2,128,256]{2,1,0:T(8,128)(2,1)S(1)}, u32[]{:S(2)}, u32[]{:S(2)}) collective-permute-start(bf16[2,128,256]{2,1,0:T(8,128)(2,1)S(1)} %get-tuple-element.81), channel_id=1, source_target_pairs={{0,24},{8,0},{16,8},{24,16},{1,25},{9,1},{17,9},{25,17},{2,26},{10... | collective-permute-start | bytes 393224 | tf_op jit(solution)/shard_map/reduce_outer/ppermute | solution.py:20
  150.0 1.3 collective-permute-start.35
  151.4 6.9 %collective-permute-start.38 = (f32[128,128]{1,0:T(8,128)S(1)}, f32[128,128]{1,0:T(8,128)S(1)}, u32[]{:S(2)}, u32[]{:S(2)}) collective-permute-start(f32[128,128]{1,0:T(8,128)S(1)} %add.105), channel_id=1, source_target_pairs={{0,6},{2,0},{4,2},{6,4},{1,7},{3,1},{5,3},{7,5},{8,14},{10,8},{12,... | collective-permute-start | bytes 196616 | tf_op jit(solution)/shard_map/reduce_gram/ppermute | solution.py:20
  156.4 6.5 %collective-permute-start.37 = (f32[128,128]{1,0:T(8,128)S(1)}, f32[128,128]{1,0:T(8,128)S(1)}, u32[]{:S(2)}, u32[]{:S(2)}) collective-permute-start(f32[128,128]{1,0:T(8,128)S(1)} %add.105), channel_id=1, source_target_pairs={{0,2},{2,4},{4,6},{6,0},{1,3},{3,5},{5,7},{7,1},{8,10},{10,12},{12... | collective-permute-start | bytes 196616 | tf_op jit(solution)/shard_map/reduce_gram/ppermute | solution.py:20
  156.4 6.5 %collective-permute-start.36 = (f32[128,128]{1,0:T(8,128)S(1)}, f32[128,128]{1,0:T(8,128)S(1)}, u32[]{:S(2)}, u32[]{:S(2)}) collective-permute-start(f32[128,128]{1,0:T(8,128)S(1)} %add.105), channel_id=1, source_target_pairs={{0,4},{2,6},{4,0},{6,2},{1,5},{3,7},{5,1},{7,3},{8,12},{10,14},{12... | collective-permute-start | bytes 196616 | tf_op jit(solution)/shard_map/reduce_gram/ppermute | solution.py:20
  162.9 4.3 %collective-permute-start.41 = (f32[128,128]{1,0:T(8,128)S(1)}, f32[128,128]{1,0:T(8,128)S(1)}, u32[]{:S(2)}, u32[]{:S(2)}) collective-permute-start(f32[128,128]{1,0:T(8,128)S(1)} %add_add_fusion.2), channel_id=1, source_target_pairs={{0,24},{8,0},{16,8},{24,16},{1,25},{9,1},{17,9},{25,17},{2,26},{10... | collective-permute-start | bytes 196616 | tf_op jit(solution)/shard_map/reduce_gram/ppermute | solution.py:20
  165.3 6.2 %collective-permute-start.40 = (f32[128,128]{1,0:T(8,128)S(1)}, f32[128,128]{1,0:T(8,128)S(1)}, u32[]{:S(2)}, u32[]{:S(2)}) collective-permute-start(f32[128,128]{1,0:T(8,128)S(1)} %add_add_fusion.2), channel_id=1, source_target_pairs={{0,8},{8,16},{16,24},{24,0},{1,9},{9,17},{17,25},{25,1},{2,10},{10... | collective-permute-start | bytes 196616 | tf_op jit(solution)/shard_map/reduce_gram/ppermute | solution.py:20
  165.3 6.2 %collective-permute-start.39 = (f32[128,128]{1,0:T(8,128)S(1)}, f32[128,128]{1,0:T(8,128)S(1)}, u32[]{:S(2)}, u32[]{:S(2)}) collective-permute-start(f32[128,128]{1,0:T(8,128)S(1)} %add_add_fusion.2), channel_id=1, source_target_pairs={{0,16},{8,24},{16,0},{24,8},{1,17},{9,25},{17,1},{25,9},{2,18},{10... | collective-permute-start | bytes 196616 | tf_op jit(solution)/shard_map/reduce_gram/ppermute | solution.py:20
  171.5 6.3 %collective-permute-start.44 = (f32[128,128]{1,0:T(8,128)S(1)}, f32[128,128]{1,0:T(8,128)S(1)}, u32[]{:S(2)}, u32[]{:S(2)}) collective-permute-start(f32[128,128]{1,0:T(8,128)S(1)} %add_add_fusion.1), channel_id=1, source_target_pairs={{0,96},{32,0},{64,32},{96,64},{1,97},{33,1},{65,33},{97,65},{2,98}... | collective-permute-start | bytes 196616 | tf_op jit(solution)/shard_map/reduce_gram/ppermute | solution.py:20
  175.3 6.2 %collective-permute-start.43 = (f32[128,128]{1,0:T(8,128)S(1)}, f32[128,128]{1,0:T(8,128)S(1)}, u32[]{:S(2)}, u32[]{:S(2)}) collective-permute-start(f32[128,128]{1,0:T(8,128)S(1)} %add_add_fusion.1), channel_id=1, source_target_pairs={{0,32},{32,64},{64,96},{96,0},{1,33},{33,65},{65,97},{97,1},{2,34}... | collective-permute-start | bytes 196616 | tf_op jit(solution)/shard_map/reduce_gram/ppermute | solution.py:20
  175.3 6.2 %collective-permute-start.42 = (f32[128,128]{1,0:T(8,128)S(1)}, f32[128,128]{1,0:T(8,128)S(1)}, u32[]{:S(2)}, u32[]{:S(2)}) collective-permute-start(f32[128,128]{1,0:T(8,128)S(1)} %add_add_fusion.1), channel_id=1, source_target_pairs={{0,64},{32,96},{64,0},{96,32},{1,65},{33,97},{65,1},{97,33},{2,66}... | collective-permute-start | bytes 196616 | tf_op jit(solution)/shard_map/reduce_gram/ppermute | solution.py:20

commit v4 on v3

--- a/solution.py
+++ b/solution.py
@@ -75,7 +75,7 @@
 
 
 def forward_kernel(count, row_at, col_at, tiles, *rest):
-    pieces, (keep, away, held, total, sems) = rest[:8], rest[8:]
+    pieces, (total, away, held, sems) = rest[:-4], rest[-4:]
     chunks = (count[0] + CHUNK - 1) // CHUNK
     copies = load_pieces(pieces, held, sems)
     total[...] = jnp.zeros_like(total)
@@ -91,36 +91,32 @@
         return 0
 
     lax.fori_loop(0, chunks, body, 0)
-    half = keep.shape[0]
-    one = pltpu.make_async_copy(total.at[pl.ds(half, half)], away, sems.at[0])
-    two = pltpu.make_async_copy(total.at[pl.ds(0, half)], keep, sems.at[1])
-    one.start()
-    two.start()
-    one.wait()
-    two.wait()
+    away[...] = total[pl.ds(16, 16)]
 
 
 def forward(count, row_at, col_at, tiles, pieces):
     any_spec = pl.BlockSpec(memory_space=pl.ANY)
-    half = jax.ShapeDtypeStruct((16, SIDE, RANK), F32)
     return pl.pallas_call(
         forward_kernel,
-        out_shape=(half, half),
-        in_specs=[pl.BlockSpec(memory_space=pltpu.SMEM)] * 3 + whole(1) + [any_spec] * 8,
-        out_specs=(any_spec, any_spec),
+        out_shape=(
+            jax.ShapeDtypeStruct((33, SIDE, RANK), F32),
+            jax.ShapeDtypeStruct((16, SIDE, RANK), F32),
+        ),
+        in_specs=[pl.BlockSpec(memory_space=pltpu.SMEM)] * 3
+        + whole(1)
+        + [any_spec] * len(pieces),
+        out_specs=tuple(whole(2)),
         scratch_shapes=[
             pltpu.VMEM((64, SIDE, RANK), BF16),
-            pltpu.VMEM((33, SIDE, RANK), F32),
-            pltpu.SemaphoreType.DMA((8,)),
+            pltpu.SemaphoreType.DMA((len(pieces),)),
         ],
-        compiler_params=limits(11),
+        compiler_params=limits(8),
         name="forward",
     )(count, row_at, col_at, tiles, *pieces)
 
 
 def backward_kernel(count, row_at, col_at, tiles, *rest):
-    pieces, keeps, aways = rest[:8], rest[8:10], rest[10:16]
-    held, total, sems = rest[16:]
+    pieces, (total, *aways, held, sems) = rest[:8], rest[8:]
     chunks = (count[0] + CHUNK - 1) // CHUNK
     copies = load_pieces(pieces, held, sems)
     total[...] = jnp.zeros_like(total)
@@ -137,29 +133,27 @@
 
     lax.fori_loop(0, chunks, body, 0)
     for h in range(2):
-        keeps[h][...] = total[pl.ds(32 * h, 8)]
-        for d in range(3):
-            aways[3 * h + d][...] = total[pl.ds(32 * h + 8 * (d + 1), 8)].astype(BF16)
+        for half in range(2):
+            at = pl.ds(32 * h + 16 + 4 * half, 4)
+            aways[2 * h + half][...] = total[at].astype(BF16)
 
 
 def backward(count, row_at, col_at, tiles, pieces):
     any_spec = pl.BlockSpec(memory_space=pl.ANY)
-    part = jax.ShapeDtypeStruct((8, RANK, SIDE), BF16)
-    keep = jax.ShapeDtypeStruct((8, RANK, SIDE), F32)
-    outs = pl.pallas_call(
+    part = jax.ShapeDtypeStruct((4, RANK, SIDE), BF16)
+    total, *aways = pl.pallas_call(
         backward_kernel,
-        out_shape=(keep,) * 2 + (part,) * 6,
+        out_shape=(jax.ShapeDtypeStruct((65, RANK, SIDE), F32),) + (part,) * 4,
         in_specs=[pl.BlockSpec(memory_space=pltpu.SMEM)] * 3 + whole(1) + [any_spec] * 8,
-        out_specs=tuple(whole(8)),
+        out_specs=tuple(whole(5)),
         scratch_shapes=[
             pltpu.VMEM((32, RANK, SIDE), BF16),
-            pltpu.VMEM((65, RANK, SIDE), F32),
             pltpu.SemaphoreType.DMA((8,)),
         ],
-        compiler_params=limits(14),
+        compiler_params=limits(6),
         name="backward",
     )(count, row_at, col_at, tiles, *pieces)
-    return outs[:2], (outs[2:5], outs[5:8])
+    return total, (aways[:2], aways[2:])
 
 
 def core_sum_kernel(keep, came, kept, *outs):
@@ -208,26 +202,48 @@
     )(kept, *parts)
 
 
-def middle_kernel(keep, a, b, c, next_keep, *aways):
-    for d in range(4):
-        at = pl.ds(2 * d, 2)
-        total = (keep[at] + a[at].astype(F32)) + (b[at].astype(F32) + c[at].astype(F32))
-        if d == 0:
-            next_keep[...] = total
-        else:
-            aways[d - 1][...] = total.astype(BF16)
-
-
-def middle_sum(keep, came):
+def relay_sum(total, came, half):
+    part = jax.ShapeDtypeStruct((8, RANK, SIDE), BF16)
+
+    def kernel(total, a, b, right, left):
+        low, high = pl.ds(0, 4), pl.ds(4, 4)
+        at = 32 * half + 8
+        right[low] = (total[pl.ds(at, 4)] + a[...].astype(F32)).astype(BF16)
+        right[high] = total[pl.ds(at + 4, 4)].astype(BF16)
+        at = 32 * half + 24
+        left[low] = total[pl.ds(at, 4)].astype(BF16)
+        left[high] = (total[pl.ds(at + 4, 4)] + b[...].astype(F32)).astype(BF16)
+
+    return pl.pallas_call(
+        kernel,
+        out_shape=(part, part),
+        in_specs=whole(3),
+        out_specs=tuple(whole(2)),
+        compiler_params=limits(6),
+        name="relay_sum",
+    )(total, *came)
+
+
+def middle_sum(total, came, half):
     part = jax.ShapeDtypeStruct((2, RANK, SIDE), BF16)
+
+    def kernel(total, a, b, keep, *aways):
+        for d in range(4):
+            at = pl.ds(2 * d, 2)
+            one = total[pl.ds(32 * half + 2 * d, 2)] + (a[at].astype(F32) + b[at].astype(F32))
+            if d == 0:
+                keep[...] = one
+            else:
+                aways[d - 1][...] = one.astype(BF16)
+
     keep, *aways = pl.pallas_call(
-        middle_kernel,
+        kernel,
         out_shape=(jax.ShapeDtypeStruct((2, RANK, SIDE), F32),) + (part,) * 3,
-        in_specs=whole(4),
+        in_specs=whole(3),
         out_specs=tuple(whole(4)),
         compiler_params=limits(6),
         name="middle_sum",
-    )(keep, *came)
+    )(total, *came)
     return keep, aways
 
 
@@ -361,9 +377,11 @@
         near, first_tiles = lax.optimization_barrier((near, tiles))
         firsts = [jnp.concatenate(four, axis=0) for four in near]
         pieces = []
-        for first, order in zip(firsts, orders):
-            pieces += [first] + [send(first, order[1], -d) for d in (1, 2, 3)]
-        pieces = [piece.reshape(8, SIDE, RANK) for piece in pieces]
+        for first, (_, axis) in zip(firsts, orders):
+            first = first.reshape(8, SIDE, RANK)
+            right, left = send(first, axis, 1), send(first, axis, -1)
+            over = (send(right[:4], axis, 1), send(left[4:], axis, -1))
+            pieces += [first, left, *over, right]
 
     held = hold_tiles(tile_count, first_tiles)
     keep, away = forward(tile_count, jnp.where(used, row_at, 32), col_at, held, pieces)
@@ -381,15 +399,18 @@
         mine = [inner] + [send(inner, "z", -d) for d in (1, 2, 3)]
         theirs = [send(one, "core", 1) for one in mine]
 
-    keeps, aways = backward(
+    total, aways = backward(
         tile_count, row_at, jnp.where(used, col_at, 64), held, mine + theirs
     )
 
     with jax.named_scope("reduce_outer"):
         last_keeps, last_came = [], []
-        for keep, away, (first, then) in zip(keeps, aways, (("y", "x"), ("x", "y"))):
-            came = [send(one, first, d) for d, one in zip((1, 2, 3), away)]
-            keep, away = middle_sum(keep, came)
+        for half, (first, then) in enumerate((("y", "x"), ("x", "y"))):
+            over = aways[half]
+            came = (send(over[0], first, 1), send(over[1], first, -1))
+            right, left = relay_sum(total, came, half)
+            came = (send(right, first, 1), send(left, first, -1))
+            keep, away = middle_sum(total, came, half)
             last_keeps.append(keep)
             last_came += [send(one, then, d) for d, one in zip((1, 2, 3), away)]
         outer, gram = outer_sum(last_keeps, last_came)

time: 187 us -> 172 us (0.920)
  waiting for transfers between devices: 94.6 us -> 65.1 us
  starting transfers between devices: 65.5 us -> 71.9 us
  Pallas kernels: 23.6 us -> 27.8 us
  local copies, waits for them, and re-layouts: 1.13 us -> 3.88 us
    ppermute x45 -> x49, waiting for transfers between devices: 94.6 us -> 65.1 us  [send(): lax.ppermute(array, axis, [(i, (i + step) % size) for i in range(size)])]
    ppermute x45 -> x49, starting transfers between devices: 65.5 us -> 71.9 us  [send(): lax.ppermute(array, axis, [(i, (i + step) % size) for i in range(size)])]
    slice x0 -> x4, local copies, waits for them, and re-layouts: none -> 2.89 us  [shards(): over = (send(right[:4], axis, 1), send(left[4:], axis, -1))]
    pallas_call x2, Pallas kernels: 7.03 us -> 9.42 us  [hold_tiles(): pl.pallas_call(hold_kernel, out_shape=jax.ShapeDtypeStruct(tiles.shape, t...]
    pallas_call x4 -> x6, Pallas kernels: 9.3 us -> 11.1 us  [the longest x1 6 us: forward(): pl.pallas_call(forward_kernel, out_shape=(jax.ShapeDtypeStruct((33, SIDE,...]
  transfers between devices with their start and end apart: 45 -> 49, of which waited for: 28 -> 27; matrix products, arithmetic and copies ran while one was open for 0% -> 2% of each run, Pallas kernels for 4% -> 6%
where the time goes in v4:
time: 172 us; the launch traced here: 171 us
  starting transfers between devices  71.9 us (42%)
  waiting for transfers between devices  65.1 us (38%)
  Pallas kernels  27.8 us (16%)
  local copies, waits for them, and re-layouts  3.88 us (2%)
    ppermute x49, starting transfers between devices, send(): lax.ppermute(array, axis, [(i, (i + step) % size) for i in range(size)])  71.9 us
    ppermute x49, waiting for transfers between devices, send(): lax.ppermute(array, axis, [(i, (i + step) % size) for i in range(size)])  65.1 us
    pallas_call x2, Pallas kernels, hold_tiles(): pl.pallas_call(hold_kernel, out_shape=jax.ShapeDtypeStruct(tiles.shape, t...  9.42 us
    pallas_call x1, Pallas kernels, forward(): pl.pallas_call(forward_kernel, out_shape=(jax.ShapeDtypeStruct((33, SIDE,...  6 us
    pallas_call x1, Pallas kernels, finish(): pl.pallas_call(kernel, out_shape=(jax.ShapeDtypeStruct((4 * SIDE, RANK),...  5.91 us
    pallas_call x1, Pallas kernels, backward(): pl.pallas_call(backward_kernel, out_shape=(jax.ShapeDtypeStruct((65, RANK...  4.42 us
  transfers between devices with their start and end apart: 49, of which 27 were waited for; matrix products, arithmetic and copies ran while one was open for 2% of the time, Pallas kernels for 6%

profile of v4, /device:TPU:0, one launch (start us, length us, event | category | flops | bytes accessed | tf_op | source)
XLA Modules:
  0.0 171.3 jit_solution(9117438550393424214)
XLA Ops:
  0.6 1.0 fusion.12
  1.6 1.7 %collective-permute-start.5 = (bf16[512,128]{1,0:T(8,128)(2,1)S(1)}, bf16[512,128]{1,0:T(8,128)(2,1)S(1)}, u32[]{:S(2)}, u32[]{:S(2)}) collective-permute-start(bf16[512,128]{1,0:T(8,128)(2,1)S(1)} %get-tuple-element.49), channel_id=1, source_target_pairs={{0,8},{8,16},{16,24},{24,0},{1,9},{9,17},{17,25},{25,1},{2,10},{10... | collective-permute-start | bytes 393224 | tf_op jit(solution)/shard_map/gather_basis/ppermute | solution.py:20
  3.3 2.9 %collective-permute-start.4 = (bf16[512,128]{1,0:T(8,128)(2,1)S(1)}, bf16[512,128]{1,0:T(8,128)(2,1)S(1)}, u32[]{:S(2)}, u32[]{:S(2)}) collective-permute-start(bf16[512,128]{1,0:T(8,128)(2,1)S(1)} %get-tuple-element.49), channel_id=1, source_target_pairs={{0,16},{8,24},{16,0},{24,8},{1,17},{9,25},{17,1},{25,9},{2,18},{10... | collective-permute-start | bytes 393224 | tf_op jit(solution)/shard_map/gather_basis/ppermute | solution.py:20
  6.2 1.3 collective-permute-start.3
  7.6 1.5 collective-permute-start.2
  9.1 2.7 %collective-permute-start.1 = (bf16[512,128]{1,0:T(8,128)(2,1)S(1)}, bf16[512,128]{1,0:T(8,128)(2,1)S(1)}, u32[]{:S(2)}, u32[]{:S(2)}) collective-permute-start(bf16[512,128]{1,0:T(8,128)(2,1)S(1)} %get-tuple-element.45), channel_id=1, source_target_pairs={{0,64},{32,96},{64,0},{96,32},{1,65},{33,97},{65,1},{97,33},{2,66}... | collective-permute-start | bytes 393224 | tf_op jit(solution)/shard_map/gather_basis/ppermute | solution.py:20
  11.8 1.4 collective-permute-start
  13.3 1.9 %collective-permute-done.2 = bf16[512,128]{1,0:T(8,128)(2,1)S(1)} collective-permute-done((bf16[512,128]{1,0:T(8,128)(2,1)S(1)}, bf16[512,128]{1,0:T(8,128)(2,1)S(1)}, u32[]{:S(2)}, u32[]{:S(2)}) %collective-permute-start.2) | collective-permute-done | bytes 131104 | tf_op jit(solution)/shard_map/gather_basis/ppermute | solution.py:20
  15.2 1.8 %collective-permute-done.1 = bf16[512,128]{1,0:T(8,128)(2,1)S(1)} collective-permute-done((bf16[512,128]{1,0:T(8,128)(2,1)S(1)}, bf16[512,128]{1,0:T(8,128)(2,1)S(1)}, u32[]{:S(2)}, u32[]{:S(2)}) %collective-permute-start.1) | collective-permute-done | bytes 131104 | tf_op jit(solution)/shard_map/gather_basis/ppermute | solution.py:20
  17.1 1.3 collective-permute-start.11
  18.5 2.0 %collective-permute-start.10 = (bf16[8,256,128]{2,1,0:T(8,128)(2,1)S(1)}, bf16[8,256,128]{2,1,0:T(8,128)(2,1)S(1)}, u32[]{:S(2)}, u32[]{:S(2)}) collective-permute-start(bf16[8,256,128]{2,1,0:T(8,128)(2,1)S(1)} %bitcast.7), channel_id=1, source_target_pairs={{0,96},{32,0},{64,32},{96,64},{1,97},{33,1},{65,33},{97,65},{2,98}... | collective-permute-start | bytes 1572872 | tf_op jit(solution)/shard_map/gather_basis/ppermute | solution.py:20
  20.4 0.7 collective-permute-start.7
  21.2 2.6 %collective-permute-start.6 = (bf16[8,256,128]{2,1,0:T(8,128)(2,1)S(1)}, bf16[8,256,128]{2,1,0:T(8,128)(2,1)S(1)}, u32[]{:S(2)}, u32[]{:S(2)}) collective-permute-start(bf16[8,256,128]{2,1,0:T(8,128)(2,1)S(1)} %bitcast.10), channel_id=1, source_target_pairs={{0,24},{8,0},{16,8},{24,16},{1,25},{9,1},{17,9},{25,17},{2,26},{10... | collective-permute-start | bytes 1572872 | tf_op jit(solution)/shard_map/gather_basis/ppermute | solution.py:20
  23.8 6.7 %collective-permute-done.11.rest_9_ = bf16[8,256,128]{2,1,0:T(8,128)(2,1)S(1)} collective-permute-done((bf16[8,256,128]{2,1,0:T(8,128)(2,1)S(1)}, bf16[8,256,128]{2,1,0:T(8,128)(2,1)S(1)}, u32[]{:S(2)}, u32[]{:S(2)}) %collective-permute-start.11) | collective-permute-done | bytes 524320 | tf_op jit(solution)/shard_map/gather_basis/ppermute | solution.py:20
  30.4 0.7 slice.35
  31.2 0.7 slice.36
  31.9 3.2 %collective-permute-start.13 = (bf16[4,256,128]{2,1,0:T(8,128)(2,1)}, bf16[4,256,128]{2,1,0:T(8,128)(2,1)}, u32[]{:S(2)}, u32[]{:S(2)}) collective-permute-start(bf16[4,256,128]{2,1,0:T(8,128)(2,1)} %slice.36), channel_id=1, source_target_pairs={{0,96},{32,0},{64,32},{96,64},{1,97},{33,1},{65,33},{97,65},{2,98}... | collective-permute-start | bytes 786440 | tf_op jit(solution)/shard_map/gather_basis/ppermute | solution.py:20
  35.1 0.7 slice.33
  35.9 0.7 collective-permute-start.8
  36.5 0.7 slice.34
  37.3 2.6 %collective-permute-start.9 = (bf16[4,256,128]{2,1,0:T(8,128)(2,1)}, bf16[4,256,128]{2,1,0:T(8,128)(2,1)}, u32[]{:S(2)}, u32[]{:S(2)}) collective-permute-start(bf16[4,256,128]{2,1,0:T(8,128)(2,1)} %slice.34), channel_id=1, source_target_pairs={{0,24},{8,0},{16,8},{24,16},{1,25},{9,1},{17,9},{25,17},{2,26},{10... | collective-permute-start | bytes 786440 | tf_op jit(solution)/shard_map/gather_basis/ppermute | solution.py:20
  39.8 0.8 fusion.13
  41.3 4.7 %hold_tiles.2.tiles = bf16[160,256,256]{2,1,0:T(8,128)(2,1)S(1)} custom-call(s32[1]{0:T(128)} %copy.6.count, bf16[160,256,256]{2,1,0:T(8,128)(2,1)} %tiles.1), custom_call_target="tpu_custom_call" | custom-call | bytes 41943040 | tf_op jit(solution)/shard_map/hold_tiles/pallas_call | solution.py:63
  46.0 6.0 %forward.1 = (f32[33,256,128]{2,1,0:T(8,128)S(1)}, f32[16,256,128]{2,1,0:T(8,128)S(1)}) custom-call(s32[1]{0:T(128)} %copy.6.count, s32[160]{0:T(256)S(1)} %get-tuple-element.86.row_at, s32[160]{0:T(256)S(1)} %get-tuple-element.95.col_at, bf16[160,256,256]{2,1,0:T(8,128)(2,1)S(1)} %hold_tiles.2.tiles, bf16[8,256,128]{2,1,0:T(8,128)(2,1)S(1)} %bitcast.11, ...), custom_call_target="tpu_custom_call" | custom-call | tf_op jit(solution)/shard_map/forward/pallas_call | solution.py:99
  52.1 4.1 %collective-permute-done.14.came = f32[16,256,128]{2,1,0:T(8,128)S(1)} collective-permute-done((f32[16,256,128]{2,1,0:T(8,128)S(1)}, f32[16,256,128]{2,1,0:T(8,128)S(1)}, u32[]{:S(2)}, u32[]{:S(2)}) %collective-permute-start.14) | collective-permute-done | bytes 2097184 | tf_op jit(solution)/shard_map/reduce_inner/ppermute | solution.py:20
  56.9 1.6 collective-permute-start.17
  58.5 1.3 collective-permute-start.15
  59.8 4.7 %hold_tiles.3.tiles = bf16[160,256,256]{2,1,0:T(8,128)(2,1)S(1)} custom-call(s32[1]{0:T(128)} %copy.6.count, bf16[160,256,256]{2,1,0:T(8,128)(2,1)} %tiles.1), custom_call_target="tpu_custom_call" | custom-call | bytes 41943040 | tf_op jit(solution)/shard_map/reduce_inner/hold_tiles/pallas_call | solution.py:63
  64.5 1.8 %collective-permute-done.17 = f16[1040,128]{1,0:T(8,128)(2,1)S(1)} collective-permute-done((f16[1040,128]{1,0:T(8,128)(2,1)S(1)}, f16[1040,128]{1,0:T(8,128)(2,1)S(1)}, u32[]{:S(2)}, u32[]{:S(2)}) %collective-permute-start.17) | collective-permute-done | bytes 266272 | tf_op jit(solution)/shard_map/reduce_inner/ppermute | solution.py:20
  66.2 3.1 %collective-permute-done.16 = f16[1040,128]{1,0:T(8,128)(2,1)S(1)} collective-permute-done((f16[1040,128]{1,0:T(8,128)(2,1)S(1)}, f16[1040,128]{1,0:T(8,128)(2,1)S(1)}, u32[]{:S(2)}, u32[]{:S(2)}) %collective-permute-start.16) | collective-permute-done | bytes 266272 | tf_op jit(solution)/shard_map/reduce_inner/ppermute | solution.py:20
  69.3 4.3 %collective-permute-done.15 = f16[1040,128]{1,0:T(8,128)(2,1)S(1)} collective-permute-done((f16[1040,128]{1,0:T(8,128)(2,1)S(1)}, f16[1040,128]{1,0:T(8,128)(2,1)S(1)}, u32[]{:S(2)}, u32[]{:S(2)}) %collective-permute-start.15) | collective-permute-done | bytes 266272 | tf_op jit(solution)/shard_map/reduce_inner/ppermute | solution.py:20
  74.1 2.3 %collective-permute-start.19 = (bf16[4,128,256]{2,1,0:T(8,128)(2,1)S(1)}, bf16[4,128,256]{2,1,0:T(8,128)(2,1)S(1)}, u32[]{:S(2)}, u32[]{:S(2)}) collective-permute-start(bf16[4,128,256]{2,1,0:T(8,128)(2,1)S(1)} %inner_sum.1.rest_0_), channel_id=1, source_target_pairs={{0,4},{2,6},{4,0},{6,2},{1,5},{3,7},{5,1},{7,3},{8,12},{10,14},{12... | collective-permute-start | bytes 786440 | tf_op jit(solution)/shard_map/gather_inner/ppermute | solution.py:20
  76.4 0.9 collective-permute-start.18
  77.3 11.5 %collective-permute-done.20.rest_3_ = bf16[4,128,256]{2,1,0:T(8,128)(2,1)S(1)} collective-permute-done((bf16[4,128,256]{2,1,0:T(8,128)(2,1)S(1)}, bf16[4,128,256]{2,1,0:T(8,128)(2,1)S(1)}, u32[]{:S(2)}, u32[]{:S(2)}) %collective-permute-start.20) | collective-permute-done | bytes 262176 | tf_op jit(solution)/shard_map/gather_inner/ppermute | solution.py:20
  89.6 0.7 collective-permute-done.24.rest_7_
  91.1 4.4 %backward.1 = (f32[65,128,256]{2,1,0:T(8,128)S(1)}, bf16[4,128,256]{2,1,0:T(8,128)(2,1)S(1)}, bf16[4,128,256]{2,1,0:T(8,128)(2,1)S(1)}, bf16[4,128,256]{2,1,0:T(8,128)(2,1)S(1)}, bf16[4,128,256]{2,1,0:T(8,128)(2,1)S(1)}) custom-call(s32[1]{0:T(128)} %copy.6.count, s32[160]{0:T(256)S(1)} %get-tuple-element.87.row_at, s32[160]{0:T(256)S(1)} %get-tuple-element.94.col_at, ...), custom_call_target="tpu_custom_call" | custom-call | tf_op jit(solution)/shard_map/backward/pallas_call | solution.py:144
  95.5 2.1 %collective-permute-start.25 = (bf16[4,128,256]{2,1,0:T(8,128)(2,1)S(1)}, bf16[4,128,256]{2,1,0:T(8,128)(2,1)S(1)}, u32[]{:S(2)}, u32[]{:S(2)}) collective-permute-start(bf16[4,128,256]{2,1,0:T(8,128)(2,1)S(1)} %get-tuple-element.68), channel_id=1, source_target_pairs={{0,8},{8,16},{16,24},{24,0},{1,9},{9,17},{17,25},{25,1},{2,10},{10... | collective-permute-start | bytes 786440 | tf_op jit(solution)/shard_map/reduce_outer/ppermute | solution.py:20
  97.6 2.3 %collective-permute-start.26 = (bf16[4,128,256]{2,1,0:T(8,128)(2,1)S(1)}, bf16[4,128,256]{2,1,0:T(8,128)(2,1)S(1)}, u32[]{:S(2)}, u32[]{:S(2)}) collective-permute-start(bf16[4,128,256]{2,1,0:T(8,128)(2,1)S(1)} %get-tuple-element.69), channel_id=1, source_target_pairs={{0,24},{8,0},{16,8},{24,16},{1,25},{9,1},{17,9},{25,17},{2,26},{10... | collective-permute-start | bytes 786440 | tf_op jit(solution)/shard_map/reduce_outer/ppermute | solution.py:20
  100.4 2.7 %collective-permute-start.30 = (bf16[4,128,256]{2,1,0:T(8,128)(2,1)S(1)}, bf16[4,128,256]{2,1,0:T(8,128)(2,1)S(1)}, u32[]{:S(2)}, u32[]{:S(2)}) collective-permute-start(bf16[4,128,256]{2,1,0:T(8,128)(2,1)S(1)} %get-tuple-element.74), channel_id=1, source_target_pairs={{0,96},{32,0},{64,32},{96,64},{1,97},{33,1},{65,33},{97,65},{2,98}... | collective-permute-start | bytes 786440 | tf_op jit(solution)/shard_map/reduce_outer/ppermute | solution.py:20
  103.1 2.3 %collective-permute-done.25.a = bf16[4,128,256]{2,1,0:T(8,128)(2,1)S(1)} collective-permute-done((bf16[4,128,256]{2,1,0:T(8,128)(2,1)S(1)}, bf16[4,128,256]{2,1,0:T(8,128)(2,1)S(1)}, u32[]{:S(2)}, u32[]{:S(2)}) %collective-permute-start.25) | collective-permute-done | bytes 262176 | tf_op jit(solution)/shard_map/reduce_outer/ppermute | solution.py:20
  105.8 1.7 collective-permute-start.27
  107.5 1.6 collective-permute-start.28
  109.3 2.9 %collective-permute-start.31 = (bf16[8,128,256]{2,1,0:T(8,128)(2,1)S(1)}, bf16[8,128,256]{2,1,0:T(8,128)(2,1)S(1)}, u32[]{:S(2)}, u32[]{:S(2)}) collective-permute-start(bf16[8,128,256]{2,1,0:T(8,128)(2,1)S(1)} %get-tuple-element.75), channel_id=1, source_target_pairs={{0,32},{32,64},{64,96},{96,0},{1,33},{33,65},{65,97},{97,1},{2,34}... | collective-permute-start | bytes 1572872 | tf_op jit(solution)/shard_map/reduce_outer/ppermute | solution.py:20
  112.6 7.3 %collective-permute-done.27.a = bf16[8,128,256]{2,1,0:T(8,128)(2,1)S(1)} collective-permute-done((bf16[8,128,256]{2,1,0:T(8,128)(2,1)S(1)}, bf16[8,128,256]{2,1,0:T(8,128)(2,1)S(1)}, u32[]{:S(2)}, u32[]{:S(2)}) %collective-permute-start.27) | collective-permute-done | bytes 524320 | tf_op jit(solution)/shard_map/reduce_outer/ppermute | solution.py:20
  120.2 2.8 %collective-permute-start.33 = (bf16[2,128,256]{2,1,0:T(8,128)(2,1)S(1)}, bf16[2,128,256]{2,1,0:T(8,128)(2,1)S(1)}, u32[]{:S(2)}, u32[]{:S(2)}) collective-permute-start(bf16[2,128,256]{2,1,0:T(8,128)(2,1)S(1)} %get-tuple-element.78), channel_id=1, source_target_pairs={{0,32},{32,64},{64,96},{96,0},{1,33},{33,65},{65,97},{97,1},{2,34}... | collective-permute-start | bytes 393224 | tf_op jit(solution)/shard_map/reduce_outer/ppermute | solution.py:20
  123.0 1.6 collective-permute-start.34
  124.6 2.5 %collective-permute-start.35 = (bf16[2,128,256]{2,1,0:T(8,128)(2,1)S(1)}, bf16[2,128,256]{2,1,0:T(8,128)(2,1)S(1)}, u32[]{:S(2)}, u32[]{:S(2)}) collective-permute-start(bf16[2,128,256]{2,1,0:T(8,128)(2,1)S(1)} %get-tuple-element.80), channel_id=1, source_target_pairs={{0,96},{32,0},{64,32},{96,64},{1,97},{33,1},{65,33},{97,65},{2,98}... | collective-permute-start | bytes 393224 | tf_op jit(solution)/shard_map/reduce_outer/ppermute | solution.py:20
  127.3 1.2 collective-permute-start.36
  128.6 3.4 %collective-permute-start.37 = (bf16[2,128,256]{2,1,0:T(8,128)(2,1)S(1)}, bf16[2,128,256]{2,1,0:T(8,128)(2,1)S(1)}, u32[]{:S(2)}, u32[]{:S(2)}) collective-permute-start(bf16[2,128,256]{2,1,0:T(8,128)(2,1)S(1)} %get-tuple-element.82), channel_id=1, source_target_pairs={{0,16},{8,24},{16,0},{24,8},{1,17},{9,25},{17,1},{25,9},{2,18},{10... | collective-permute-start | bytes 393224 | tf_op jit(solution)/shard_map/reduce_outer/ppermute | solution.py:20
  131.9 1.1 collective-permute-start.38
  133.0 2.0 %collective-permute-done.36.refs_5_ = bf16[2,128,256]{2,1,0:T(8,128)(2,1)S(1)} collective-permute-done((bf16[2,128,256]{2,1,0:T(8,128)(2,1)S(1)}, bf16[2,128,256]{2,1,0:T(8,128)(2,1)S(1)}, u32[]{:S(2)}, u32[]{:S(2)}) %collective-permute-start.36) | collective-permute-done | bytes 131104 | tf_op jit(solution)/shard_map/reduce_outer/ppermute | solution.py:20
  135.0 1.4 collective-permute-done.37.refs_6_
  137.6 1.2 collective-permute-done.39
  138.8 3.5 %collective-permute-start.42 = (f32[128,128]{1,0:T(8,128)S(1)}, f32[128,128]{1,0:T(8,128)S(1)}, u32[]{:S(2)}, u32[]{:S(2)}) collective-permute-start(f32[128,128]{1,0:T(8,128)S(1)} %add.105), channel_id=1, source_target_pairs={{0,6},{2,0},{4,2},{6,4},{1,7},{3,1},{5,3},{7,5},{8,14},{10,8},{12,... | collective-permute-start | bytes 196616 | tf_op jit(solution)/shard_map/reduce_gram/ppermute | solution.py:20
  142.3 1.5 collective-permute-start.40
  144.2 4.6 %collective-permute-done.41 = f32[128,128]{1,0:T(8,128)S(1)} collective-permute-done((f32[128,128]{1,0:T(8,128)S(1)}, f32[128,128]{1,0:T(8,128)S(1)}, u32[]{:S(2)}, u32[]{:S(2)}) %collective-permute-start.41) | collective-permute-done | bytes 65568 | tf_op jit(solution)/shard_map/reduce_gram/ppermute | solution.py:20
  148.8 2.5 %collective-permute-start.45 = (f32[128,128]{1,0:T(8,128)S(1)}, f32[128,128]{1,0:T(8,128)S(1)}, u32[]{:S(2)}, u32[]{:S(2)}) collective-permute-start(f32[128,128]{1,0:T(8,128)S(1)} %add_add_fusion.2), channel_id=1, source_target_pairs={{0,24},{8,0},{16,8},{24,16},{1,25},{9,1},{17,9},{25,17},{2,26},{10... | collective-permute-start | bytes 196616 | tf_op jit(solution)/shard_map/reduce_gram/ppermute | solution.py:20
  151.3 1.6 collective-permute-start.43
  153.2 4.3 %collective-permute-done.44 = f32[128,128]{1,0:T(8,128)S(1)} collective-permute-done((f32[128,128]{1,0:T(8,128)S(1)}, f32[128,128]{1,0:T(8,128)S(1)}, u32[]{:S(2)}, u32[]{:S(2)}) %collective-permute-start.44) | collective-permute-done | bytes 65568 | tf_op jit(solution)/shard_map/reduce_gram/ppermute | solution.py:20
  157.7 1.9 %collective-permute-start.47 = (f32[128,128]{1,0:T(8,128)S(1)}, f32[128,128]{1,0:T(8,128)S(1)}, u32[]{:S(2)}, u32[]{:S(2)}) collective-permute-start(f32[128,128]{1,0:T(8,128)S(1)} %add_add_fusion.1), channel_id=1, source_target_pairs={{0,32},{32,64},{64,96},{96,0},{1,33},{33,65},{65,97},{97,1},{2,34}... | collective-permute-start | bytes 196616 | tf_op jit(solution)/shard_map/reduce_gram/ppermute | solution.py:20
  159.6 2.2 %collective-permute-start.46 = (f32[128,128]{1,0:T(8,128)S(1)}, f32[128,128]{1,0:T(8,128)S(1)}, u32[]{:S(2)}, u32[]{:S(2)}) collective-permute-start(f32[128,128]{1,0:T(8,128)S(1)} %add_add_fusion.1), channel_id=1, source_target_pairs={{0,64},{32,96},{64,0},{96,32},{1,65},{33,97},{65,1},{97,33},{2,66}... | collective-permute-start | bytes 196616 | tf_op jit(solution)/shard_map/reduce_gram/ppermute | solution.py:20
  161.9 1.3 collective-permute-done.47
  163.1 2.2 %collective-permute-done.46 = f32[128,128]{1,0:T(8,128)S(1)} collective-permute-done((f32[128,128]{1,0:T(8,128)S(1)}, f32[128,128]{1,0:T(8,128)S(1)}, u32[]{:S(2)}, u32[]{:S(2)}) %collective-permute-start.46) | collective-permute-done | bytes 65568 | tf_op jit(solution)/shard_map/reduce_gram/ppermute | solution.py:20
  165.4 5.9 %finish.1 = (f32[1024,128]{1,0:T(8,128)}, f32[128,128]{1,0:T(8,128)}) custom-call(f32[128,128]{1,0:T(8,128)S(1)} %add_add_fusion.refs_0_, f32[4,128,256]{2,1,0:T(8,128)S(1)} %get-tuple-element.85.refs_1_), custom_call_target="tpu_custom_call" | custom-call | tf_op jit(solution)/shard_map/finish/pallas_call | solution.py:342
  (65 shorter events, 7.0 us)
Async XLA Ops:
  1.6 10.2 %collective-permute-start.5 = (bf16[512,128]{1,0:T(8,128)(2,1)S(1)}, bf16[512,128]{1,0:T(8,128)(2,1)S(1)}, u32[]{:S(2)}, u32[]{:S(2)}) collective-permute-start(bf16[512,128]{1,0:T(8,128)(2,1)S(1)} %get-tuple-element.49), channel_id=1, source_target_pairs={{0,8},{8,16},{16,24},{24,0},{1,9},{9,17},{17,25},{25,1},{2,10},{10... | collective-permute-start | bytes 393224 | tf_op jit(solution)/shard_map/gather_basis/ppermute | solution.py:20
  3.3 9.9 %collective-permute-start.4 = (bf16[512,128]{1,0:T(8,128)(2,1)S(1)}, bf16[512,128]{1,0:T(8,128)(2,1)S(1)}, u32[]{:S(2)}, u32[]{:S(2)}) collective-permute-start(bf16[512,128]{1,0:T(8,128)(2,1)S(1)} %get-tuple-element.49), channel_id=1, source_target_pairs={{0,16},{8,24},{16,0},{24,8},{1,17},{9,25},{17,1},{25,9},{2,18},{10... | collective-permute-start | bytes 393224 | tf_op jit(solution)/shard_map/gather_basis/ppermute | solution.py:20
  6.2 7.0 %collective-permute-start.3 = (bf16[512,128]{1,0:T(8,128)(2,1)S(1)}, bf16[512,128]{1,0:T(8,128)(2,1)S(1)}, u32[]{:S(2)}, u32[]{:S(2)}) collective-permute-start(bf16[512,128]{1,0:T(8,128)(2,1)S(1)} %get-tuple-element.49), channel_id=1, source_target_pairs={{0,24},{8,0},{16,8},{24,16},{1,25},{9,1},{17,9},{25,17},{2,26},{10... | collective-permute-start | bytes 393224 | tf_op jit(solution)/shard_map/gather_basis/ppermute | solution.py:20
  7.6 7.6 %collective-permute-start.2 = (bf16[512,128]{1,0:T(8,128)(2,1)S(1)}, bf16[512,128]{1,0:T(8,128)(2,1)S(1)}, u32[]{:S(2)}, u32[]{:S(2)}) collective-permute-start(bf16[512,128]{1,0:T(8,128)(2,1)S(1)} %get-tuple-element.45), channel_id=1, source_target_pairs={{0,32},{32,64},{64,96},{96,0},{1,33},{33,65},{65,97},{97,1},{2,34}... | collective-permute-start | bytes 393224 | tf_op jit(solution)/shard_map/gather_basis/ppermute | solution.py:20
  9.1 7.9 %collective-permute-start.1 = (bf16[512,128]{1,0:T(8,128)(2,1)S(1)}, bf16[512,128]{1,0:T(8,128)(2,1)S(1)}, u32[]{:S(2)}, u32[]{:S(2)}) collective-permute-start(bf16[512,128]{1,0:T(8,128)(2,1)S(1)} %get-tuple-element.45), channel_id=1, source_target_pairs={{0,64},{32,96},{64,0},{96,32},{1,65},{33,97},{65,1},{97,33},{2,66}... | collective-permute-start | bytes 393224 | tf_op jit(solution)/shard_map/gather_basis/ppermute | solution.py:20
  11.8 5.2 %collective-permute-start = (bf16[512,128]{1,0:T(8,128)(2,1)S(1)}, bf16[512,128]{1,0:T(8,128)(2,1)S(1)}, u32[]{:S(2)}, u32[]{:S(2)}) collective-permute-start(bf16[512,128]{1,0:T(8,128)(2,1)S(1)} %get-tuple-element.45), channel_id=1, source_target_pairs={{0,96},{32,0},{64,32},{96,64},{1,97},{33,1},{65,33},{97,65},{2,98}... | collective-permute-start | bytes 393224 | tf_op jit(solution)/shard_map/gather_basis/ppermute | solution.py:20
  17.1 13.3 %collective-permute-start.11 = (bf16[8,256,128]{2,1,0:T(8,128)(2,1)S(1)}, bf16[8,256,128]{2,1,0:T(8,128)(2,1)S(1)}, u32[]{:S(2)}, u32[]{:S(2)}) collective-permute-start(bf16[8,256,128]{2,1,0:T(8,128)(2,1)S(1)} %bitcast.6), channel_id=1, source_target_pairs={{0,32},{32,64},{64,96},{96,0},{1,33},{33,65},{65,97},{97,1},{2,34}... | collective-permute-start | bytes 1572872 | tf_op jit(solution)/shard_map/gather_basis/ppermute | solution.py:20
  18.5 12.7 %collective-permute-start.10 = (bf16[8,256,128]{2,1,0:T(8,128)(2,1)S(1)}, bf16[8,256,128]{2,1,0:T(8,128)(2,1)S(1)}, u32[]{:S(2)}, u32[]{:S(2)}) collective-permute-start(bf16[8,256,128]{2,1,0:T(8,128)(2,1)S(1)} %bitcast.7), channel_id=1, source_target_pairs={{0,96},{32,0},{64,32},{96,64},{1,97},{33,1},{65,33},{97,65},{2,98}... | collective-permute-start | bytes 1572872 | tf_op jit(solution)/shard_map/gather_basis/ppermute | solution.py:20
  20.4 14.7 %collective-permute-start.7 = (bf16[8,256,128]{2,1,0:T(8,128)(2,1)S(1)}, bf16[8,256,128]{2,1,0:T(8,128)(2,1)S(1)}, u32[]{:S(2)}, u32[]{:S(2)}) collective-permute-start(bf16[8,256,128]{2,1,0:T(8,128)(2,1)S(1)} %bitcast.9), channel_id=1, source_target_pairs={{0,8},{8,16},{16,24},{24,0},{1,9},{9,17},{17,25},{25,1},{2,10},{10... | collective-permute-start | bytes 1572872 | tf_op jit(solution)/shard_map/gather_basis/ppermute | solution.py:20
  21.2 15.3 %collective-permute-start.6 = (bf16[8,256,128]{2,1,0:T(8,128)(2,1)S(1)}, bf16[8,256,128]{2,1,0:T(8,128)(2,1)S(1)}, u32[]{:S(2)}, u32[]{:S(2)}) collective-permute-start(bf16[8,256,128]{2,1,0:T(8,128)(2,1)S(1)} %bitcast.10), channel_id=1, source_target_pairs={{0,24},{8,0},{16,8},{24,16},{1,25},{9,1},{17,9},{25,17},{2,26},{10... | collective-permute-start | bytes 1572872 | tf_op jit(solution)/shard_map/gather_basis/ppermute | solution.py:20
  31.2 14.8 %collective-permute-start.12 = (bf16[4,256,128]{2,1,0:T(8,128)(2,1)}, bf16[4,256,128]{2,1,0:T(8,128)(2,1)S(1)}, u32[]{:S(2)}, u32[]{:S(2)}) collective-permute-start(bf16[4,256,128]{2,1,0:T(8,128)(2,1)} %slice.35), channel_id=1, source_target_pairs={{0,32},{32,64},{64,96},{96,0},{1,33},{33,65},{65,97},{97,1},{2,34}... | collective-permute-start | bytes 786440 | tf_op jit(solution)/shard_map/gather_basis/ppermute | solution.py:20
  31.9 14.1 %collective-permute-start.13 = (bf16[4,256,128]{2,1,0:T(8,128)(2,1)}, bf16[4,256,128]{2,1,0:T(8,128)(2,1)}, u32[]{:S(2)}, u32[]{:S(2)}) collective-permute-start(bf16[4,256,128]{2,1,0:T(8,128)(2,1)} %slice.36), channel_id=1, source_target_pairs={{0,96},{32,0},{64,32},{96,64},{1,97},{33,1},{65,33},{97,65},{2,98}... | collective-permute-start | bytes 786440 | tf_op jit(solution)/shard_map/gather_basis/ppermute | solution.py:20
  35.9 10.2 %collective-permute-start.8 = (bf16[4,256,128]{2,1,0:T(8,128)(2,1)}, bf16[4,256,128]{2,1,0:T(8,128)(2,1)}, u32[]{:S(2)}, u32[]{:S(2)}) collective-permute-start(bf16[4,256,128]{2,1,0:T(8,128)(2,1)} %slice.33), channel_id=1, source_target_pairs={{0,8},{8,16},{16,24},{24,0},{1,9},{9,17},{17,25},{25,1},{2,10},{10... | collective-permute-start | bytes 786440 | tf_op jit(solution)/shard_map/gather_basis/ppermute | solution.py:20
  37.3 8.8 %collective-permute-start.9 = (bf16[4,256,128]{2,1,0:T(8,128)(2,1)}, bf16[4,256,128]{2,1,0:T(8,128)(2,1)}, u32[]{:S(2)}, u32[]{:S(2)}) collective-permute-start(bf16[4,256,128]{2,1,0:T(8,128)(2,1)} %slice.34), channel_id=1, source_target_pairs={{0,24},{8,0},{16,8},{24,16},{1,25},{9,1},{17,9},{25,17},{2,26},{10... | collective-permute-start | bytes 786440 | tf_op jit(solution)/shard_map/gather_basis/ppermute | solution.py:20
  52.0 4.2 %collective-permute-start.14 = (f32[16,256,128]{2,1,0:T(8,128)S(1)}, f32[16,256,128]{2,1,0:T(8,128)S(1)}, u32[]{:S(2)}, u32[]{:S(2)}) collective-permute-start(f32[16,256,128]{2,1,0:T(8,128)S(1)} %get-tuple-element.54), channel_id=1, source_target_pairs={{0,1},{1,0},{2,3},{3,2},{4,5},{5,4},{6,7},{7,6},{8,9},{9,8},{10,11... | collective-permute-start | bytes 6291464 | tf_op jit(solution)/shard_map/reduce_inner/ppermute | solution.py:20
  56.9 9.3 %collective-permute-start.17 = (f16[1040,128]{1,0:T(8,128)(2,1)S(1)}, f16[1040,128]{1,0:T(8,128)(2,1)S(1)}, u32[]{:S(2)}, u32[]{:S(2)}) collective-permute-start(f16[1040,128]{1,0:T(8,128)(2,1)S(1)} %convert_element_type.20), channel_id=1, source_target_pairs={{0,6},{2,0},{4,2},{6,4},{1,7},{3,1},{5,3},{7,5},{8,14},{10,8},{12,... | collective-permute-start | bytes 798728 | tf_op jit(solution)/shard_map/reduce_inner/ppermute | solution.py:20
  58.5 10.8 %collective-permute-start.16 = (f16[1040,128]{1,0:T(8,128)(2,1)S(1)}, f16[1040,128]{1,0:T(8,128)(2,1)S(1)}, u32[]{:S(2)}, u32[]{:S(2)}) collective-permute-start(f16[1040,128]{1,0:T(8,128)(2,1)S(1)} %convert_element_type.19), channel_id=1, source_target_pairs={{0,4},{2,6},{4,0},{6,2},{1,5},{3,7},{5,1},{7,3},{8,12},{10,14},{12... | collective-permute-start | bytes 798728 | tf_op jit(solution)/shard_map/reduce_inner/ppermute | solution.py:20
  58.5 15.1 %collective-permute-start.15 = (f16[1040,128]{1,0:T(8,128)(2,1)S(1)}, f16[1040,128]{1,0:T(8,128)(2,1)S(1)}, u32[]{:S(2)}, u32[]{:S(2)}) collective-permute-start(f16[1040,128]{1,0:T(8,128)(2,1)S(1)} %convert_element_type.18), channel_id=1, source_target_pairs={{0,2},{2,4},{4,6},{6,0},{1,3},{3,5},{5,7},{7,1},{8,10},{10,12},{12... | collective-permute-start | bytes 798728 | tf_op jit(solution)/shard_map/reduce_inner/ppermute | solution.py:20
  74.0 14.8 %collective-permute-start.20 = (bf16[4,128,256]{2,1,0:T(8,128)(2,1)S(1)}, bf16[4,128,256]{2,1,0:T(8,128)(2,1)S(1)}, u32[]{:S(2)}, u32[]{:S(2)}) collective-permute-start(bf16[4,128,256]{2,1,0:T(8,128)(2,1)S(1)} %inner_sum.1.rest_0_), channel_id=1, source_target_pairs={{0,2},{2,4},{4,6},{6,0},{1,3},{3,5},{5,7},{7,1},{8,10},{10,12},{12... | collective-permute-start | bytes 786440 | tf_op jit(solution)/shard_map/gather_inner/ppermute | solution.py:20
  74.1 14.7 %collective-permute-start.19 = (bf16[4,128,256]{2,1,0:T(8,128)(2,1)S(1)}, bf16[4,128,256]{2,1,0:T(8,128)(2,1)S(1)}, u32[]{:S(2)}, u32[]{:S(2)}) collective-permute-start(bf16[4,128,256]{2,1,0:T(8,128)(2,1)S(1)} %inner_sum.1.rest_0_), channel_id=1, source_target_pairs={{0,4},{2,6},{4,0},{6,2},{1,5},{3,7},{5,1},{7,3},{8,12},{10,14},{12... | collective-permute-start | bytes 786440 | tf_op jit(solution)/shard_map/gather_inner/ppermute | solution.py:20
  76.4 13.0 %collective-permute-start.18 = (bf16[4,128,256]{2,1,0:T(8,128)(2,1)S(1)}, bf16[4,128,256]{2,1,0:T(8,128)(2,1)S(1)}, u32[]{:S(2)}, u32[]{:S(2)}) collective-permute-start(bf16[4,128,256]{2,1,0:T(8,128)(2,1)S(1)} %inner_sum.1.rest_0_), channel_id=1, source_target_pairs={{0,6},{2,0},{4,2},{6,4},{1,7},{3,1},{5,3},{7,5},{8,14},{10,8},{12,... | collective-permute-start | bytes 786440 | tf_op jit(solution)/shard_map/gather_inner/ppermute | solution.py:20
  77.3 12.3 %collective-permute-start.21 = (bf16[4,128,256]{2,1,0:T(8,128)(2,1)S(1)}, bf16[4,128,256]{2,1,0:T(8,128)(2,1)S(1)}, u32[]{:S(2)}, u32[]{:S(2)}) collective-permute-start(bf16[4,128,256]{2,1,0:T(8,128)(2,1)S(1)} %inner_sum.1.rest_0_), channel_id=1, source_target_pairs={{0,1},{1,0},{2,3},{3,2},{4,5},{5,4},{6,7},{7,6},{8,9},{9,8},{10,11... | collective-permute-start | bytes 786440 | tf_op jit(solution)/shard_map/gather_inner/ppermute | solution.py:20
  88.8 1.5 collective-permute-start.24
  88.8 1.9 %collective-permute-start.23 = (bf16[4,128,256]{2,1,0:T(8,128)(2,1)S(1)}, bf16[4,128,256]{2,1,0:T(8,128)(2,1)S(1)}, u32[]{:S(2)}, u32[]{:S(2)}) collective-permute-start(bf16[4,128,256]{2,1,0:T(8,128)(2,1)S(1)} %collective-permute-done.19.rest_2_), channel_id=1, source_target_pairs={{0,1},{1,0},{2,3},{3,2},{4,5},{5,4},{6,7},{7,6},{8,9},{9,8},{10,11... | collective-permute-start | bytes 786440 | tf_op jit(solution)/shard_map/gather_inner/ppermute | solution.py:20
  89.4 1.7 collective-permute-start.22
  95.5 9.9 %collective-permute-start.25 = (bf16[4,128,256]{2,1,0:T(8,128)(2,1)S(1)}, bf16[4,128,256]{2,1,0:T(8,128)(2,1)S(1)}, u32[]{:S(2)}, u32[]{:S(2)}) collective-permute-start(bf16[4,128,256]{2,1,0:T(8,128)(2,1)S(1)} %get-tuple-element.68), channel_id=1, source_target_pairs={{0,8},{8,16},{16,24},{24,0},{1,9},{9,17},{17,25},{25,1},{2,10},{10... | collective-permute-start | bytes 786440 | tf_op jit(solution)/shard_map/reduce_outer/ppermute | solution.py:20
  97.6 8.1 %collective-permute-start.26 = (bf16[4,128,256]{2,1,0:T(8,128)(2,1)S(1)}, bf16[4,128,256]{2,1,0:T(8,128)(2,1)S(1)}, u32[]{:S(2)}, u32[]{:S(2)}) collective-permute-start(bf16[4,128,256]{2,1,0:T(8,128)(2,1)S(1)} %get-tuple-element.69), channel_id=1, source_target_pairs={{0,24},{8,0},{16,8},{24,16},{1,25},{9,1},{17,9},{25,17},{2,26},{10... | collective-permute-start | bytes 786440 | tf_op jit(solution)/shard_map/reduce_outer/ppermute | solution.py:20
  99.9 9.3 %collective-permute-start.29 = (bf16[4,128,256]{2,1,0:T(8,128)(2,1)S(1)}, bf16[4,128,256]{2,1,0:T(8,128)(2,1)S(1)}, u32[]{:S(2)}, u32[]{:S(2)}) collective-permute-start(bf16[4,128,256]{2,1,0:T(8,128)(2,1)S(1)} %get-tuple-element.73), channel_id=1, source_target_pairs={{0,32},{32,64},{64,96},{96,0},{1,33},{33,65},{65,97},{97,1},{2,34}... | collective-permute-start | bytes 786440 | tf_op jit(solution)/shard_map/reduce_outer/ppermute | solution.py:20
  100.4 8.7 %collective-permute-start.30 = (bf16[4,128,256]{2,1,0:T(8,128)(2,1)S(1)}, bf16[4,128,256]{2,1,0:T(8,128)(2,1)S(1)}, u32[]{:S(2)}, u32[]{:S(2)}) collective-permute-start(bf16[4,128,256]{2,1,0:T(8,128)(2,1)S(1)} %get-tuple-element.74), channel_id=1, source_target_pairs={{0,96},{32,0},{64,32},{96,64},{1,97},{33,1},{65,33},{97,65},{2,98}... | collective-permute-start | bytes 786440 | tf_op jit(solution)/shard_map/reduce_outer/ppermute | solution.py:20
  105.8 14.1 %collective-permute-start.27 = (bf16[8,128,256]{2,1,0:T(8,128)(2,1)S(1)}, bf16[8,128,256]{2,1,0:T(8,128)(2,1)S(1)}, u32[]{:S(2)}, u32[]{:S(2)}) collective-permute-start(bf16[8,128,256]{2,1,0:T(8,128)(2,1)S(1)} %get-tuple-element.70), channel_id=1, source_target_pairs={{0,8},{8,16},{16,24},{24,0},{1,9},{9,17},{17,25},{25,1},{2,10},{10... | collective-permute-start | bytes 1572872 | tf_op jit(solution)/shard_map/reduce_outer/ppermute | solution.py:20
  107.5 12.5 %collective-permute-start.28 = (bf16[8,128,256]{2,1,0:T(8,128)(2,1)S(1)}, bf16[8,128,256]{2,1,0:T(8,128)(2,1)S(1)}, u32[]{:S(2)}, u32[]{:S(2)}) collective-permute-start(bf16[8,128,256]{2,1,0:T(8,128)(2,1)S(1)} %get-tuple-element.71), channel_id=1, source_target_pairs={{0,24},{8,0},{16,8},{24,16},{1,25},{9,1},{17,9},{25,17},{2,26},{10... | collective-permute-start | bytes 1572872 | tf_op jit(solution)/shard_map/reduce_outer/ppermute | solution.py:20
  109.3 17.9 %collective-permute-start.31 = (bf16[8,128,256]{2,1,0:T(8,128)(2,1)S(1)}, bf16[8,128,256]{2,1,0:T(8,128)(2,1)S(1)}, u32[]{:S(2)}, u32[]{:S(2)}) collective-permute-start(bf16[8,128,256]{2,1,0:T(8,128)(2,1)S(1)} %get-tuple-element.75), channel_id=1, source_target_pairs={{0,32},{32,64},{64,96},{96,0},{1,33},{33,65},{65,97},{97,1},{2,34}... | collective-permute-start | bytes 1572872 | tf_op jit(solution)/shard_map/reduce_outer/ppermute | solution.py:20
  112.2 15.0 %collective-permute-start.32 = (bf16[8,128,256]{2,1,0:T(8,128)(2,1)S(1)}, bf16[8,128,256]{2,1,0:T(8,128)(2,1)S(1)}, u32[]{:S(2)}, u32[]{:S(2)}) collective-permute-start(bf16[8,128,256]{2,1,0:T(8,128)(2,1)S(1)} %get-tuple-element.76), channel_id=1, source_target_pairs={{0,96},{32,0},{64,32},{96,64},{1,97},{33,1},{65,33},{97,65},{2,98}... | collective-permute-start | bytes 1572872 | tf_op jit(solution)/shard_map/reduce_outer/ppermute | solution.py:20
  120.2 11.7 %collective-permute-start.33 = (bf16[2,128,256]{2,1,0:T(8,128)(2,1)S(1)}, bf16[2,128,256]{2,1,0:T(8,128)(2,1)S(1)}, u32[]{:S(2)}, u32[]{:S(2)}) collective-permute-start(bf16[2,128,256]{2,1,0:T(8,128)(2,1)S(1)} %get-tuple-element.78), channel_id=1, source_target_pairs={{0,32},{32,64},{64,96},{96,0},{1,33},{33,65},{65,97},{97,1},{2,34}... | collective-permute-start | bytes 393224 | tf_op jit(solution)/shard_map/reduce_outer/ppermute | solution.py:20
  123.0 10.0 %collective-permute-start.34 = (bf16[2,128,256]{2,1,0:T(8,128)(2,1)S(1)}, bf16[2,128,256]{2,1,0:T(8,128)(2,1)S(1)}, u32[]{:S(2)}, u32[]{:S(2)}) collective-permute-start(bf16[2,128,256]{2,1,0:T(8,128)(2,1)S(1)} %get-tuple-element.79), channel_id=1, source_target_pairs={{0,64},{32,96},{64,0},{96,32},{1,65},{33,97},{65,1},{97,33},{2,66}... | collective-permute-start | bytes 393224 | tf_op jit(solution)/shard_map/reduce_outer/ppermute | solution.py:20
  124.6 8.3 %collective-permute-start.35 = (bf16[2,128,256]{2,1,0:T(8,128)(2,1)S(1)}, bf16[2,128,256]{2,1,0:T(8,128)(2,1)S(1)}, u32[]{:S(2)}, u32[]{:S(2)}) collective-permute-start(bf16[2,128,256]{2,1,0:T(8,128)(2,1)S(1)} %get-tuple-element.80), channel_id=1, source_target_pairs={{0,96},{32,0},{64,32},{96,64},{1,97},{33,1},{65,33},{97,65},{2,98}... | collective-permute-start | bytes 393224 | tf_op jit(solution)/shard_map/reduce_outer/ppermute | solution.py:20
  127.3 7.6 %collective-permute-start.36 = (bf16[2,128,256]{2,1,0:T(8,128)(2,1)S(1)}, bf16[2,128,256]{2,1,0:T(8,128)(2,1)S(1)}, u32[]{:S(2)}, u32[]{:S(2)}) collective-permute-start(bf16[2,128,256]{2,1,0:T(8,128)(2,1)S(1)} %get-tuple-element.81), channel_id=1, source_target_pairs={{0,8},{8,16},{16,24},{24,0},{1,9},{9,17},{17,25},{25,1},{2,10},{10... | collective-permute-start | bytes 393224 | tf_op jit(solution)/shard_map/reduce_outer/ppermute | solution.py:20
  128.6 7.8 %collective-permute-start.37 = (bf16[2,128,256]{2,1,0:T(8,128)(2,1)S(1)}, bf16[2,128,256]{2,1,0:T(8,128)(2,1)S(1)}, u32[]{:S(2)}, u32[]{:S(2)}) collective-permute-start(bf16[2,128,256]{2,1,0:T(8,128)(2,1)S(1)} %get-tuple-element.82), channel_id=1, source_target_pairs={{0,16},{8,24},{16,0},{24,8},{1,17},{9,25},{17,1},{25,9},{2,18},{10... | collective-permute-start | bytes 393224 | tf_op jit(solution)/shard_map/reduce_outer/ppermute | solution.py:20
  131.9 5.0 %collective-permute-start.38 = (bf16[2,128,256]{2,1,0:T(8,128)(2,1)S(1)}, bf16[2,128,256]{2,1,0:T(8,128)(2,1)S(1)}, u32[]{:S(2)}, u32[]{:S(2)}) collective-permute-start(bf16[2,128,256]{2,1,0:T(8,128)(2,1)S(1)} %get-tuple-element.83), channel_id=1, source_target_pairs={{0,24},{8,0},{16,8},{24,16},{1,25},{9,1},{17,9},{25,17},{2,26},{10... | collective-permute-start | bytes 393224 | tf_op jit(solution)/shard_map/reduce_outer/ppermute | solution.py:20
  137.5 1.3 collective-permute-start.39
  138.8 5.4 %collective-permute-start.42 = (f32[128,128]{1,0:T(8,128)S(1)}, f32[128,128]{1,0:T(8,128)S(1)}, u32[]{:S(2)}, u32[]{:S(2)}) collective-permute-start(f32[128,128]{1,0:T(8,128)S(1)} %add.105), channel_id=1, source_target_pairs={{0,6},{2,0},{4,2},{6,4},{1,7},{3,1},{5,3},{7,5},{8,14},{10,8},{12,... | collective-permute-start | bytes 196616 | tf_op jit(solution)/shard_map/reduce_gram/ppermute | solution.py:20
  142.3 6.5 %collective-permute-start.41 = (f32[128,128]{1,0:T(8,128)S(1)}, f32[128,128]{1,0:T(8,128)S(1)}, u32[]{:S(2)}, u32[]{:S(2)}) collective-permute-start(f32[128,128]{1,0:T(8,128)S(1)} %add.105), channel_id=1, source_target_pairs={{0,2},{2,4},{4,6},{6,0},{1,3},{3,5},{5,7},{7,1},{8,10},{10,12},{12... | collective-permute-start | bytes 196616 | tf_op jit(solution)/shard_map/reduce_gram/ppermute | solution.py:20
  142.3 6.5 %collective-permute-start.40 = (f32[128,128]{1,0:T(8,128)S(1)}, f32[128,128]{1,0:T(8,128)S(1)}, u32[]{:S(2)}, u32[]{:S(2)}) collective-permute-start(f32[128,128]{1,0:T(8,128)S(1)} %add.105), channel_id=1, source_target_pairs={{0,4},{2,6},{4,0},{6,2},{1,5},{3,7},{5,1},{7,3},{8,12},{10,14},{12... | collective-permute-start | bytes 196616 | tf_op jit(solution)/shard_map/reduce_gram/ppermute | solution.py:20
  148.8 4.4 %collective-permute-start.45 = (f32[128,128]{1,0:T(8,128)S(1)}, f32[128,128]{1,0:T(8,128)S(1)}, u32[]{:S(2)}, u32[]{:S(2)}) collective-permute-start(f32[128,128]{1,0:T(8,128)S(1)} %add_add_fusion.2), channel_id=1, source_target_pairs={{0,24},{8,0},{16,8},{24,16},{1,25},{9,1},{17,9},{25,17},{2,26},{10... | collective-permute-start | bytes 196616 | tf_op jit(solution)/shard_map/reduce_gram/ppermute | solution.py:20
  151.3 6.2 %collective-permute-start.44 = (f32[128,128]{1,0:T(8,128)S(1)}, f32[128,128]{1,0:T(8,128)S(1)}, u32[]{:S(2)}, u32[]{:S(2)}) collective-permute-start(f32[128,128]{1,0:T(8,128)S(1)} %add_add_fusion.2), channel_id=1, source_target_pairs={{0,8},{8,16},{16,24},{24,0},{1,9},{9,17},{17,25},{25,1},{2,10},{10... | collective-permute-start | bytes 196616 | tf_op jit(solution)/shard_map/reduce_gram/ppermute | solution.py:20
  151.3 6.2 %collective-permute-start.43 = (f32[128,128]{1,0:T(8,128)S(1)}, f32[128,128]{1,0:T(8,128)S(1)}, u32[]{:S(2)}, u32[]{:S(2)}) collective-permute-start(f32[128,128]{1,0:T(8,128)S(1)} %add_add_fusion.2), channel_id=1, source_target_pairs={{0,16},{8,24},{16,0},{24,8},{1,17},{9,25},{17,1},{25,9},{2,18},{10... | collective-permute-start | bytes 196616 | tf_op jit(solution)/shard_map/reduce_gram/ppermute | solution.py:20
  157.5 4.3 %collective-permute-start.48 = (f32[128,128]{1,0:T(8,128)S(1)}, f32[128,128]{1,0:T(8,128)S(1)}, u32[]{:S(2)}, u32[]{:S(2)}) collective-permute-start(f32[128,128]{1,0:T(8,128)S(1)} %add_add_fusion.1), channel_id=1, source_target_pairs={{0,96},{32,0},{64,32},{96,64},{1,97},{33,1},{65,33},{97,65},{2,98}... | collective-permute-start | bytes 196616 | tf_op jit(solution)/shard_map/reduce_gram/ppermute | solution.py:20
  157.7 5.5 %collective-permute-start.47 = (f32[128,128]{1,0:T(8,128)S(1)}, f32[128,128]{1,0:T(8,128)S(1)}, u32[]{:S(2)}, u32[]{:S(2)}) collective-permute-start(f32[128,128]{1,0:T(8,128)S(1)} %add_add_fusion.1), channel_id=1, source_target_pairs={{0,32},{32,64},{64,96},{96,0},{1,33},{33,65},{65,97},{97,1},{2,34}... | collective-permute-start | bytes 196616 | tf_op jit(solution)/shard_map/reduce_gram/ppermute | solution.py:20
  159.6 5.8 %collective-permute-start.46 = (f32[128,128]{1,0:T(8,128)S(1)}, f32[128,128]{1,0:T(8,128)S(1)}, u32[]{:S(2)}, u32[]{:S(2)}) collective-permute-start(f32[128,128]{1,0:T(8,128)S(1)} %add_add_fusion.1), channel_id=1, source_target_pairs={{0,64},{32,96},{64,0},{96,32},{1,65},{33,97},{65,1},{97,33},{2,66}... | collective-permute-start | bytes 196616 | tf_op jit(solution)/shard_map/reduce_gram/ppermute | solution.py:20

commit v5 on v4

--- a/solution.py
+++ b/solution.py
@@ -1,3 +1,5 @@
+import itertools
+
 import jax
 import jax.numpy as jnp
 from jax import lax
@@ -18,6 +20,24 @@
 def send(array, axis, step):
     size = SIZES[axis]
     return lax.ppermute(array, axis, [(i, (i + step) % size) for i in range(size)])
+
+
+def cross(array, axes, step):
+    names = AXES[:3]
+    pairs = []
+    for place in itertools.product(*(range(SIZES[name]) for name in AXES)):
+        there = list(place)
+        at = names.index(axes[place[3]])
+        there[at] = (there[at] + step) % SIZES[names[at]]
+        pairs.append((linear(place), linear(there)))
+    return lax.ppermute(array, AXES, pairs)
+
+
+def linear(place):
+    index = 0
+    for name, one in zip(AXES, place):
+        index = index * SIZES[name] + one
+    return index
 
 
 def limits(mib):
@@ -132,20 +152,18 @@
         return 0
 
     lax.fori_loop(0, chunks, body, 0)
-    for h in range(2):
-        for half in range(2):
-            at = pl.ds(32 * h + 16 + 4 * half, 4)
-            aways[2 * h + half][...] = total[at].astype(BF16)
+    for half in range(2):
+        aways[half][...] = total[pl.ds(32 + 8 * half, 8)].astype(BF16)
 
 
 def backward(count, row_at, col_at, tiles, pieces):
     any_spec = pl.BlockSpec(memory_space=pl.ANY)
-    part = jax.ShapeDtypeStruct((4, RANK, SIDE), BF16)
+    part = jax.ShapeDtypeStruct((8, RANK, SIDE), BF16)
     total, *aways = pl.pallas_call(
         backward_kernel,
-        out_shape=(jax.ShapeDtypeStruct((65, RANK, SIDE), F32),) + (part,) * 4,
+        out_shape=(jax.ShapeDtypeStruct((65, RANK, SIDE), F32),) + (part,) * 2,
         in_specs=[pl.BlockSpec(memory_space=pltpu.SMEM)] * 3 + whole(1) + [any_spec] * 8,
-        out_specs=tuple(whole(5)),
+        out_specs=tuple(whole(3)),
         scratch_shapes=[
             pltpu.VMEM((32, RANK, SIDE), BF16),
             pltpu.SemaphoreType.DMA((8,)),
@@ -153,7 +171,7 @@
         compiler_params=limits(6),
         name="backward",
     )(count, row_at, col_at, tiles, *pieces)
-    return total, (aways[:2], aways[2:])
+    return total, aways
 
 
 def core_sum_kernel(keep, came, kept, *outs):
@@ -202,20 +220,18 @@
     )(kept, *parts)
 
 
-def relay_sum(total, came, half):
-    part = jax.ShapeDtypeStruct((8, RANK, SIDE), BF16)
-
-    def kernel(total, a, b, right, left):
-        low, high = pl.ds(0, 4), pl.ds(4, 4)
-        at = 32 * half + 8
-        right[low] = (total[pl.ds(at, 4)] + a[...].astype(F32)).astype(BF16)
-        right[high] = total[pl.ds(at + 4, 4)].astype(BF16)
-        at = 32 * half + 24
-        left[low] = total[pl.ds(at, 4)].astype(BF16)
-        left[high] = (total[pl.ds(at + 4, 4)] + b[...].astype(F32)).astype(BF16)
-
-    return pl.pallas_call(
-        kernel,
+def relay_kernel(total, a, b, right, left):
+    low, high = pl.ds(0, 8), pl.ds(8, 8)
+    right[low] = (total[pl.ds(16, 8)] + a[...].astype(F32)).astype(BF16)
+    right[high] = total[pl.ds(24, 8)].astype(BF16)
+    left[low] = total[pl.ds(48, 8)].astype(BF16)
+    left[high] = (total[pl.ds(56, 8)] + b[...].astype(F32)).astype(BF16)
+
+
+def relay_sum(total, came):
+    part = jax.ShapeDtypeStruct((16, RANK, SIDE), BF16)
+    return pl.pallas_call(
+        relay_kernel,
         out_shape=(part, part),
         in_specs=whole(3),
         out_specs=tuple(whole(2)),
@@ -224,21 +240,21 @@
     )(total, *came)
 
 
-def middle_sum(total, came, half):
-    part = jax.ShapeDtypeStruct((2, RANK, SIDE), BF16)
-
-    def kernel(total, a, b, keep, *aways):
-        for d in range(4):
-            at = pl.ds(2 * d, 2)
-            one = total[pl.ds(32 * half + 2 * d, 2)] + (a[at].astype(F32) + b[at].astype(F32))
-            if d == 0:
-                keep[...] = one
-            else:
-                aways[d - 1][...] = one.astype(BF16)
-
+def middle_kernel(total, a, b, keep, *aways):
+    for d in range(4):
+        at = pl.ds(4 * d, 4)
+        one = total[at] + (a[at].astype(F32) + b[at].astype(F32))
+        if d == 0:
+            keep[...] = one
+        else:
+            aways[d - 1][...] = one.astype(BF16)
+
+
+def middle_sum(total, came):
+    part = jax.ShapeDtypeStruct((4, RANK, SIDE), BF16)
     keep, *aways = pl.pallas_call(
-        kernel,
-        out_shape=(jax.ShapeDtypeStruct((2, RANK, SIDE), F32),) + (part,) * 3,
+        middle_kernel,
+        out_shape=(jax.ShapeDtypeStruct((4, RANK, SIDE), F32),) + (part,) * 3,
         in_specs=whole(3),
         out_specs=tuple(whole(4)),
         compiler_params=limits(6),
@@ -253,31 +269,27 @@
     )
 
 
-def outer_kernel(*refs):
-    keeps, came, outer, gram = refs[:2], refs[2:8], refs[8], refs[9]
+def outer_kernel(keep, a, b, c, outer, gram):
     gram_total = jnp.zeros((RANK, RANK), F32)
-    for h in range(2):
-        for b in range(2):
-            total = keeps[h][b]
-            for one in came[3 * h : 3 * h + 3]:
-                total += one[b].astype(F32)
-            outer[2 * h + b] = total
-            gram_total += exact_dot(total, total, ((1,), (1,)))
+    for i in range(outer.shape[0]):
+        total = (keep[i] + a[i].astype(F32)) + (b[i].astype(F32) + c[i].astype(F32))
+        outer[i] = total
+        gram_total += exact_dot(total, total, ((1,), (1,)))
     gram[...] = gram_total
 
 
-def outer_sum(keeps, came):
+def outer_sum(keep, came):
     return pl.pallas_call(
         outer_kernel,
         out_shape=(
             jax.ShapeDtypeStruct((4, RANK, SIDE), F32),
             jax.ShapeDtypeStruct((RANK, RANK), F32),
         ),
-        in_specs=whole(8),
+        in_specs=whole(4),
         out_specs=tuple(whole(2)),
         compiler_params=limits(6),
         name="outer_sum",
-    )(*keeps, *came)
+    )(keep, *came)
 
 
 def wide(value):
@@ -365,25 +377,21 @@
     b = tile_coords[:, 1] % 4
     dx = (row_group // 4 - x) % 4
     dy = (row_group % 4 - y) % 4
-    col_at = jnp.where(b < 2, dy * 8 + dx * 2 + b, 32 + dx * 8 + dy * 2 + b - 2)
+    near_axes, far_axes = ("x", "y"), ("y", "x")
+    near_at = jnp.where(core == 0, dx, dy)
+    far_at = jnp.where(core == 0, dy, dx)
+    col_at = far_at * 16 + near_at * 4 + b
 
     with jax.named_scope("gather_basis"):
-        halves = (basis_in[: 2 * SIDE], basis_in[2 * SIDE :])
-        orders = (("x", "y"), ("y", "x"))
-        near = [
-            [half] + [send(half, order[0], -d) for d in (1, 2, 3)]
-            for half, order in zip(halves, orders)
-        ]
+        near = [basis_in] + [cross(basis_in, near_axes, -d) for d in (1, 2, 3)]
         near, first_tiles = lax.optimization_barrier((near, tiles))
-        firsts = [jnp.concatenate(four, axis=0) for four in near]
-        pieces = []
-        for first, (_, axis) in zip(firsts, orders):
-            first = first.reshape(8, SIDE, RANK)
-            right, left = send(first, axis, 1), send(first, axis, -1)
-            over = (send(right[:4], axis, 1), send(left[4:], axis, -1))
-            pieces += [first, left, *over, right]
-
-    held = hold_tiles(tile_count, first_tiles)
+        first = jnp.concatenate(near, axis=0).reshape(16, SIDE, RANK)
+        right, left = cross(first, far_axes, 1), cross(first, far_axes, -1)
+        held = hold_tiles(tile_count, first_tiles)
+        right, left, held = lax.optimization_barrier((right, left, held))
+        over = (cross(right[:8], far_axes, 1), cross(left[8:], far_axes, -1))
+        pieces = [first, left, *over, right]
+
     keep, away = forward(tile_count, jnp.where(used, row_at, 32), col_at, held, pieces)
 
     with jax.named_scope("reduce_inner"):
@@ -404,16 +412,12 @@
     )
 
     with jax.named_scope("reduce_outer"):
-        last_keeps, last_came = [], []
-        for half, (first, then) in enumerate((("y", "x"), ("x", "y"))):
-            over = aways[half]
-            came = (send(over[0], first, 1), send(over[1], first, -1))
-            right, left = relay_sum(total, came, half)
-            came = (send(right, first, 1), send(left, first, -1))
-            keep, away = middle_sum(total, came, half)
-            last_keeps.append(keep)
-            last_came += [send(one, then, d) for d, one in zip((1, 2, 3), away)]
-        outer, gram = outer_sum(last_keeps, last_came)
+        came = (cross(aways[0], far_axes, 1), cross(aways[1], far_axes, -1))
+        right, left = relay_sum(total, came)
+        came = (cross(right, far_axes, 1), cross(left, far_axes, -1))
+        keep, aways = middle_sum(total, came)
+        came = [cross(one, near_axes, d) for d, one in zip((1, 2, 3), aways)]
+        outer, gram = outer_sum(keep, came)
 
     with jax.named_scope("reduce_gram"):
         gram = gram + send(gram, "core", 1)

time: 172 us -> 180 us (1.047)
  waiting for transfers between devices: 65.1 us -> 80.2 us
  starting transfers between devices: 71.9 us -> 59.1 us
  local copies, waits for them, and re-layouts: 3.88 us -> 15.6 us
  Pallas kernels: 27.8 us -> 23.1 us
    ppermute x0 -> x14, waiting for transfers between devices: none -> 43.6 us  [cross(): return lax.ppermute(array, AXES, pairs)]
    ppermute x49 -> x21, starting transfers between devices: 71.9 us -> 33.6 us  [send(): lax.ppermute(array, axis, [(i, (i + step) % size) for i in range(size)])]
    ppermute x49 -> x21, waiting for transfers between devices: 65.1 us -> 36.6 us  [send(): lax.ppermute(array, axis, [(i, (i + step) % size) for i in range(size)])]
    ppermute x0 -> x14, starting transfers between devices: none -> 25.5 us  [cross(): return lax.ppermute(array, AXES, pairs)]
    unnamed x0 -> x6, local copies, waits for them, and re-layouts: none -> 13.9 us
    pallas_call x2, Pallas kernels: 9.42 us -> 7.03 us  [hold_tiles(): pl.pallas_call(hold_kernel, out_shape=jax.ShapeDtypeStruct(tiles.shape, t...]
    slice x5 -> x2, local copies, waits for them, and re-layouts: 3.88 us -> 1.66 us  [shards(): over = (cross(right[:8], far_axes, 1), cross(left[8:], far_axes, -1))]
  transfers between devices with their start and end apart: 49 -> 35, of which waited for: 27 -> 25; matrix products, arithmetic and copies ran while one was open for 2% -> 0% of each run, Pallas kernels for 6% -> 4%
where the time goes in v5:
time: 180 us; the launch traced here: 181 us
  waiting for transfers between devices  80.2 us (45%)
  starting transfers between devices  59.1 us (33%)
  Pallas kernels  23.1 us (13%)
  local copies, waits for them, and re-layouts  15.6 us (9%)
    ppermute x14, waiting for transfers between devices, cross(): return lax.ppermute(array, AXES, pairs)  43.6 us
    ppermute x21, waiting for transfers between devices, send(): lax.ppermute(array, axis, [(i, (i + step) % size) for i in range(size)])  36.6 us
    ppermute x21, starting transfers between devices, send(): lax.ppermute(array, axis, [(i, (i + step) % size) for i in range(size)])  33.6 us
    ppermute x14, starting transfers between devices, cross(): return lax.ppermute(array, AXES, pairs)  25.5 us
    unnamed x6, local copies, waits for them, and re-layouts  13.9 us
    pallas_call x2, Pallas kernels, hold_tiles(): pl.pallas_call(hold_kernel, out_shape=jax.ShapeDtypeStruct(tiles.shape, t...  7.03 us
    pallas_call x1, Pallas kernels, finish(): pl.pallas_call(kernel, out_shape=(jax.ShapeDtypeStruct((4 * SIDE, RANK),...  5.91 us
    pallas_call x1, Pallas kernels, forward(): pl.pallas_call(forward_kernel, out_shape=(jax.ShapeDtypeStruct((33, SIDE,...  4.72 us
  transfers between devices with their start and end apart: 35, of which 25 were waited for; matrix products, arithmetic and copies ran while one was open for 0% of the time, Pallas kernels for 4%

profile of v5, /device:TPU:0, one launch (start us, length us, event | category | flops | bytes accessed | tf_op | source)
XLA Modules:
  0.0 180.8 jit_solution(4151299537601450692)
XLA Ops:
  0.6 3.2 %collective-permute-start.1 = (bf16[1024,128]{1,0:T(8,128)(2,1)}, bf16[1024,128]{1,0:T(8,128)(2,1)S(1)}, u32[]{:S(2)}, u32[]{:S(2)}) collective-permute-start(bf16[1024,128]{1,0:T(8,128)(2,1)} %param.4), channel_id=1, source_target_pairs={{0,64},{1,17},{2,66},{3,19},{4,68},{5,21},{6,70},{7,23},{8,72},{9,... | collective-permute-start | bytes 786440 | tf_op jit(solution)/shard_map/gather_basis/ppermute | solution.py:33
  3.8 1.1 collective-permute-start
  5.0 0.9 collective-permute-start.2
  5.8 3.0 %collective-permute-done.1 = bf16[1024,128]{1,0:T(8,128)(2,1)S(1)} collective-permute-done((bf16[1024,128]{1,0:T(8,128)(2,1)}, bf16[1024,128]{1,0:T(8,128)(2,1)S(1)}, u32[]{:S(2)}, u32[]{:S(2)}) %collective-permute-start.1) | collective-permute-done | bytes 262176 | tf_op jit(solution)/shard_map/gather_basis/ppermute | solution.py:33
  8.8 3.0 %collective-permute-done = bf16[1024,128]{1,0:T(8,128)(2,1)S(1)} collective-permute-done((bf16[1024,128]{1,0:T(8,128)(2,1)}, bf16[1024,128]{1,0:T(8,128)(2,1)S(1)}, u32[]{:S(2)}, u32[]{:S(2)}) %collective-permute-start) | collective-permute-done | bytes 262176 | tf_op jit(solution)/shard_map/gather_basis/ppermute | solution.py:33
  11.8 1.0 collective-permute-done.2
  12.8 1.0 pad_maximum_fusion
  13.8 3.1 %collective-permute-start.4 = (bf16[16,256,128]{2,1,0:T(8,128)(2,1)S(1)}, bf16[16,256,128]{2,1,0:T(8,128)(2,1)S(1)}, u32[]{:S(2)}, u32[]{:S(2)}) collective-permute-start(bf16[16,256,128]{2,1,0:T(8,128)(2,1)S(1)} %bitcast.5), channel_id=1, source_target_pairs={{0,24},{1,97},{2,26},{3,99},{4,28},{5,101},{6,30},{7,103},{8,0},{9... | collective-permute-start | bytes 3145736 | tf_op jit(solution)/shard_map/gather_basis/ppermute | solution.py:33
  17.5 3.5 %hold_tiles.2.tiles = bf16[160,256,256]{2,1,0:T(8,128)(2,1)S(1)} custom-call(s32[1]{0:T(128)} %copy.6.count, bf16[160,256,256]{2,1,0:T(8,128)(2,1)} %tiles.1), custom_call_target="tpu_custom_call" | custom-call | bytes 41943040 | tf_op jit(solution)/shard_map/gather_basis/hold_tiles/pallas_call | solution.py:83
  21.1 7.0 %copy-done = bf16[160,256,256]{2,1,0:T(8,128)(2,1)} copy-done((bf16[160,256,256]{2,1,0:T(8,128)(2,1)}, bf16[160,256,256]{2,1,0:T(8,128)(2,1)S(1)}, u32[]{:S(2)}) %copy-start) | copy-done | bytes 20971544
  28.0 1.1 collective-permute-done.4.rest_1_
  29.2 3.7 %collective-permute-done.3.rest_4_ = bf16[16,256,128]{2,1,0:T(8,128)(2,1)S(1)} collective-permute-done((bf16[16,256,128]{2,1,0:T(8,128)(2,1)S(1)}, bf16[16,256,128]{2,1,0:T(8,128)(2,1)S(1)}, u32[]{:S(2)}, u32[]{:S(2)}) %collective-permute-start.3) | collective-permute-done | bytes 1048608 | tf_op jit(solution)/shard_map/gather_basis/ppermute | solution.py:33
  32.9 0.8 slice.16
  33.7 0.8 slice.15
  34.5 3.2 %collective-permute-start.6 = (bf16[8,256,128]{2,1,0:T(8,128)(2,1)}, bf16[8,256,128]{2,1,0:T(8,128)(2,1)}, u32[]{:S(2)}, u32[]{:S(2)}) collective-permute-start(bf16[8,256,128]{2,1,0:T(8,128)(2,1)} %slice.16), channel_id=1, source_target_pairs={{0,24},{1,97},{2,26},{3,99},{4,28},{5,101},{6,30},{7,103},{8,0},{9... | collective-permute-start | bytes 1572872 | tf_op jit(solution)/shard_map/gather_basis/ppermute | solution.py:33
  37.8 7.4 %collective-permute-done.5.rest_2_ = bf16[8,256,128]{2,1,0:T(8,128)(2,1)} collective-permute-done((bf16[8,256,128]{2,1,0:T(8,128)(2,1)}, bf16[8,256,128]{2,1,0:T(8,128)(2,1)}, u32[]{:S(2)}, u32[]{:S(2)}) %collective-permute-start.5) | collective-permute-done | bytes 524320 | tf_op jit(solution)/shard_map/gather_basis/ppermute | solution.py:33
  45.2 7.0 %copy-done.1 = bf16[160,256,256]{2,1,0:T(8,128)(2,1)S(1)} copy-done((bf16[160,256,256]{2,1,0:T(8,128)(2,1)S(1)}, bf16[160,256,256]{2,1,0:T(8,128)(2,1)}, u32[]{:S(2)}) %copy-start.1) | copy-done | bytes 20971544
  52.2 4.7 %forward.1 = (f32[33,256,128]{2,1,0:T(8,128)S(1)}, f32[16,256,128]{2,1,0:T(8,128)S(1)}) custom-call(s32[1]{0:T(128)} %copy.6.count, s32[160]{0:T(256)S(1)} %get-tuple-element.68.row_at, s32[160]{0:T(256)S(1)} %get-tuple-element.75.col_at, bf16[160,256,256]{2,1,0:T(8,128)(2,1)S(1)} %copy-done.1, bf16[16,256,128]{2,1,0:T(8,128)(2,1)S(1)} %bitcast.7, ...), custom_call_target="tpu_custom_call" | custom-call | tf_op jit(solution)/shard_map/forward/pallas_call | solution.py:119
  57.0 4.1 %collective-permute-done.7.came = f32[16,256,128]{2,1,0:T(8,128)S(1)} collective-permute-done((f32[16,256,128]{2,1,0:T(8,128)S(1)}, f32[16,256,128]{2,1,0:T(8,128)S(1)}, u32[]{:S(2)}, u32[]{:S(2)}) %collective-permute-start.7) | collective-permute-done | bytes 2097184 | tf_op jit(solution)/shard_map/reduce_inner/ppermute | solution.py:22
  61.2 0.5 core_sum.1
  61.8 4.1 %collective-permute-start.10 = (f16[1040,128]{1,0:T(8,128)(2,1)S(1)}, f16[1040,128]{1,0:T(8,128)(2,1)S(1)}, u32[]{:S(2)}, u32[]{:S(2)}) collective-permute-start(f16[1040,128]{1,0:T(8,128)(2,1)S(1)} %convert_element_type.20), channel_id=1, source_target_pairs={{0,6},{2,0},{4,2},{6,4},{1,7},{3,1},{5,3},{7,5},{8,14},{10,8},{12,... | collective-permute-start | bytes 798728 | tf_op jit(solution)/shard_map/reduce_inner/ppermute | solution.py:22
  65.9 1.3 collective-permute-start.9
  67.2 1.3 collective-permute-start.8
  68.5 3.5 %hold_tiles.3.tiles = bf16[160,256,256]{2,1,0:T(8,128)(2,1)S(1)} custom-call(s32[1]{0:T(128)} %copy.6.count, bf16[160,256,256]{2,1,0:T(8,128)(2,1)} %tiles.1), custom_call_target="tpu_custom_call" | custom-call | bytes 41943040 | tf_op jit(solution)/shard_map/reduce_inner/hold_tiles/pallas_call | solution.py:83
  72.0 5.6 %collective-permute-done.10 = f16[1040,128]{1,0:T(8,128)(2,1)S(1)} collective-permute-done((f16[1040,128]{1,0:T(8,128)(2,1)S(1)}, f16[1040,128]{1,0:T(8,128)(2,1)S(1)}, u32[]{:S(2)}, u32[]{:S(2)}) %collective-permute-start.10) | collective-permute-done | bytes 266272 | tf_op jit(solution)/shard_map/reduce_inner/ppermute | solution.py:22
  77.6 3.7 %collective-permute-done.8 = f16[1040,128]{1,0:T(8,128)(2,1)S(1)} collective-permute-done((f16[1040,128]{1,0:T(8,128)(2,1)S(1)}, f16[1040,128]{1,0:T(8,128)(2,1)S(1)}, u32[]{:S(2)}, u32[]{:S(2)}) %collective-permute-start.8) | collective-permute-done | bytes 266272 | tf_op jit(solution)/shard_map/reduce_inner/ppermute | solution.py:22
  81.4 0.2 inner_sum.1.rest_0_
  81.7 0.1 collective-permute-start.13
  81.8 2.0 %collective-permute-start.12 = (bf16[4,128,256]{2,1,0:T(8,128)(2,1)S(1)}, bf16[4,128,256]{2,1,0:T(8,128)(2,1)S(1)}, u32[]{:S(2)}, u32[]{:S(2)}) collective-permute-start(bf16[4,128,256]{2,1,0:T(8,128)(2,1)S(1)} %inner_sum.1.rest_0_), channel_id=1, source_target_pairs={{0,4},{2,6},{4,0},{6,2},{1,5},{3,7},{5,1},{7,3},{8,12},{10,14},{12... | collective-permute-start | bytes 786440 | tf_op jit(solution)/shard_map/gather_inner/ppermute | solution.py:22
  83.8 2.1 %collective-permute-start.11 = (bf16[4,128,256]{2,1,0:T(8,128)(2,1)S(1)}, bf16[4,128,256]{2,1,0:T(8,128)(2,1)S(1)}, u32[]{:S(2)}, u32[]{:S(2)}) collective-permute-start(bf16[4,128,256]{2,1,0:T(8,128)(2,1)S(1)} %inner_sum.1.rest_0_), channel_id=1, source_target_pairs={{0,6},{2,0},{4,2},{6,4},{1,7},{3,1},{5,3},{7,5},{8,14},{10,8},{12,... | collective-permute-start | bytes 786440 | tf_op jit(solution)/shard_map/gather_inner/ppermute | solution.py:22
  85.9 10.9 %collective-permute-done.13.rest_3_ = bf16[4,128,256]{2,1,0:T(8,128)(2,1)S(1)} collective-permute-done((bf16[4,128,256]{2,1,0:T(8,128)(2,1)S(1)}, bf16[4,128,256]{2,1,0:T(8,128)(2,1)S(1)}, u32[]{:S(2)}, u32[]{:S(2)}) %collective-permute-start.13) | collective-permute-done | bytes 262176 | tf_op jit(solution)/shard_map/gather_inner/ppermute | solution.py:22
  96.8 0.5 collective-permute-start.16
  97.3 0.1 collective-permute-done.11.rest_1_
  97.4 0.9 collective-permute-done.17.rest_7_
  98.3 0.4 collective-permute-done.16.rest_6_
  98.7 0.4 collective-permute-done.15.rest_5_
  99.1 3.4 %backward.1 = (f32[65,128,256]{2,1,0:T(8,128)S(1)}, bf16[8,128,256]{2,1,0:T(8,128)(2,1)S(1)}, bf16[8,128,256]{2,1,0:T(8,128)(2,1)S(1)}) custom-call(s32[1]{0:T(128)} %copy.6.count, s32[160]{0:T(256)S(1)} %get-tuple-element.69.row_at, s32[160]{0:T(256)S(1)} %get-tuple-element.74.col_at, bf16[160,256,256]{2,1,0:T(8,128)(2,1)S(1)} %hold_tiles.3.tiles, ...), custom_call_target="tpu_custom_call" | custom-call | tf_op jit(solution)/shard_map/backward/pallas_call | solution.py:162
  102.6 3.3 %collective-permute-start.19 = (bf16[8,128,256]{2,1,0:T(8,128)(2,1)S(1)}, bf16[8,128,256]{2,1,0:T(8,128)(2,1)S(1)}, u32[]{:S(2)}, u32[]{:S(2)}) collective-permute-start(bf16[8,128,256]{2,1,0:T(8,128)(2,1)S(1)} %get-tuple-element.59), channel_id=1, source_target_pairs={{0,24},{1,97},{2,26},{3,99},{4,28},{5,101},{6,30},{7,103},{8,0},{9... | collective-permute-start | bytes 1572872 | tf_op jit(solution)/shard_map/reduce_outer/ppermute | solution.py:33
  105.9 7.1 %collective-permute-done.18.a = bf16[8,128,256]{2,1,0:T(8,128)(2,1)S(1)} collective-permute-done((bf16[8,128,256]{2,1,0:T(8,128)(2,1)S(1)}, bf16[8,128,256]{2,1,0:T(8,128)(2,1)S(1)}, u32[]{:S(2)}, u32[]{:S(2)}) %collective-permute-start.18) | collective-permute-done | bytes 524320 | tf_op jit(solution)/shard_map/reduce_outer/ppermute | solution.py:33
  113.0 0.3 relay_sum.1
  113.3 1.7 collective-permute-start.20
  115.0 2.0 %collective-permute-start.21 = (bf16[16,128,256]{2,1,0:T(8,128)(2,1)S(1)}, bf16[16,128,256]{2,1,0:T(8,128)(2,1)S(1)}, u32[]{:S(2)}, u32[]{:S(2)}) collective-permute-start(bf16[16,128,256]{2,1,0:T(8,128)(2,1)S(1)} %get-tuple-element.61), channel_id=1, source_target_pairs={{0,24},{1,97},{2,26},{3,99},{4,28},{5,101},{6,30},{7,103},{8,0},{9... | collective-permute-start | bytes 3145736 | tf_op jit(solution)/shard_map/reduce_outer/ppermute | solution.py:33
  117.0 12.7 %collective-permute-done.20.a = bf16[16,128,256]{2,1,0:T(8,128)(2,1)S(1)} collective-permute-done((bf16[16,128,256]{2,1,0:T(8,128)(2,1)S(1)}, bf16[16,128,256]{2,1,0:T(8,128)(2,1)S(1)}, u32[]{:S(2)}, u32[]{:S(2)}) %collective-permute-start.20) | collective-permute-done | bytes 1048608 | tf_op jit(solution)/shard_map/reduce_outer/ppermute | solution.py:33
  129.6 0.1 collective-permute-done.21.b
  129.8 0.3 middle_sum.1
  130.1 1.3 collective-permute-start.22
  131.4 3.2 %collective-permute-start.23 = (bf16[4,128,256]{2,1,0:T(8,128)(2,1)S(1)}, bf16[4,128,256]{2,1,0:T(8,128)(2,1)S(1)}, u32[]{:S(2)}, u32[]{:S(2)}) collective-permute-start(bf16[4,128,256]{2,1,0:T(8,128)(2,1)S(1)} %get-tuple-element.64), channel_id=1, source_target_pairs={{0,64},{1,17},{2,66},{3,19},{4,68},{5,21},{6,70},{7,23},{8,72},{9,... | collective-permute-start | bytes 786440 | tf_op jit(solution)/shard_map/reduce_outer/ppermute | solution.py:33
  134.5 2.5 %collective-permute-start.24 = (bf16[4,128,256]{2,1,0:T(8,128)(2,1)S(1)}, bf16[4,128,256]{2,1,0:T(8,128)(2,1)S(1)}, u32[]{:S(2)}, u32[]{:S(2)}) collective-permute-start(bf16[4,128,256]{2,1,0:T(8,128)(2,1)S(1)} %get-tuple-element.65), channel_id=1, source_target_pairs={{0,96},{1,25},{2,98},{3,27},{4,100},{5,29},{6,102},{7,31},{8,104},... | collective-permute-start | bytes 786440 | tf_op jit(solution)/shard_map/reduce_outer/ppermute | solution.py:33
  137.1 0.7 collective-permute-done.22.a
  137.8 3.8 %collective-permute-done.23.b = bf16[4,128,256]{2,1,0:T(8,128)(2,1)S(1)} collective-permute-done((bf16[4,128,256]{2,1,0:T(8,128)(2,1)S(1)}, bf16[4,128,256]{2,1,0:T(8,128)(2,1)S(1)}, u32[]{:S(2)}, u32[]{:S(2)}) %collective-permute-start.23) | collective-permute-done | bytes 262176 | tf_op jit(solution)/shard_map/reduce_outer/ppermute | solution.py:33
  141.6 0.6 outer_sum.1
  142.3 1.2 collective-permute-done.25
  143.6 2.6 %collective-permute-start.28 = (f32[128,128]{1,0:T(8,128)S(1)}, f32[128,128]{1,0:T(8,128)S(1)}, u32[]{:S(2)}, u32[]{:S(2)}) collective-permute-start(f32[128,128]{1,0:T(8,128)S(1)} %add.91), channel_id=1, source_target_pairs={{0,6},{2,0},{4,2},{6,4},{1,7},{3,1},{5,3},{7,5},{8,14},{10,8},{12,... | collective-permute-start | bytes 196616 | tf_op jit(solution)/shard_map/reduce_gram/ppermute | solution.py:22
  146.1 3.5 %collective-permute-start.26 = (f32[128,128]{1,0:T(8,128)S(1)}, f32[128,128]{1,0:T(8,128)S(1)}, u32[]{:S(2)}, u32[]{:S(2)}) collective-permute-start(f32[128,128]{1,0:T(8,128)S(1)} %add.91), channel_id=1, source_target_pairs={{0,4},{2,6},{4,0},{6,2},{1,5},{3,7},{5,1},{7,3},{8,12},{10,14},{12... | collective-permute-start | bytes 196616 | tf_op jit(solution)/shard_map/reduce_gram/ppermute | solution.py:22
  149.6 2.5 %collective-permute-done.27 = f32[128,128]{1,0:T(8,128)S(1)} collective-permute-done((f32[128,128]{1,0:T(8,128)S(1)}, f32[128,128]{1,0:T(8,128)S(1)}, u32[]{:S(2)}, u32[]{:S(2)}) %collective-permute-start.27) | collective-permute-done | bytes 65568 | tf_op jit(solution)/shard_map/reduce_gram/ppermute | solution.py:22
  152.2 0.7 collective-permute-done.26
  152.9 6.1 %collective-permute-start.31 = (f32[128,128]{1,0:T(8,128)S(1)}, f32[128,128]{1,0:T(8,128)S(1)}, u32[]{:S(2)}, u32[]{:S(2)}) collective-permute-start(f32[128,128]{1,0:T(8,128)S(1)} %add_add_fusion.2), channel_id=1, source_target_pairs={{0,24},{8,0},{16,8},{24,16},{1,25},{9,1},{17,9},{25,17},{2,26},{10... | collective-permute-start | bytes 196616 | tf_op jit(solution)/shard_map/reduce_gram/ppermute | solution.py:22
  159.0 3.6 %collective-permute-start.29 = (f32[128,128]{1,0:T(8,128)S(1)}, f32[128,128]{1,0:T(8,128)S(1)}, u32[]{:S(2)}, u32[]{:S(2)}) collective-permute-start(f32[128,128]{1,0:T(8,128)S(1)} %add_add_fusion.2), channel_id=1, source_target_pairs={{0,16},{8,24},{16,0},{24,8},{1,17},{9,25},{17,1},{25,9},{2,18},{10... | collective-permute-start | bytes 196616 | tf_op jit(solution)/shard_map/reduce_gram/ppermute | solution.py:22
  162.6 1.8 %collective-permute-done.30 = f32[128,128]{1,0:T(8,128)S(1)} collective-permute-done((f32[128,128]{1,0:T(8,128)S(1)}, f32[128,128]{1,0:T(8,128)S(1)}, u32[]{:S(2)}, u32[]{:S(2)}) %collective-permute-start.30) | collective-permute-done | bytes 65568 | tf_op jit(solution)/shard_map/reduce_gram/ppermute | solution.py:22
  164.4 1.1 collective-permute-done.29
  165.5 3.1 %collective-permute-start.34 = (f32[128,128]{1,0:T(8,128)S(1)}, f32[128,128]{1,0:T(8,128)S(1)}, u32[]{:S(2)}, u32[]{:S(2)}) collective-permute-start(f32[128,128]{1,0:T(8,128)S(1)} %add_add_fusion.1), channel_id=1, source_target_pairs={{0,96},{32,0},{64,32},{96,64},{1,97},{33,1},{65,33},{97,65},{2,98}... | collective-permute-start | bytes 196616 | tf_op jit(solution)/shard_map/reduce_gram/ppermute | solution.py:22
  168.7 3.1 %collective-permute-start.32 = (f32[128,128]{1,0:T(8,128)S(1)}, f32[128,128]{1,0:T(8,128)S(1)}, u32[]{:S(2)}, u32[]{:S(2)}) collective-permute-start(f32[128,128]{1,0:T(8,128)S(1)} %add_add_fusion.1), channel_id=1, source_target_pairs={{0,64},{32,96},{64,0},{96,32},{1,65},{33,97},{65,1},{97,33},{2,66}... | collective-permute-start | bytes 196616 | tf_op jit(solution)/shard_map/reduce_gram/ppermute | solution.py:22
  171.8 3.1 %collective-permute-done.33 = f32[128,128]{1,0:T(8,128)S(1)} collective-permute-done((f32[128,128]{1,0:T(8,128)S(1)}, f32[128,128]{1,0:T(8,128)S(1)}, u32[]{:S(2)}, u32[]{:S(2)}) %collective-permute-start.33) | collective-permute-done | bytes 65568 | tf_op jit(solution)/shard_map/reduce_gram/ppermute | solution.py:22
  174.9 5.9 %finish.1 = (f32[1024,128]{1,0:T(8,128)}, f32[128,128]{1,0:T(8,128)}) custom-call(f32[128,128]{1,0:T(8,128)S(1)} %add_add_fusion.refs_0_, f32[4,128,256]{2,1,0:T(8,128)S(1)} %get-tuple-element.67.refs_1_), custom_call_target="tpu_custom_call" | custom-call | tf_op jit(solution)/shard_map/finish/pallas_call | solution.py:354
  (37 shorter events, 0.6 us)
Async XLA Ops:
  0.6 8.2 %collective-permute-start.1 = (bf16[1024,128]{1,0:T(8,128)(2,1)}, bf16[1024,128]{1,0:T(8,128)(2,1)S(1)}, u32[]{:S(2)}, u32[]{:S(2)}) collective-permute-start(bf16[1024,128]{1,0:T(8,128)(2,1)} %param.4), channel_id=1, source_target_pairs={{0,64},{1,17},{2,66},{3,19},{4,68},{5,21},{6,70},{7,23},{8,72},{9,... | collective-permute-start | bytes 786440 | tf_op jit(solution)/shard_map/gather_basis/ppermute | solution.py:33
  3.8 8.0 %collective-permute-start = (bf16[1024,128]{1,0:T(8,128)(2,1)}, bf16[1024,128]{1,0:T(8,128)(2,1)S(1)}, u32[]{:S(2)}, u32[]{:S(2)}) collective-permute-start(bf16[1024,128]{1,0:T(8,128)(2,1)} %param.4), channel_id=1, source_target_pairs={{0,96},{1,25},{2,98},{3,27},{4,100},{5,29},{6,102},{7,31},{8,104},... | collective-permute-start | bytes 786440 | tf_op jit(solution)/shard_map/gather_basis/ppermute | solution.py:33
  5.0 7.8 %collective-permute-start.2 = (bf16[1024,128]{1,0:T(8,128)(2,1)}, bf16[1024,128]{1,0:T(8,128)(2,1)S(1)}, u32[]{:S(2)}, u32[]{:S(2)}) collective-permute-start(bf16[1024,128]{1,0:T(8,128)(2,1)} %param.4), channel_id=1, source_target_pairs={{0,32},{1,9},{2,34},{3,11},{4,36},{5,13},{6,38},{7,15},{8,40},{9,1... | collective-permute-start | bytes 786440 | tf_op jit(solution)/shard_map/gather_basis/ppermute | solution.py:33
  13.8 15.4 %collective-permute-start.4 = (bf16[16,256,128]{2,1,0:T(8,128)(2,1)S(1)}, bf16[16,256,128]{2,1,0:T(8,128)(2,1)S(1)}, u32[]{:S(2)}, u32[]{:S(2)}) collective-permute-start(bf16[16,256,128]{2,1,0:T(8,128)(2,1)S(1)} %bitcast.5), channel_id=1, source_target_pairs={{0,24},{1,97},{2,26},{3,99},{4,28},{5,101},{6,30},{7,103},{8,0},{9... | collective-permute-start | bytes 3145736 | tf_op jit(solution)/shard_map/gather_basis/ppermute | solution.py:33
  16.9 16.0 %collective-permute-start.3 = (bf16[16,256,128]{2,1,0:T(8,128)(2,1)S(1)}, bf16[16,256,128]{2,1,0:T(8,128)(2,1)S(1)}, u32[]{:S(2)}, u32[]{:S(2)}) collective-permute-start(bf16[16,256,128]{2,1,0:T(8,128)(2,1)S(1)} %bitcast.6), channel_id=1, source_target_pairs={{0,8},{1,33},{2,10},{3,35},{4,12},{5,37},{6,14},{7,39},{8,16},{9,4... | collective-permute-start | bytes 3145736 | tf_op jit(solution)/shard_map/gather_basis/ppermute | solution.py:33
  21.0 7.0 %copy-start = (bf16[160,256,256]{2,1,0:T(8,128)(2,1)}, bf16[160,256,256]{2,1,0:T(8,128)(2,1)S(1)}, u32[]{:S(2)}) copy-start(bf16[160,256,256]{2,1,0:T(8,128)(2,1)S(1)} %hold_tiles.2.tiles) | copy-start | bytes 62914564
  28.0 9.7 %copy-start.2 = (s32[160,2]{0,1:T(2,128)S(1)}, s32[160,2]{0,1:T(2,128)}, u32[]{:S(2)}) copy-start(s32[160,2]{0,1:T(2,128)} %param.6) | copy-start | bytes 3844
  34.5 10.7 %collective-permute-start.5 = (bf16[8,256,128]{2,1,0:T(8,128)(2,1)}, bf16[8,256,128]{2,1,0:T(8,128)(2,1)}, u32[]{:S(2)}, u32[]{:S(2)}) collective-permute-start(bf16[8,256,128]{2,1,0:T(8,128)(2,1)} %slice.15), channel_id=1, source_target_pairs={{0,8},{1,33},{2,10},{3,35},{4,12},{5,37},{6,14},{7,39},{8,16},{9,4... | collective-permute-start | bytes 1572872 | tf_op jit(solution)/shard_map/gather_basis/ppermute | solution.py:33
  34.5 10.7 %collective-permute-start.6 = (bf16[8,256,128]{2,1,0:T(8,128)(2,1)}, bf16[8,256,128]{2,1,0:T(8,128)(2,1)}, u32[]{:S(2)}, u32[]{:S(2)}) collective-permute-start(bf16[8,256,128]{2,1,0:T(8,128)(2,1)} %slice.16), channel_id=1, source_target_pairs={{0,24},{1,97},{2,26},{3,99},{4,28},{5,101},{6,30},{7,103},{8,0},{9... | collective-permute-start | bytes 1572872 | tf_op jit(solution)/shard_map/gather_basis/ppermute | solution.py:33
  45.2 7.0 %copy-start.1 = (bf16[160,256,256]{2,1,0:T(8,128)(2,1)S(1)}, bf16[160,256,256]{2,1,0:T(8,128)(2,1)}, u32[]{:S(2)}) copy-start(bf16[160,256,256]{2,1,0:T(8,128)(2,1)} %copy-done) | copy-start | bytes 62914564
  56.9 4.2 %collective-permute-start.7 = (f32[16,256,128]{2,1,0:T(8,128)S(1)}, f32[16,256,128]{2,1,0:T(8,128)S(1)}, u32[]{:S(2)}, u32[]{:S(2)}) collective-permute-start(f32[16,256,128]{2,1,0:T(8,128)S(1)} %get-tuple-element.44), channel_id=1, source_target_pairs={{0,1},{1,0},{2,3},{3,2},{4,5},{5,4},{6,7},{7,6},{8,9},{9,8},{10,11... | collective-permute-start | bytes 6291464 | tf_op jit(solution)/shard_map/reduce_inner/ppermute | solution.py:22
  61.8 15.8 %collective-permute-start.10 = (f16[1040,128]{1,0:T(8,128)(2,1)S(1)}, f16[1040,128]{1,0:T(8,128)(2,1)S(1)}, u32[]{:S(2)}, u32[]{:S(2)}) collective-permute-start(f16[1040,128]{1,0:T(8,128)(2,1)S(1)} %convert_element_type.20), channel_id=1, source_target_pairs={{0,6},{2,0},{4,2},{6,4},{1,7},{3,1},{5,3},{7,5},{8,14},{10,8},{12,... | collective-permute-start | bytes 798728 | tf_op jit(solution)/shard_map/reduce_inner/ppermute | solution.py:22
  65.9 11.7 %collective-permute-start.9 = (f16[1040,128]{1,0:T(8,128)(2,1)S(1)}, f16[1040,128]{1,0:T(8,128)(2,1)S(1)}, u32[]{:S(2)}, u32[]{:S(2)}) collective-permute-start(f16[1040,128]{1,0:T(8,128)(2,1)S(1)} %convert_element_type.19), channel_id=1, source_target_pairs={{0,4},{2,6},{4,0},{6,2},{1,5},{3,7},{5,1},{7,3},{8,12},{10,14},{12... | collective-permute-start | bytes 798728 | tf_op jit(solution)/shard_map/reduce_inner/ppermute | solution.py:22
  67.2 14.1 %collective-permute-start.8 = (f16[1040,128]{1,0:T(8,128)(2,1)S(1)}, f16[1040,128]{1,0:T(8,128)(2,1)S(1)}, u32[]{:S(2)}, u32[]{:S(2)}) collective-permute-start(f16[1040,128]{1,0:T(8,128)(2,1)S(1)} %convert_element_type.18), channel_id=1, source_target_pairs={{0,2},{2,4},{4,6},{6,0},{1,3},{3,5},{5,7},{7,1},{8,10},{10,12},{12... | collective-permute-start | bytes 798728 | tf_op jit(solution)/shard_map/reduce_inner/ppermute | solution.py:22
  81.7 15.1 %collective-permute-start.13 = (bf16[4,128,256]{2,1,0:T(8,128)(2,1)S(1)}, bf16[4,128,256]{2,1,0:T(8,128)(2,1)S(1)}, u32[]{:S(2)}, u32[]{:S(2)}) collective-permute-start(bf16[4,128,256]{2,1,0:T(8,128)(2,1)S(1)} %inner_sum.1.rest_0_), channel_id=1, source_target_pairs={{0,2},{2,4},{4,6},{6,0},{1,3},{3,5},{5,7},{7,1},{8,10},{10,12},{12... | collective-permute-start | bytes 786440 | tf_op jit(solution)/shard_map/gather_inner/ppermute | solution.py:22
  81.8 15.0 %collective-permute-start.12 = (bf16[4,128,256]{2,1,0:T(8,128)(2,1)S(1)}, bf16[4,128,256]{2,1,0:T(8,128)(2,1)S(1)}, u32[]{:S(2)}, u32[]{:S(2)}) collective-permute-start(bf16[4,128,256]{2,1,0:T(8,128)(2,1)S(1)} %inner_sum.1.rest_0_), channel_id=1, source_target_pairs={{0,4},{2,6},{4,0},{6,2},{1,5},{3,7},{5,1},{7,3},{8,12},{10,14},{12... | collective-permute-start | bytes 786440 | tf_op jit(solution)/shard_map/gather_inner/ppermute | solution.py:22
  83.8 13.6 %collective-permute-start.11 = (bf16[4,128,256]{2,1,0:T(8,128)(2,1)S(1)}, bf16[4,128,256]{2,1,0:T(8,128)(2,1)S(1)}, u32[]{:S(2)}, u32[]{:S(2)}) collective-permute-start(bf16[4,128,256]{2,1,0:T(8,128)(2,1)S(1)} %inner_sum.1.rest_0_), channel_id=1, source_target_pairs={{0,6},{2,0},{4,2},{6,4},{1,7},{3,1},{5,3},{7,5},{8,14},{10,8},{12,... | collective-permute-start | bytes 786440 | tf_op jit(solution)/shard_map/gather_inner/ppermute | solution.py:22
  85.9 11.5 %collective-permute-start.14 = (bf16[4,128,256]{2,1,0:T(8,128)(2,1)S(1)}, bf16[4,128,256]{2,1,0:T(8,128)(2,1)S(1)}, u32[]{:S(2)}, u32[]{:S(2)}) collective-permute-start(bf16[4,128,256]{2,1,0:T(8,128)(2,1)S(1)} %inner_sum.1.rest_0_), channel_id=1, source_target_pairs={{0,1},{1,0},{2,3},{3,2},{4,5},{5,4},{6,7},{7,6},{8,9},{9,8},{10,11... | collective-permute-start | bytes 786440 | tf_op jit(solution)/shard_map/gather_inner/ppermute | solution.py:22
  96.8 1.5 collective-permute-start.17
  96.8 1.9 %collective-permute-start.16 = (bf16[4,128,256]{2,1,0:T(8,128)(2,1)S(1)}, bf16[4,128,256]{2,1,0:T(8,128)(2,1)S(1)}, u32[]{:S(2)}, u32[]{:S(2)}) collective-permute-start(bf16[4,128,256]{2,1,0:T(8,128)(2,1)S(1)} %collective-permute-done.12.rest_2_), channel_id=1, source_target_pairs={{0,1},{1,0},{2,3},{3,2},{4,5},{5,4},{6,7},{7,6},{8,9},{9,8},{10,11... | collective-permute-start | bytes 786440 | tf_op jit(solution)/shard_map/gather_inner/ppermute | solution.py:22
  97.4 1.7 collective-permute-start.15
  102.5 10.5 %collective-permute-start.18 = (bf16[8,128,256]{2,1,0:T(8,128)(2,1)S(1)}, bf16[8,128,256]{2,1,0:T(8,128)(2,1)S(1)}, u32[]{:S(2)}, u32[]{:S(2)}) collective-permute-start(bf16[8,128,256]{2,1,0:T(8,128)(2,1)S(1)} %get-tuple-element.58), channel_id=1, source_target_pairs={{0,8},{1,33},{2,10},{3,35},{4,12},{5,37},{6,14},{7,39},{8,16},{9,4... | collective-permute-start | bytes 1572872 | tf_op jit(solution)/shard_map/reduce_outer/ppermute | solution.py:33
  102.6 10.4 %collective-permute-start.19 = (bf16[8,128,256]{2,1,0:T(8,128)(2,1)S(1)}, bf16[8,128,256]{2,1,0:T(8,128)(2,1)S(1)}, u32[]{:S(2)}, u32[]{:S(2)}) collective-permute-start(bf16[8,128,256]{2,1,0:T(8,128)(2,1)S(1)} %get-tuple-element.59), channel_id=1, source_target_pairs={{0,24},{1,97},{2,26},{3,99},{4,28},{5,101},{6,30},{7,103},{8,0},{9... | collective-permute-start | bytes 1572872 | tf_op jit(solution)/shard_map/reduce_outer/ppermute | solution.py:33
  113.3 16.3 %collective-permute-start.20 = (bf16[16,128,256]{2,1,0:T(8,128)(2,1)S(1)}, bf16[16,128,256]{2,1,0:T(8,128)(2,1)S(1)}, u32[]{:S(2)}, u32[]{:S(2)}) collective-permute-start(bf16[16,128,256]{2,1,0:T(8,128)(2,1)S(1)} %get-tuple-element.60), channel_id=1, source_target_pairs={{0,8},{1,33},{2,10},{3,35},{4,12},{5,37},{6,14},{7,39},{8,16},{9,4... | collective-permute-start | bytes 3145736 | tf_op jit(solution)/shard_map/reduce_outer/ppermute | solution.py:33
  115.0 14.8 %collective-permute-start.21 = (bf16[16,128,256]{2,1,0:T(8,128)(2,1)S(1)}, bf16[16,128,256]{2,1,0:T(8,128)(2,1)S(1)}, u32[]{:S(2)}, u32[]{:S(2)}) collective-permute-start(bf16[16,128,256]{2,1,0:T(8,128)(2,1)S(1)} %get-tuple-element.61), channel_id=1, source_target_pairs={{0,24},{1,97},{2,26},{3,99},{4,28},{5,101},{6,30},{7,103},{8,0},{9... | collective-permute-start | bytes 3145736 | tf_op jit(solution)/shard_map/reduce_outer/ppermute | solution.py:33
  130.1 7.7 %collective-permute-start.22 = (bf16[4,128,256]{2,1,0:T(8,128)(2,1)S(1)}, bf16[4,128,256]{2,1,0:T(8,128)(2,1)S(1)}, u32[]{:S(2)}, u32[]{:S(2)}) collective-permute-start(bf16[4,128,256]{2,1,0:T(8,128)(2,1)S(1)} %get-tuple-element.63), channel_id=1, source_target_pairs={{0,32},{1,9},{2,34},{3,11},{4,36},{5,13},{6,38},{7,15},{8,40},{9,1... | collective-permute-start | bytes 786440 | tf_op jit(solution)/shard_map/reduce_outer/ppermute | solution.py:33
  131.4 10.2 %collective-permute-start.23 = (bf16[4,128,256]{2,1,0:T(8,128)(2,1)S(1)}, bf16[4,128,256]{2,1,0:T(8,128)(2,1)S(1)}, u32[]{:S(2)}, u32[]{:S(2)}) collective-permute-start(bf16[4,128,256]{2,1,0:T(8,128)(2,1)S(1)} %get-tuple-element.64), channel_id=1, source_target_pairs={{0,64},{1,17},{2,66},{3,19},{4,68},{5,21},{6,70},{7,23},{8,72},{9,... | collective-permute-start | bytes 786440 | tf_op jit(solution)/shard_map/reduce_outer/ppermute | solution.py:33
  134.5 7.1 %collective-permute-start.24 = (bf16[4,128,256]{2,1,0:T(8,128)(2,1)S(1)}, bf16[4,128,256]{2,1,0:T(8,128)(2,1)S(1)}, u32[]{:S(2)}, u32[]{:S(2)}) collective-permute-start(bf16[4,128,256]{2,1,0:T(8,128)(2,1)S(1)} %get-tuple-element.65), channel_id=1, source_target_pairs={{0,96},{1,25},{2,98},{3,27},{4,100},{5,29},{6,102},{7,31},{8,104},... | collective-permute-start | bytes 786440 | tf_op jit(solution)/shard_map/reduce_outer/ppermute | solution.py:33
  142.2 1.3 collective-permute-start.25
  143.6 6.0 %collective-permute-start.28 = (f32[128,128]{1,0:T(8,128)S(1)}, f32[128,128]{1,0:T(8,128)S(1)}, u32[]{:S(2)}, u32[]{:S(2)}) collective-permute-start(f32[128,128]{1,0:T(8,128)S(1)} %add.91), channel_id=1, source_target_pairs={{0,6},{2,0},{4,2},{6,4},{1,7},{3,1},{5,3},{7,5},{8,14},{10,8},{12,... | collective-permute-start | bytes 196616 | tf_op jit(solution)/shard_map/reduce_gram/ppermute | solution.py:22
  146.1 6.0 %collective-permute-start.27 = (f32[128,128]{1,0:T(8,128)S(1)}, f32[128,128]{1,0:T(8,128)S(1)}, u32[]{:S(2)}, u32[]{:S(2)}) collective-permute-start(f32[128,128]{1,0:T(8,128)S(1)} %add.91), channel_id=1, source_target_pairs={{0,2},{2,4},{4,6},{6,0},{1,3},{3,5},{5,7},{7,1},{8,10},{10,12},{12... | collective-permute-start | bytes 196616 | tf_op jit(solution)/shard_map/reduce_gram/ppermute | solution.py:22
  146.1 6.7 %collective-permute-start.26 = (f32[128,128]{1,0:T(8,128)S(1)}, f32[128,128]{1,0:T(8,128)S(1)}, u32[]{:S(2)}, u32[]{:S(2)}) collective-permute-start(f32[128,128]{1,0:T(8,128)S(1)} %add.91), channel_id=1, source_target_pairs={{0,4},{2,6},{4,0},{6,2},{1,5},{3,7},{5,1},{7,3},{8,12},{10,14},{12... | collective-permute-start | bytes 196616 | tf_op jit(solution)/shard_map/reduce_gram/ppermute | solution.py:22
  152.9 9.7 %collective-permute-start.31 = (f32[128,128]{1,0:T(8,128)S(1)}, f32[128,128]{1,0:T(8,128)S(1)}, u32[]{:S(2)}, u32[]{:S(2)}) collective-permute-start(f32[128,128]{1,0:T(8,128)S(1)} %add_add_fusion.2), channel_id=1, source_target_pairs={{0,24},{8,0},{16,8},{24,16},{1,25},{9,1},{17,9},{25,17},{2,26},{10... | collective-permute-start | bytes 196616 | tf_op jit(solution)/shard_map/reduce_gram/ppermute | solution.py:22
  158.9 5.5 %collective-permute-start.30 = (f32[128,128]{1,0:T(8,128)S(1)}, f32[128,128]{1,0:T(8,128)S(1)}, u32[]{:S(2)}, u32[]{:S(2)}) collective-permute-start(f32[128,128]{1,0:T(8,128)S(1)} %add_add_fusion.2), channel_id=1, source_target_pairs={{0,8},{8,16},{16,24},{24,0},{1,9},{9,17},{17,25},{25,1},{2,10},{10... | collective-permute-start | bytes 196616 | tf_op jit(solution)/shard_map/reduce_gram/ppermute | solution.py:22
  159.0 6.6 %collective-permute-start.29 = (f32[128,128]{1,0:T(8,128)S(1)}, f32[128,128]{1,0:T(8,128)S(1)}, u32[]{:S(2)}, u32[]{:S(2)}) collective-permute-start(f32[128,128]{1,0:T(8,128)S(1)} %add_add_fusion.2), channel_id=1, source_target_pairs={{0,16},{8,24},{16,0},{24,8},{1,17},{9,25},{17,1},{25,9},{2,18},{10... | collective-permute-start | bytes 196616 | tf_op jit(solution)/shard_map/reduce_gram/ppermute | solution.py:22
  165.5 6.2 %collective-permute-start.34 = (f32[128,128]{1,0:T(8,128)S(1)}, f32[128,128]{1,0:T(8,128)S(1)}, u32[]{:S(2)}, u32[]{:S(2)}) collective-permute-start(f32[128,128]{1,0:T(8,128)S(1)} %add_add_fusion.1), channel_id=1, source_target_pairs={{0,96},{32,0},{64,32},{96,64},{1,97},{33,1},{65,33},{97,65},{2,98}... | collective-permute-start | bytes 196616 | tf_op jit(solution)/shard_map/reduce_gram/ppermute | solution.py:22
  168.7 6.2 %collective-permute-start.33 = (f32[128,128]{1,0:T(8,128)S(1)}, f32[128,128]{1,0:T(8,128)S(1)}, u32[]{:S(2)}, u32[]{:S(2)}) collective-permute-start(f32[128,128]{1,0:T(8,128)S(1)} %add_add_fusion.1), channel_id=1, source_target_pairs={{0,32},{32,64},{64,96},{96,0},{1,33},{33,65},{65,97},{97,1},{2,34}... | collective-permute-start | bytes 196616 | tf_op jit(solution)/shard_map/reduce_gram/ppermute | solution.py:22
  168.7 6.2 %collective-permute-start.32 = (f32[128,128]{1,0:T(8,128)S(1)}, f32[128,128]{1,0:T(8,128)S(1)}, u32[]{:S(2)}, u32[]{:S(2)}) collective-permute-start(f32[128,128]{1,0:T(8,128)S(1)} %add_add_fusion.1), channel_id=1, source_target_pairs={{0,64},{32,96},{64,0},{96,32},{1,65},{33,97},{65,1},{97,33},{2,66}... | collective-permute-start | bytes 196616 | tf_op jit(solution)/shard_map/reduce_gram/ppermute | solution.py:22

commit v6 on v5

--- a/solution.py
+++ b/solution.py
@@ -13,6 +13,7 @@
 RANK = 128
 CHUNK = 32
 EXTRA = 16
+SPARE = 32 * 256 + 64 * 65536
 F32 = jnp.float32
 BF16 = jnp.bfloat16
 
@@ -60,7 +61,7 @@
     return copies
 
 
-def hold_kernel(count, tiles, held, sems):
+def hold_copies(count, tiles, held, sems):
     chunks = (count[0] + CHUNK - 1) // CHUNK
 
     def copy(i):
@@ -75,103 +76,226 @@
         copy(i).wait()
         return 0
 
-    lax.fori_loop(0, chunks, start, 0)
-    lax.fori_loop(0, chunks, wait, 0)
-
-
-def hold_tiles(count, tiles):
-    return pl.pallas_call(
-        hold_kernel,
-        out_shape=jax.ShapeDtypeStruct(tiles.shape, tiles.dtype),
-        in_specs=[pl.BlockSpec(memory_space=pltpu.SMEM), pl.BlockSpec(memory_space=pl.ANY)],
-        out_specs=whole(1)[0],
+    return (lambda: lax.fori_loop(0, chunks, start, 0)), (
+        lambda: lax.fori_loop(0, chunks, wait, 0)
+    )
+
+
+def hold_kernel(count, tiles, held, sems):
+    start, wait = hold_copies(count, tiles, held, sems)
+    start()
+    wait()
+
+
+def plan_kernel(count, row_at, col_at, tiles, held, counts, near, far, sems):
+    start, wait = hold_copies(count, tiles, held, sems)
+    start()
+
+    def place(slot, ends):
+        near_end, far_end = ends
+        col = col_at[slot]
+        entry = slot + row_at[slot] * 256 + col * 65536
+        near[near_end] = entry
+        far[far_end] = entry
+        over = (col >> 4 == 2).astype(jnp.int32)
+        return near_end + 1 - over, far_end + over
+
+    zero = jnp.int32(0)
+    near_end, far_end = lax.fori_loop(0, count[0], place, (zero, zero))
+    for k in range(CHUNK):
+        near[near_end + k] = SPARE
+        far[far_end + k] = SPARE
+    counts[0] = near_end
+    counts[1] = far_end
+    wait()
+
+
+def hold_parameters(tiles):
+    return dict(
         scratch_shapes=[pltpu.SemaphoreType.DMA((tiles.shape[0] // CHUNK,))],
-        compiler_params=limits(27),
+        compiler_params=limits(22),
         cost_estimate=pl.CostEstimate(
             flops=0, bytes_accessed=2 * tiles.size * tiles.dtype.itemsize, transcendentals=0
         ),
+    )
+
+
+def scalars(count):
+    return [pl.BlockSpec(memory_space=pltpu.SMEM)] * count
+
+
+def anywhere(count):
+    return [pl.BlockSpec(memory_space=pl.ANY)] * count
+
+
+def hold_tiles(count, tiles):
+    return pl.pallas_call(
+        hold_kernel,
+        out_shape=jax.ShapeDtypeStruct(tiles.shape, tiles.dtype),
+        in_specs=scalars(1) + anywhere(1),
+        out_specs=whole(1)[0],
         name="hold_tiles",
+        **hold_parameters(tiles),
     )(count, tiles)
 
 
-def forward_kernel(count, row_at, col_at, tiles, *rest):
-    pieces, (total, away, held, sems) = rest[:-4], rest[-4:]
-    chunks = (count[0] + CHUNK - 1) // CHUNK
+def plan_tiles(count, row_at, col_at, tiles):
+    entries = jax.ShapeDtypeStruct((tiles.shape[0] + CHUNK,), jnp.int32)
+    return pl.pallas_call(
+        plan_kernel,
+        out_shape=(
+            jax.ShapeDtypeStruct(tiles.shape, tiles.dtype),
+            jax.ShapeDtypeStruct((2,), jnp.int32),
+            entries,
+            entries,
+        ),
+        in_specs=scalars(3) + anywhere(1),
+        out_specs=tuple(whole(1) + scalars(3)),
+        name="plan_tiles",
+        **hold_parameters(tiles),
+    )(count, row_at, col_at, tiles)
+
+
+def listed(total, entries, chunk, body):
+    def step(i, _):
+        for k in range(chunk):
+            entry = entries[i * chunk + k]
+            body(entry & 255, (entry >> 8) & 255, entry >> 16)
+        return 0
+
+    lax.fori_loop(0, (total + chunk - 1) // chunk, step, 0)
+
+
+def dot(a, b):
+    return jnp.dot(a, b, preferred_element_type=F32)
+
+
+def product_cost(share):
+    return pl.CostEstimate(
+        flops=int(share * 160 * 2 * SIDE * SIDE * RANK), bytes_accessed=1 << 20, transcendentals=0
+    )
+
+
+def forward_near_kernel(counts, near, tiles, first, left, right, total, held, sems):
+    copies = load_pieces([first, left], held, sems)
+    last = pltpu.make_async_copy(right, held.at[pl.ds(48, 16)], sems.at[2])
+    last.start()
+    total[...] = jnp.zeros_like(total)
+    for one in copies + [last]:
+        one.wait()
+
+    def body(slot, row, col):
+        total[row] += dot(tiles[slot], held[col])
+
+    listed(counts[0], near, 32, body)
+
+
+def forward_near(counts, near, tiles, pieces):
+    return pl.pallas_call(
+        forward_near_kernel,
+        out_shape=jax.ShapeDtypeStruct((33, SIDE, RANK), F32),
+        in_specs=scalars(2) + whole(1) + anywhere(3),
+        out_specs=whole(1)[0],
+        scratch_shapes=[
+            pltpu.VMEM((65, SIDE, RANK), BF16),
+            pltpu.SemaphoreType.DMA((3,)),
+        ],
+        compiler_params=limits(8),
+        cost_estimate=product_cost(0.75),
+        name="forward_near",
+    )(counts, near, tiles, *pieces)
+
+
+def forward_far_kernel(counts, far, tiles, a, b, before, total, away, held, sems):
+    copies = load_pieces([a, b], held, sems)
+    for one in copies:
+        one.wait()
+
+    def body(slot, row, col):
+        total[row] += dot(tiles[slot], held[jnp.minimum(col - 32, 16)])
+
+    listed(counts[1], far, 16, body)
+    away[...] = total[pl.ds(16, 16)]
+
+
+def forward_far(counts, far, tiles, pieces, before):
+    return pl.pallas_call(
+        forward_far_kernel,
+        out_shape=(
+            jax.ShapeDtypeStruct((33, SIDE, RANK), F32),
+            jax.ShapeDtypeStruct((16, SIDE, RANK), F32),
+        ),
+        in_specs=scalars(2) + whole(1) + anywhere(2) + whole(1),
+        out_specs=tuple(whole(2)),
+        scratch_shapes=[
+            pltpu.VMEM((17, SIDE, RANK), BF16),
+            pltpu.SemaphoreType.DMA((2,)),
+        ],
+        input_output_aliases={5: 0},
+        compiler_params=limits(4),
+        name="forward_far",
+    )(counts, far, tiles, *pieces, before)
+
+
+def backward_far_kernel(counts, far, tiles, *rest):
+    pieces, (a, b, held, total, sems) = rest[:8], rest[8:]
     copies = load_pieces(pieces, held, sems)
     total[...] = jnp.zeros_like(total)
     for one in copies:
         one.wait()
 
-    def body(i, _):
-        for k in range(CHUNK):
-            slot = i * CHUNK + k
-            total[row_at[slot]] += jnp.dot(
-                tiles[slot], held[col_at[slot]], preferred_element_type=F32
-            )
-        return 0
-
-    lax.fori_loop(0, chunks, body, 0)
-    away[...] = total[pl.ds(16, 16)]
-
-
-def forward(count, row_at, col_at, tiles, pieces):
-    any_spec = pl.BlockSpec(memory_space=pl.ANY)
-    return pl.pallas_call(
-        forward_kernel,
-        out_shape=(
-            jax.ShapeDtypeStruct((33, SIDE, RANK), F32),
-            jax.ShapeDtypeStruct((16, SIDE, RANK), F32),
-        ),
-        in_specs=[pl.BlockSpec(memory_space=pltpu.SMEM)] * 3
-        + whole(1)
-        + [any_spec] * len(pieces),
+    def body(slot, row, col):
+        total[jnp.minimum(col - 32, 16)] += dot(held[row], tiles[slot])
+
+    listed(counts[1], far, 16, body)
+    a[...] = total[pl.ds(0, 8)].astype(BF16)
+    b[...] = total[pl.ds(8, 8)].astype(BF16)
+
+
+def backward_far(counts, far, tiles, pieces):
+    part = jax.ShapeDtypeStruct((8, RANK, SIDE), BF16)
+    return pl.pallas_call(
+        backward_far_kernel,
+        out_shape=(part, part),
+        in_specs=scalars(2) + whole(1) + anywhere(8),
         out_specs=tuple(whole(2)),
         scratch_shapes=[
-            pltpu.VMEM((64, SIDE, RANK), BF16),
-            pltpu.SemaphoreType.DMA((len(pieces),)),
+            pltpu.VMEM((33, RANK, SIDE), BF16),
+            pltpu.VMEM((17, RANK, SIDE), F32),
+            pltpu.SemaphoreType.DMA((8,)),
         ],
         compiler_params=limits(8),
-        name="forward",
-    )(count, row_at, col_at, tiles, *pieces)
-
-
-def backward_kernel(count, row_at, col_at, tiles, *rest):
-    pieces, (total, *aways, held, sems) = rest[:8], rest[8:]
-    chunks = (count[0] + CHUNK - 1) // CHUNK
+        name="backward_far",
+    )(counts, far, tiles, *pieces)
+
+
+def backward_near_kernel(counts, near, tiles, *rest):
+    pieces, (total, held, sems) = rest[:8], rest[8:]
     copies = load_pieces(pieces, held, sems)
     total[...] = jnp.zeros_like(total)
     for one in copies:
         one.wait()
 
-    def body(i, _):
-        for k in range(CHUNK):
-            slot = i * CHUNK + k
-            total[col_at[slot]] += jnp.dot(
-                held[row_at[slot]], tiles[slot], preferred_element_type=F32
-            )
-        return 0
-
-    lax.fori_loop(0, chunks, body, 0)
-    for half in range(2):
-        aways[half][...] = total[pl.ds(32 + 8 * half, 8)].astype(BF16)
-
-
-def backward(count, row_at, col_at, tiles, pieces):
-    any_spec = pl.BlockSpec(memory_space=pl.ANY)
-    part = jax.ShapeDtypeStruct((8, RANK, SIDE), BF16)
-    total, *aways = pl.pallas_call(
-        backward_kernel,
-        out_shape=(jax.ShapeDtypeStruct((65, RANK, SIDE), F32),) + (part,) * 2,
-        in_specs=[pl.BlockSpec(memory_space=pltpu.SMEM)] * 3 + whole(1) + [any_spec] * 8,
-        out_specs=tuple(whole(3)),
+    def body(slot, row, col):
+        total[col] += dot(held[row], tiles[slot])
+
+    listed(counts[0], near, 32, body)
+
+
+def backward_near(counts, near, tiles, pieces):
+    return pl.pallas_call(
+        backward_near_kernel,
+        out_shape=jax.ShapeDtypeStruct((65, RANK, SIDE), F32),
+        in_specs=scalars(2) + whole(1) + anywhere(8),
+        out_specs=whole(1)[0],
         scratch_shapes=[
-            pltpu.VMEM((32, RANK, SIDE), BF16),
+            pltpu.VMEM((33, RANK, SIDE), BF16),
             pltpu.SemaphoreType.DMA((8,)),
         ],
         compiler_params=limits(6),
-        name="backward",
-    )(count, row_at, col_at, tiles, *pieces)
-    return total, aways
+        cost_estimate=product_cost(0.75),
+        name="backward_near",
+    )(counts, near, tiles, *pieces)
 
 
 def core_sum_kernel(keep, came, kept, *outs):
@@ -367,8 +491,6 @@
 
 def shards(basis_in, tiles, tile_coords, tile_count):
     x, y, z, core = (lax.axis_index(name) for name in AXES)
-    slots = tiles.shape[0]
-    used = jnp.arange(slots, dtype=jnp.int32) < tile_count[0]
     local_row = tile_coords[:, 0] - (x * 4 + y) * 32
     dz = (local_row // 8 - z) % 4
     dc = (local_row // 4 - core) % 2
@@ -384,15 +506,15 @@
 
     with jax.named_scope("gather_basis"):
         near = [basis_in] + [cross(basis_in, near_axes, -d) for d in (1, 2, 3)]
-        near, first_tiles = lax.optimization_barrier((near, tiles))
+        near, first_tiles, row_at, col_at = lax.optimization_barrier((near, tiles, row_at, col_at))
         first = jnp.concatenate(near, axis=0).reshape(16, SIDE, RANK)
         right, left = cross(first, far_axes, 1), cross(first, far_axes, -1)
-        held = hold_tiles(tile_count, first_tiles)
+        held, counts, near_list, far_list = plan_tiles(tile_count, row_at, col_at, first_tiles)
         right, left, held = lax.optimization_barrier((right, left, held))
         over = (cross(right[:8], far_axes, 1), cross(left[8:], far_axes, -1))
-        pieces = [first, left, *over, right]
-
-    keep, away = forward(tile_count, jnp.where(used, row_at, 32), col_at, held, pieces)
+
+    keep = forward_near(counts, near_list, held, (first, left, right))
+    keep, away = forward_far(counts, far_list, held, over, keep)
 
     with jax.named_scope("reduce_inner"):
         came = send(away, "core", 1)
@@ -407,12 +529,11 @@
         mine = [inner] + [send(inner, "z", -d) for d in (1, 2, 3)]
         theirs = [send(one, "core", 1) for one in mine]
 
-    total, aways = backward(
-        tile_count, row_at, jnp.where(used, col_at, 64), held, mine + theirs
-    )
+    aways = backward_far(counts, far_list, held, mine + theirs)
 
     with jax.named_scope("reduce_outer"):
         came = (cross(aways[0], far_axes, 1), cross(aways[1], far_axes, -1))
+        total = backward_near(counts, near_list, held, mine + theirs)
         right, left = relay_sum(total, came)
         came = (cross(right, far_axes, 1), cross(left, far_axes, -1))
         keep, aways = middle_sum(total, came)

time: 180 us -> 163 us (0.906)
  starting transfers between devices: 59.1 us -> 41.3 us
  Pallas kernels: 23.1 us -> 40.6 us
  local copies, waits for them, and re-layouts: 15.6 us -> 0.07 us
  waiting for transfers between devices: 80.2 us -> 76.9 us
    pallas_call x2 -> x5, Pallas kernels: 8.15 us -> 25.7 us  [the longest x1 8.3 us: plan_tiles(): pl.pallas_call(plan_kernel, out_shape=(jax.ShapeDtypeStruct(tiles.shape,...]
    unnamed x6 -> x0, local copies, waits for them, and re-layouts: 13.9 us -> none
    ppermute x21, starting transfers between devices: 33.6 us -> 20.6 us  [send(): lax.ppermute(array, axis, [(i, (i + step) % size) for i in range(size)])]
    ppermute x14, waiting for transfers between devices: 43.6 us -> 37.4 us  [cross(): return lax.ppermute(array, AXES, pairs)]
    ppermute x14, starting transfers between devices: 25.5 us -> 20.7 us  [cross(): return lax.ppermute(array, AXES, pairs)]
    ppermute x21, waiting for transfers between devices: 36.6 us -> 39.5 us  [send(): lax.ppermute(array, axis, [(i, (i + step) % size) for i in range(size)])]
    pallas_call x2 -> x1, Pallas kernels: 7.03 us -> 7.09 us  [hold_tiles(): pl.pallas_call(hold_kernel, out_shape=jax.ShapeDtypeStruct(tiles.shape, t...]
  transfers between devices with their start and end apart: 35 -> 35, of which waited for: 25 -> 26; matrix products, arithmetic and copies ran while one was open for 0% -> 0% of each run, Pallas kernels for 4% -> 17%
where the time goes in v6:
time: 163 us
  waiting for transfers between devices  76.9 us (47%)
  starting transfers between devices  41.3 us (25%)
  Pallas kernels  40.6 us (25%)
  other arithmetic  2.09 us (1%)
    ppermute x21, waiting for transfers between devices, send(): lax.ppermute(array, axis, [(i, (i + step) % size) for i in range(size)])  39.5 us
    ppermute x14, waiting for transfers between devices, cross(): return lax.ppermute(array, AXES, pairs)  37.4 us
    ppermute x14, starting transfers between devices, cross(): return lax.ppermute(array, AXES, pairs)  20.7 us
    ppermute x21, starting transfers between devices, send(): lax.ppermute(array, axis, [(i, (i + step) % size) for i in range(size)])  20.6 us
    pallas_call x1, Pallas kernels, plan_tiles(): pl.pallas_call(plan_kernel, out_shape=(jax.ShapeDtypeStruct(tiles.shape,...  8.3 us
    pallas_call x1, Pallas kernels, hold_tiles(): pl.pallas_call(hold_kernel, out_shape=jax.ShapeDtypeStruct(tiles.shape, t...  7.09 us
    pallas_call x1, Pallas kernels, forward_near(): pl.pallas_call(forward_near_kernel, out_shape=jax.ShapeDtypeStruct((33, S...  6.34 us
    pallas_call x1, Pallas kernels, finish(): pl.pallas_call(kernel, out_shape=(jax.ShapeDtypeStruct((4 * SIDE, RANK),...  5.91 us
  transfers between devices with their start and end apart: 35, of which 26 were waited for; matrix products, arithmetic and copies ran while one was open for 0% of the time, Pallas kernels for 17%

profile of v6, /device:TPU:0, one launch (start us, length us, event | category | flops | bytes accessed | tf_op | source)
XLA Modules:
  0.0 162.5 jit_solution(14335156905631925616)
XLA Ops:
  0.6 3.2 %collective-permute-start.1 = (bf16[1024,128]{1,0:T(8,128)(2,1)}, bf16[1024,128]{1,0:T(8,128)(2,1)S(1)}, u32[]{:S(2)}, u32[]{:S(2)}) collective-permute-start(bf16[1024,128]{1,0:T(8,128)(2,1)} %param.4), channel_id=1, source_target_pairs={{0,64},{1,17},{2,66},{3,19},{4,68},{5,21},{6,70},{7,23},{8,72},{9,... | collective-permute-start | bytes 786440 | tf_op jit(solution)/shard_map/gather_basis/ppermute | solution.py:34
  3.8 1.1 collective-permute-start
  5.0 0.9 collective-permute-start.2
  5.8 0.8 fusion.10
  6.6 2.2 %collective-permute-done.1 = bf16[1024,128]{1,0:T(8,128)(2,1)S(1)} collective-permute-done((bf16[1024,128]{1,0:T(8,128)(2,1)}, bf16[1024,128]{1,0:T(8,128)(2,1)S(1)}, u32[]{:S(2)}, u32[]{:S(2)}) %collective-permute-start.1) | collective-permute-done | bytes 262176 | tf_op jit(solution)/shard_map/gather_basis/ppermute | solution.py:34
  8.8 3.0 %collective-permute-done = bf16[1024,128]{1,0:T(8,128)(2,1)S(1)} collective-permute-done((bf16[1024,128]{1,0:T(8,128)(2,1)}, bf16[1024,128]{1,0:T(8,128)(2,1)S(1)}, u32[]{:S(2)}, u32[]{:S(2)}) %collective-permute-start) | collective-permute-done | bytes 262176 | tf_op jit(solution)/shard_map/gather_basis/ppermute | solution.py:34
  11.8 1.0 collective-permute-done.2
  12.8 1.0 pad_maximum_fusion
  13.8 3.1 %collective-permute-start.4 = (bf16[16,256,128]{2,1,0:T(8,128)(2,1)S(1)}, bf16[16,256,128]{2,1,0:T(8,128)(2,1)S(1)}, u32[]{:S(2)}, u32[]{:S(2)}) collective-permute-start(bf16[16,256,128]{2,1,0:T(8,128)(2,1)S(1)} %bitcast.3), channel_id=1, source_target_pairs={{0,24},{1,97},{2,26},{3,99},{4,28},{5,101},{6,30},{7,103},{8,0},{9... | collective-permute-start | bytes 3145736 | tf_op jit(solution)/shard_map/gather_basis/ppermute | solution.py:34
  17.5 8.3 %plan_tiles.1 = (bf16[160,256,256]{2,1,0:T(8,128)(2,1)S(1)}, s32[2]{0:T(128)S(1)}, s32[192]{0:T(256)S(1)}, s32[192]{0:T(256)S(1)}) custom-call(s32[1]{0:T(128)S(6)} %copy.8.count, s32[160]{0:T(256)S(1)} %get-tuple-element.40.row_at, s32[160]{0:T(256)S(1)} %get-tuple-element.41.col_at, bf16[160,256,256]{2,1,0:T(8,128)(2,1)} %tiles.1), custom_call_target="tpu_custom_call" | custom-call | bytes 41943040 | tf_op jit(solution)/shard_map/gather_basis/plan_tiles/pallas_call | solution.py:144
  25.8 3.4 %collective-permute-done.4.left = bf16[16,256,128]{2,1,0:T(8,128)(2,1)S(1)} collective-permute-done((bf16[16,256,128]{2,1,0:T(8,128)(2,1)S(1)}, bf16[16,256,128]{2,1,0:T(8,128)(2,1)S(1)}, u32[]{:S(2)}, u32[]{:S(2)}) %collective-permute-start.4) | collective-permute-done | bytes 1048608 | tf_op jit(solution)/shard_map/gather_basis/ppermute | solution.py:34
  29.2 3.7 %collective-permute-done.3.right = bf16[16,256,128]{2,1,0:T(8,128)(2,1)S(1)} collective-permute-done((bf16[16,256,128]{2,1,0:T(8,128)(2,1)S(1)}, bf16[16,256,128]{2,1,0:T(8,128)(2,1)S(1)}, u32[]{:S(2)}, u32[]{:S(2)}) %collective-permute-start.3) | collective-permute-done | bytes 1048608 | tf_op jit(solution)/shard_map/gather_basis/ppermute | solution.py:34
  33.0 2.0 %collective-permute-start.5 = (bf16[8,256,128]{2,1,0:T(8,128)(2,1)S(1)}, bf16[8,256,128]{2,1,0:T(8,128)(2,1)S(1)}, u32[]{:S(2)}, u32[]{:S(2)}) collective-permute-start(bf16[8,256,128]{2,1,0:T(8,128)(2,1)S(1)} %slice.15), channel_id=1, source_target_pairs={{0,8},{1,33},{2,10},{3,35},{4,12},{5,37},{6,14},{7,39},{8,16},{9,4... | collective-permute-start | bytes 1572872 | tf_op jit(solution)/shard_map/gather_basis/ppermute | solution.py:34
  35.0 6.3 %forward_near.1.before = f32[33,256,128]{2,1,0:T(8,128)S(1)} custom-call(s32[2]{0:T(128)S(1)} %get-tuple-element.43.counts, s32[192]{0:T(256)S(1)} %get-tuple-element.44.near, bf16[160,256,256]{2,1,0:T(8,128)(2,1)S(1)} %get-tuple-element.51.tiles, bf16[16,256,128]{2,1,0:T(8,128)(2,1)S(1)} %bitcast.5, bf16[16,256,128]{2,1,0:T(8,128)(2,1)S(1)} %collective-permute-done.4.left, ...), custom_call_target="tpu_custom_call" | custom-call | flops 2013265920 | bytes 1048576 | tf_op jit(solution)/shard_map/forward_near/pallas_call | solution.py:194
  41.4 0.8 collective-permute-done.6.b
  42.2 1.3 collective-permute-done.5.a
  43.5 3.0 %forward_far.1 = (f32[33,256,128]{2,1,0:T(8,128)S(1)}, f32[16,256,128]{2,1,0:T(8,128)S(1)}) custom-call(s32[2]{0:T(128)S(1)} %get-tuple-element.43.counts, s32[192]{0:T(256)S(1)} %get-tuple-element.45.far, bf16[160,256,256]{2,1,0:T(8,128)(2,1)S(1)} %get-tuple-element.51.tiles, ...), custom_call_target="tpu_custom_call", output_to_operand_aliasing={{0}: (5, {})} | custom-call | tf_op jit(solution)/shard_map/forward_far/pallas_call | solution.py:222
  46.5 0.1 collective-permute-start.7
  46.6 4.1 %collective-permute-done.7.came = f32[16,256,128]{2,1,0:T(8,128)S(1)} collective-permute-done((f32[16,256,128]{2,1,0:T(8,128)S(1)}, f32[16,256,128]{2,1,0:T(8,128)S(1)}, u32[]{:S(2)}, u32[]{:S(2)}) %collective-permute-start.7) | collective-permute-done | bytes 2097184 | tf_op jit(solution)/shard_map/reduce_inner/ppermute | solution.py:23
  50.8 0.5 core_sum.1
  51.4 2.6 %collective-permute-start.10 = (f16[1040,128]{1,0:T(8,128)(2,1)S(1)}, f16[1040,128]{1,0:T(8,128)(2,1)S(1)}, u32[]{:S(2)}, u32[]{:S(2)}) collective-permute-start(f16[1040,128]{1,0:T(8,128)(2,1)S(1)} %convert_element_type.20), channel_id=1, source_target_pairs={{0,6},{2,0},{4,2},{6,4},{1,7},{3,1},{5,3},{7,5},{8,14},{10,8},{12,... | collective-permute-start | bytes 798728 | tf_op jit(solution)/shard_map/reduce_inner/ppermute | solution.py:23
  54.0 1.3 collective-permute-start.8
  55.3 7.1 %hold_tiles.1.tiles = bf16[160,256,256]{2,1,0:T(8,128)(2,1)S(1)} custom-call(s32[1]{0:T(128)S(6)} %copy.8.count, bf16[160,256,256]{2,1,0:T(8,128)(2,1)} %tiles.1), custom_call_target="tpu_custom_call" | custom-call | bytes 41943040 | tf_op jit(solution)/shard_map/reduce_inner/hold_tiles/pallas_call | solution.py:132
  62.4 3.3 %collective-permute-done.10 = f16[1040,128]{1,0:T(8,128)(2,1)S(1)} collective-permute-done((f16[1040,128]{1,0:T(8,128)(2,1)S(1)}, f16[1040,128]{1,0:T(8,128)(2,1)S(1)}, u32[]{:S(2)}, u32[]{:S(2)}) %collective-permute-start.10) | collective-permute-done | bytes 266272 | tf_op jit(solution)/shard_map/reduce_inner/ppermute | solution.py:23
  65.7 3.4 %collective-permute-done.8 = f16[1040,128]{1,0:T(8,128)(2,1)S(1)} collective-permute-done((f16[1040,128]{1,0:T(8,128)(2,1)S(1)}, f16[1040,128]{1,0:T(8,128)(2,1)S(1)}, u32[]{:S(2)}, u32[]{:S(2)}) %collective-permute-start.8) | collective-permute-done | bytes 266272 | tf_op jit(solution)/shard_map/reduce_inner/ppermute | solution.py:23
  69.2 0.2 inner_sum.1.rest_0_
  69.5 2.3 %collective-permute-start.12 = (bf16[4,128,256]{2,1,0:T(8,128)(2,1)S(1)}, bf16[4,128,256]{2,1,0:T(8,128)(2,1)S(1)}, u32[]{:S(2)}, u32[]{:S(2)}) collective-permute-start(bf16[4,128,256]{2,1,0:T(8,128)(2,1)S(1)} %inner_sum.1.rest_0_), channel_id=1, source_target_pairs={{0,4},{2,6},{4,0},{6,2},{1,5},{3,7},{5,1},{7,3},{8,12},{10,14},{12... | collective-permute-start | bytes 786440 | tf_op jit(solution)/shard_map/gather_inner/ppermute | solution.py:23
  71.9 0.9 collective-permute-start.11
  72.8 11.5 %collective-permute-done.13.rest_3_ = bf16[4,128,256]{2,1,0:T(8,128)(2,1)S(1)} collective-permute-done((bf16[4,128,256]{2,1,0:T(8,128)(2,1)S(1)}, bf16[4,128,256]{2,1,0:T(8,128)(2,1)S(1)}, u32[]{:S(2)}, u32[]{:S(2)}) %collective-permute-start.13) | collective-permute-done | bytes 262176 | tf_op jit(solution)/shard_map/gather_inner/ppermute | solution.py:23
  84.3 0.5 collective-permute-start.16
  84.8 0.1 collective-permute-done.11.rest_1_
  84.9 0.9 collective-permute-done.17.rest_7_
  85.8 0.4 collective-permute-done.16.rest_6_
  86.2 0.4 collective-permute-done.15.rest_5_
  86.6 2.6 %backward_far.1 = (bf16[8,128,256]{2,1,0:T(8,128)(2,1)S(1)}, bf16[8,128,256]{2,1,0:T(8,128)(2,1)S(1)}) custom-call(s32[2]{0:T(128)S(1)} %get-tuple-element.43.counts, s32[192]{0:T(256)S(1)} %get-tuple-element.45.far, bf16[160,256,256]{2,1,0:T(8,128)(2,1)S(1)} %hold_tiles.1.tiles, bf16[4,128,256]{2,1,0:T(8,128)(2,1)S(1)} %inner_sum.1.rest_0_, ...), custom_call_target="tpu_custom_call" | custom-call | tf_op jit(solution)/shard_map/backward_far/pallas_call | solution.py:257
  89.2 0.5 collective-permute-start.18
  89.7 2.8 %collective-permute-start.19 = (bf16[8,128,256]{2,1,0:T(8,128)(2,1)S(1)}, bf16[8,128,256]{2,1,0:T(8,128)(2,1)S(1)}, u32[]{:S(2)}, u32[]{:S(2)}) collective-permute-start(bf16[8,128,256]{2,1,0:T(8,128)(2,1)S(1)} %get-tuple-element.69), channel_id=1, source_target_pairs={{0,24},{1,97},{2,26},{3,99},{4,28},{5,101},{6,30},{7,103},{8,0},{9... | collective-permute-start | bytes 1572872 | tf_op jit(solution)/shard_map/reduce_outer/ppermute | solution.py:34
  92.5 5.4 %backward_near.1.total = f32[65,128,256]{2,1,0:T(8,128)S(1)} custom-call(s32[2]{0:T(128)S(1)} %get-tuple-element.43.counts, s32[192]{0:T(256)S(1)} %get-tuple-element.44.near, bf16[160,256,256]{2,1,0:T(8,128)(2,1)S(1)} %hold_tiles.1.tiles, bf16[4,128,256]{2,1,0:T(8,128)(2,1)S(1)} %inner_sum.1.rest_0_, ...), custom_call_target="tpu_custom_call" | custom-call | flops 2013265920 | bytes 1048576 | tf_op jit(solution)/shard_map/reduce_outer/backward_near/pallas_call | solution.py:286
  97.9 1.7 %collective-permute-done.18.a = bf16[8,128,256]{2,1,0:T(8,128)(2,1)S(1)} collective-permute-done((bf16[8,128,256]{2,1,0:T(8,128)(2,1)S(1)}, bf16[8,128,256]{2,1,0:T(8,128)(2,1)S(1)}, u32[]{:S(2)}, u32[]{:S(2)}) %collective-permute-start.18) | collective-permute-done | bytes 524320 | tf_op jit(solution)/shard_map/reduce_outer/ppermute | solution.py:34
  99.7 0.3 relay_sum.1
  100.0 3.3 %collective-permute-start.21 = (bf16[16,128,256]{2,1,0:T(8,128)(2,1)S(1)}, bf16[16,128,256]{2,1,0:T(8,128)(2,1)S(1)}, u32[]{:S(2)}, u32[]{:S(2)}) collective-permute-start(bf16[16,128,256]{2,1,0:T(8,128)(2,1)S(1)} %get-tuple-element.71), channel_id=1, source_target_pairs={{0,24},{1,97},{2,26},{3,99},{4,28},{5,101},{6,30},{7,103},{8,0},{9... | collective-permute-start | bytes 3145736 | tf_op jit(solution)/shard_map/reduce_outer/ppermute | solution.py:34
  103.3 12.7 %collective-permute-done.20.a = bf16[16,128,256]{2,1,0:T(8,128)(2,1)S(1)} collective-permute-done((bf16[16,128,256]{2,1,0:T(8,128)(2,1)S(1)}, bf16[16,128,256]{2,1,0:T(8,128)(2,1)S(1)}, u32[]{:S(2)}, u32[]{:S(2)}) %collective-permute-start.20) | collective-permute-done | bytes 1048608 | tf_op jit(solution)/shard_map/reduce_outer/ppermute | solution.py:34
  116.0 0.3 middle_sum.1
  116.4 2.6 %collective-permute-start.23 = (bf16[4,128,256]{2,1,0:T(8,128)(2,1)S(1)}, bf16[4,128,256]{2,1,0:T(8,128)(2,1)S(1)}, u32[]{:S(2)}, u32[]{:S(2)}) collective-permute-start(bf16[4,128,256]{2,1,0:T(8,128)(2,1)S(1)} %get-tuple-element.74), channel_id=1, source_target_pairs={{0,64},{1,17},{2,66},{3,19},{4,68},{5,21},{6,70},{7,23},{8,72},{9,... | collective-permute-start | bytes 786440 | tf_op jit(solution)/shard_map/reduce_outer/ppermute | solution.py:34
  119.1 0.9 collective-permute-start.24
  120.0 6.8 %collective-permute-done.22.a = bf16[4,128,256]{2,1,0:T(8,128)(2,1)S(1)} collective-permute-done((bf16[4,128,256]{2,1,0:T(8,128)(2,1)S(1)}, bf16[4,128,256]{2,1,0:T(8,128)(2,1)S(1)}, u32[]{:S(2)}, u32[]{:S(2)}) %collective-permute-start.22) | collective-permute-done | bytes 262176 | tf_op jit(solution)/shard_map/reduce_outer/ppermute | solution.py:34
  126.8 0.9 collective-permute-done.24.c
  127.7 0.6 outer_sum.1
  128.3 0.1 collective-permute-start.25
  128.4 1.2 collective-permute-done.25
  129.7 2.0 %collective-permute-start.28 = (f32[128,128]{1,0:T(8,128)S(1)}, f32[128,128]{1,0:T(8,128)S(1)}, u32[]{:S(2)}, u32[]{:S(2)}) collective-permute-start(f32[128,128]{1,0:T(8,128)S(1)} %add.91), channel_id=1, source_target_pairs={{0,6},{2,0},{4,2},{6,4},{1,7},{3,1},{5,3},{7,5},{8,14},{10,8},{12,... | collective-permute-start | bytes 196616 | tf_op jit(solution)/shard_map/reduce_gram/ppermute | solution.py:23
  131.7 0.1 collective-permute-start.27
  131.8 1.5 collective-permute-start.26
  133.2 0.8 collective-permute-done.28
  134.0 4.2 %collective-permute-done.27 = f32[128,128]{1,0:T(8,128)S(1)} collective-permute-done((f32[128,128]{1,0:T(8,128)S(1)}, f32[128,128]{1,0:T(8,128)S(1)}, u32[]{:S(2)}, u32[]{:S(2)}) %collective-permute-start.27) | collective-permute-done | bytes 65568 | tf_op jit(solution)/shard_map/reduce_gram/ppermute | solution.py:23
  138.2 3.3 %collective-permute-start.31 = (f32[128,128]{1,0:T(8,128)S(1)}, f32[128,128]{1,0:T(8,128)S(1)}, u32[]{:S(2)}, u32[]{:S(2)}) collective-permute-start(f32[128,128]{1,0:T(8,128)S(1)} %add_add_fusion.2), channel_id=1, source_target_pairs={{0,24},{8,0},{16,8},{24,16},{1,25},{9,1},{17,9},{25,17},{2,26},{10... | collective-permute-start | bytes 196616 | tf_op jit(solution)/shard_map/reduce_gram/ppermute | solution.py:23
  141.5 1.7 %collective-permute-start.29 = (f32[128,128]{1,0:T(8,128)S(1)}, f32[128,128]{1,0:T(8,128)S(1)}, u32[]{:S(2)}, u32[]{:S(2)}) collective-permute-start(f32[128,128]{1,0:T(8,128)S(1)} %add_add_fusion.2), channel_id=1, source_target_pairs={{0,16},{8,24},{16,0},{24,8},{1,17},{9,25},{17,1},{25,9},{2,18},{10... | collective-permute-start | bytes 196616 | tf_op jit(solution)/shard_map/reduce_gram/ppermute | solution.py:23
  143.2 0.2 collective-permute-done.31
  143.4 4.3 %collective-permute-done.30 = f32[128,128]{1,0:T(8,128)S(1)} collective-permute-done((f32[128,128]{1,0:T(8,128)S(1)}, f32[128,128]{1,0:T(8,128)S(1)}, u32[]{:S(2)}, u32[]{:S(2)}) %collective-permute-start.30) | collective-permute-done | bytes 65568 | tf_op jit(solution)/shard_map/reduce_gram/ppermute | solution.py:23
  147.7 2.7 %collective-permute-start.34 = (f32[128,128]{1,0:T(8,128)S(1)}, f32[128,128]{1,0:T(8,128)S(1)}, u32[]{:S(2)}, u32[]{:S(2)}) collective-permute-start(f32[128,128]{1,0:T(8,128)S(1)} %add_add_fusion.1), channel_id=1, source_target_pairs={{0,96},{32,0},{64,32},{96,64},{1,97},{33,1},{65,33},{97,65},{2,98}... | collective-permute-start | bytes 196616 | tf_op jit(solution)/shard_map/reduce_gram/ppermute | solution.py:23
  150.4 1.5 collective-permute-start.32
  151.9 1.0 collective-permute-done.34
  152.9 3.7 %collective-permute-done.33 = f32[128,128]{1,0:T(8,128)S(1)} collective-permute-done((f32[128,128]{1,0:T(8,128)S(1)}, f32[128,128]{1,0:T(8,128)S(1)}, u32[]{:S(2)}, u32[]{:S(2)}) %collective-permute-start.33) | collective-permute-done | bytes 65568 | tf_op jit(solution)/shard_map/reduce_gram/ppermute | solution.py:23
  156.6 5.9 %finish.1 = (f32[1024,128]{1,0:T(8,128)}, f32[128,128]{1,0:T(8,128)}) custom-call(f32[128,128]{1,0:T(8,128)S(1)} %add_add_fusion.refs_0_, f32[4,128,256]{2,1,0:T(8,128)S(1)} %get-tuple-element.77.refs_1_), custom_call_target="tpu_custom_call" | custom-call | tf_op jit(solution)/shard_map/finish/pallas_call | solution.py:478
  (33 shorter events, 0.7 us)
Async XLA Ops:
  0.6 8.2 %collective-permute-start.1 = (bf16[1024,128]{1,0:T(8,128)(2,1)}, bf16[1024,128]{1,0:T(8,128)(2,1)S(1)}, u32[]{:S(2)}, u32[]{:S(2)}) collective-permute-start(bf16[1024,128]{1,0:T(8,128)(2,1)} %param.4), channel_id=1, source_target_pairs={{0,64},{1,17},{2,66},{3,19},{4,68},{5,21},{6,70},{7,23},{8,72},{9,... | collective-permute-start | bytes 786440 | tf_op jit(solution)/shard_map/gather_basis/ppermute | solution.py:34
  3.8 8.0 %collective-permute-start = (bf16[1024,128]{1,0:T(8,128)(2,1)}, bf16[1024,128]{1,0:T(8,128)(2,1)S(1)}, u32[]{:S(2)}, u32[]{:S(2)}) collective-permute-start(bf16[1024,128]{1,0:T(8,128)(2,1)} %param.4), channel_id=1, source_target_pairs={{0,96},{1,25},{2,98},{3,27},{4,100},{5,29},{6,102},{7,31},{8,104},... | collective-permute-start | bytes 786440 | tf_op jit(solution)/shard_map/gather_basis/ppermute | solution.py:34
  5.0 7.8 %collective-permute-start.2 = (bf16[1024,128]{1,0:T(8,128)(2,1)}, bf16[1024,128]{1,0:T(8,128)(2,1)S(1)}, u32[]{:S(2)}, u32[]{:S(2)}) collective-permute-start(bf16[1024,128]{1,0:T(8,128)(2,1)} %param.4), channel_id=1, source_target_pairs={{0,32},{1,9},{2,34},{3,11},{4,36},{5,13},{6,38},{7,15},{8,40},{9,1... | collective-permute-start | bytes 786440 | tf_op jit(solution)/shard_map/gather_basis/ppermute | solution.py:34
  13.8 15.4 %collective-permute-start.4 = (bf16[16,256,128]{2,1,0:T(8,128)(2,1)S(1)}, bf16[16,256,128]{2,1,0:T(8,128)(2,1)S(1)}, u32[]{:S(2)}, u32[]{:S(2)}) collective-permute-start(bf16[16,256,128]{2,1,0:T(8,128)(2,1)S(1)} %bitcast.3), channel_id=1, source_target_pairs={{0,24},{1,97},{2,26},{3,99},{4,28},{5,101},{6,30},{7,103},{8,0},{9... | collective-permute-start | bytes 3145736 | tf_op jit(solution)/shard_map/gather_basis/ppermute | solution.py:34
  16.9 16.0 %collective-permute-start.3 = (bf16[16,256,128]{2,1,0:T(8,128)(2,1)S(1)}, bf16[16,256,128]{2,1,0:T(8,128)(2,1)S(1)}, u32[]{:S(2)}, u32[]{:S(2)}) collective-permute-start(bf16[16,256,128]{2,1,0:T(8,128)(2,1)S(1)} %bitcast.4), channel_id=1, source_target_pairs={{0,8},{1,33},{2,10},{3,35},{4,12},{5,37},{6,14},{7,39},{8,16},{9,4... | collective-permute-start | bytes 3145736 | tf_op jit(solution)/shard_map/gather_basis/ppermute | solution.py:34
  32.9 9.2 %collective-permute-start.6 = (bf16[8,256,128]{2,1,0:T(8,128)(2,1)S(1)}, bf16[8,256,128]{2,1,0:T(8,128)(2,1)S(1)}, u32[]{:S(2)}, u32[]{:S(2)}) collective-permute-start(bf16[8,256,128]{2,1,0:T(8,128)(2,1)S(1)} %slice.16), channel_id=1, source_target_pairs={{0,24},{1,97},{2,26},{3,99},{4,28},{5,101},{6,30},{7,103},{8,0},{9... | collective-permute-start | bytes 1572872 | tf_op jit(solution)/shard_map/gather_basis/ppermute | solution.py:34
  33.0 10.5 %collective-permute-start.5 = (bf16[8,256,128]{2,1,0:T(8,128)(2,1)S(1)}, bf16[8,256,128]{2,1,0:T(8,128)(2,1)S(1)}, u32[]{:S(2)}, u32[]{:S(2)}) collective-permute-start(bf16[8,256,128]{2,1,0:T(8,128)(2,1)S(1)} %slice.15), channel_id=1, source_target_pairs={{0,8},{1,33},{2,10},{3,35},{4,12},{5,37},{6,14},{7,39},{8,16},{9,4... | collective-permute-start | bytes 1572872 | tf_op jit(solution)/shard_map/gather_basis/ppermute | solution.py:34
  46.5 4.2 %collective-permute-start.7 = (f32[16,256,128]{2,1,0:T(8,128)S(1)}, f32[16,256,128]{2,1,0:T(8,128)S(1)}, u32[]{:S(2)}, u32[]{:S(2)}) collective-permute-start(f32[16,256,128]{2,1,0:T(8,128)S(1)} %get-tuple-element.55), channel_id=1, source_target_pairs={{0,1},{1,0},{2,3},{3,2},{4,5},{5,4},{6,7},{7,6},{8,9},{9,8},{10,11... | collective-permute-start | bytes 6291464 | tf_op jit(solution)/shard_map/reduce_inner/ppermute | solution.py:23
  51.4 14.3 %collective-permute-start.10 = (f16[1040,128]{1,0:T(8,128)(2,1)S(1)}, f16[1040,128]{1,0:T(8,128)(2,1)S(1)}, u32[]{:S(2)}, u32[]{:S(2)}) collective-permute-start(f16[1040,128]{1,0:T(8,128)(2,1)S(1)} %convert_element_type.20), channel_id=1, source_target_pairs={{0,6},{2,0},{4,2},{6,4},{1,7},{3,1},{5,3},{7,5},{8,14},{10,8},{12,... | collective-permute-start | bytes 798728 | tf_op jit(solution)/shard_map/reduce_inner/ppermute | solution.py:23
  54.0 11.7 %collective-permute-start.9 = (f16[1040,128]{1,0:T(8,128)(2,1)S(1)}, f16[1040,128]{1,0:T(8,128)(2,1)S(1)}, u32[]{:S(2)}, u32[]{:S(2)}) collective-permute-start(f16[1040,128]{1,0:T(8,128)(2,1)S(1)} %convert_element_type.19), channel_id=1, source_target_pairs={{0,4},{2,6},{4,0},{6,2},{1,5},{3,7},{5,1},{7,3},{8,12},{10,14},{12... | collective-permute-start | bytes 798728 | tf_op jit(solution)/shard_map/reduce_inner/ppermute | solution.py:23
  54.0 15.1 %collective-permute-start.8 = (f16[1040,128]{1,0:T(8,128)(2,1)S(1)}, f16[1040,128]{1,0:T(8,128)(2,1)S(1)}, u32[]{:S(2)}, u32[]{:S(2)}) collective-permute-start(f16[1040,128]{1,0:T(8,128)(2,1)S(1)} %convert_element_type.18), channel_id=1, source_target_pairs={{0,2},{2,4},{4,6},{6,0},{1,3},{3,5},{5,7},{7,1},{8,10},{10,12},{12... | collective-permute-start | bytes 798728 | tf_op jit(solution)/shard_map/reduce_inner/ppermute | solution.py:23
  69.5 14.8 %collective-permute-start.13 = (bf16[4,128,256]{2,1,0:T(8,128)(2,1)S(1)}, bf16[4,128,256]{2,1,0:T(8,128)(2,1)S(1)}, u32[]{:S(2)}, u32[]{:S(2)}) collective-permute-start(bf16[4,128,256]{2,1,0:T(8,128)(2,1)S(1)} %inner_sum.1.rest_0_), channel_id=1, source_target_pairs={{0,2},{2,4},{4,6},{6,0},{1,3},{3,5},{5,7},{7,1},{8,10},{10,12},{12... | collective-permute-start | bytes 786440 | tf_op jit(solution)/shard_map/gather_inner/ppermute | solution.py:23
  69.5 14.7 %collective-permute-start.12 = (bf16[4,128,256]{2,1,0:T(8,128)(2,1)S(1)}, bf16[4,128,256]{2,1,0:T(8,128)(2,1)S(1)}, u32[]{:S(2)}, u32[]{:S(2)}) collective-permute-start(bf16[4,128,256]{2,1,0:T(8,128)(2,1)S(1)} %inner_sum.1.rest_0_), channel_id=1, source_target_pairs={{0,4},{2,6},{4,0},{6,2},{1,5},{3,7},{5,1},{7,3},{8,12},{10,14},{12... | collective-permute-start | bytes 786440 | tf_op jit(solution)/shard_map/gather_inner/ppermute | solution.py:23
  71.9 13.0 %collective-permute-start.11 = (bf16[4,128,256]{2,1,0:T(8,128)(2,1)S(1)}, bf16[4,128,256]{2,1,0:T(8,128)(2,1)S(1)}, u32[]{:S(2)}, u32[]{:S(2)}) collective-permute-start(bf16[4,128,256]{2,1,0:T(8,128)(2,1)S(1)} %inner_sum.1.rest_0_), channel_id=1, source_target_pairs={{0,6},{2,0},{4,2},{6,4},{1,7},{3,1},{5,3},{7,5},{8,14},{10,8},{12,... | collective-permute-start | bytes 786440 | tf_op jit(solution)/shard_map/gather_inner/ppermute | solution.py:23
  72.8 12.1 %collective-permute-start.14 = (bf16[4,128,256]{2,1,0:T(8,128)(2,1)S(1)}, bf16[4,128,256]{2,1,0:T(8,128)(2,1)S(1)}, u32[]{:S(2)}, u32[]{:S(2)}) collective-permute-start(bf16[4,128,256]{2,1,0:T(8,128)(2,1)S(1)} %inner_sum.1.rest_0_), channel_id=1, source_target_pairs={{0,1},{1,0},{2,3},{3,2},{4,5},{5,4},{6,7},{7,6},{8,9},{9,8},{10,11... | collective-permute-start | bytes 786440 | tf_op jit(solution)/shard_map/gather_inner/ppermute | solution.py:23
  84.3 1.5 collective-permute-start.17
  84.3 1.9 %collective-permute-start.16 = (bf16[4,128,256]{2,1,0:T(8,128)(2,1)S(1)}, bf16[4,128,256]{2,1,0:T(8,128)(2,1)S(1)}, u32[]{:S(2)}, u32[]{:S(2)}) collective-permute-start(bf16[4,128,256]{2,1,0:T(8,128)(2,1)S(1)} %collective-permute-done.12.rest_2_), channel_id=1, source_target_pairs={{0,1},{1,0},{2,3},{3,2},{4,5},{5,4},{6,7},{7,6},{8,9},{9,8},{10,11... | collective-permute-start | bytes 786440 | tf_op jit(solution)/shard_map/gather_inner/ppermute | solution.py:23
  84.9 1.7 %collective-permute-start.15 = (bf16[4,128,256]{2,1,0:T(8,128)(2,1)S(1)}, bf16[4,128,256]{2,1,0:T(8,128)(2,1)S(1)}, u32[]{:S(2)}, u32[]{:S(2)}) collective-permute-start(bf16[4,128,256]{2,1,0:T(8,128)(2,1)S(1)} %collective-permute-done.11.rest_1_), channel_id=1, source_target_pairs={{0,1},{1,0},{2,3},{3,2},{4,5},{5,4},{6,7},{7,6},{8,9},{9,8},{10,11... | collective-permute-start | bytes 786440 | tf_op jit(solution)/shard_map/gather_inner/ppermute | solution.py:23
  89.2 10.5 %collective-permute-start.18 = (bf16[8,128,256]{2,1,0:T(8,128)(2,1)S(1)}, bf16[8,128,256]{2,1,0:T(8,128)(2,1)S(1)}, u32[]{:S(2)}, u32[]{:S(2)}) collective-permute-start(bf16[8,128,256]{2,1,0:T(8,128)(2,1)S(1)} %get-tuple-element.68), channel_id=1, source_target_pairs={{0,8},{1,33},{2,10},{3,35},{4,12},{5,37},{6,14},{7,39},{8,16},{9,4... | collective-permute-start | bytes 1572872 | tf_op jit(solution)/shard_map/reduce_outer/ppermute | solution.py:34
  89.7 10.0 %collective-permute-start.19 = (bf16[8,128,256]{2,1,0:T(8,128)(2,1)S(1)}, bf16[8,128,256]{2,1,0:T(8,128)(2,1)S(1)}, u32[]{:S(2)}, u32[]{:S(2)}) collective-permute-start(bf16[8,128,256]{2,1,0:T(8,128)(2,1)S(1)} %get-tuple-element.69), channel_id=1, source_target_pairs={{0,24},{1,97},{2,26},{3,99},{4,28},{5,101},{6,30},{7,103},{8,0},{9... | collective-permute-start | bytes 1572872 | tf_op jit(solution)/shard_map/reduce_outer/ppermute | solution.py:34
  99.9 16.1 %collective-permute-start.20 = (bf16[16,128,256]{2,1,0:T(8,128)(2,1)S(1)}, bf16[16,128,256]{2,1,0:T(8,128)(2,1)S(1)}, u32[]{:S(2)}, u32[]{:S(2)}) collective-permute-start(bf16[16,128,256]{2,1,0:T(8,128)(2,1)S(1)} %get-tuple-element.70), channel_id=1, source_target_pairs={{0,8},{1,33},{2,10},{3,35},{4,12},{5,37},{6,14},{7,39},{8,16},{9,4... | collective-permute-start | bytes 3145736 | tf_op jit(solution)/shard_map/reduce_outer/ppermute | solution.py:34
  100.0 16.0 %collective-permute-start.21 = (bf16[16,128,256]{2,1,0:T(8,128)(2,1)S(1)}, bf16[16,128,256]{2,1,0:T(8,128)(2,1)S(1)}, u32[]{:S(2)}, u32[]{:S(2)}) collective-permute-start(bf16[16,128,256]{2,1,0:T(8,128)(2,1)S(1)} %get-tuple-element.71), channel_id=1, source_target_pairs={{0,24},{1,97},{2,26},{3,99},{4,28},{5,101},{6,30},{7,103},{8,0},{9... | collective-permute-start | bytes 3145736 | tf_op jit(solution)/shard_map/reduce_outer/ppermute | solution.py:34
  116.3 10.5 %collective-permute-start.22 = (bf16[4,128,256]{2,1,0:T(8,128)(2,1)S(1)}, bf16[4,128,256]{2,1,0:T(8,128)(2,1)S(1)}, u32[]{:S(2)}, u32[]{:S(2)}) collective-permute-start(bf16[4,128,256]{2,1,0:T(8,128)(2,1)S(1)} %get-tuple-element.73), channel_id=1, source_target_pairs={{0,32},{1,9},{2,34},{3,11},{4,36},{5,13},{6,38},{7,15},{8,40},{9,1... | collective-permute-start | bytes 786440 | tf_op jit(solution)/shard_map/reduce_outer/ppermute | solution.py:34
  116.4 10.4 %collective-permute-start.23 = (bf16[4,128,256]{2,1,0:T(8,128)(2,1)S(1)}, bf16[4,128,256]{2,1,0:T(8,128)(2,1)S(1)}, u32[]{:S(2)}, u32[]{:S(2)}) collective-permute-start(bf16[4,128,256]{2,1,0:T(8,128)(2,1)S(1)} %get-tuple-element.74), channel_id=1, source_target_pairs={{0,64},{1,17},{2,66},{3,19},{4,68},{5,21},{6,70},{7,23},{8,72},{9,... | collective-permute-start | bytes 786440 | tf_op jit(solution)/shard_map/reduce_outer/ppermute | solution.py:34
  119.1 8.7 %collective-permute-start.24 = (bf16[4,128,256]{2,1,0:T(8,128)(2,1)S(1)}, bf16[4,128,256]{2,1,0:T(8,128)(2,1)S(1)}, u32[]{:S(2)}, u32[]{:S(2)}) collective-permute-start(bf16[4,128,256]{2,1,0:T(8,128)(2,1)S(1)} %get-tuple-element.75), channel_id=1, source_target_pairs={{0,96},{1,25},{2,98},{3,27},{4,100},{5,29},{6,102},{7,31},{8,104},... | collective-permute-start | bytes 786440 | tf_op jit(solution)/shard_map/reduce_outer/ppermute | solution.py:34
  128.3 1.3 collective-permute-start.25
  129.7 4.3 %collective-permute-start.28 = (f32[128,128]{1,0:T(8,128)S(1)}, f32[128,128]{1,0:T(8,128)S(1)}, u32[]{:S(2)}, u32[]{:S(2)}) collective-permute-start(f32[128,128]{1,0:T(8,128)S(1)} %add.91), channel_id=1, source_target_pairs={{0,6},{2,0},{4,2},{6,4},{1,7},{3,1},{5,3},{7,5},{8,14},{10,8},{12,... | collective-permute-start | bytes 196616 | tf_op jit(solution)/shard_map/reduce_gram/ppermute | solution.py:23
  131.7 6.5 %collective-permute-start.27 = (f32[128,128]{1,0:T(8,128)S(1)}, f32[128,128]{1,0:T(8,128)S(1)}, u32[]{:S(2)}, u32[]{:S(2)}) collective-permute-start(f32[128,128]{1,0:T(8,128)S(1)} %add.91), channel_id=1, source_target_pairs={{0,2},{2,4},{4,6},{6,0},{1,3},{3,5},{5,7},{7,1},{8,10},{10,12},{12... | collective-permute-start | bytes 196616 | tf_op jit(solution)/shard_map/reduce_gram/ppermute | solution.py:23
  131.8 6.4 %collective-permute-start.26 = (f32[128,128]{1,0:T(8,128)S(1)}, f32[128,128]{1,0:T(8,128)S(1)}, u32[]{:S(2)}, u32[]{:S(2)}) collective-permute-start(f32[128,128]{1,0:T(8,128)S(1)} %add.91), channel_id=1, source_target_pairs={{0,4},{2,6},{4,0},{6,2},{1,5},{3,7},{5,1},{7,3},{8,12},{10,14},{12... | collective-permute-start | bytes 196616 | tf_op jit(solution)/shard_map/reduce_gram/ppermute | solution.py:23
  138.2 5.2 %collective-permute-start.31 = (f32[128,128]{1,0:T(8,128)S(1)}, f32[128,128]{1,0:T(8,128)S(1)}, u32[]{:S(2)}, u32[]{:S(2)}) collective-permute-start(f32[128,128]{1,0:T(8,128)S(1)} %add_add_fusion.2), channel_id=1, source_target_pairs={{0,24},{8,0},{16,8},{24,16},{1,25},{9,1},{17,9},{25,17},{2,26},{10... | collective-permute-start | bytes 196616 | tf_op jit(solution)/shard_map/reduce_gram/ppermute | solution.py:23
  141.5 6.2 %collective-permute-start.30 = (f32[128,128]{1,0:T(8,128)S(1)}, f32[128,128]{1,0:T(8,128)S(1)}, u32[]{:S(2)}, u32[]{:S(2)}) collective-permute-start(f32[128,128]{1,0:T(8,128)S(1)} %add_add_fusion.2), channel_id=1, source_target_pairs={{0,8},{8,16},{16,24},{24,0},{1,9},{9,17},{17,25},{25,1},{2,10},{10... | collective-permute-start | bytes 196616 | tf_op jit(solution)/shard_map/reduce_gram/ppermute | solution.py:23
  141.5 6.2 %collective-permute-start.29 = (f32[128,128]{1,0:T(8,128)S(1)}, f32[128,128]{1,0:T(8,128)S(1)}, u32[]{:S(2)}, u32[]{:S(2)}) collective-permute-start(f32[128,128]{1,0:T(8,128)S(1)} %add_add_fusion.2), channel_id=1, source_target_pairs={{0,16},{8,24},{16,0},{24,8},{1,17},{9,25},{17,1},{25,9},{2,18},{10... | collective-permute-start | bytes 196616 | tf_op jit(solution)/shard_map/reduce_gram/ppermute | solution.py:23
  147.7 5.2 %collective-permute-start.34 = (f32[128,128]{1,0:T(8,128)S(1)}, f32[128,128]{1,0:T(8,128)S(1)}, u32[]{:S(2)}, u32[]{:S(2)}) collective-permute-start(f32[128,128]{1,0:T(8,128)S(1)} %add_add_fusion.1), channel_id=1, source_target_pairs={{0,96},{32,0},{64,32},{96,64},{1,97},{33,1},{65,33},{97,65},{2,98}... | collective-permute-start | bytes 196616 | tf_op jit(solution)/shard_map/reduce_gram/ppermute | solution.py:23
  150.4 6.2 %collective-permute-start.33 = (f32[128,128]{1,0:T(8,128)S(1)}, f32[128,128]{1,0:T(8,128)S(1)}, u32[]{:S(2)}, u32[]{:S(2)}) collective-permute-start(f32[128,128]{1,0:T(8,128)S(1)} %add_add_fusion.1), channel_id=1, source_target_pairs={{0,32},{32,64},{64,96},{96,0},{1,33},{33,65},{65,97},{97,1},{2,34}... | collective-permute-start | bytes 196616 | tf_op jit(solution)/shard_map/reduce_gram/ppermute | solution.py:23
  150.4 6.2 %collective-permute-start.32 = (f32[128,128]{1,0:T(8,128)S(1)}, f32[128,128]{1,0:T(8,128)S(1)}, u32[]{:S(2)}, u32[]{:S(2)}) collective-permute-start(f32[128,128]{1,0:T(8,128)S(1)} %add_add_fusion.1), channel_id=1, source_target_pairs={{0,64},{32,96},{64,0},{96,32},{1,65},{33,97},{65,1},{97,33},{2,66}... | collective-permute-start | bytes 196616 | tf_op jit(solution)/shard_map/reduce_gram/ppermute | solution.py:23

commit v7 on v6

--- a/solution.py
+++ b/solution.py
@@ -81,12 +81,6 @@
     )
 
 
-def hold_kernel(count, tiles, held, sems):
-    start, wait = hold_copies(count, tiles, held, sems)
-    start()
-    wait()
-
-
 def plan_kernel(count, row_at, col_at, tiles, held, counts, near, far, sems):
     start, wait = hold_copies(count, tiles, held, sems)
     start()
@@ -126,17 +120,6 @@
 
 def anywhere(count):
     return [pl.BlockSpec(memory_space=pl.ANY)] * count
-
-
-def hold_tiles(count, tiles):
-    return pl.pallas_call(
-        hold_kernel,
-        out_shape=jax.ShapeDtypeStruct(tiles.shape, tiles.dtype),
-        in_specs=scalars(1) + anywhere(1),
-        out_specs=whole(1)[0],
-        name="hold_tiles",
-        **hold_parameters(tiles),
-    )(count, tiles)
 
 
 def plan_tiles(count, row_at, col_at, tiles):
@@ -206,7 +189,8 @@
     )(counts, near, tiles, *pieces)
 
 
-def forward_far_kernel(counts, far, tiles, a, b, before, total, away, held, sems):
+def forward_far_kernel(counts, far, tiles, a, b, before, total, *rest):
+    *aways, held, sems = rest
     copies = load_pieces([a, b], held, sems)
     for one in copies:
         one.wait()
@@ -215,18 +199,17 @@
         total[row] += dot(tiles[slot], held[jnp.minimum(col - 32, 16)])
 
     listed(counts[1], far, 16, body)
-    away[...] = total[pl.ds(16, 16)]
+    for d, away in enumerate(aways):
+        away[...] = total[pl.ds(16 + 4 * d, 4)]
 
 
 def forward_far(counts, far, tiles, pieces, before):
     return pl.pallas_call(
         forward_far_kernel,
-        out_shape=(
-            jax.ShapeDtypeStruct((33, SIDE, RANK), F32),
-            jax.ShapeDtypeStruct((16, SIDE, RANK), F32),
-        ),
+        out_shape=(jax.ShapeDtypeStruct((33, SIDE, RANK), F32),)
+        + (jax.ShapeDtypeStruct((4, SIDE, RANK), F32),) * 4,
         in_specs=scalars(2) + whole(1) + anywhere(2) + whole(1),
-        out_specs=tuple(whole(2)),
+        out_specs=tuple(whole(5)),
         scratch_shapes=[
             pltpu.VMEM((17, SIDE, RANK), BF16),
             pltpu.SemaphoreType.DMA((2,)),
@@ -298,11 +281,9 @@
     )(counts, near, tiles, *pieces)
 
 
-def core_sum_kernel(keep, came, kept, *outs):
-    kept[...] = keep[pl.ds(0, 4)] + came[pl.ds(0, 4)]
-    for d, out in enumerate(outs):
-        at = pl.ds(4 * (d + 1), 4)
-        total = keep[at] + came[at]
+def core_sum(keep, came, d):
+    def kernel(keep, came, out):
+        total = keep[pl.ds(4 * d, 4)] + came[...]
         largest = jnp.max(jnp.abs(total), axis=0)
         largest = jnp.max(jnp.max(largest, axis=0, keepdims=True), axis=1, keepdims=True)
         power = jnp.floor(jnp.log2(jnp.maximum(largest, 1e-30))) - 13.0
@@ -311,37 +292,34 @@
             out[pl.ds(SIDE * i, SIDE), :] = total[i] * scale
         out[pl.ds(4 * SIDE, EXTRA), :] = jnp.broadcast_to(power, (EXTRA, RANK))
 
-
-def core_sum(keep, came):
-    part = jax.ShapeDtypeStruct((4 * SIDE + EXTRA, RANK), F32)
-    return pl.pallas_call(
-        core_sum_kernel,
-        out_shape=(jax.ShapeDtypeStruct((4, SIDE, RANK), F32),) + (part,) * 3,
+    return pl.pallas_call(
+        kernel,
+        out_shape=jax.ShapeDtypeStruct((4 * SIDE + EXTRA, RANK), F32),
         in_specs=whole(2),
-        out_specs=tuple(whole(4)),
+        out_specs=whole(1)[0],
         compiler_params=limits(6),
         name="core_sum",
     )(keep, came)
 
 
-def inner_kernel(kept, a, b, c, out):
+def inner_kernel(keep, came, a, b, c, out):
     scales = [jnp.exp2(one[pl.ds(4 * SIDE, 1), :]) for one in (a, b, c)]
     for i in range(out.shape[0]):
-        summed = kept[i]
+        summed = keep[i] + came[i]
         for one, scale in zip((a, b, c), scales):
             summed += one[pl.ds(SIDE * i, SIDE), :] * scale
         out[i] = summed.T.astype(BF16)
 
 
-def inner_sum(kept, parts):
+def inner_sum(keep, came, parts):
     return pl.pallas_call(
         inner_kernel,
         out_shape=jax.ShapeDtypeStruct((4, RANK, SIDE), BF16),
-        in_specs=whole(4),
+        in_specs=whole(5),
         out_specs=whole(1)[0],
         compiler_params=limits(6),
         name="inner_sum",
-    )(kept, *parts)
+    )(keep, came, *parts)
 
 
 def relay_kernel(total, a, b, right, left):
@@ -414,6 +392,11 @@
         compiler_params=limits(6),
         name="outer_sum",
     )(keep, *came)
+
+
+def halved(value):
+    large = value.astype(BF16)
+    return large, (value - large.astype(F32)).astype(BF16)
 
 
 def wide(value):
@@ -464,9 +447,11 @@
                     block = block - column[k] * upper[k][h]
                 work[g : g + 8, h * RANK : (h + 1) * RANK] = block
     factor[...] = jnp.where(cols >= rows, work[:, :RANK], 0.0) * (1.0 / scale)
-    inverse = work[:, RANK:] * scale
+    inverse, rest = halved(work[:, RANK:] * scale)
     for b in range(outer.shape[0]):
-        basis[pl.ds(b * SIDE, SIDE), :] = exact_dot(outer[b], inverse, ((0,), (1,)))
+        large, small = halved(outer[b])
+        product = dot(inverse, large) + (dot(rest, large) + dot(inverse, small))
+        basis[pl.ds(b * SIDE, SIDE), :] = product.T
 
 
 def finish(gram, outer, entities):
@@ -514,16 +499,14 @@
         over = (cross(right[:8], far_axes, 1), cross(left[8:], far_axes, -1))
 
     keep = forward_near(counts, near_list, held, (first, left, right))
-    keep, away = forward_far(counts, far_list, held, over, keep)
+    keep, *aways = forward_far(counts, far_list, held, over, keep)
 
     with jax.named_scope("reduce_inner"):
-        came = send(away, "core", 1)
-        kept, *sums = core_sum(keep, came)
-        sums, second_tiles = lax.optimization_barrier((sums, tiles))
-        held = hold_tiles(tile_count, second_tiles)
-        sums = [send(one.astype(jnp.float16), "z", d) for d, one in zip((1, 2, 3), sums)]
-        sums, held = lax.optimization_barrier((sums, held))
-        inner = inner_sum(kept, [one.astype(F32) for one in sums])
+        parts = []
+        for d in (2, 1, 3):
+            one = core_sum(keep, send(aways[d], "core", 1), d)
+            parts.append(send(one.astype(jnp.float16), "z", d).astype(F32))
+        inner = inner_sum(keep, send(aways[0], "core", 1), parts)
 
     with jax.named_scope("gather_inner"):
         mine = [inner] + [send(inner, "z", -d) for d in (1, 2, 3)]

time: 163 us -> 158 us (0.969)
  Pallas kernels: 40.6 us -> 24.8 us
  starting transfers between devices: 41.3 us -> 47.7 us
  waiting for transfers between devices: 76.9 us -> 81 us
    pallas_call x2 -> x3, Pallas kernels: 7.6 us -> 0.56 us  [core_sum(): pl.pallas_call(kernel, out_shape=jax.ShapeDtypeStruct((4 * SIDE + EXTRA,...]
    ppermute x14, waiting for transfers between devices: 37.4 us -> 44.1 us  [cross(): return lax.ppermute(array, AXES, pairs)]
    ppermute x21 -> x24, starting transfers between devices: 20.6 us -> 26.4 us  [send(): lax.ppermute(array, axis, [(i, (i + step) % size) for i in range(size)])]
    pallas_call x1, Pallas kernels: 6.34 us -> 3.71 us  [forward_near(): pl.pallas_call(forward_near_kernel, out_shape=jax.ShapeDtypeStruct((33, S...]
    ppermute x21 -> x24, waiting for transfers between devices: 39.5 us -> 36.9 us  [send(): lax.ppermute(array, axis, [(i, (i + step) % size) for i in range(size)])]
    pallas_call x1, Pallas kernels: 8.3 us -> 5.91 us  [plan_tiles(): pl.pallas_call(plan_kernel, out_shape=(jax.ShapeDtypeStruct(tiles.shape,...]
    pallas_call x1, Pallas kernels: 5.41 us -> 3.23 us  [backward_near(): pl.pallas_call(backward_near_kernel, out_shape=jax.ShapeDtypeStruct((65,...]
  transfers between devices with their start and end apart: 35 -> 38, of which waited for: 26 -> 27; matrix products, arithmetic and copies ran while one was open for 0% -> 1% of each run, Pallas kernels for 17% -> 9%
where the time goes in v7:
time: 158 us; the launch traced here: 157 us
  waiting for transfers between devices  81 us (51%)
  starting transfers between devices  47.7 us (30%)
  Pallas kernels  24.8 us (16%)
  other arithmetic  2.09 us (1%)
    ppermute x14, waiting for transfers between devices, cross(): return lax.ppermute(array, AXES, pairs)  44.1 us
    ppermute x24, waiting for transfers between devices, send(): lax.ppermute(array, axis, [(i, (i + step) % size) for i in range(size)])  36.9 us
    ppermute x24, starting transfers between devices, send(): lax.ppermute(array, axis, [(i, (i + step) % size) for i in range(size)])  26.4 us
    ppermute x14, starting transfers between devices, cross(): return lax.ppermute(array, AXES, pairs)  21.2 us
    pallas_call x1, Pallas kernels, plan_tiles(): pl.pallas_call(plan_kernel, out_shape=(jax.ShapeDtypeStruct(tiles.shape,...  5.91 us
    pallas_call x1, Pallas kernels, finish(): pl.pallas_call(kernel, out_shape=(jax.ShapeDtypeStruct((4 * SIDE, RANK),...  5.51 us
    pallas_call x1, Pallas kernels, forward_near(): pl.pallas_call(forward_near_kernel, out_shape=jax.ShapeDtypeStruct((33, S...  3.71 us
    pallas_call x1, Pallas kernels, backward_near(): pl.pallas_call(backward_near_kernel, out_shape=jax.ShapeDtypeStruct((65,...  3.23 us
  transfers between devices with their start and end apart: 38, of which 27 were waited for; matrix products, arithmetic and copies ran while one was open for 1% of the time, Pallas kernels for 9%

profile of v7, /device:TPU:0, one launch (start us, length us, event | category | flops | bytes accessed | tf_op | source)
XLA Modules:
  0.0 157.1 jit_solution(284007303687226255)
XLA Ops:
  0.6 3.2 %collective-permute-start.1 = (bf16[1024,128]{1,0:T(8,128)(2,1)}, bf16[1024,128]{1,0:T(8,128)(2,1)S(1)}, u32[]{:S(2)}, u32[]{:S(2)}) collective-permute-start(bf16[1024,128]{1,0:T(8,128)(2,1)} %param.4), channel_id=1, source_target_pairs={{0,64},{1,17},{2,66},{3,19},{4,68},{5,21},{6,70},{7,23},{8,72},{9,... | collective-permute-start | bytes 786440 | tf_op jit(solution)/shard_map/gather_basis/ppermute | solution.py:34
  3.8 1.1 collective-permute-start
  5.0 0.9 collective-permute-start.2
  5.8 0.8 fusion.10
  6.6 2.2 %collective-permute-done.1 = bf16[1024,128]{1,0:T(8,128)(2,1)S(1)} collective-permute-done((bf16[1024,128]{1,0:T(8,128)(2,1)}, bf16[1024,128]{1,0:T(8,128)(2,1)S(1)}, u32[]{:S(2)}, u32[]{:S(2)}) %collective-permute-start.1) | collective-permute-done | bytes 262176 | tf_op jit(solution)/shard_map/gather_basis/ppermute | solution.py:34
  8.8 3.0 %collective-permute-done = bf16[1024,128]{1,0:T(8,128)(2,1)S(1)} collective-permute-done((bf16[1024,128]{1,0:T(8,128)(2,1)}, bf16[1024,128]{1,0:T(8,128)(2,1)S(1)}, u32[]{:S(2)}, u32[]{:S(2)}) %collective-permute-start) | collective-permute-done | bytes 262176 | tf_op jit(solution)/shard_map/gather_basis/ppermute | solution.py:34
  11.8 1.0 collective-permute-done.2
  12.8 1.0 pad_maximum_fusion
  13.8 3.1 %collective-permute-start.4 = (bf16[16,256,128]{2,1,0:T(8,128)(2,1)S(1)}, bf16[16,256,128]{2,1,0:T(8,128)(2,1)S(1)}, u32[]{:S(2)}, u32[]{:S(2)}) collective-permute-start(bf16[16,256,128]{2,1,0:T(8,128)(2,1)S(1)} %bitcast.3), channel_id=1, source_target_pairs={{0,24},{1,97},{2,26},{3,99},{4,28},{5,101},{6,30},{7,103},{8,0},{9... | collective-permute-start | bytes 3145736 | tf_op jit(solution)/shard_map/gather_basis/ppermute | solution.py:34
  17.5 5.9 %plan_tiles.1 = (bf16[160,256,256]{2,1,0:T(8,128)(2,1)S(1)}, s32[2]{0:T(128)S(1)}, s32[192]{0:T(256)S(1)}, s32[192]{0:T(256)S(1)}) custom-call(s32[1]{0:T(128)S(6)} %copy.8.count, s32[160]{0:T(256)S(1)} %get-tuple-element.31.row_at, s32[160]{0:T(256)S(1)} %get-tuple-element.32.col_at, bf16[160,256,256]{2,1,0:T(8,128)(2,1)} %tiles), custom_call_target="tpu_custom_call" | custom-call | bytes 41943040 | tf_op jit(solution)/shard_map/gather_basis/plan_tiles/pallas_call | solution.py:127
  23.4 5.7 %collective-permute-done.4.left = bf16[16,256,128]{2,1,0:T(8,128)(2,1)S(1)} collective-permute-done((bf16[16,256,128]{2,1,0:T(8,128)(2,1)S(1)}, bf16[16,256,128]{2,1,0:T(8,128)(2,1)S(1)}, u32[]{:S(2)}, u32[]{:S(2)}) %collective-permute-start.4) | collective-permute-done | bytes 1048608 | tf_op jit(solution)/shard_map/gather_basis/ppermute | solution.py:34
  29.2 3.7 %collective-permute-done.3.right = bf16[16,256,128]{2,1,0:T(8,128)(2,1)S(1)} collective-permute-done((bf16[16,256,128]{2,1,0:T(8,128)(2,1)S(1)}, bf16[16,256,128]{2,1,0:T(8,128)(2,1)S(1)}, u32[]{:S(2)}, u32[]{:S(2)}) %collective-permute-start.3) | collective-permute-done | bytes 1048608 | tf_op jit(solution)/shard_map/gather_basis/ppermute | solution.py:34
  33.0 2.0 %collective-permute-start.5 = (bf16[8,256,128]{2,1,0:T(8,128)(2,1)S(1)}, bf16[8,256,128]{2,1,0:T(8,128)(2,1)S(1)}, u32[]{:S(2)}, u32[]{:S(2)}) collective-permute-start(bf16[8,256,128]{2,1,0:T(8,128)(2,1)S(1)} %slice.15), channel_id=1, source_target_pairs={{0,8},{1,33},{2,10},{3,35},{4,12},{5,37},{6,14},{7,39},{8,16},{9,4... | collective-permute-start | bytes 1572872 | tf_op jit(solution)/shard_map/gather_basis/ppermute | solution.py:34
  35.0 3.7 %forward_near.1.before = f32[33,256,128]{2,1,0:T(8,128)S(1)} custom-call(s32[2]{0:T(128)S(1)} %get-tuple-element.34.counts, s32[192]{0:T(256)S(1)} %get-tuple-element.35.near, bf16[160,256,256]{2,1,0:T(8,128)(2,1)S(1)} %get-tuple-element.41.tiles, bf16[16,256,128]{2,1,0:T(8,128)(2,1)S(1)} %bitcast.5, bf16[16,256,128]{2,1,0:T(8,128)(2,1)S(1)} %collective-permute-done.4.left, ...), custom_call_target="tpu_custom_call" | custom-call | flops 2013265920 | bytes 1048576 | tf_op jit(solution)/shard_map/forward_near/pallas_call | solution.py:177
  38.8 3.4 %collective-permute-done.6.b = bf16[8,256,128]{2,1,0:T(8,128)(2,1)S(1)} collective-permute-done((bf16[8,256,128]{2,1,0:T(8,128)(2,1)S(1)}, bf16[8,256,128]{2,1,0:T(8,128)(2,1)S(1)}, u32[]{:S(2)}, u32[]{:S(2)}) %collective-permute-start.6) | collective-permute-done | bytes 524320 | tf_op jit(solution)/shard_map/gather_basis/ppermute | solution.py:34
  42.2 1.3 collective-permute-done.5.a
  43.5 2.3 %forward_far.1 = (f32[33,256,128]{2,1,0:T(8,128)S(1)}, f32[4,256,128]{2,1,0:T(8,128)S(1)}, f32[4,256,128]{2,1,0:T(8,128)S(1)}, f32[4,256,128]{2,1,0:T(8,128)S(1)}, f32[4,256,128]{2,1,0:T(8,128)S(1)}) custom-call(s32[2]{0:T(128)S(1)} %get-tuple-element.34.counts, s32[192]{0:T(256)S(1)} %get-tuple-element.42.far, ...), custom_call_target="tpu_custom_call", output_to_operand_aliasing={{0}: (5, {})} | custom-call | tf_op jit(solution)/shard_map/forward_far/pallas_call | solution.py:207
  45.9 0.5 collective-permute-start.10
  46.5 0.4 collective-permute-start.7
  46.9 0.9 collective-permute-done.8.came
  48.0 3.2 %collective-permute-start.9 = (f16[1040,128]{1,0:T(8,128)(2,1)S(1)}, f16[1040,128]{1,0:T(8,128)(2,1)S(1)}, u32[]{:S(2)}, u32[]{:S(2)}) collective-permute-start(f16[1040,128]{1,0:T(8,128)(2,1)S(1)} %convert_element_type.18), channel_id=1, source_target_pairs={{0,4},{2,6},{4,0},{6,2},{1,5},{3,7},{5,1},{7,3},{8,12},{10,14},{12... | collective-permute-start | bytes 798728 | tf_op jit(solution)/shard_map/reduce_inner/ppermute | solution.py:23
  51.5 1.1 collective-permute-start.11
  52.8 2.3 %collective-permute-start.13 = (f16[1040,128]{1,0:T(8,128)(2,1)S(1)}, f16[1040,128]{1,0:T(8,128)(2,1)S(1)}, u32[]{:S(2)}, u32[]{:S(2)}) collective-permute-start(f16[1040,128]{1,0:T(8,128)(2,1)S(1)} %convert_element_type.22), channel_id=1, source_target_pairs={{0,6},{2,0},{4,2},{6,4},{1,7},{3,1},{5,3},{7,5},{8,14},{10,8},{12,... | collective-permute-start | bytes 798728 | tf_op jit(solution)/shard_map/reduce_inner/ppermute | solution.py:23
  55.1 3.8 %collective-permute-done.9 = f16[1040,128]{1,0:T(8,128)(2,1)S(1)} collective-permute-done((f16[1040,128]{1,0:T(8,128)(2,1)S(1)}, f16[1040,128]{1,0:T(8,128)(2,1)S(1)}, u32[]{:S(2)}, u32[]{:S(2)}) %collective-permute-start.9) | collective-permute-done | bytes 266272 | tf_op jit(solution)/shard_map/reduce_inner/ppermute | solution.py:23
  58.9 4.8 %collective-permute-done.11 = f16[1040,128]{1,0:T(8,128)(2,1)S(1)} collective-permute-done((f16[1040,128]{1,0:T(8,128)(2,1)S(1)}, f16[1040,128]{1,0:T(8,128)(2,1)S(1)}, u32[]{:S(2)}, u32[]{:S(2)}) %collective-permute-start.11) | collective-permute-done | bytes 266272 | tf_op jit(solution)/shard_map/reduce_inner/ppermute | solution.py:23
  63.8 0.6 collective-permute-done.13
  64.7 1.1 collective-permute-start.16
  65.8 3.0 %collective-permute-start.15 = (bf16[4,128,256]{2,1,0:T(8,128)(2,1)S(1)}, bf16[4,128,256]{2,1,0:T(8,128)(2,1)S(1)}, u32[]{:S(2)}, u32[]{:S(2)}) collective-permute-start(bf16[4,128,256]{2,1,0:T(8,128)(2,1)S(1)} %inner_sum.1.rest_0_), channel_id=1, source_target_pairs={{0,4},{2,6},{4,0},{6,2},{1,5},{3,7},{5,1},{7,3},{8,12},{10,14},{12... | collective-permute-start | bytes 786440 | tf_op jit(solution)/shard_map/gather_inner/ppermute | solution.py:23
  68.9 0.9 collective-permute-start.14
  69.8 4.1 %collective-permute-done.16.rest_3_ = bf16[4,128,256]{2,1,0:T(8,128)(2,1)S(1)} collective-permute-done((bf16[4,128,256]{2,1,0:T(8,128)(2,1)S(1)}, bf16[4,128,256]{2,1,0:T(8,128)(2,1)S(1)}, u32[]{:S(2)}, u32[]{:S(2)}) %collective-permute-start.16) | collective-permute-done | bytes 262176 | tf_op jit(solution)/shard_map/gather_inner/ppermute | solution.py:23
  73.9 6.8 %collective-permute-done.15.rest_2_ = bf16[4,128,256]{2,1,0:T(8,128)(2,1)S(1)} collective-permute-done((bf16[4,128,256]{2,1,0:T(8,128)(2,1)S(1)}, bf16[4,128,256]{2,1,0:T(8,128)(2,1)S(1)}, u32[]{:S(2)}, u32[]{:S(2)}) %collective-permute-start.15) | collective-permute-done | bytes 262176 | tf_op jit(solution)/shard_map/gather_inner/ppermute | solution.py:23
  80.7 0.5 collective-permute-start.18
  81.2 1.0 collective-permute-done.19.rest_6_
  82.2 0.4 collective-permute-done.18.rest_5_
  82.6 2.1 %backward_far.1 = (bf16[8,128,256]{2,1,0:T(8,128)(2,1)S(1)}, bf16[8,128,256]{2,1,0:T(8,128)(2,1)S(1)}) custom-call(s32[2]{0:T(128)S(1)} %get-tuple-element.34.counts, s32[192]{0:T(256)S(1)} %get-tuple-element.42.far, bf16[160,256,256]{2,1,0:T(8,128)(2,1)S(1)} %get-tuple-element.41.tiles, bf16[4,128,256]{2,1,0:T(8,128)(2,1)S(1)} %inner_sum.1.rest_0_, ...), custom_call_target="tpu_custom_call" | custom-call | tf_op jit(solution)/shard_map/backward_far/pallas_call | solution.py:240
  84.7 0.8 collective-permute-start.21
  85.5 2.5 %collective-permute-start.22 = (bf16[8,128,256]{2,1,0:T(8,128)(2,1)S(1)}, bf16[8,128,256]{2,1,0:T(8,128)(2,1)S(1)}, u32[]{:S(2)}, u32[]{:S(2)}) collective-permute-start(bf16[8,128,256]{2,1,0:T(8,128)(2,1)S(1)} %get-tuple-element.51), channel_id=1, source_target_pairs={{0,24},{1,97},{2,26},{3,99},{4,28},{5,101},{6,30},{7,103},{8,0},{9... | collective-permute-start | bytes 1572872 | tf_op jit(solution)/shard_map/reduce_outer/ppermute | solution.py:34
  88.0 3.2 %backward_near.1.total = f32[65,128,256]{2,1,0:T(8,128)S(1)} custom-call(s32[2]{0:T(128)S(1)} %get-tuple-element.34.counts, s32[192]{0:T(256)S(1)} %get-tuple-element.35.near, bf16[160,256,256]{2,1,0:T(8,128)(2,1)S(1)} %get-tuple-element.41.tiles, bf16[4,128,256]{2,1,0:T(8,128)(2,1)S(1)} %inner_sum.1.rest_0_, ...), custom_call_target="tpu_custom_call" | custom-call | flops 2013265920 | bytes 1048576 | tf_op jit(solution)/shard_map/reduce_outer/backward_near/pallas_call | solution.py:269
  91.2 3.9 %collective-permute-done.21.a = bf16[8,128,256]{2,1,0:T(8,128)(2,1)S(1)} collective-permute-done((bf16[8,128,256]{2,1,0:T(8,128)(2,1)S(1)}, bf16[8,128,256]{2,1,0:T(8,128)(2,1)S(1)}, u32[]{:S(2)}, u32[]{:S(2)}) %collective-permute-start.21) | collective-permute-done | bytes 524320 | tf_op jit(solution)/shard_map/reduce_outer/ppermute | solution.py:34
  95.1 0.3 relay_sum.1
  95.5 3.3 %collective-permute-start.24 = (bf16[16,128,256]{2,1,0:T(8,128)(2,1)S(1)}, bf16[16,128,256]{2,1,0:T(8,128)(2,1)S(1)}, u32[]{:S(2)}, u32[]{:S(2)}) collective-permute-start(bf16[16,128,256]{2,1,0:T(8,128)(2,1)S(1)} %get-tuple-element.53), channel_id=1, source_target_pairs={{0,24},{1,97},{2,26},{3,99},{4,28},{5,101},{6,30},{7,103},{8,0},{9... | collective-permute-start | bytes 3145736 | tf_op jit(solution)/shard_map/reduce_outer/ppermute | solution.py:34
  98.8 12.7 %collective-permute-done.23.a = bf16[16,128,256]{2,1,0:T(8,128)(2,1)S(1)} collective-permute-done((bf16[16,128,256]{2,1,0:T(8,128)(2,1)S(1)}, bf16[16,128,256]{2,1,0:T(8,128)(2,1)S(1)}, u32[]{:S(2)}, u32[]{:S(2)}) %collective-permute-start.23) | collective-permute-done | bytes 1048608 | tf_op jit(solution)/shard_map/reduce_outer/ppermute | solution.py:34
  111.5 0.3 middle_sum.1
  111.9 3.1 %collective-permute-start.26 = (bf16[4,128,256]{2,1,0:T(8,128)(2,1)S(1)}, bf16[4,128,256]{2,1,0:T(8,128)(2,1)S(1)}, u32[]{:S(2)}, u32[]{:S(2)}) collective-permute-start(bf16[4,128,256]{2,1,0:T(8,128)(2,1)S(1)} %get-tuple-element.56), channel_id=1, source_target_pairs={{0,64},{1,17},{2,66},{3,19},{4,68},{5,21},{6,70},{7,23},{8,72},{9,... | collective-permute-start | bytes 786440 | tf_op jit(solution)/shard_map/reduce_outer/ppermute | solution.py:34
  115.1 0.9 collective-permute-start.27
  116.0 3.5 %collective-permute-done.25.a = bf16[4,128,256]{2,1,0:T(8,128)(2,1)S(1)} collective-permute-done((bf16[4,128,256]{2,1,0:T(8,128)(2,1)S(1)}, bf16[4,128,256]{2,1,0:T(8,128)(2,1)S(1)}, u32[]{:S(2)}, u32[]{:S(2)}) %collective-permute-start.25) | collective-permute-done | bytes 262176 | tf_op jit(solution)/shard_map/reduce_outer/ppermute | solution.py:34
  119.5 2.8 %collective-permute-done.26.b = bf16[4,128,256]{2,1,0:T(8,128)(2,1)S(1)} collective-permute-done((bf16[4,128,256]{2,1,0:T(8,128)(2,1)S(1)}, bf16[4,128,256]{2,1,0:T(8,128)(2,1)S(1)}, u32[]{:S(2)}, u32[]{:S(2)}) %collective-permute-start.26) | collective-permute-done | bytes 262176 | tf_op jit(solution)/shard_map/reduce_outer/ppermute | solution.py:34
  122.3 0.9 collective-permute-done.27.c
  123.2 0.6 outer_sum.1
  123.9 1.2 collective-permute-done.28
  125.2 1.3 collective-permute-start.31
  126.5 0.8 collective-permute-start.30
  127.3 1.1 collective-permute-start.29
  128.4 1.1 collective-permute-done.31
  129.5 3.1 %collective-permute-done.30 = f32[128,128]{1,0:T(8,128)S(1)} collective-permute-done((f32[128,128]{1,0:T(8,128)S(1)}, f32[128,128]{1,0:T(8,128)S(1)}, u32[]{:S(2)}, u32[]{:S(2)}) %collective-permute-start.30) | collective-permute-done | bytes 65568 | tf_op jit(solution)/shard_map/reduce_gram/ppermute | solution.py:23
  132.6 0.5 collective-permute-done.29
  133.1 3.4 %collective-permute-start.34 = (f32[128,128]{1,0:T(8,128)S(1)}, f32[128,128]{1,0:T(8,128)S(1)}, u32[]{:S(2)}, u32[]{:S(2)}) collective-permute-start(f32[128,128]{1,0:T(8,128)S(1)} %add_add_fusion.2), channel_id=1, source_target_pairs={{0,24},{8,0},{16,8},{24,16},{1,25},{9,1},{17,9},{25,17},{2,26},{10... | collective-permute-start | bytes 196616 | tf_op jit(solution)/shard_map/reduce_gram/ppermute | solution.py:23
  136.5 2.2 %collective-permute-start.32 = (f32[128,128]{1,0:T(8,128)S(1)}, f32[128,128]{1,0:T(8,128)S(1)}, u32[]{:S(2)}, u32[]{:S(2)}) collective-permute-start(f32[128,128]{1,0:T(8,128)S(1)} %add_add_fusion.2), channel_id=1, source_target_pairs={{0,16},{8,24},{16,0},{24,8},{1,17},{9,25},{17,1},{25,9},{2,18},{10... | collective-permute-start | bytes 196616 | tf_op jit(solution)/shard_map/reduce_gram/ppermute | solution.py:23
  138.7 4.0 %collective-permute-done.33 = f32[128,128]{1,0:T(8,128)S(1)} collective-permute-done((f32[128,128]{1,0:T(8,128)S(1)}, f32[128,128]{1,0:T(8,128)S(1)}, u32[]{:S(2)}, u32[]{:S(2)}) %collective-permute-start.33) | collective-permute-done | bytes 65568 | tf_op jit(solution)/shard_map/reduce_gram/ppermute | solution.py:23
  142.7 2.7 %collective-permute-start.37 = (f32[128,128]{1,0:T(8,128)S(1)}, f32[128,128]{1,0:T(8,128)S(1)}, u32[]{:S(2)}, u32[]{:S(2)}) collective-permute-start(f32[128,128]{1,0:T(8,128)S(1)} %add_add_fusion.1), channel_id=1, source_target_pairs={{0,96},{32,0},{64,32},{96,64},{1,97},{33,1},{65,33},{97,65},{2,98}... | collective-permute-start | bytes 196616 | tf_op jit(solution)/shard_map/reduce_gram/ppermute | solution.py:23
  145.4 1.5 collective-permute-start.35
  146.9 0.6 collective-permute-done.37
  147.5 4.0 %collective-permute-done.36 = f32[128,128]{1,0:T(8,128)S(1)} collective-permute-done((f32[128,128]{1,0:T(8,128)S(1)}, f32[128,128]{1,0:T(8,128)S(1)}, u32[]{:S(2)}, u32[]{:S(2)}) %collective-permute-start.36) | collective-permute-done | bytes 65568 | tf_op jit(solution)/shard_map/reduce_gram/ppermute | solution.py:23
  151.6 5.5 %finish.1 = (f32[1024,128]{1,0:T(8,128)}, f32[128,128]{1,0:T(8,128)}) custom-call(f32[128,128]{1,0:T(8,128)S(1)} %add_add_fusion.refs_0_, f32[4,128,256]{2,1,0:T(8,128)S(1)} %get-tuple-element.59.refs_1_), custom_call_target="tpu_custom_call" | custom-call | tf_op jit(solution)/shard_map/finish/pallas_call | solution.py:463
  (40 shorter events, 1.7 us)
Async XLA Ops:
  0.6 8.2 %collective-permute-start.1 = (bf16[1024,128]{1,0:T(8,128)(2,1)}, bf16[1024,128]{1,0:T(8,128)(2,1)S(1)}, u32[]{:S(2)}, u32[]{:S(2)}) collective-permute-start(bf16[1024,128]{1,0:T(8,128)(2,1)} %param.4), channel_id=1, source_target_pairs={{0,64},{1,17},{2,66},{3,19},{4,68},{5,21},{6,70},{7,23},{8,72},{9,... | collective-permute-start | bytes 786440 | tf_op jit(solution)/shard_map/gather_basis/ppermute | solution.py:34
  3.8 8.0 %collective-permute-start = (bf16[1024,128]{1,0:T(8,128)(2,1)}, bf16[1024,128]{1,0:T(8,128)(2,1)S(1)}, u32[]{:S(2)}, u32[]{:S(2)}) collective-permute-start(bf16[1024,128]{1,0:T(8,128)(2,1)} %param.4), channel_id=1, source_target_pairs={{0,96},{1,25},{2,98},{3,27},{4,100},{5,29},{6,102},{7,31},{8,104},... | collective-permute-start | bytes 786440 | tf_op jit(solution)/shard_map/gather_basis/ppermute | solution.py:34
  5.0 7.8 %collective-permute-start.2 = (bf16[1024,128]{1,0:T(8,128)(2,1)}, bf16[1024,128]{1,0:T(8,128)(2,1)S(1)}, u32[]{:S(2)}, u32[]{:S(2)}) collective-permute-start(bf16[1024,128]{1,0:T(8,128)(2,1)} %param.4), channel_id=1, source_target_pairs={{0,32},{1,9},{2,34},{3,11},{4,36},{5,13},{6,38},{7,15},{8,40},{9,1... | collective-permute-start | bytes 786440 | tf_op jit(solution)/shard_map/gather_basis/ppermute | solution.py:34
  13.8 15.4 %collective-permute-start.4 = (bf16[16,256,128]{2,1,0:T(8,128)(2,1)S(1)}, bf16[16,256,128]{2,1,0:T(8,128)(2,1)S(1)}, u32[]{:S(2)}, u32[]{:S(2)}) collective-permute-start(bf16[16,256,128]{2,1,0:T(8,128)(2,1)S(1)} %bitcast.3), channel_id=1, source_target_pairs={{0,24},{1,97},{2,26},{3,99},{4,28},{5,101},{6,30},{7,103},{8,0},{9... | collective-permute-start | bytes 3145736 | tf_op jit(solution)/shard_map/gather_basis/ppermute | solution.py:34
  16.9 16.0 %collective-permute-start.3 = (bf16[16,256,128]{2,1,0:T(8,128)(2,1)S(1)}, bf16[16,256,128]{2,1,0:T(8,128)(2,1)S(1)}, u32[]{:S(2)}, u32[]{:S(2)}) collective-permute-start(bf16[16,256,128]{2,1,0:T(8,128)(2,1)S(1)} %bitcast.4), channel_id=1, source_target_pairs={{0,8},{1,33},{2,10},{3,35},{4,12},{5,37},{6,14},{7,39},{8,16},{9,4... | collective-permute-start | bytes 3145736 | tf_op jit(solution)/shard_map/gather_basis/ppermute | solution.py:34
  32.9 9.2 %collective-permute-start.6 = (bf16[8,256,128]{2,1,0:T(8,128)(2,1)S(1)}, bf16[8,256,128]{2,1,0:T(8,128)(2,1)S(1)}, u32[]{:S(2)}, u32[]{:S(2)}) collective-permute-start(bf16[8,256,128]{2,1,0:T(8,128)(2,1)S(1)} %slice.16), channel_id=1, source_target_pairs={{0,24},{1,97},{2,26},{3,99},{4,28},{5,101},{6,30},{7,103},{8,0},{9... | collective-permute-start | bytes 1572872 | tf_op jit(solution)/shard_map/gather_basis/ppermute | solution.py:34
  33.0 10.5 %collective-permute-start.5 = (bf16[8,256,128]{2,1,0:T(8,128)(2,1)S(1)}, bf16[8,256,128]{2,1,0:T(8,128)(2,1)S(1)}, u32[]{:S(2)}, u32[]{:S(2)}) collective-permute-start(bf16[8,256,128]{2,1,0:T(8,128)(2,1)S(1)} %slice.15), channel_id=1, source_target_pairs={{0,8},{1,33},{2,10},{3,35},{4,12},{5,37},{6,14},{7,39},{8,16},{9,4... | collective-permute-start | bytes 1572872 | tf_op jit(solution)/shard_map/gather_basis/ppermute | solution.py:34
  45.8 2.0 %collective-permute-start.8 = (f32[4,256,128]{2,1,0:T(8,128)S(1)}, f32[4,256,128]{2,1,0:T(8,128)S(1)}, u32[]{:S(2)}, u32[]{:S(2)}) collective-permute-start(f32[4,256,128]{2,1,0:T(8,128)S(1)} %get-tuple-element.47), channel_id=1, source_target_pairs={{0,1},{1,0},{2,3},{3,2},{4,5},{5,4},{6,7},{7,6},{8,9},{9,8},{10,11... | collective-permute-start | bytes 1572872 | tf_op jit(solution)/shard_map/reduce_inner/ppermute | solution.py:23
  45.9 5.4 %collective-permute-start.10 = (f32[4,256,128]{2,1,0:T(8,128)S(1)}, f32[4,256,128]{2,1,0:T(8,128)S(1)}, u32[]{:S(2)}, u32[]{:S(2)}) collective-permute-start(f32[4,256,128]{2,1,0:T(8,128)S(1)} %get-tuple-element.48), channel_id=1, source_target_pairs={{0,1},{1,0},{2,3},{3,2},{4,5},{5,4},{6,7},{7,6},{8,9},{9,8},{10,11... | collective-permute-start | bytes 1572872 | tf_op jit(solution)/shard_map/reduce_inner/ppermute | solution.py:23
  46.4 6.2 %collective-permute-start.12 = (f32[4,256,128]{2,1,0:T(8,128)S(1)}, f32[4,256,128]{2,1,0:T(8,128)S(1)}, u32[]{:S(2)}, u32[]{:S(2)}) collective-permute-start(f32[4,256,128]{2,1,0:T(8,128)S(1)} %get-tuple-element.49), channel_id=1, source_target_pairs={{0,1},{1,0},{2,3},{3,2},{4,5},{5,4},{6,7},{7,6},{8,9},{9,8},{10,11... | collective-permute-start | bytes 1572872 | tf_op jit(solution)/shard_map/reduce_inner/ppermute | solution.py:23
  46.5 18.0 %collective-permute-start.7 = (f32[4,256,128]{2,1,0:T(8,128)S(1)}, f32[4,256,128]{2,1,0:T(8,128)S(1)}, u32[]{:S(2)}, u32[]{:S(2)}) collective-permute-start(f32[4,256,128]{2,1,0:T(8,128)S(1)} %get-tuple-element.46), channel_id=1, source_target_pairs={{0,1},{1,0},{2,3},{3,2},{4,5},{5,4},{6,7},{7,6},{8,9},{9,8},{10,11... | collective-permute-start | bytes 1572872 | tf_op jit(solution)/shard_map/reduce_inner/ppermute | solution.py:23
  48.0 10.9 %collective-permute-start.9 = (f16[1040,128]{1,0:T(8,128)(2,1)S(1)}, f16[1040,128]{1,0:T(8,128)(2,1)S(1)}, u32[]{:S(2)}, u32[]{:S(2)}) collective-permute-start(f16[1040,128]{1,0:T(8,128)(2,1)S(1)} %convert_element_type.18), channel_id=1, source_target_pairs={{0,4},{2,6},{4,0},{6,2},{1,5},{3,7},{5,1},{7,3},{8,12},{10,14},{12... | collective-permute-start | bytes 798728 | tf_op jit(solution)/shard_map/reduce_inner/ppermute | solution.py:23
  51.5 12.3 %collective-permute-start.11 = (f16[1040,128]{1,0:T(8,128)(2,1)S(1)}, f16[1040,128]{1,0:T(8,128)(2,1)S(1)}, u32[]{:S(2)}, u32[]{:S(2)}) collective-permute-start(f16[1040,128]{1,0:T(8,128)(2,1)S(1)} %convert_element_type.20), channel_id=1, source_target_pairs={{0,2},{2,4},{4,6},{6,0},{1,3},{3,5},{5,7},{7,1},{8,10},{10,12},{12... | collective-permute-start | bytes 798728 | tf_op jit(solution)/shard_map/reduce_inner/ppermute | solution.py:23
  52.8 11.6 %collective-permute-start.13 = (f16[1040,128]{1,0:T(8,128)(2,1)S(1)}, f16[1040,128]{1,0:T(8,128)(2,1)S(1)}, u32[]{:S(2)}, u32[]{:S(2)}) collective-permute-start(f16[1040,128]{1,0:T(8,128)(2,1)S(1)} %convert_element_type.22), channel_id=1, source_target_pairs={{0,6},{2,0},{4,2},{6,4},{1,7},{3,1},{5,3},{7,5},{8,14},{10,8},{12,... | collective-permute-start | bytes 798728 | tf_op jit(solution)/shard_map/reduce_inner/ppermute | solution.py:23
  64.7 9.2 %collective-permute-start.16 = (bf16[4,128,256]{2,1,0:T(8,128)(2,1)S(1)}, bf16[4,128,256]{2,1,0:T(8,128)(2,1)S(1)}, u32[]{:S(2)}, u32[]{:S(2)}) collective-permute-start(bf16[4,128,256]{2,1,0:T(8,128)(2,1)S(1)} %inner_sum.1.rest_0_), channel_id=1, source_target_pairs={{0,2},{2,4},{4,6},{6,0},{1,3},{3,5},{5,7},{7,1},{8,10},{10,12},{12... | collective-permute-start | bytes 786440 | tf_op jit(solution)/shard_map/gather_inner/ppermute | solution.py:23
  65.8 14.8 %collective-permute-start.15 = (bf16[4,128,256]{2,1,0:T(8,128)(2,1)S(1)}, bf16[4,128,256]{2,1,0:T(8,128)(2,1)S(1)}, u32[]{:S(2)}, u32[]{:S(2)}) collective-permute-start(bf16[4,128,256]{2,1,0:T(8,128)(2,1)S(1)} %inner_sum.1.rest_0_), channel_id=1, source_target_pairs={{0,4},{2,6},{4,0},{6,2},{1,5},{3,7},{5,1},{7,3},{8,12},{10,14},{12... | collective-permute-start | bytes 786440 | tf_op jit(solution)/shard_map/gather_inner/ppermute | solution.py:23
  68.9 11.8 %collective-permute-start.14 = (bf16[4,128,256]{2,1,0:T(8,128)(2,1)S(1)}, bf16[4,128,256]{2,1,0:T(8,128)(2,1)S(1)}, u32[]{:S(2)}, u32[]{:S(2)}) collective-permute-start(bf16[4,128,256]{2,1,0:T(8,128)(2,1)S(1)} %inner_sum.1.rest_0_), channel_id=1, source_target_pairs={{0,6},{2,0},{4,2},{6,4},{1,7},{3,1},{5,3},{7,5},{8,14},{10,8},{12,... | collective-permute-start | bytes 786440 | tf_op jit(solution)/shard_map/gather_inner/ppermute | solution.py:23
  69.8 11.4 %collective-permute-start.17 = (bf16[4,128,256]{2,1,0:T(8,128)(2,1)S(1)}, bf16[4,128,256]{2,1,0:T(8,128)(2,1)S(1)}, u32[]{:S(2)}, u32[]{:S(2)}) collective-permute-start(bf16[4,128,256]{2,1,0:T(8,128)(2,1)S(1)} %inner_sum.1.rest_0_), channel_id=1, source_target_pairs={{0,1},{1,0},{2,3},{3,2},{4,5},{5,4},{6,7},{7,6},{8,9},{9,8},{10,11... | collective-permute-start | bytes 786440 | tf_op jit(solution)/shard_map/gather_inner/ppermute | solution.py:23
  73.9 7.3 %collective-permute-start.20 = (bf16[4,128,256]{2,1,0:T(8,128)(2,1)S(1)}, bf16[4,128,256]{2,1,0:T(8,128)(2,1)S(1)}, u32[]{:S(2)}, u32[]{:S(2)}) collective-permute-start(bf16[4,128,256]{2,1,0:T(8,128)(2,1)S(1)} %collective-permute-done.16.rest_3_), channel_id=1, source_target_pairs={{0,1},{1,0},{2,3},{3,2},{4,5},{5,4},{6,7},{7,6},{8,9},{9,8},{10,11... | collective-permute-start | bytes 786440 | tf_op jit(solution)/shard_map/gather_inner/ppermute | solution.py:23
  80.7 1.5 collective-permute-start.19
  80.7 1.9 %collective-permute-start.18 = (bf16[4,128,256]{2,1,0:T(8,128)(2,1)S(1)}, bf16[4,128,256]{2,1,0:T(8,128)(2,1)S(1)}, u32[]{:S(2)}, u32[]{:S(2)}) collective-permute-start(bf16[4,128,256]{2,1,0:T(8,128)(2,1)S(1)} %collective-permute-done.14.rest_1_), channel_id=1, source_target_pairs={{0,1},{1,0},{2,3},{3,2},{4,5},{5,4},{6,7},{7,6},{8,9},{9,8},{10,11... | collective-permute-start | bytes 786440 | tf_op jit(solution)/shard_map/gather_inner/ppermute | solution.py:23
  84.7 10.5 %collective-permute-start.21 = (bf16[8,128,256]{2,1,0:T(8,128)(2,1)S(1)}, bf16[8,128,256]{2,1,0:T(8,128)(2,1)S(1)}, u32[]{:S(2)}, u32[]{:S(2)}) collective-permute-start(bf16[8,128,256]{2,1,0:T(8,128)(2,1)S(1)} %get-tuple-element.50), channel_id=1, source_target_pairs={{0,8},{1,33},{2,10},{3,35},{4,12},{5,37},{6,14},{7,39},{8,16},{9,4... | collective-permute-start | bytes 1572872 | tf_op jit(solution)/shard_map/reduce_outer/ppermute | solution.py:34
  85.5 9.7 %collective-permute-start.22 = (bf16[8,128,256]{2,1,0:T(8,128)(2,1)S(1)}, bf16[8,128,256]{2,1,0:T(8,128)(2,1)S(1)}, u32[]{:S(2)}, u32[]{:S(2)}) collective-permute-start(bf16[8,128,256]{2,1,0:T(8,128)(2,1)S(1)} %get-tuple-element.51), channel_id=1, source_target_pairs={{0,24},{1,97},{2,26},{3,99},{4,28},{5,101},{6,30},{7,103},{8,0},{9... | collective-permute-start | bytes 1572872 | tf_op jit(solution)/shard_map/reduce_outer/ppermute | solution.py:34
  95.5 16.1 %collective-permute-start.23 = (bf16[16,128,256]{2,1,0:T(8,128)(2,1)S(1)}, bf16[16,128,256]{2,1,0:T(8,128)(2,1)S(1)}, u32[]{:S(2)}, u32[]{:S(2)}) collective-permute-start(bf16[16,128,256]{2,1,0:T(8,128)(2,1)S(1)} %get-tuple-element.52), channel_id=1, source_target_pairs={{0,8},{1,33},{2,10},{3,35},{4,12},{5,37},{6,14},{7,39},{8,16},{9,4... | collective-permute-start | bytes 3145736 | tf_op jit(solution)/shard_map/reduce_outer/ppermute | solution.py:34
  95.5 16.0 %collective-permute-start.24 = (bf16[16,128,256]{2,1,0:T(8,128)(2,1)S(1)}, bf16[16,128,256]{2,1,0:T(8,128)(2,1)S(1)}, u32[]{:S(2)}, u32[]{:S(2)}) collective-permute-start(bf16[16,128,256]{2,1,0:T(8,128)(2,1)S(1)} %get-tuple-element.53), channel_id=1, source_target_pairs={{0,24},{1,97},{2,26},{3,99},{4,28},{5,101},{6,30},{7,103},{8,0},{9... | collective-permute-start | bytes 3145736 | tf_op jit(solution)/shard_map/reduce_outer/ppermute | solution.py:34
  111.8 7.7 %collective-permute-start.25 = (bf16[4,128,256]{2,1,0:T(8,128)(2,1)S(1)}, bf16[4,128,256]{2,1,0:T(8,128)(2,1)S(1)}, u32[]{:S(2)}, u32[]{:S(2)}) collective-permute-start(bf16[4,128,256]{2,1,0:T(8,128)(2,1)S(1)} %get-tuple-element.55), channel_id=1, source_target_pairs={{0,32},{1,9},{2,34},{3,11},{4,36},{5,13},{6,38},{7,15},{8,40},{9,1... | collective-permute-start | bytes 786440 | tf_op jit(solution)/shard_map/reduce_outer/ppermute | solution.py:34
  111.9 10.4 %collective-permute-start.26 = (bf16[4,128,256]{2,1,0:T(8,128)(2,1)S(1)}, bf16[4,128,256]{2,1,0:T(8,128)(2,1)S(1)}, u32[]{:S(2)}, u32[]{:S(2)}) collective-permute-start(bf16[4,128,256]{2,1,0:T(8,128)(2,1)S(1)} %get-tuple-element.56), channel_id=1, source_target_pairs={{0,64},{1,17},{2,66},{3,19},{4,68},{5,21},{6,70},{7,23},{8,72},{9,... | collective-permute-start | bytes 786440 | tf_op jit(solution)/shard_map/reduce_outer/ppermute | solution.py:34
  115.1 8.1 %collective-permute-start.27 = (bf16[4,128,256]{2,1,0:T(8,128)(2,1)S(1)}, bf16[4,128,256]{2,1,0:T(8,128)(2,1)S(1)}, u32[]{:S(2)}, u32[]{:S(2)}) collective-permute-start(bf16[4,128,256]{2,1,0:T(8,128)(2,1)S(1)} %get-tuple-element.57), channel_id=1, source_target_pairs={{0,96},{1,25},{2,98},{3,27},{4,100},{5,29},{6,102},{7,31},{8,104},... | collective-permute-start | bytes 786440 | tf_op jit(solution)/shard_map/reduce_outer/ppermute | solution.py:34
  123.8 1.3 collective-permute-start.28
  125.2 4.3 %collective-permute-start.31 = (f32[128,128]{1,0:T(8,128)S(1)}, f32[128,128]{1,0:T(8,128)S(1)}, u32[]{:S(2)}, u32[]{:S(2)}) collective-permute-start(f32[128,128]{1,0:T(8,128)S(1)} %add.91), channel_id=1, source_target_pairs={{0,6},{2,0},{4,2},{6,4},{1,7},{3,1},{5,3},{7,5},{8,14},{10,8},{12,... | collective-permute-start | bytes 196616 | tf_op jit(solution)/shard_map/reduce_gram/ppermute | solution.py:23
  126.5 6.2 %collective-permute-start.30 = (f32[128,128]{1,0:T(8,128)S(1)}, f32[128,128]{1,0:T(8,128)S(1)}, u32[]{:S(2)}, u32[]{:S(2)}) collective-permute-start(f32[128,128]{1,0:T(8,128)S(1)} %add.91), channel_id=1, source_target_pairs={{0,2},{2,4},{4,6},{6,0},{1,3},{3,5},{5,7},{7,1},{8,10},{10,12},{12... | collective-permute-start | bytes 196616 | tf_op jit(solution)/shard_map/reduce_gram/ppermute | solution.py:23
  127.3 5.8 %collective-permute-start.29 = (f32[128,128]{1,0:T(8,128)S(1)}, f32[128,128]{1,0:T(8,128)S(1)}, u32[]{:S(2)}, u32[]{:S(2)}) collective-permute-start(f32[128,128]{1,0:T(8,128)S(1)} %add.91), channel_id=1, source_target_pairs={{0,4},{2,6},{4,0},{6,2},{1,5},{3,7},{5,1},{7,3},{8,12},{10,14},{12... | collective-permute-start | bytes 196616 | tf_op jit(solution)/shard_map/reduce_gram/ppermute | solution.py:23
  133.1 5.6 %collective-permute-start.34 = (f32[128,128]{1,0:T(8,128)S(1)}, f32[128,128]{1,0:T(8,128)S(1)}, u32[]{:S(2)}, u32[]{:S(2)}) collective-permute-start(f32[128,128]{1,0:T(8,128)S(1)} %add_add_fusion.2), channel_id=1, source_target_pairs={{0,24},{8,0},{16,8},{24,16},{1,25},{9,1},{17,9},{25,17},{2,26},{10... | collective-permute-start | bytes 196616 | tf_op jit(solution)/shard_map/reduce_gram/ppermute | solution.py:23
  136.5 6.2 %collective-permute-start.33 = (f32[128,128]{1,0:T(8,128)S(1)}, f32[128,128]{1,0:T(8,128)S(1)}, u32[]{:S(2)}, u32[]{:S(2)}) collective-permute-start(f32[128,128]{1,0:T(8,128)S(1)} %add_add_fusion.2), channel_id=1, source_target_pairs={{0,8},{8,16},{16,24},{24,0},{1,9},{9,17},{17,25},{25,1},{2,10},{10... | collective-permute-start | bytes 196616 | tf_op jit(solution)/shard_map/reduce_gram/ppermute | solution.py:23
  136.5 6.2 %collective-permute-start.32 = (f32[128,128]{1,0:T(8,128)S(1)}, f32[128,128]{1,0:T(8,128)S(1)}, u32[]{:S(2)}, u32[]{:S(2)}) collective-permute-start(f32[128,128]{1,0:T(8,128)S(1)} %add_add_fusion.2), channel_id=1, source_target_pairs={{0,16},{8,24},{16,0},{24,8},{1,17},{9,25},{17,1},{25,9},{2,18},{10... | collective-permute-start | bytes 196616 | tf_op jit(solution)/shard_map/reduce_gram/ppermute | solution.py:23
  142.7 4.8 %collective-permute-start.37 = (f32[128,128]{1,0:T(8,128)S(1)}, f32[128,128]{1,0:T(8,128)S(1)}, u32[]{:S(2)}, u32[]{:S(2)}) collective-permute-start(f32[128,128]{1,0:T(8,128)S(1)} %add_add_fusion.1), channel_id=1, source_target_pairs={{0,96},{32,0},{64,32},{96,64},{1,97},{33,1},{65,33},{97,65},{2,98}... | collective-permute-start | bytes 196616 | tf_op jit(solution)/shard_map/reduce_gram/ppermute | solution.py:23
  145.4 6.2 %collective-permute-start.36 = (f32[128,128]{1,0:T(8,128)S(1)}, f32[128,128]{1,0:T(8,128)S(1)}, u32[]{:S(2)}, u32[]{:S(2)}) collective-permute-start(f32[128,128]{1,0:T(8,128)S(1)} %add_add_fusion.1), channel_id=1, source_target_pairs={{0,32},{32,64},{64,96},{96,0},{1,33},{33,65},{65,97},{97,1},{2,34}... | collective-permute-start | bytes 196616 | tf_op jit(solution)/shard_map/reduce_gram/ppermute | solution.py:23
  145.4 6.2 %collective-permute-start.35 = (f32[128,128]{1,0:T(8,128)S(1)}, f32[128,128]{1,0:T(8,128)S(1)}, u32[]{:S(2)}, u32[]{:S(2)}) collective-permute-start(f32[128,128]{1,0:T(8,128)S(1)} %add_add_fusion.1), channel_id=1, source_target_pairs={{0,64},{32,96},{64,0},{96,32},{1,65},{33,97},{65,1},{97,33},{2,66}... | collective-permute-start | bytes 196616 | tf_op jit(solution)/shard_map/reduce_gram/ppermute | solution.py:23

commit v8 on v7

--- a/solution.py
+++ b/solution.py
@@ -27,6 +27,8 @@
     names = AXES[:3]
     pairs = []
     for place in itertools.product(*(range(SIZES[name]) for name in AXES)):
+        if axes[place[3]] is None:
+            continue
         there = list(place)
         at = names.index(axes[place[3]])
         there[at] = (there[at] + step) % SIZES[names[at]]
@@ -159,12 +161,15 @@
     )
 
 
-def forward_near_kernel(counts, near, tiles, first, left, right, total, held, sems):
-    copies = load_pieces([first, left], held, sems)
-    last = pltpu.make_async_copy(right, held.at[pl.ds(48, 16)], sems.at[2])
-    last.start()
+def forward_near_kernel(counts, near, tiles, *rest):
+    pieces, (total, held, sems) = rest[:6], rest[6:]
+    copies = []
+    for i, at in enumerate((0, 8, 16, 24, 48, 56)):
+        copies.append(pltpu.make_async_copy(pieces[i], held.at[pl.ds(at, 8)], sems.at[i]))
+    for one in copies:
+        one.start()
     total[...] = jnp.zeros_like(total)
-    for one in copies + [last]:
+    for one in copies:
         one.wait()
 
     def body(slot, row, col):
@@ -177,11 +182,11 @@
     return pl.pallas_call(
         forward_near_kernel,
         out_shape=jax.ShapeDtypeStruct((33, SIDE, RANK), F32),
-        in_specs=scalars(2) + whole(1) + anywhere(3),
+        in_specs=scalars(2) + whole(1) + anywhere(6),
         out_specs=whole(1)[0],
         scratch_shapes=[
             pltpu.VMEM((65, SIDE, RANK), BF16),
-            pltpu.SemaphoreType.DMA((3,)),
+            pltpu.SemaphoreType.DMA((6,)),
         ],
         compiler_params=limits(8),
         cost_estimate=product_cost(0.75),
@@ -253,7 +258,7 @@
 
 
 def backward_near_kernel(counts, near, tiles, *rest):
-    pieces, (total, held, sems) = rest[:8], rest[8:]
+    pieces, (total, right, left, held, sems) = rest[:8], rest[8:]
     copies = load_pieces(pieces, held, sems)
     total[...] = jnp.zeros_like(total)
     for one in copies:
@@ -263,14 +268,17 @@
         total[col] += dot(held[row], tiles[slot])
 
     listed(counts[0], near, 32, body)
+    right[...] = total[pl.ds(24, 8)].astype(BF16)
+    left[...] = total[pl.ds(48, 8)].astype(BF16)
 
 
 def backward_near(counts, near, tiles, pieces):
+    part = jax.ShapeDtypeStruct((8, RANK, SIDE), BF16)
     return pl.pallas_call(
         backward_near_kernel,
-        out_shape=jax.ShapeDtypeStruct((65, RANK, SIDE), F32),
+        out_shape=(jax.ShapeDtypeStruct((65, RANK, SIDE), F32), part, part),
         in_specs=scalars(2) + whole(1) + anywhere(8),
-        out_specs=whole(1)[0],
+        out_specs=tuple(whole(3)),
         scratch_shapes=[
             pltpu.VMEM((33, RANK, SIDE), BF16),
             pltpu.SemaphoreType.DMA((8,)),
@@ -322,47 +330,37 @@
     )(keep, came, *parts)
 
 
-def relay_kernel(total, a, b, right, left):
-    low, high = pl.ds(0, 8), pl.ds(8, 8)
-    right[low] = (total[pl.ds(16, 8)] + a[...].astype(F32)).astype(BF16)
-    right[high] = total[pl.ds(24, 8)].astype(BF16)
-    left[low] = total[pl.ds(48, 8)].astype(BF16)
-    left[high] = (total[pl.ds(56, 8)] + b[...].astype(F32)).astype(BF16)
-
-
-def relay_sum(total, came):
-    part = jax.ShapeDtypeStruct((16, RANK, SIDE), BF16)
-    return pl.pallas_call(
-        relay_kernel,
-        out_shape=(part, part),
+def relay_sum(total, came, at):
+    def kernel(total, came, out):
+        out[...] = (total[pl.ds(at, 8)] + came[...].astype(F32)).astype(BF16)
+
+    return pl.pallas_call(
+        kernel,
+        out_shape=jax.ShapeDtypeStruct((8, RANK, SIDE), BF16),
+        in_specs=whole(2),
+        out_specs=whole(1)[0],
+        compiler_params=limits(6),
+        name="relay_sum",
+    )(total, came)
+
+
+def middle_sum(total, came, at):
+    def kernel(total, a, b, *outs):
+        for d, out in enumerate(outs):
+            here = pl.ds(4 * d, 4)
+            one = total[pl.ds(at + 4 * d, 4)] + (a[here].astype(F32) + b[here].astype(F32))
+            out[...] = one.astype(out.dtype)
+
+    return pl.pallas_call(
+        kernel,
+        out_shape=tuple(
+            jax.ShapeDtypeStruct((4, RANK, SIDE), F32 if at + d == 0 else BF16) for d in range(2)
+        ),
         in_specs=whole(3),
         out_specs=tuple(whole(2)),
         compiler_params=limits(6),
-        name="relay_sum",
-    )(total, *came)
-
-
-def middle_kernel(total, a, b, keep, *aways):
-    for d in range(4):
-        at = pl.ds(4 * d, 4)
-        one = total[at] + (a[at].astype(F32) + b[at].astype(F32))
-        if d == 0:
-            keep[...] = one
-        else:
-            aways[d - 1][...] = one.astype(BF16)
-
-
-def middle_sum(total, came):
-    part = jax.ShapeDtypeStruct((4, RANK, SIDE), BF16)
-    keep, *aways = pl.pallas_call(
-        middle_kernel,
-        out_shape=(jax.ShapeDtypeStruct((4, RANK, SIDE), F32),) + (part,) * 3,
-        in_specs=whole(3),
-        out_specs=tuple(whole(4)),
-        compiler_params=limits(6),
         name="middle_sum",
     )(total, *came)
-    return keep, aways
 
 
 def exact_dot(a, b, dims):
@@ -491,14 +489,18 @@
 
     with jax.named_scope("gather_basis"):
         near = [basis_in] + [cross(basis_in, near_axes, -d) for d in (1, 2, 3)]
-        near, first_tiles, row_at, col_at = lax.optimization_barrier((near, tiles, row_at, col_at))
-        first = jnp.concatenate(near, axis=0).reshape(16, SIDE, RANK)
-        right, left = cross(first, far_axes, 1), cross(first, far_axes, -1)
-        held, counts, near_list, far_list = plan_tiles(tile_count, row_at, col_at, first_tiles)
-        right, left, held = lax.optimization_barrier((right, left, held))
-        over = (cross(right[:8], far_axes, 1), cross(left[8:], far_axes, -1))
-
-    keep = forward_near(counts, near_list, held, (first, left, right))
+        held, counts, near_list, far_list = plan_tiles(tile_count, row_at, col_at, tiles)
+        near, held = lax.optimization_barrier((near, held))
+        low, high = (
+            jnp.concatenate(pair, axis=0).reshape(8, SIDE, RANK) for pair in (near[:2], near[2:])
+        )
+        right_low, left_high = cross(low, far_axes, 1), cross(high, far_axes, -1)
+        left_low, right_high = cross(low, far_axes, -1), cross(high, far_axes, 1)
+        over = (cross(right_low, far_axes, 1), cross(left_high, far_axes, -1))
+
+    keep = forward_near(
+        counts, near_list, held, (low, high, left_low, left_high, right_low, right_high)
+    )
     keep, *aways = forward_far(counts, far_list, held, over, keep)
 
     with jax.named_scope("reduce_inner"):
@@ -515,19 +517,22 @@
     aways = backward_far(counts, far_list, held, mine + theirs)
 
     with jax.named_scope("reduce_outer"):
-        came = (cross(aways[0], far_axes, 1), cross(aways[1], far_axes, -1))
-        total = backward_near(counts, near_list, held, mine + theirs)
-        right, left = relay_sum(total, came)
-        came = (cross(right, far_axes, 1), cross(left, far_axes, -1))
-        keep, aways = middle_sum(total, came)
-        came = [cross(one, near_axes, d) for d, one in zip((1, 2, 3), aways)]
+        over = (cross(aways[0], far_axes, 1), cross(aways[1], far_axes, -1))
+        total, right_high, left_low = backward_near(counts, near_list, held, mine + theirs)
+        right_high, left_low = cross(right_high, far_axes, 1), cross(left_low, far_axes, -1)
+        right_low = cross(relay_sum(total, over[0], 16), far_axes, 1)
+        left_high = cross(relay_sum(total, over[1], 56), far_axes, -1)
+        keep, one = middle_sum(total, (right_low, left_low), 0)
+        two, three = middle_sum(total, (right_high, left_high), 8)
+        came = [cross(part, near_axes, d) for d, part in ((1, one), (2, two), (3, three))]
         outer, gram = outer_sum(keep, came)
 
     with jax.named_scope("reduce_gram"):
-        gram = gram + send(gram, "core", 1)
+        gram = gram + lax.ppermute(gram, "core", [(0, 1)])
         for axis in ("z", "y", "x"):
-            parts = [send(gram, axis, d) for d in (1, 2, 3)]
+            parts = [cross(gram, (None, axis), d) for d in (1, 2, 3)]
             gram = (gram + parts[1]) + (parts[0] + parts[2])
+        gram = jnp.where(core == 1, gram, lax.ppermute(gram, "core", [(1, 0)]))
 
     entities = basis_in.shape[0] * 128
     return finish(gram, outer, entities)

time: 158 us -> 171 us (1.082)
  waiting for transfers between devices: 81 us -> 94.9 us
  Pallas kernels: 24.8 us -> 21.7 us
    ppermute x0 -> x2, waiting for transfers between devices: none -> 33 us  [the longest x1 32.1 us: shards(): gram = jnp.where(core == 1, gram, lax.ppermute(gram, 'core', [(1, 0)]))]
    ppermute x24 -> x14, starting transfers between devices: 26.4 us -> 11.8 us  [send(): lax.ppermute(array, axis, [(i, (i + step) % size) for i in range(size)])]
    ppermute x14 -> x27, starting transfers between devices: 21.2 us -> 34.7 us  [cross(): return lax.ppermute(array, AXES, pairs)]
    ppermute x24 -> x14, waiting for transfers between devices: 36.9 us -> 24.6 us  [send(): lax.ppermute(array, axis, [(i, (i + step) % size) for i in range(size)])]
    ppermute x14 -> x27, waiting for transfers between devices: 44.1 us -> 37.3 us  [cross(): return lax.ppermute(array, AXES, pairs)]
    ppermute x0 -> x2, starting transfers between devices: none -> 2.59 us  [the longest x1 1.29 us: shards(): gram = gram + lax.ppermute(gram, 'core', [(0, 1)])]
    pallas_call x3 -> x5, Pallas kernels: 3.85 us -> 3.07 us  [the longest x1 2.48 us: backward_near(): pl.pallas_call(backward_near_kernel, out_shape=(jax.ShapeDtypeStruct((65,...]
  transfers between devices with their start and end apart: 38 -> 43, of which waited for: 27 -> 21; matrix products, arithmetic and copies ran while one was open for 1% -> 1% of each run, Pallas kernels for 9% -> 6%
where the time goes in v8:
time: 171 us; the launch traced here: 169 us
  waiting for transfers between devices  94.9 us (55%)
  starting transfers between devices  49.1 us (29%)
  Pallas kernels  21.7 us (13%)
  between operations  1.73 us (1%)
    ppermute x27, waiting for transfers between devices, cross(): return lax.ppermute(array, AXES, pairs)  37.3 us
    ppermute x27, starting transfers between devices, cross(): return lax.ppermute(array, AXES, pairs)  34.7 us
    ppermute x1, waiting for transfers between devices, shards(): gram = jnp.where(core == 1, gram, lax.ppermute(gram, 'core', [(1, 0)]))  32.1 us
    ppermute x14, waiting for transfers between devices, send(): lax.ppermute(array, axis, [(i, (i + step) % size) for i in range(size)])  24.6 us
    ppermute x14, starting transfers between devices, send(): lax.ppermute(array, axis, [(i, (i + step) % size) for i in range(size)])  11.8 us
    pallas_call x1, Pallas kernels, finish(): pl.pallas_call(kernel, out_shape=(jax.ShapeDtypeStruct((4 * SIDE, RANK),...  5.5 us
    pallas_call x1, Pallas kernels, plan_tiles(): pl.pallas_call(plan_kernel, out_shape=(jax.ShapeDtypeStruct(tiles.shape,...  4.72 us
  transfers between devices with their start and end apart: 43, of which 21 were waited for; matrix products, arithmetic and copies ran while one was open for 1% of the time, Pallas kernels for 6%

profile of v8, /device:TPU:0, one launch (start us, length us, event | category | flops | bytes accessed | tf_op | source)
XLA Modules:
  0.0 168.6 jit_solution(14975130719635816765)
XLA Ops:
  0.6 3.2 %collective-permute-start.1 = (bf16[1024,128]{1,0:T(8,128)(2,1)}, bf16[1024,128]{1,0:T(8,128)(2,1)S(1)}, u32[]{:S(2)}, u32[]{:S(2)}) collective-permute-start(bf16[1024,128]{1,0:T(8,128)(2,1)} %param.4), channel_id=1, source_target_pairs={{0,64},{1,17},{2,66},{3,19},{4,68},{5,21},{6,70},{7,23},{8,72},{9,... | collective-permute-start | bytes 786440 | tf_op jit(solution)/shard_map/gather_basis/ppermute | solution.py:36
  3.8 1.1 collective-permute-start
  5.0 0.9 collective-permute-start.2
  5.8 0.8 fusion.10
  7.3 4.7 %plan_tiles.1 = (bf16[160,256,256]{2,1,0:T(8,128)(2,1)S(1)}, s32[2]{0:T(128)S(1)}, s32[192]{0:T(256)S(1)}, s32[192]{0:T(256)S(1)}) custom-call(s32[1]{0:T(128)S(6)} %copy.8.count, s32[160]{0:T(256)S(1)} %get-tuple-element.55.row_at, s32[160]{0:T(256)S(1)} %get-tuple-element.54.col_at, bf16[160,256,256]{2,1,0:T(8,128)(2,1)} %tiles.1), custom_call_target="tpu_custom_call" | custom-call | bytes 41943040 | tf_op jit(solution)/shard_map/gather_basis/plan_tiles/pallas_call | solution.py:129
  12.1 0.7 collective-permute-done.2
  12.8 3.6 %collective-permute-start.5 = (bf16[8,256,128]{2,1,0:T(8,128)(2,1)S(1)}, bf16[8,256,128]{2,1,0:T(8,128)(2,1)S(1)}, u32[]{:S(2)}, u32[]{:S(2)}) collective-permute-start(bf16[8,256,128]{2,1,0:T(8,128)(2,1)S(1)} %bitcast.4), channel_id=1, source_target_pairs={{0,24},{1,97},{2,26},{3,99},{4,28},{5,101},{6,30},{7,103},{8,0},{9... | collective-permute-start | bytes 1572872 | tf_op jit(solution)/shard_map/gather_basis/ppermute | solution.py:36
  16.7 3.2 %collective-permute-start.7 = (bf16[8,256,128]{2,1,0:T(8,128)(2,1)S(1)}, bf16[8,256,128]{2,1,0:T(8,128)(2,1)S(1)}, u32[]{:S(2)}, u32[]{:S(2)}) collective-permute-start(bf16[8,256,128]{2,1,0:T(8,128)(2,1)S(1)} %bitcast.8), channel_id=1, source_target_pairs={{0,24},{1,97},{2,26},{3,99},{4,28},{5,101},{6,30},{7,103},{8,0},{9... | collective-permute-start | bytes 1572872 | tf_op jit(solution)/shard_map/gather_basis/ppermute | solution.py:36
  19.8 3.3 %collective-permute-done.5.rest_3_ = bf16[8,256,128]{2,1,0:T(8,128)(2,1)S(1)} collective-permute-done((bf16[8,256,128]{2,1,0:T(8,128)(2,1)S(1)}, bf16[8,256,128]{2,1,0:T(8,128)(2,1)S(1)}, u32[]{:S(2)}, u32[]{:S(2)}) %collective-permute-start.5) | collective-permute-done | bytes 524320 | tf_op jit(solution)/shard_map/gather_basis/ppermute | solution.py:36
  23.1 3.7 %collective-permute-start.6 = (bf16[8,256,128]{2,1,0:T(8,128)(2,1)S(1)}, bf16[8,256,128]{2,1,0:T(8,128)(2,1)S(1)}, u32[]{:S(2)}, u32[]{:S(2)}) collective-permute-start(bf16[8,256,128]{2,1,0:T(8,128)(2,1)S(1)} %collective-permute-done.5.rest_3_), channel_id=1, source_target_pairs={{0,24},{1,97},{2,26},{3,99},{4,28},{5,101},{6,30},{7,103},{8,0},{9... | collective-permute-start | bytes 1572872 | tf_op jit(solution)/shard_map/gather_basis/ppermute | solution.py:36
  26.9 5.6 %collective-permute-done.8.rest_5_ = bf16[8,256,128]{2,1,0:T(8,128)(2,1)S(1)} collective-permute-done((bf16[8,256,128]{2,1,0:T(8,128)(2,1)S(1)}, bf16[8,256,128]{2,1,0:T(8,128)(2,1)S(1)}, u32[]{:S(2)}, u32[]{:S(2)}) %collective-permute-start.8) | collective-permute-done | bytes 524320 | tf_op jit(solution)/shard_map/gather_basis/ppermute | solution.py:36
  32.5 2.4 %forward_near.1.before = f32[33,256,128]{2,1,0:T(8,128)S(1)} custom-call(s32[2]{0:T(128)S(1)} %get-tuple-element.27.counts, s32[192]{0:T(256)S(1)} %get-tuple-element.28.near, bf16[160,256,256]{2,1,0:T(8,128)(2,1)S(1)} %get-tuple-element.30.tiles, bf16[8,256,128]{2,1,0:T(8,128)(2,1)S(1)} %bitcast.9, bf16[8,256,128]{2,1,0:T(8,128)(2,1)S(1)} %bitcast.6, ...), custom_call_target="tpu_custom_call" | custom-call | flops 2013265920 | bytes 1048576 | tf_op jit(solution)/shard_map/forward_near/pallas_call | solution.py:182
  35.0 3.2 %collective-permute-done.4.a = bf16[8,256,128]{2,1,0:T(8,128)(2,1)S(1)} collective-permute-done((bf16[8,256,128]{2,1,0:T(8,128)(2,1)S(1)}, bf16[8,256,128]{2,1,0:T(8,128)(2,1)S(1)}, u32[]{:S(2)}, u32[]{:S(2)}) %collective-permute-start.4) | collective-permute-done | bytes 524320 | tf_op jit(solution)/shard_map/gather_basis/ppermute | solution.py:36
  38.1 2.3 %forward_far.1 = (f32[33,256,128]{2,1,0:T(8,128)S(1)}, f32[4,256,128]{2,1,0:T(8,128)S(1)}, f32[4,256,128]{2,1,0:T(8,128)S(1)}, f32[4,256,128]{2,1,0:T(8,128)S(1)}, f32[4,256,128]{2,1,0:T(8,128)S(1)}) custom-call(s32[2]{0:T(128)S(1)} %get-tuple-element.27.counts, s32[192]{0:T(256)S(1)} %get-tuple-element.31.far, ...), custom_call_target="tpu_custom_call", output_to_operand_aliasing={{0}: (5, {})} | custom-call | tf_op jit(solution)/shard_map/forward_far/pallas_call | solution.py:212
  40.5 0.5 collective-permute-start.12
  41.1 0.4 collective-permute-start.9
  41.5 0.9 collective-permute-done.10.came
  42.4 0.2 core_sum.3
  42.7 2.7 %collective-permute-start.11 = (f16[1040,128]{1,0:T(8,128)(2,1)S(1)}, f16[1040,128]{1,0:T(8,128)(2,1)S(1)}, u32[]{:S(2)}, u32[]{:S(2)}) collective-permute-start(f16[1040,128]{1,0:T(8,128)(2,1)S(1)} %convert_element_type.18), channel_id=1, source_target_pairs={{0,4},{2,6},{4,0},{6,2},{1,5},{3,7},{5,1},{7,3},{8,12},{10,14},{12... | collective-permute-start | bytes 798728 | tf_op jit(solution)/shard_map/reduce_inner/ppermute | solution.py:23
  45.4 0.2 core_sum.4
  45.6 2.3 %collective-permute-start.13 = (f16[1040,128]{1,0:T(8,128)(2,1)S(1)}, f16[1040,128]{1,0:T(8,128)(2,1)S(1)}, u32[]{:S(2)}, u32[]{:S(2)}) collective-permute-start(f16[1040,128]{1,0:T(8,128)(2,1)S(1)} %convert_element_type.20), channel_id=1, source_target_pairs={{0,2},{2,4},{4,6},{6,0},{1,3},{3,5},{5,7},{7,1},{8,10},{10,12},{12... | collective-permute-start | bytes 798728 | tf_op jit(solution)/shard_map/reduce_inner/ppermute | solution.py:23
  48.0 0.2 core_sum.5
  48.2 1.0 collective-permute-start.15
  49.3 4.3 %collective-permute-done.11 = f16[1040,128]{1,0:T(8,128)(2,1)S(1)} collective-permute-done((f16[1040,128]{1,0:T(8,128)(2,1)S(1)}, f16[1040,128]{1,0:T(8,128)(2,1)S(1)}, u32[]{:S(2)}, u32[]{:S(2)}) %collective-permute-start.11) | collective-permute-done | bytes 266272 | tf_op jit(solution)/shard_map/reduce_inner/ppermute | solution.py:23
  53.6 4.8 %collective-permute-done.13 = f16[1040,128]{1,0:T(8,128)(2,1)S(1)} collective-permute-done((f16[1040,128]{1,0:T(8,128)(2,1)S(1)}, f16[1040,128]{1,0:T(8,128)(2,1)S(1)}, u32[]{:S(2)}, u32[]{:S(2)}) %collective-permute-start.13) | collective-permute-done | bytes 266272 | tf_op jit(solution)/shard_map/reduce_inner/ppermute | solution.py:23
  58.4 1.4 collective-permute-done.15
  59.8 0.3 inner_sum.1.rest_0_
  60.1 0.3 collective-permute-start.18
  60.4 3.8 %collective-permute-start.17 = (bf16[4,128,256]{2,1,0:T(8,128)(2,1)S(1)}, bf16[4,128,256]{2,1,0:T(8,128)(2,1)S(1)}, u32[]{:S(2)}, u32[]{:S(2)}) collective-permute-start(bf16[4,128,256]{2,1,0:T(8,128)(2,1)S(1)} %inner_sum.1.rest_0_), channel_id=1, source_target_pairs={{0,4},{2,6},{4,0},{6,2},{1,5},{3,7},{5,1},{7,3},{8,12},{10,14},{12... | collective-permute-start | bytes 786440 | tf_op jit(solution)/shard_map/gather_inner/ppermute | solution.py:23
  64.3 5.0 %collective-permute-done.18.rest_3_ = bf16[4,128,256]{2,1,0:T(8,128)(2,1)S(1)} collective-permute-done((bf16[4,128,256]{2,1,0:T(8,128)(2,1)S(1)}, bf16[4,128,256]{2,1,0:T(8,128)(2,1)S(1)}, u32[]{:S(2)}, u32[]{:S(2)}) %collective-permute-start.18) | collective-permute-done | bytes 262176 | tf_op jit(solution)/shard_map/gather_inner/ppermute | solution.py:23
  69.3 6.8 %collective-permute-done.17.rest_2_ = bf16[4,128,256]{2,1,0:T(8,128)(2,1)S(1)} collective-permute-done((bf16[4,128,256]{2,1,0:T(8,128)(2,1)S(1)}, bf16[4,128,256]{2,1,0:T(8,128)(2,1)S(1)}, u32[]{:S(2)}, u32[]{:S(2)}) %collective-permute-start.17) | collective-permute-done | bytes 262176 | tf_op jit(solution)/shard_map/gather_inner/ppermute | solution.py:23
  76.1 0.5 collective-permute-start.20
  76.6 1.0 collective-permute-done.21.rest_6_
  77.6 0.4 collective-permute-done.20.rest_5_
  78.0 2.3 %backward_far.1 = (bf16[8,128,256]{2,1,0:T(8,128)(2,1)S(1)}, bf16[8,128,256]{2,1,0:T(8,128)(2,1)S(1)}) custom-call(s32[2]{0:T(128)S(1)} %get-tuple-element.27.counts, s32[192]{0:T(256)S(1)} %get-tuple-element.31.far, bf16[160,256,256]{2,1,0:T(8,128)(2,1)S(1)} %get-tuple-element.30.tiles, bf16[4,128,256]{2,1,0:T(8,128)(2,1)S(1)} %inner_sum.1.rest_0_, ...), custom_call_target="tpu_custom_call" | custom-call | tf_op jit(solution)/shard_map/backward_far/pallas_call | solution.py:245
  80.3 3.2 %collective-permute-start.28 = (bf16[8,128,256]{2,1,0:T(8,128)(2,1)S(1)}, bf16[8,128,256]{2,1,0:T(8,128)(2,1)S(1)}, u32[]{:S(2)}, u32[]{:S(2)}) collective-permute-start(bf16[8,128,256]{2,1,0:T(8,128)(2,1)S(1)} %get-tuple-element.47), channel_id=1, source_target_pairs={{0,24},{1,97},{2,26},{3,99},{4,28},{5,101},{6,30},{7,103},{8,0},{9... | collective-permute-start | bytes 1572872 | tf_op jit(solution)/shard_map/reduce_outer/ppermute | solution.py:36
  83.6 2.5 %backward_near.1 = (f32[65,128,256]{2,1,0:T(8,128)S(1)}, bf16[8,128,256]{2,1,0:T(8,128)(2,1)S(1)}, bf16[8,128,256]{2,1,0:T(8,128)(2,1)S(1)}) custom-call(s32[2]{0:T(128)S(1)} %get-tuple-element.27.counts, s32[192]{0:T(256)S(1)} %get-tuple-element.28.near, bf16[160,256,256]{2,1,0:T(8,128)(2,1)S(1)} %get-tuple-element.30.tiles, ...), custom_call_target="tpu_custom_call" | custom-call | flops 2013265920 | bytes 1048576 | tf_op jit(solution)/shard_map/reduce_outer/backward_near/pallas_call | solution.py:277
  86.0 1.1 collective-permute-start.25
  87.2 3.6 %collective-permute-done.23.came = bf16[8,128,256]{2,1,0:T(8,128)(2,1)S(1)} collective-permute-done((bf16[8,128,256]{2,1,0:T(8,128)(2,1)S(1)}, bf16[8,128,256]{2,1,0:T(8,128)(2,1)S(1)}, u32[]{:S(2)}, u32[]{:S(2)}) %collective-permute-start.23) | collective-permute-done | bytes 524320 | tf_op jit(solution)/shard_map/reduce_outer/ppermute | solution.py:36
  91.1 3.3 %collective-permute-start.29 = (bf16[8,128,256]{2,1,0:T(8,128)(2,1)S(1)}, bf16[8,128,256]{2,1,0:T(8,128)(2,1)S(1)}, u32[]{:S(2)}, u32[]{:S(2)}) collective-permute-start(bf16[8,128,256]{2,1,0:T(8,128)(2,1)S(1)} %relay_sum.3), channel_id=1, source_target_pairs={{0,24},{1,97},{2,26},{3,99},{4,28},{5,101},{6,30},{7,103},{8,0},{9... | collective-permute-start | bytes 1572872 | tf_op jit(solution)/shard_map/reduce_outer/ppermute | solution.py:36
  94.4 1.5 collective-permute-done.25.b
  95.9 5.4 %collective-permute-done.24.a = bf16[8,128,256]{2,1,0:T(8,128)(2,1)S(1)} collective-permute-done((bf16[8,128,256]{2,1,0:T(8,128)(2,1)S(1)}, bf16[8,128,256]{2,1,0:T(8,128)(2,1)S(1)}, u32[]{:S(2)}, u32[]{:S(2)}) %collective-permute-start.24) | collective-permute-done | bytes 524320 | tf_op jit(solution)/shard_map/reduce_outer/ppermute | solution.py:36
  101.3 0.2 middle_sum.2
  101.6 8.2 %collective-permute-done.27.a = bf16[8,128,256]{2,1,0:T(8,128)(2,1)S(1)} collective-permute-done((bf16[8,128,256]{2,1,0:T(8,128)(2,1)S(1)}, bf16[8,128,256]{2,1,0:T(8,128)(2,1)S(1)}, u32[]{:S(2)}, u32[]{:S(2)}) %collective-permute-start.27) | collective-permute-done | bytes 524320 | tf_op jit(solution)/shard_map/reduce_outer/ppermute | solution.py:36
  109.7 0.2 middle_sum.3
  109.9 4.3 %collective-permute-start.30 = (bf16[4,128,256]{2,1,0:T(8,128)(2,1)S(1)}, bf16[4,128,256]{2,1,0:T(8,128)(2,1)S(1)}, u32[]{:S(2)}, u32[]{:S(2)}) collective-permute-start(bf16[4,128,256]{2,1,0:T(8,128)(2,1)S(1)} %get-tuple-element.48), channel_id=1, source_target_pairs={{0,64},{1,17},{2,66},{3,19},{4,68},{5,21},{6,70},{7,23},{8,72},{9,... | collective-permute-start | bytes 786440 | tf_op jit(solution)/shard_map/reduce_outer/ppermute | solution.py:36
  114.3 0.6 collective-permute-start.31
  114.8 3.8 %collective-permute-done.30.b = bf16[4,128,256]{2,1,0:T(8,128)(2,1)S(1)} collective-permute-done((bf16[4,128,256]{2,1,0:T(8,128)(2,1)S(1)}, bf16[4,128,256]{2,1,0:T(8,128)(2,1)S(1)}, u32[]{:S(2)}, u32[]{:S(2)}) %collective-permute-start.30) | collective-permute-done | bytes 262176 | tf_op jit(solution)/shard_map/reduce_outer/ppermute | solution.py:36
  118.6 2.0 %collective-permute-done.31.c = bf16[4,128,256]{2,1,0:T(8,128)(2,1)S(1)} collective-permute-done((bf16[4,128,256]{2,1,0:T(8,128)(2,1)S(1)}, bf16[4,128,256]{2,1,0:T(8,128)(2,1)S(1)}, u32[]{:S(2)}, u32[]{:S(2)}) %collective-permute-start.31) | collective-permute-done | bytes 262176 | tf_op jit(solution)/shard_map/reduce_outer/ppermute | solution.py:36
  120.6 0.6 outer_sum.1
  121.2 1.3 collective-permute-start.32
  122.5 0.9 collective-permute-done.32
  123.4 0.7 collective-permute-start.35
  124.1 0.7 collective-permute-start.34
  124.8 0.7 collective-permute-start.33
  125.5 0.7 collective-permute-start.38
  126.2 0.7 collective-permute-start.37
  126.9 0.7 collective-permute-start.36
  127.6 0.7 collective-permute-start.41
  128.3 0.7 collective-permute-start.40
  128.9 0.7 collective-permute-start.39
  129.7 1.3 collective-permute-start.42
  131.0 32.1 %collective-permute-done.42 = f32[128,128]{1,0:T(8,128)S(1)} collective-permute-done((f32[128,128]{1,0:T(8,128)S(1)}, f32[128,128]{1,0:T(8,128)S(1)}, u32[]{:S(2)}, u32[]{:S(2)}) %collective-permute-start.42) | collective-permute-done | bytes 65568 | tf_op jit(solution)/shard_map/reduce_gram/ppermute | solution.py:535
  163.1 5.5 %finish.1 = (f32[1024,128]{1,0:T(8,128)}, f32[128,128]{1,0:T(8,128)}) custom-call(f32[128,128]{1,0:T(8,128)S(1)} %broadcast_select_fusion.refs_0_, f32[4,128,256]{2,1,0:T(8,128)S(1)} %get-tuple-element.51.refs_1_), custom_call_target="tpu_custom_call" | custom-call | tf_op jit(solution)/shard_map/finish/pallas_call | solution.py:461
  (54 shorter events, 1.5 us)
Async XLA Ops:
  0.6 11.4 %collective-permute-start.1 = (bf16[1024,128]{1,0:T(8,128)(2,1)}, bf16[1024,128]{1,0:T(8,128)(2,1)S(1)}, u32[]{:S(2)}, u32[]{:S(2)}) collective-permute-start(bf16[1024,128]{1,0:T(8,128)(2,1)} %param.4), channel_id=1, source_target_pairs={{0,64},{1,17},{2,66},{3,19},{4,68},{5,21},{6,70},{7,23},{8,72},{9,... | collective-permute-start | bytes 786440 | tf_op jit(solution)/shard_map/gather_basis/ppermute | solution.py:36
  3.8 8.2 %collective-permute-start = (bf16[1024,128]{1,0:T(8,128)(2,1)}, bf16[1024,128]{1,0:T(8,128)(2,1)S(1)}, u32[]{:S(2)}, u32[]{:S(2)}) collective-permute-start(bf16[1024,128]{1,0:T(8,128)(2,1)} %param.4), channel_id=1, source_target_pairs={{0,96},{1,25},{2,98},{3,27},{4,100},{5,29},{6,102},{7,31},{8,104},... | collective-permute-start | bytes 786440 | tf_op jit(solution)/shard_map/gather_basis/ppermute | solution.py:36
  5.0 7.8 %collective-permute-start.2 = (bf16[1024,128]{1,0:T(8,128)(2,1)}, bf16[1024,128]{1,0:T(8,128)(2,1)S(1)}, u32[]{:S(2)}, u32[]{:S(2)}) collective-permute-start(bf16[1024,128]{1,0:T(8,128)(2,1)} %param.4), channel_id=1, source_target_pairs={{0,32},{1,9},{2,34},{3,11},{4,36},{5,13},{6,38},{7,15},{8,40},{9,1... | collective-permute-start | bytes 786440 | tf_op jit(solution)/shard_map/gather_basis/ppermute | solution.py:36
  7.3 9.1 %copy-start = (bf16[1024,128]{1,0:T(8,128)(2,1)S(1)}, bf16[1024,128]{1,0:T(8,128)(2,1)}, u32[]{:S(2)}) copy-start(bf16[1024,128]{1,0:T(8,128)(2,1)} %param.4) | copy-start | bytes 786436
  12.8 10.3 %collective-permute-start.5 = (bf16[8,256,128]{2,1,0:T(8,128)(2,1)S(1)}, bf16[8,256,128]{2,1,0:T(8,128)(2,1)S(1)}, u32[]{:S(2)}, u32[]{:S(2)}) collective-permute-start(bf16[8,256,128]{2,1,0:T(8,128)(2,1)S(1)} %bitcast.4), channel_id=1, source_target_pairs={{0,24},{1,97},{2,26},{3,99},{4,28},{5,101},{6,30},{7,103},{8,0},{9... | collective-permute-start | bytes 1572872 | tf_op jit(solution)/shard_map/gather_basis/ppermute | solution.py:36
  16.4 10.5 %collective-permute-start.3 = (bf16[8,256,128]{2,1,0:T(8,128)(2,1)S(1)}, bf16[8,256,128]{2,1,0:T(8,128)(2,1)S(1)}, u32[]{:S(2)}, u32[]{:S(2)}) collective-permute-start(bf16[8,256,128]{2,1,0:T(8,128)(2,1)S(1)} %bitcast.7), channel_id=1, source_target_pairs={{0,8},{1,33},{2,10},{3,35},{4,12},{5,37},{6,14},{7,39},{8,16},{9,4... | collective-permute-start | bytes 1572872 | tf_op jit(solution)/shard_map/gather_basis/ppermute | solution.py:36
  16.5 16.0 %collective-permute-start.8 = (bf16[8,256,128]{2,1,0:T(8,128)(2,1)S(1)}, bf16[8,256,128]{2,1,0:T(8,128)(2,1)S(1)}, u32[]{:S(2)}, u32[]{:S(2)}) collective-permute-start(bf16[8,256,128]{2,1,0:T(8,128)(2,1)S(1)} %bitcast.5), channel_id=1, source_target_pairs={{0,8},{1,33},{2,10},{3,35},{4,12},{5,37},{6,14},{7,39},{8,16},{9,4... | collective-permute-start | bytes 1572872 | tf_op jit(solution)/shard_map/gather_basis/ppermute | solution.py:36
  16.7 15.8 %collective-permute-start.7 = (bf16[8,256,128]{2,1,0:T(8,128)(2,1)S(1)}, bf16[8,256,128]{2,1,0:T(8,128)(2,1)S(1)}, u32[]{:S(2)}, u32[]{:S(2)}) collective-permute-start(bf16[8,256,128]{2,1,0:T(8,128)(2,1)S(1)} %bitcast.8), channel_id=1, source_target_pairs={{0,24},{1,97},{2,26},{3,99},{4,28},{5,101},{6,30},{7,103},{8,0},{9... | collective-permute-start | bytes 1572872 | tf_op jit(solution)/shard_map/gather_basis/ppermute | solution.py:36
  23.1 11.9 %collective-permute-start.6 = (bf16[8,256,128]{2,1,0:T(8,128)(2,1)S(1)}, bf16[8,256,128]{2,1,0:T(8,128)(2,1)S(1)}, u32[]{:S(2)}, u32[]{:S(2)}) collective-permute-start(bf16[8,256,128]{2,1,0:T(8,128)(2,1)S(1)} %collective-permute-done.5.rest_3_), channel_id=1, source_target_pairs={{0,24},{1,97},{2,26},{3,99},{4,28},{5,101},{6,30},{7,103},{8,0},{9... | collective-permute-start | bytes 1572872 | tf_op jit(solution)/shard_map/gather_basis/ppermute | solution.py:36
  26.9 11.2 %collective-permute-start.4 = (bf16[8,256,128]{2,1,0:T(8,128)(2,1)S(1)}, bf16[8,256,128]{2,1,0:T(8,128)(2,1)S(1)}, u32[]{:S(2)}, u32[]{:S(2)}) collective-permute-start(bf16[8,256,128]{2,1,0:T(8,128)(2,1)S(1)} %collective-permute-done.3.rest_4_), channel_id=1, source_target_pairs={{0,8},{1,33},{2,10},{3,35},{4,12},{5,37},{6,14},{7,39},{8,16},{9,4... | collective-permute-start | bytes 1572872 | tf_op jit(solution)/shard_map/gather_basis/ppermute | solution.py:36
  40.4 2.0 %collective-permute-start.10 = (f32[4,256,128]{2,1,0:T(8,128)S(1)}, f32[4,256,128]{2,1,0:T(8,128)S(1)}, u32[]{:S(2)}, u32[]{:S(2)}) collective-permute-start(f32[4,256,128]{2,1,0:T(8,128)S(1)} %get-tuple-element.38), channel_id=1, source_target_pairs={{0,1},{1,0},{2,3},{3,2},{4,5},{5,4},{6,7},{7,6},{8,9},{9,8},{10,11... | collective-permute-start | bytes 1572872 | tf_op jit(solution)/shard_map/reduce_inner/ppermute | solution.py:23
  40.5 4.9 %collective-permute-start.12 = (f32[4,256,128]{2,1,0:T(8,128)S(1)}, f32[4,256,128]{2,1,0:T(8,128)S(1)}, u32[]{:S(2)}, u32[]{:S(2)}) collective-permute-start(f32[4,256,128]{2,1,0:T(8,128)S(1)} %get-tuple-element.39), channel_id=1, source_target_pairs={{0,1},{1,0},{2,3},{3,2},{4,5},{5,4},{6,7},{7,6},{8,9},{9,8},{10,11... | collective-permute-start | bytes 1572872 | tf_op jit(solution)/shard_map/reduce_inner/ppermute | solution.py:23
  41.0 7.0 %collective-permute-start.14 = (f32[4,256,128]{2,1,0:T(8,128)S(1)}, f32[4,256,128]{2,1,0:T(8,128)S(1)}, u32[]{:S(2)}, u32[]{:S(2)}) collective-permute-start(f32[4,256,128]{2,1,0:T(8,128)S(1)} %get-tuple-element.40), channel_id=1, source_target_pairs={{0,1},{1,0},{2,3},{3,2},{4,5},{5,4},{6,7},{7,6},{8,9},{9,8},{10,11... | collective-permute-start | bytes 1572872 | tf_op jit(solution)/shard_map/reduce_inner/ppermute | solution.py:23
  41.1 18.7 %collective-permute-start.9 = (f32[4,256,128]{2,1,0:T(8,128)S(1)}, f32[4,256,128]{2,1,0:T(8,128)S(1)}, u32[]{:S(2)}, u32[]{:S(2)}) collective-permute-start(f32[4,256,128]{2,1,0:T(8,128)S(1)} %get-tuple-element.37), channel_id=1, source_target_pairs={{0,1},{1,0},{2,3},{3,2},{4,5},{5,4},{6,7},{7,6},{8,9},{9,8},{10,11... | collective-permute-start | bytes 1572872 | tf_op jit(solution)/shard_map/reduce_inner/ppermute | solution.py:23
  42.7 10.9 %collective-permute-start.11 = (f16[1040,128]{1,0:T(8,128)(2,1)S(1)}, f16[1040,128]{1,0:T(8,128)(2,1)S(1)}, u32[]{:S(2)}, u32[]{:S(2)}) collective-permute-start(f16[1040,128]{1,0:T(8,128)(2,1)S(1)} %convert_element_type.18), channel_id=1, source_target_pairs={{0,4},{2,6},{4,0},{6,2},{1,5},{3,7},{5,1},{7,3},{8,12},{10,14},{12... | collective-permute-start | bytes 798728 | tf_op jit(solution)/shard_map/reduce_inner/ppermute | solution.py:23
  45.6 12.8 %collective-permute-start.13 = (f16[1040,128]{1,0:T(8,128)(2,1)S(1)}, f16[1040,128]{1,0:T(8,128)(2,1)S(1)}, u32[]{:S(2)}, u32[]{:S(2)}) collective-permute-start(f16[1040,128]{1,0:T(8,128)(2,1)S(1)} %convert_element_type.20), channel_id=1, source_target_pairs={{0,2},{2,4},{4,6},{6,0},{1,3},{3,5},{5,7},{7,1},{8,10},{10,12},{12... | collective-permute-start | bytes 798728 | tf_op jit(solution)/shard_map/reduce_inner/ppermute | solution.py:23
  48.2 11.6 %collective-permute-start.15 = (f16[1040,128]{1,0:T(8,128)(2,1)S(1)}, f16[1040,128]{1,0:T(8,128)(2,1)S(1)}, u32[]{:S(2)}, u32[]{:S(2)}) collective-permute-start(f16[1040,128]{1,0:T(8,128)(2,1)S(1)} %convert_element_type.22), channel_id=1, source_target_pairs={{0,6},{2,0},{4,2},{6,4},{1,7},{3,1},{5,3},{7,5},{8,14},{10,8},{12,... | collective-permute-start | bytes 798728 | tf_op jit(solution)/shard_map/reduce_inner/ppermute | solution.py:23
  60.1 9.2 %collective-permute-start.18 = (bf16[4,128,256]{2,1,0:T(8,128)(2,1)S(1)}, bf16[4,128,256]{2,1,0:T(8,128)(2,1)S(1)}, u32[]{:S(2)}, u32[]{:S(2)}) collective-permute-start(bf16[4,128,256]{2,1,0:T(8,128)(2,1)S(1)} %inner_sum.1.rest_0_), channel_id=1, source_target_pairs={{0,2},{2,4},{4,6},{6,0},{1,3},{3,5},{5,7},{7,1},{8,10},{10,12},{12... | collective-permute-start | bytes 786440 | tf_op jit(solution)/shard_map/gather_inner/ppermute | solution.py:23
  60.4 15.7 %collective-permute-start.17 = (bf16[4,128,256]{2,1,0:T(8,128)(2,1)S(1)}, bf16[4,128,256]{2,1,0:T(8,128)(2,1)S(1)}, u32[]{:S(2)}, u32[]{:S(2)}) collective-permute-start(bf16[4,128,256]{2,1,0:T(8,128)(2,1)S(1)} %inner_sum.1.rest_0_), channel_id=1, source_target_pairs={{0,4},{2,6},{4,0},{6,2},{1,5},{3,7},{5,1},{7,3},{8,12},{10,14},{12... | collective-permute-start | bytes 786440 | tf_op jit(solution)/shard_map/gather_inner/ppermute | solution.py:23
  64.3 11.8 %collective-permute-start.16 = (bf16[4,128,256]{2,1,0:T(8,128)(2,1)S(1)}, bf16[4,128,256]{2,1,0:T(8,128)(2,1)S(1)}, u32[]{:S(2)}, u32[]{:S(2)}) collective-permute-start(bf16[4,128,256]{2,1,0:T(8,128)(2,1)S(1)} %inner_sum.1.rest_0_), channel_id=1, source_target_pairs={{0,6},{2,0},{4,2},{6,4},{1,7},{3,1},{5,3},{7,5},{8,14},{10,8},{12,... | collective-permute-start | bytes 786440 | tf_op jit(solution)/shard_map/gather_inner/ppermute | solution.py:23
  64.3 12.3 %collective-permute-start.19 = (bf16[4,128,256]{2,1,0:T(8,128)(2,1)S(1)}, bf16[4,128,256]{2,1,0:T(8,128)(2,1)S(1)}, u32[]{:S(2)}, u32[]{:S(2)}) collective-permute-start(bf16[4,128,256]{2,1,0:T(8,128)(2,1)S(1)} %inner_sum.1.rest_0_), channel_id=1, source_target_pairs={{0,1},{1,0},{2,3},{3,2},{4,5},{5,4},{6,7},{7,6},{8,9},{9,8},{10,11... | collective-permute-start | bytes 786440 | tf_op jit(solution)/shard_map/gather_inner/ppermute | solution.py:23
  69.3 7.3 %collective-permute-start.22 = (bf16[4,128,256]{2,1,0:T(8,128)(2,1)S(1)}, bf16[4,128,256]{2,1,0:T(8,128)(2,1)S(1)}, u32[]{:S(2)}, u32[]{:S(2)}) collective-permute-start(bf16[4,128,256]{2,1,0:T(8,128)(2,1)S(1)} %collective-permute-done.18.rest_3_), channel_id=1, source_target_pairs={{0,1},{1,0},{2,3},{3,2},{4,5},{5,4},{6,7},{7,6},{8,9},{9,8},{10,11... | collective-permute-start | bytes 786440 | tf_op jit(solution)/shard_map/gather_inner/ppermute | solution.py:23
  76.1 1.5 collective-permute-start.21
  76.1 1.9 %collective-permute-start.20 = (bf16[4,128,256]{2,1,0:T(8,128)(2,1)S(1)}, bf16[4,128,256]{2,1,0:T(8,128)(2,1)S(1)}, u32[]{:S(2)}, u32[]{:S(2)}) collective-permute-start(bf16[4,128,256]{2,1,0:T(8,128)(2,1)S(1)} %collective-permute-done.16.rest_1_), channel_id=1, source_target_pairs={{0,1},{1,0},{2,3},{3,2},{4,5},{5,4},{6,7},{7,6},{8,9},{9,8},{10,11... | collective-permute-start | bytes 786440 | tf_op jit(solution)/shard_map/gather_inner/ppermute | solution.py:23
  80.3 10.5 %collective-permute-start.23 = (bf16[8,128,256]{2,1,0:T(8,128)(2,1)S(1)}, bf16[8,128,256]{2,1,0:T(8,128)(2,1)S(1)}, u32[]{:S(2)}, u32[]{:S(2)}) collective-permute-start(bf16[8,128,256]{2,1,0:T(8,128)(2,1)S(1)} %get-tuple-element.42), channel_id=1, source_target_pairs={{0,8},{1,33},{2,10},{3,35},{4,12},{5,37},{6,14},{7,39},{8,16},{9,4... | collective-permute-start | bytes 1572872 | tf_op jit(solution)/shard_map/reduce_outer/ppermute | solution.py:36
  80.3 10.7 %collective-permute-start.28 = (bf16[8,128,256]{2,1,0:T(8,128)(2,1)S(1)}, bf16[8,128,256]{2,1,0:T(8,128)(2,1)S(1)}, u32[]{:S(2)}, u32[]{:S(2)}) collective-permute-start(bf16[8,128,256]{2,1,0:T(8,128)(2,1)S(1)} %get-tuple-element.47), channel_id=1, source_target_pairs={{0,24},{1,97},{2,26},{3,99},{4,28},{5,101},{6,30},{7,103},{8,0},{9... | collective-permute-start | bytes 1572872 | tf_op jit(solution)/shard_map/reduce_outer/ppermute | solution.py:36
  86.0 9.8 %collective-permute-start.25 = (bf16[8,128,256]{2,1,0:T(8,128)(2,1)S(1)}, bf16[8,128,256]{2,1,0:T(8,128)(2,1)S(1)}, u32[]{:S(2)}, u32[]{:S(2)}) collective-permute-start(bf16[8,128,256]{2,1,0:T(8,128)(2,1)S(1)} %get-tuple-element.43), channel_id=1, source_target_pairs={{0,24},{1,97},{2,26},{3,99},{4,28},{5,101},{6,30},{7,103},{8,0},{9... | collective-permute-start | bytes 1572872 | tf_op jit(solution)/shard_map/reduce_outer/ppermute | solution.py:36
  90.8 10.5 %collective-permute-start.24 = (bf16[8,128,256]{2,1,0:T(8,128)(2,1)S(1)}, bf16[8,128,256]{2,1,0:T(8,128)(2,1)S(1)}, u32[]{:S(2)}, u32[]{:S(2)}) collective-permute-start(bf16[8,128,256]{2,1,0:T(8,128)(2,1)S(1)} %relay_sum.2), channel_id=1, source_target_pairs={{0,8},{1,33},{2,10},{3,35},{4,12},{5,37},{6,14},{7,39},{8,16},{9,4... | collective-permute-start | bytes 1572872 | tf_op jit(solution)/shard_map/reduce_outer/ppermute | solution.py:36
  90.9 18.8 %collective-permute-start.27 = (bf16[8,128,256]{2,1,0:T(8,128)(2,1)S(1)}, bf16[8,128,256]{2,1,0:T(8,128)(2,1)S(1)}, u32[]{:S(2)}, u32[]{:S(2)}) collective-permute-start(bf16[8,128,256]{2,1,0:T(8,128)(2,1)S(1)} %get-tuple-element.46), channel_id=1, source_target_pairs={{0,8},{1,33},{2,10},{3,35},{4,12},{5,37},{6,14},{7,39},{8,16},{9,4... | collective-permute-start | bytes 1572872 | tf_op jit(solution)/shard_map/reduce_outer/ppermute | solution.py:36
  91.1 18.6 %collective-permute-start.29 = (bf16[8,128,256]{2,1,0:T(8,128)(2,1)S(1)}, bf16[8,128,256]{2,1,0:T(8,128)(2,1)S(1)}, u32[]{:S(2)}, u32[]{:S(2)}) collective-permute-start(bf16[8,128,256]{2,1,0:T(8,128)(2,1)S(1)} %relay_sum.3), channel_id=1, source_target_pairs={{0,24},{1,97},{2,26},{3,99},{4,28},{5,101},{6,30},{7,103},{8,0},{9... | collective-permute-start | bytes 1572872 | tf_op jit(solution)/shard_map/reduce_outer/ppermute | solution.py:36
  101.5 13.3 %collective-permute-start.26 = (bf16[4,128,256]{2,1,0:T(8,128)(2,1)S(1)}, bf16[4,128,256]{2,1,0:T(8,128)(2,1)S(1)}, u32[]{:S(2)}, u32[]{:S(2)}) collective-permute-start(bf16[4,128,256]{2,1,0:T(8,128)(2,1)S(1)} %get-tuple-element.45), channel_id=1, source_target_pairs={{0,32},{1,9},{2,34},{3,11},{4,36},{5,13},{6,38},{7,15},{8,40},{9,1... | collective-permute-start | bytes 786440 | tf_op jit(solution)/shard_map/reduce_outer/ppermute | solution.py:36
  109.9 8.7 %collective-permute-start.30 = (bf16[4,128,256]{2,1,0:T(8,128)(2,1)S(1)}, bf16[4,128,256]{2,1,0:T(8,128)(2,1)S(1)}, u32[]{:S(2)}, u32[]{:S(2)}) collective-permute-start(bf16[4,128,256]{2,1,0:T(8,128)(2,1)S(1)} %get-tuple-element.48), channel_id=1, source_target_pairs={{0,64},{1,17},{2,66},{3,19},{4,68},{5,21},{6,70},{7,23},{8,72},{9,... | collective-permute-start | bytes 786440 | tf_op jit(solution)/shard_map/reduce_outer/ppermute | solution.py:36
  114.3 6.4 %collective-permute-start.31 = (bf16[4,128,256]{2,1,0:T(8,128)(2,1)S(1)}, bf16[4,128,256]{2,1,0:T(8,128)(2,1)S(1)}, u32[]{:S(2)}, u32[]{:S(2)}) collective-permute-start(bf16[4,128,256]{2,1,0:T(8,128)(2,1)S(1)} %get-tuple-element.49), channel_id=1, source_target_pairs={{0,96},{1,25},{2,98},{3,27},{4,100},{5,29},{6,102},{7,31},{8,104},... | collective-permute-start | bytes 786440 | tf_op jit(solution)/shard_map/reduce_outer/ppermute | solution.py:36
  121.2 2.2 %collective-permute-start.32 = (f32[128,128]{1,0:T(8,128)S(1)}, f32[128,128]{1,0:T(8,128)S(1)}, u32[]{:S(2)}, u32[]{:S(2)}) collective-permute-start(f32[128,128]{1,0:T(8,128)S(1)} %get-tuple-element.50), channel_id=1, source_target_pairs={{0,1},{2,3},{4,5},{6,7},{8,9},{10,11},{12,13},{14,15},{16,17},{18,... | collective-permute-start | bytes 196616 | tf_op jit(solution)/shard_map/reduce_gram/ppermute | solution.py:531
  123.4 2.0 %collective-permute-start.35 = (f32[128,128]{1,0:T(8,128)S(1)}, f32[128,128]{1,0:T(8,128)S(1)}, u32[]{:S(2)}, u32[]{:S(2)}) collective-permute-start(f32[128,128]{1,0:T(8,128)S(1)} %add.91), channel_id=1, source_target_pairs={{1,7},{3,1},{5,3},{7,5},{9,15},{11,9},{13,11},{15,13},{17,23},{19,... | collective-permute-start | bytes 196616 | tf_op jit(solution)/shard_map/reduce_gram/ppermute | solution.py:36
  124.1 1.4 collective-permute-start.34
  124.8 0.7 collective-permute-start.33
  125.5 2.0 %collective-permute-start.38 = (f32[128,128]{1,0:T(8,128)S(1)}, f32[128,128]{1,0:T(8,128)S(1)}, u32[]{:S(2)}, u32[]{:S(2)}) collective-permute-start(f32[128,128]{1,0:T(8,128)S(1)} %add_add_fusion.2), channel_id=1, source_target_pairs={{1,25},{3,27},{5,29},{7,31},{9,1},{11,3},{13,5},{15,7},{17,9},{19,... | collective-permute-start | bytes 196616 | tf_op jit(solution)/shard_map/reduce_gram/ppermute | solution.py:36
  126.2 1.4 collective-permute-start.37
  126.9 0.7 collective-permute-start.36
  127.6 2.0 %collective-permute-start.41 = (f32[128,128]{1,0:T(8,128)S(1)}, f32[128,128]{1,0:T(8,128)S(1)}, u32[]{:S(2)}, u32[]{:S(2)}) collective-permute-start(f32[128,128]{1,0:T(8,128)S(1)} %add_add_fusion.1), channel_id=1, source_target_pairs={{1,97},{3,99},{5,101},{7,103},{9,105},{11,107},{13,109},{15,111},{... | collective-permute-start | bytes 196616 | tf_op jit(solution)/shard_map/reduce_gram/ppermute | solution.py:36
  128.3 1.4 collective-permute-start.40
  128.9 0.7 collective-permute-start.39
  129.7 33.4 %collective-permute-start.42 = (f32[128,128]{1,0:T(8,128)S(1)}, f32[128,128]{1,0:T(8,128)S(1)}, u32[]{:S(2)}, u32[]{:S(2)}) collective-permute-start(f32[128,128]{1,0:T(8,128)S(1)} %add_add_fusion), channel_id=1, source_target_pairs={{1,0},{3,2},{5,4},{7,6},{9,8},{11,10},{13,12},{15,14},{17,16},{19,... | collective-permute-start | bytes 196616 | tf_op jit(solution)/shard_map/reduce_gram/ppermute | solution.py:535

commit v9 on v7

--- a/solution.py
+++ b/solution.py
@@ -159,12 +159,15 @@
     )
 
 
-def forward_near_kernel(counts, near, tiles, first, left, right, total, held, sems):
-    copies = load_pieces([first, left], held, sems)
-    last = pltpu.make_async_copy(right, held.at[pl.ds(48, 16)], sems.at[2])
-    last.start()
+def forward_near_kernel(counts, near, tiles, *rest):
+    pieces, (total, held, sems) = rest[:6], rest[6:]
+    copies = []
+    for i, at in enumerate((0, 8, 16, 24, 48, 56)):
+        copies.append(pltpu.make_async_copy(pieces[i], held.at[pl.ds(at, 8)], sems.at[i]))
+    for one in copies:
+        one.start()
     total[...] = jnp.zeros_like(total)
-    for one in copies + [last]:
+    for one in copies:
         one.wait()
 
     def body(slot, row, col):
@@ -177,11 +180,11 @@
     return pl.pallas_call(
         forward_near_kernel,
         out_shape=jax.ShapeDtypeStruct((33, SIDE, RANK), F32),
-        in_specs=scalars(2) + whole(1) + anywhere(3),
+        in_specs=scalars(2) + whole(1) + anywhere(6),
         out_specs=whole(1)[0],
         scratch_shapes=[
             pltpu.VMEM((65, SIDE, RANK), BF16),
-            pltpu.SemaphoreType.DMA((3,)),
+            pltpu.SemaphoreType.DMA((6,)),
         ],
         compiler_params=limits(8),
         cost_estimate=product_cost(0.75),
@@ -491,14 +494,18 @@
 
     with jax.named_scope("gather_basis"):
         near = [basis_in] + [cross(basis_in, near_axes, -d) for d in (1, 2, 3)]
-        near, first_tiles, row_at, col_at = lax.optimization_barrier((near, tiles, row_at, col_at))
-        first = jnp.concatenate(near, axis=0).reshape(16, SIDE, RANK)
-        right, left = cross(first, far_axes, 1), cross(first, far_axes, -1)
-        held, counts, near_list, far_list = plan_tiles(tile_count, row_at, col_at, first_tiles)
-        right, left, held = lax.optimization_barrier((right, left, held))
-        over = (cross(right[:8], far_axes, 1), cross(left[8:], far_axes, -1))
-
-    keep = forward_near(counts, near_list, held, (first, left, right))
+        held, counts, near_list, far_list = plan_tiles(tile_count, row_at, col_at, tiles)
+        near, held = lax.optimization_barrier((near, held))
+        low, high = (
+            jnp.concatenate(pair, axis=0).reshape(8, SIDE, RANK) for pair in (near[:2], near[2:])
+        )
+        right_low, left_high = cross(low, far_axes, 1), cross(high, far_axes, -1)
+        left_low, right_high = cross(low, far_axes, -1), cross(high, far_axes, 1)
+        over = (cross(right_low, far_axes, 1), cross(left_high, far_axes, -1))
+
+    keep = forward_near(
+        counts, near_list, held, (low, high, left_low, left_high, right_low, right_high)
+    )
     keep, *aways = forward_far(counts, far_list, held, over, keep)
 
     with jax.named_scope("reduce_inner"):

time: 158 us -> 153 us (0.968)
  waiting for transfers between devices: 81 us -> 73.4 us
  starting transfers between devices: 47.7 us -> 51.5 us
    ppermute x14 -> x16, waiting for transfers between devices: 44.1 us -> 34.9 us  [cross(): return lax.ppermute(array, AXES, pairs)]
    ppermute x14 -> x16, starting transfers between devices: 21.2 us -> 25.5 us  [cross(): return lax.ppermute(array, AXES, pairs)]
    ppermute x24, waiting for transfers between devices: 36.9 us -> 38.6 us  [send(): lax.ppermute(array, axis, [(i, (i + step) % size) for i in range(size)])]
  transfers between devices with their start and end apart: 38 -> 40, of which waited for: 27 -> 22; matrix products, arithmetic and copies ran while one was open for 1% -> 1% of each run, Pallas kernels for 9% -> 9%
where the time goes in v9:
time: 153 us
  waiting for transfers between devices  73.4 us (48%)
  starting transfers between devices  51.5 us (34%)
  Pallas kernels  25 us (16%)
  between operations  1.56 us (1%)
    ppermute x24, waiting for transfers between devices, send(): lax.ppermute(array, axis, [(i, (i + step) % size) for i in range(size)])  38.6 us
    ppermute x16, waiting for transfers between devices, cross(): return lax.ppermute(array, AXES, pairs)  34.9 us
    ppermute x24, starting transfers between devices, send(): lax.ppermute(array, axis, [(i, (i + step) % size) for i in range(size)])  26 us
    ppermute x16, starting transfers between devices, cross(): return lax.ppermute(array, AXES, pairs)  25.5 us
    pallas_call x1, Pallas kernels, plan_tiles(): pl.pallas_call(plan_kernel, out_shape=(jax.ShapeDtypeStruct(tiles.shape,...  5.91 us
    pallas_call x1, Pallas kernels, finish(): pl.pallas_call(kernel, out_shape=(jax.ShapeDtypeStruct((4 * SIDE, RANK),...  5.51 us
    pallas_call x1, Pallas kernels, forward_near(): pl.pallas_call(forward_near_kernel, out_shape=jax.ShapeDtypeStruct((33, S...  3.75 us
    pallas_call x1, Pallas kernels, backward_near(): pl.pallas_call(backward_near_kernel, out_shape=jax.ShapeDtypeStruct((65,...  3.23 us
  transfers between devices with their start and end apart: 40, of which 22 were waited for; matrix products, arithmetic and copies ran while one was open for 1% of the time, Pallas kernels for 9%

profile of v9, /device:TPU:0, one launch (start us, length us, event | category | flops | bytes accessed | tf_op | source)
XLA Modules:
  0.0 152.6 jit_solution(7228139900866356751)
XLA Ops:
  0.6 3.2 %collective-permute-start.1 = (bf16[1024,128]{1,0:T(8,128)(2,1)}, bf16[1024,128]{1,0:T(8,128)(2,1)S(1)}, u32[]{:S(2)}, u32[]{:S(2)}) collective-permute-start(bf16[1024,128]{1,0:T(8,128)(2,1)} %param.4), channel_id=1, source_target_pairs={{0,64},{1,17},{2,66},{3,19},{4,68},{5,21},{6,70},{7,23},{8,72},{9,... | collective-permute-start | bytes 786440 | tf_op jit(solution)/shard_map/gather_basis/ppermute | solution.py:34
  3.8 1.1 collective-permute-start
  5.0 0.9 collective-permute-start.2
  5.8 0.8 fusion.10
  7.3 5.9 %plan_tiles.1 = (bf16[160,256,256]{2,1,0:T(8,128)(2,1)S(1)}, s32[2]{0:T(128)S(1)}, s32[192]{0:T(256)S(1)}, s32[192]{0:T(256)S(1)}) custom-call(s32[1]{0:T(128)S(6)} %copy.8.count, s32[160]{0:T(256)S(1)} %get-tuple-element.53.row_at, s32[160]{0:T(256)S(1)} %get-tuple-element.52.col_at, bf16[160,256,256]{2,1,0:T(8,128)(2,1)} %tiles.1), custom_call_target="tpu_custom_call" | custom-call | bytes 41943040 | tf_op jit(solution)/shard_map/gather_basis/plan_tiles/pallas_call | solution.py:127
  13.3 2.6 %collective-permute-start.5 = (bf16[8,256,128]{2,1,0:T(8,128)(2,1)S(1)}, bf16[8,256,128]{2,1,0:T(8,128)(2,1)S(1)}, u32[]{:S(2)}, u32[]{:S(2)}) collective-permute-start(bf16[8,256,128]{2,1,0:T(8,128)(2,1)S(1)} %bitcast.4), channel_id=1, source_target_pairs={{0,24},{1,97},{2,26},{3,99},{4,28},{5,101},{6,30},{7,103},{8,0},{9... | collective-permute-start | bytes 1572872 | tf_op jit(solution)/shard_map/gather_basis/ppermute | solution.py:34
  16.0 0.6 collective-permute-start.8
  16.6 2.7 %collective-permute-start.7 = (bf16[8,256,128]{2,1,0:T(8,128)(2,1)S(1)}, bf16[8,256,128]{2,1,0:T(8,128)(2,1)S(1)}, u32[]{:S(2)}, u32[]{:S(2)}) collective-permute-start(bf16[8,256,128]{2,1,0:T(8,128)(2,1)S(1)} %bitcast.8), channel_id=1, source_target_pairs={{0,24},{1,97},{2,26},{3,99},{4,28},{5,101},{6,30},{7,103},{8,0},{9... | collective-permute-start | bytes 1572872 | tf_op jit(solution)/shard_map/gather_basis/ppermute | solution.py:34
  19.3 3.3 %collective-permute-done.5.rest_3_ = bf16[8,256,128]{2,1,0:T(8,128)(2,1)S(1)} collective-permute-done((bf16[8,256,128]{2,1,0:T(8,128)(2,1)S(1)}, bf16[8,256,128]{2,1,0:T(8,128)(2,1)S(1)}, u32[]{:S(2)}, u32[]{:S(2)}) %collective-permute-start.5) | collective-permute-done | bytes 524320 | tf_op jit(solution)/shard_map/gather_basis/ppermute | solution.py:34
  22.6 3.7 %collective-permute-start.6 = (bf16[8,256,128]{2,1,0:T(8,128)(2,1)S(1)}, bf16[8,256,128]{2,1,0:T(8,128)(2,1)S(1)}, u32[]{:S(2)}, u32[]{:S(2)}) collective-permute-start(bf16[8,256,128]{2,1,0:T(8,128)(2,1)S(1)} %collective-permute-done.5.rest_3_), channel_id=1, source_target_pairs={{0,24},{1,97},{2,26},{3,99},{4,28},{5,101},{6,30},{7,103},{8,0},{9... | collective-permute-start | bytes 1572872 | tf_op jit(solution)/shard_map/gather_basis/ppermute | solution.py:34
  26.3 0.1 collective-permute-done.3.rest_4_
  26.4 5.6 %collective-permute-done.8.rest_5_ = bf16[8,256,128]{2,1,0:T(8,128)(2,1)S(1)} collective-permute-done((bf16[8,256,128]{2,1,0:T(8,128)(2,1)S(1)}, bf16[8,256,128]{2,1,0:T(8,128)(2,1)S(1)}, u32[]{:S(2)}, u32[]{:S(2)}) %collective-permute-start.8) | collective-permute-done | bytes 524320 | tf_op jit(solution)/shard_map/gather_basis/ppermute | solution.py:34
  32.0 3.7 %forward_near.1.before = f32[33,256,128]{2,1,0:T(8,128)S(1)} custom-call(s32[2]{0:T(128)S(1)} %get-tuple-element.26.counts, s32[192]{0:T(256)S(1)} %get-tuple-element.27.near, bf16[160,256,256]{2,1,0:T(8,128)(2,1)S(1)} %get-tuple-element.29.tiles, bf16[8,256,128]{2,1,0:T(8,128)(2,1)S(1)} %bitcast.9, bf16[8,256,128]{2,1,0:T(8,128)(2,1)S(1)} %bitcast.6, ...), custom_call_target="tpu_custom_call" | custom-call | flops 2013265920 | bytes 1048576 | tf_op jit(solution)/shard_map/forward_near/pallas_call | solution.py:180
  35.8 1.8 %collective-permute-done.4.a = bf16[8,256,128]{2,1,0:T(8,128)(2,1)S(1)} collective-permute-done((bf16[8,256,128]{2,1,0:T(8,128)(2,1)S(1)}, bf16[8,256,128]{2,1,0:T(8,128)(2,1)S(1)}, u32[]{:S(2)}, u32[]{:S(2)}) %collective-permute-start.4) | collective-permute-done | bytes 524320 | tf_op jit(solution)/shard_map/gather_basis/ppermute | solution.py:34
  37.6 2.3 %forward_far.1 = (f32[33,256,128]{2,1,0:T(8,128)S(1)}, f32[4,256,128]{2,1,0:T(8,128)S(1)}, f32[4,256,128]{2,1,0:T(8,128)S(1)}, f32[4,256,128]{2,1,0:T(8,128)S(1)}, f32[4,256,128]{2,1,0:T(8,128)S(1)}) custom-call(s32[2]{0:T(128)S(1)} %get-tuple-element.26.counts, s32[192]{0:T(256)S(1)} %get-tuple-element.30.far, ...), custom_call_target="tpu_custom_call", output_to_operand_aliasing={{0}: (5, {})} | custom-call | tf_op jit(solution)/shard_map/forward_far/pallas_call | solution.py:210
  40.0 0.5 collective-permute-start.12
  40.6 0.4 collective-permute-start.9
  41.0 0.9 collective-permute-done.10.came
  41.9 0.2 core_sum.3
  42.1 3.2 %collective-permute-start.11 = (f16[1040,128]{1,0:T(8,128)(2,1)S(1)}, f16[1040,128]{1,0:T(8,128)(2,1)S(1)}, u32[]{:S(2)}, u32[]{:S(2)}) collective-permute-start(f16[1040,128]{1,0:T(8,128)(2,1)S(1)} %convert_element_type.18), channel_id=1, source_target_pairs={{0,4},{2,6},{4,0},{6,2},{1,5},{3,7},{5,1},{7,3},{8,12},{10,14},{12... | collective-permute-start | bytes 798728 | tf_op jit(solution)/shard_map/reduce_inner/ppermute | solution.py:23
  45.3 0.2 core_sum.4
  45.6 1.8 %collective-permute-start.13 = (f16[1040,128]{1,0:T(8,128)(2,1)S(1)}, f16[1040,128]{1,0:T(8,128)(2,1)S(1)}, u32[]{:S(2)}, u32[]{:S(2)}) collective-permute-start(f16[1040,128]{1,0:T(8,128)(2,1)S(1)} %convert_element_type.20), channel_id=1, source_target_pairs={{0,2},{2,4},{4,6},{6,0},{1,3},{3,5},{5,7},{7,1},{8,10},{10,12},{12... | collective-permute-start | bytes 798728 | tf_op jit(solution)/shard_map/reduce_inner/ppermute | solution.py:23
  47.4 0.2 core_sum.5
  47.7 1.6 %collective-permute-start.15 = (f16[1040,128]{1,0:T(8,128)(2,1)S(1)}, f16[1040,128]{1,0:T(8,128)(2,1)S(1)}, u32[]{:S(2)}, u32[]{:S(2)}) collective-permute-start(f16[1040,128]{1,0:T(8,128)(2,1)S(1)} %convert_element_type.22), channel_id=1, source_target_pairs={{0,6},{2,0},{4,2},{6,4},{1,7},{3,1},{5,3},{7,5},{8,14},{10,8},{12,... | collective-permute-start | bytes 798728 | tf_op jit(solution)/shard_map/reduce_inner/ppermute | solution.py:23
  49.2 3.8 %collective-permute-done.11 = f16[1040,128]{1,0:T(8,128)(2,1)S(1)} collective-permute-done((f16[1040,128]{1,0:T(8,128)(2,1)S(1)}, f16[1040,128]{1,0:T(8,128)(2,1)S(1)}, u32[]{:S(2)}, u32[]{:S(2)}) %collective-permute-start.11) | collective-permute-done | bytes 266272 | tf_op jit(solution)/shard_map/reduce_inner/ppermute | solution.py:23
  53.0 4.8 %collective-permute-done.13 = f16[1040,128]{1,0:T(8,128)(2,1)S(1)} collective-permute-done((f16[1040,128]{1,0:T(8,128)(2,1)S(1)}, f16[1040,128]{1,0:T(8,128)(2,1)S(1)}, u32[]{:S(2)}, u32[]{:S(2)}) %collective-permute-start.13) | collective-permute-done | bytes 266272 | tf_op jit(solution)/shard_map/reduce_inner/ppermute | solution.py:23
  57.9 1.4 collective-permute-done.15
  59.3 0.2 inner_sum.1.rest_0_
  59.6 0.4 collective-permute-start.18
  59.9 3.8 %collective-permute-start.17 = (bf16[4,128,256]{2,1,0:T(8,128)(2,1)S(1)}, bf16[4,128,256]{2,1,0:T(8,128)(2,1)S(1)}, u32[]{:S(2)}, u32[]{:S(2)}) collective-permute-start(bf16[4,128,256]{2,1,0:T(8,128)(2,1)S(1)} %inner_sum.1.rest_0_), channel_id=1, source_target_pairs={{0,4},{2,6},{4,0},{6,2},{1,5},{3,7},{5,1},{7,3},{8,12},{10,14},{12... | collective-permute-start | bytes 786440 | tf_op jit(solution)/shard_map/gather_inner/ppermute | solution.py:23
  63.7 0.3 collective-permute-start.16
  64.0 4.7 %collective-permute-done.18.rest_3_ = bf16[4,128,256]{2,1,0:T(8,128)(2,1)S(1)} collective-permute-done((bf16[4,128,256]{2,1,0:T(8,128)(2,1)S(1)}, bf16[4,128,256]{2,1,0:T(8,128)(2,1)S(1)}, u32[]{:S(2)}, u32[]{:S(2)}) %collective-permute-start.18) | collective-permute-done | bytes 262176 | tf_op jit(solution)/shard_map/gather_inner/ppermute | solution.py:23
  68.7 6.8 %collective-permute-done.17.rest_2_ = bf16[4,128,256]{2,1,0:T(8,128)(2,1)S(1)} collective-permute-done((bf16[4,128,256]{2,1,0:T(8,128)(2,1)S(1)}, bf16[4,128,256]{2,1,0:T(8,128)(2,1)S(1)}, u32[]{:S(2)}, u32[]{:S(2)}) %collective-permute-start.17) | collective-permute-done | bytes 262176 | tf_op jit(solution)/shard_map/gather_inner/ppermute | solution.py:23
  75.5 0.5 collective-permute-start.20
  76.1 1.0 collective-permute-done.21.rest_6_
  77.1 0.4 collective-permute-done.20.rest_5_
  77.4 2.3 %backward_far.1 = (bf16[8,128,256]{2,1,0:T(8,128)(2,1)S(1)}, bf16[8,128,256]{2,1,0:T(8,128)(2,1)S(1)}) custom-call(s32[2]{0:T(128)S(1)} %get-tuple-element.26.counts, s32[192]{0:T(256)S(1)} %get-tuple-element.30.far, bf16[160,256,256]{2,1,0:T(8,128)(2,1)S(1)} %get-tuple-element.29.tiles, bf16[4,128,256]{2,1,0:T(8,128)(2,1)S(1)} %inner_sum.1.rest_0_, ...), custom_call_target="tpu_custom_call" | custom-call | tf_op jit(solution)/shard_map/backward_far/pallas_call | solution.py:243
  79.8 3.2 %collective-permute-start.24 = (bf16[8,128,256]{2,1,0:T(8,128)(2,1)S(1)}, bf16[8,128,256]{2,1,0:T(8,128)(2,1)S(1)}, u32[]{:S(2)}, u32[]{:S(2)}) collective-permute-start(bf16[8,128,256]{2,1,0:T(8,128)(2,1)S(1)} %get-tuple-element.41), channel_id=1, source_target_pairs={{0,24},{1,97},{2,26},{3,99},{4,28},{5,101},{6,30},{7,103},{8,0},{9... | collective-permute-start | bytes 1572872 | tf_op jit(solution)/shard_map/reduce_outer/ppermute | solution.py:34
  83.0 3.2 %backward_near.1.total = f32[65,128,256]{2,1,0:T(8,128)S(1)} custom-call(s32[2]{0:T(128)S(1)} %get-tuple-element.26.counts, s32[192]{0:T(256)S(1)} %get-tuple-element.27.near, bf16[160,256,256]{2,1,0:T(8,128)(2,1)S(1)} %get-tuple-element.29.tiles, bf16[4,128,256]{2,1,0:T(8,128)(2,1)S(1)} %inner_sum.1.rest_0_, ...), custom_call_target="tpu_custom_call" | custom-call | flops 2013265920 | bytes 1048576 | tf_op jit(solution)/shard_map/reduce_outer/backward_near/pallas_call | solution.py:272
  86.3 3.9 %collective-permute-done.23.a = bf16[8,128,256]{2,1,0:T(8,128)(2,1)S(1)} collective-permute-done((bf16[8,128,256]{2,1,0:T(8,128)(2,1)S(1)}, bf16[8,128,256]{2,1,0:T(8,128)(2,1)S(1)}, u32[]{:S(2)}, u32[]{:S(2)}) %collective-permute-start.23) | collective-permute-done | bytes 524320 | tf_op jit(solution)/shard_map/reduce_outer/ppermute | solution.py:34
  90.2 0.3 relay_sum.1
  90.6 3.3 %collective-permute-start.26 = (bf16[16,128,256]{2,1,0:T(8,128)(2,1)S(1)}, bf16[16,128,256]{2,1,0:T(8,128)(2,1)S(1)}, u32[]{:S(2)}, u32[]{:S(2)}) collective-permute-start(bf16[16,128,256]{2,1,0:T(8,128)(2,1)S(1)} %get-tuple-element.43), channel_id=1, source_target_pairs={{0,24},{1,97},{2,26},{3,99},{4,28},{5,101},{6,30},{7,103},{8,0},{9... | collective-permute-start | bytes 3145736 | tf_op jit(solution)/shard_map/reduce_outer/ppermute | solution.py:34
  93.9 12.7 %collective-permute-done.25.a = bf16[16,128,256]{2,1,0:T(8,128)(2,1)S(1)} collective-permute-done((bf16[16,128,256]{2,1,0:T(8,128)(2,1)S(1)}, bf16[16,128,256]{2,1,0:T(8,128)(2,1)S(1)}, u32[]{:S(2)}, u32[]{:S(2)}) %collective-permute-start.25) | collective-permute-done | bytes 1048608 | tf_op jit(solution)/shard_map/reduce_outer/ppermute | solution.py:34
  106.6 0.3 middle_sum.1
  106.9 1.2 collective-permute-start.27
  108.1 0.8 collective-permute-start.28
  108.9 2.0 %collective-permute-start.29 = (bf16[4,128,256]{2,1,0:T(8,128)(2,1)S(1)}, bf16[4,128,256]{2,1,0:T(8,128)(2,1)S(1)}, u32[]{:S(2)}, u32[]{:S(2)}) collective-permute-start(bf16[4,128,256]{2,1,0:T(8,128)(2,1)S(1)} %get-tuple-element.47), channel_id=1, source_target_pairs={{0,96},{1,25},{2,98},{3,27},{4,100},{5,29},{6,102},{7,31},{8,104},... | collective-permute-start | bytes 786440 | tf_op jit(solution)/shard_map/reduce_outer/ppermute | solution.py:34
  110.8 6.5 %collective-permute-done.27.a = bf16[4,128,256]{2,1,0:T(8,128)(2,1)S(1)} collective-permute-done((bf16[4,128,256]{2,1,0:T(8,128)(2,1)S(1)}, bf16[4,128,256]{2,1,0:T(8,128)(2,1)S(1)}, u32[]{:S(2)}, u32[]{:S(2)}) %collective-permute-start.27) | collective-permute-done | bytes 262176 | tf_op jit(solution)/shard_map/reduce_outer/ppermute | solution.py:34
  117.4 0.9 collective-permute-done.29.c
  118.2 0.6 outer_sum.1
  119.0 1.2 collective-permute-done.30
  120.2 1.9 %collective-permute-start.33 = (f32[128,128]{1,0:T(8,128)S(1)}, f32[128,128]{1,0:T(8,128)S(1)}, u32[]{:S(2)}, u32[]{:S(2)}) collective-permute-start(f32[128,128]{1,0:T(8,128)S(1)} %add.91), channel_id=1, source_target_pairs={{0,6},{2,0},{4,2},{6,4},{1,7},{3,1},{5,3},{7,5},{8,14},{10,8},{12,... | collective-permute-start | bytes 196616 | tf_op jit(solution)/shard_map/reduce_gram/ppermute | solution.py:23
  122.1 0.2 collective-permute-start.32
  122.3 1.3 collective-permute-start.31
  123.6 0.9 collective-permute-done.33
  124.6 4.0 %collective-permute-done.32 = f32[128,128]{1,0:T(8,128)S(1)} collective-permute-done((f32[128,128]{1,0:T(8,128)S(1)}, f32[128,128]{1,0:T(8,128)S(1)}, u32[]{:S(2)}, u32[]{:S(2)}) %collective-permute-start.32) | collective-permute-done | bytes 65568 | tf_op jit(solution)/shard_map/reduce_gram/ppermute | solution.py:23
  128.6 3.4 %collective-permute-start.36 = (f32[128,128]{1,0:T(8,128)S(1)}, f32[128,128]{1,0:T(8,128)S(1)}, u32[]{:S(2)}, u32[]{:S(2)}) collective-permute-start(f32[128,128]{1,0:T(8,128)S(1)} %add_add_fusion.2), channel_id=1, source_target_pairs={{0,24},{8,0},{16,8},{24,16},{1,25},{9,1},{17,9},{25,17},{2,26},{10... | collective-permute-start | bytes 196616 | tf_op jit(solution)/shard_map/reduce_gram/ppermute | solution.py:23
  132.0 2.2 %collective-permute-start.34 = (f32[128,128]{1,0:T(8,128)S(1)}, f32[128,128]{1,0:T(8,128)S(1)}, u32[]{:S(2)}, u32[]{:S(2)}) collective-permute-start(f32[128,128]{1,0:T(8,128)S(1)} %add_add_fusion.2), channel_id=1, source_target_pairs={{0,16},{8,24},{16,0},{24,8},{1,17},{9,25},{17,1},{25,9},{2,18},{10... | collective-permute-start | bytes 196616 | tf_op jit(solution)/shard_map/reduce_gram/ppermute | solution.py:23
  134.2 4.0 %collective-permute-done.35 = f32[128,128]{1,0:T(8,128)S(1)} collective-permute-done((f32[128,128]{1,0:T(8,128)S(1)}, f32[128,128]{1,0:T(8,128)S(1)}, u32[]{:S(2)}, u32[]{:S(2)}) %collective-permute-start.35) | collective-permute-done | bytes 65568 | tf_op jit(solution)/shard_map/reduce_gram/ppermute | solution.py:23
  138.2 2.7 %collective-permute-start.39 = (f32[128,128]{1,0:T(8,128)S(1)}, f32[128,128]{1,0:T(8,128)S(1)}, u32[]{:S(2)}, u32[]{:S(2)}) collective-permute-start(f32[128,128]{1,0:T(8,128)S(1)} %add_add_fusion.1), channel_id=1, source_target_pairs={{0,96},{32,0},{64,32},{96,64},{1,97},{33,1},{65,33},{97,65},{2,98}... | collective-permute-start | bytes 196616 | tf_op jit(solution)/shard_map/reduce_gram/ppermute | solution.py:23
  140.9 1.5 %collective-permute-start.37 = (f32[128,128]{1,0:T(8,128)S(1)}, f32[128,128]{1,0:T(8,128)S(1)}, u32[]{:S(2)}, u32[]{:S(2)}) collective-permute-start(f32[128,128]{1,0:T(8,128)S(1)} %add_add_fusion.1), channel_id=1, source_target_pairs={{0,64},{32,96},{64,0},{96,32},{1,65},{33,97},{65,1},{97,33},{2,66}... | collective-permute-start | bytes 196616 | tf_op jit(solution)/shard_map/reduce_gram/ppermute | solution.py:23
  142.4 1.0 collective-permute-done.39
  143.4 3.7 %collective-permute-done.38 = f32[128,128]{1,0:T(8,128)S(1)} collective-permute-done((f32[128,128]{1,0:T(8,128)S(1)}, f32[128,128]{1,0:T(8,128)S(1)}, u32[]{:S(2)}, u32[]{:S(2)}) %collective-permute-start.38) | collective-permute-done | bytes 65568 | tf_op jit(solution)/shard_map/reduce_gram/ppermute | solution.py:23
  147.1 5.5 %finish.1 = (f32[1024,128]{1,0:T(8,128)}, f32[128,128]{1,0:T(8,128)}) custom-call(f32[128,128]{1,0:T(8,128)S(1)} %add_add_fusion.refs_0_, f32[4,128,256]{2,1,0:T(8,128)S(1)} %get-tuple-element.49.refs_1_), custom_call_target="tpu_custom_call" | custom-call | tf_op jit(solution)/shard_map/finish/pallas_call | solution.py:466
  (45 shorter events, 0.9 us)
Async XLA Ops:
  0.6 12.6 %collective-permute-start.1 = (bf16[1024,128]{1,0:T(8,128)(2,1)}, bf16[1024,128]{1,0:T(8,128)(2,1)S(1)}, u32[]{:S(2)}, u32[]{:S(2)}) collective-permute-start(bf16[1024,128]{1,0:T(8,128)(2,1)} %param.4), channel_id=1, source_target_pairs={{0,64},{1,17},{2,66},{3,19},{4,68},{5,21},{6,70},{7,23},{8,72},{9,... | collective-permute-start | bytes 786440 | tf_op jit(solution)/shard_map/gather_basis/ppermute | solution.py:34
  3.8 9.4 %collective-permute-start = (bf16[1024,128]{1,0:T(8,128)(2,1)}, bf16[1024,128]{1,0:T(8,128)(2,1)S(1)}, u32[]{:S(2)}, u32[]{:S(2)}) collective-permute-start(bf16[1024,128]{1,0:T(8,128)(2,1)} %param.4), channel_id=1, source_target_pairs={{0,96},{1,25},{2,98},{3,27},{4,100},{5,29},{6,102},{7,31},{8,104},... | collective-permute-start | bytes 786440 | tf_op jit(solution)/shard_map/gather_basis/ppermute | solution.py:34
  5.0 8.3 %collective-permute-start.2 = (bf16[1024,128]{1,0:T(8,128)(2,1)}, bf16[1024,128]{1,0:T(8,128)(2,1)S(1)}, u32[]{:S(2)}, u32[]{:S(2)}) collective-permute-start(bf16[1024,128]{1,0:T(8,128)(2,1)} %param.4), channel_id=1, source_target_pairs={{0,32},{1,9},{2,34},{3,11},{4,36},{5,13},{6,38},{7,15},{8,40},{9,1... | collective-permute-start | bytes 786440 | tf_op jit(solution)/shard_map/gather_basis/ppermute | solution.py:34
  7.3 8.6 %copy-start = (bf16[1024,128]{1,0:T(8,128)(2,1)S(1)}, bf16[1024,128]{1,0:T(8,128)(2,1)}, u32[]{:S(2)}) copy-start(bf16[1024,128]{1,0:T(8,128)(2,1)} %param.4) | copy-start | bytes 786436
  13.3 9.3 %collective-permute-start.5 = (bf16[8,256,128]{2,1,0:T(8,128)(2,1)S(1)}, bf16[8,256,128]{2,1,0:T(8,128)(2,1)S(1)}, u32[]{:S(2)}, u32[]{:S(2)}) collective-permute-start(bf16[8,256,128]{2,1,0:T(8,128)(2,1)S(1)} %bitcast.4), channel_id=1, source_target_pairs={{0,24},{1,97},{2,26},{3,99},{4,28},{5,101},{6,30},{7,103},{8,0},{9... | collective-permute-start | bytes 1572872 | tf_op jit(solution)/shard_map/gather_basis/ppermute | solution.py:34
  15.9 10.5 %collective-permute-start.3 = (bf16[8,256,128]{2,1,0:T(8,128)(2,1)S(1)}, bf16[8,256,128]{2,1,0:T(8,128)(2,1)S(1)}, u32[]{:S(2)}, u32[]{:S(2)}) collective-permute-start(bf16[8,256,128]{2,1,0:T(8,128)(2,1)S(1)} %bitcast.7), channel_id=1, source_target_pairs={{0,8},{1,33},{2,10},{3,35},{4,12},{5,37},{6,14},{7,39},{8,16},{9,4... | collective-permute-start | bytes 1572872 | tf_op jit(solution)/shard_map/gather_basis/ppermute | solution.py:34
  16.0 16.0 %collective-permute-start.8 = (bf16[8,256,128]{2,1,0:T(8,128)(2,1)S(1)}, bf16[8,256,128]{2,1,0:T(8,128)(2,1)S(1)}, u32[]{:S(2)}, u32[]{:S(2)}) collective-permute-start(bf16[8,256,128]{2,1,0:T(8,128)(2,1)S(1)} %bitcast.5), channel_id=1, source_target_pairs={{0,8},{1,33},{2,10},{3,35},{4,12},{5,37},{6,14},{7,39},{8,16},{9,4... | collective-permute-start | bytes 1572872 | tf_op jit(solution)/shard_map/gather_basis/ppermute | solution.py:34
  16.6 15.4 %collective-permute-start.7 = (bf16[8,256,128]{2,1,0:T(8,128)(2,1)S(1)}, bf16[8,256,128]{2,1,0:T(8,128)(2,1)S(1)}, u32[]{:S(2)}, u32[]{:S(2)}) collective-permute-start(bf16[8,256,128]{2,1,0:T(8,128)(2,1)S(1)} %bitcast.8), channel_id=1, source_target_pairs={{0,24},{1,97},{2,26},{3,99},{4,28},{5,101},{6,30},{7,103},{8,0},{9... | collective-permute-start | bytes 1572872 | tf_op jit(solution)/shard_map/gather_basis/ppermute | solution.py:34
  22.6 13.2 %collective-permute-start.6 = (bf16[8,256,128]{2,1,0:T(8,128)(2,1)S(1)}, bf16[8,256,128]{2,1,0:T(8,128)(2,1)S(1)}, u32[]{:S(2)}, u32[]{:S(2)}) collective-permute-start(bf16[8,256,128]{2,1,0:T(8,128)(2,1)S(1)} %collective-permute-done.5.rest_3_), channel_id=1, source_target_pairs={{0,24},{1,97},{2,26},{3,99},{4,28},{5,101},{6,30},{7,103},{8,0},{9... | collective-permute-start | bytes 1572872 | tf_op jit(solution)/shard_map/gather_basis/ppermute | solution.py:34
  26.4 11.2 %collective-permute-start.4 = (bf16[8,256,128]{2,1,0:T(8,128)(2,1)S(1)}, bf16[8,256,128]{2,1,0:T(8,128)(2,1)S(1)}, u32[]{:S(2)}, u32[]{:S(2)}) collective-permute-start(bf16[8,256,128]{2,1,0:T(8,128)(2,1)S(1)} %collective-permute-done.3.rest_4_), channel_id=1, source_target_pairs={{0,8},{1,33},{2,10},{3,35},{4,12},{5,37},{6,14},{7,39},{8,16},{9,4... | collective-permute-start | bytes 1572872 | tf_op jit(solution)/shard_map/gather_basis/ppermute | solution.py:34
  39.9 2.0 %collective-permute-start.10 = (f32[4,256,128]{2,1,0:T(8,128)S(1)}, f32[4,256,128]{2,1,0:T(8,128)S(1)}, u32[]{:S(2)}, u32[]{:S(2)}) collective-permute-start(f32[4,256,128]{2,1,0:T(8,128)S(1)} %get-tuple-element.37), channel_id=1, source_target_pairs={{0,1},{1,0},{2,3},{3,2},{4,5},{5,4},{6,7},{7,6},{8,9},{9,8},{10,11... | collective-permute-start | bytes 1572872 | tf_op jit(solution)/shard_map/reduce_inner/ppermute | solution.py:23
  40.0 5.4 %collective-permute-start.12 = (f32[4,256,128]{2,1,0:T(8,128)S(1)}, f32[4,256,128]{2,1,0:T(8,128)S(1)}, u32[]{:S(2)}, u32[]{:S(2)}) collective-permute-start(f32[4,256,128]{2,1,0:T(8,128)S(1)} %get-tuple-element.38), channel_id=1, source_target_pairs={{0,1},{1,0},{2,3},{3,2},{4,5},{5,4},{6,7},{7,6},{8,9},{9,8},{10,11... | collective-permute-start | bytes 1572872 | tf_op jit(solution)/shard_map/reduce_inner/ppermute | solution.py:23
  40.5 6.9 %collective-permute-start.14 = (f32[4,256,128]{2,1,0:T(8,128)S(1)}, f32[4,256,128]{2,1,0:T(8,128)S(1)}, u32[]{:S(2)}, u32[]{:S(2)}) collective-permute-start(f32[4,256,128]{2,1,0:T(8,128)S(1)} %get-tuple-element.39), channel_id=1, source_target_pairs={{0,1},{1,0},{2,3},{3,2},{4,5},{5,4},{6,7},{7,6},{8,9},{9,8},{10,11... | collective-permute-start | bytes 1572872 | tf_op jit(solution)/shard_map/reduce_inner/ppermute | solution.py:23
  40.6 18.7 %collective-permute-start.9 = (f32[4,256,128]{2,1,0:T(8,128)S(1)}, f32[4,256,128]{2,1,0:T(8,128)S(1)}, u32[]{:S(2)}, u32[]{:S(2)}) collective-permute-start(f32[4,256,128]{2,1,0:T(8,128)S(1)} %get-tuple-element.36), channel_id=1, source_target_pairs={{0,1},{1,0},{2,3},{3,2},{4,5},{5,4},{6,7},{7,6},{8,9},{9,8},{10,11... | collective-permute-start | bytes 1572872 | tf_op jit(solution)/shard_map/reduce_inner/ppermute | solution.py:23
  42.1 10.9 %collective-permute-start.11 = (f16[1040,128]{1,0:T(8,128)(2,1)S(1)}, f16[1040,128]{1,0:T(8,128)(2,1)S(1)}, u32[]{:S(2)}, u32[]{:S(2)}) collective-permute-start(f16[1040,128]{1,0:T(8,128)(2,1)S(1)} %convert_element_type.18), channel_id=1, source_target_pairs={{0,4},{2,6},{4,0},{6,2},{1,5},{3,7},{5,1},{7,3},{8,12},{10,14},{12... | collective-permute-start | bytes 798728 | tf_op jit(solution)/shard_map/reduce_inner/ppermute | solution.py:23
  45.6 12.3 %collective-permute-start.13 = (f16[1040,128]{1,0:T(8,128)(2,1)S(1)}, f16[1040,128]{1,0:T(8,128)(2,1)S(1)}, u32[]{:S(2)}, u32[]{:S(2)}) collective-permute-start(f16[1040,128]{1,0:T(8,128)(2,1)S(1)} %convert_element_type.20), channel_id=1, source_target_pairs={{0,2},{2,4},{4,6},{6,0},{1,3},{3,5},{5,7},{7,1},{8,10},{10,12},{12... | collective-permute-start | bytes 798728 | tf_op jit(solution)/shard_map/reduce_inner/ppermute | solution.py:23
  47.7 11.6 %collective-permute-start.15 = (f16[1040,128]{1,0:T(8,128)(2,1)S(1)}, f16[1040,128]{1,0:T(8,128)(2,1)S(1)}, u32[]{:S(2)}, u32[]{:S(2)}) collective-permute-start(f16[1040,128]{1,0:T(8,128)(2,1)S(1)} %convert_element_type.22), channel_id=1, source_target_pairs={{0,6},{2,0},{4,2},{6,4},{1,7},{3,1},{5,3},{7,5},{8,14},{10,8},{12,... | collective-permute-start | bytes 798728 | tf_op jit(solution)/shard_map/reduce_inner/ppermute | solution.py:23
  59.6 9.2 %collective-permute-start.18 = (bf16[4,128,256]{2,1,0:T(8,128)(2,1)S(1)}, bf16[4,128,256]{2,1,0:T(8,128)(2,1)S(1)}, u32[]{:S(2)}, u32[]{:S(2)}) collective-permute-start(bf16[4,128,256]{2,1,0:T(8,128)(2,1)S(1)} %inner_sum.1.rest_0_), channel_id=1, source_target_pairs={{0,2},{2,4},{4,6},{6,0},{1,3},{3,5},{5,7},{7,1},{8,10},{10,12},{12... | collective-permute-start | bytes 786440 | tf_op jit(solution)/shard_map/gather_inner/ppermute | solution.py:23
  59.9 15.6 %collective-permute-start.17 = (bf16[4,128,256]{2,1,0:T(8,128)(2,1)S(1)}, bf16[4,128,256]{2,1,0:T(8,128)(2,1)S(1)}, u32[]{:S(2)}, u32[]{:S(2)}) collective-permute-start(bf16[4,128,256]{2,1,0:T(8,128)(2,1)S(1)} %inner_sum.1.rest_0_), channel_id=1, source_target_pairs={{0,4},{2,6},{4,0},{6,2},{1,5},{3,7},{5,1},{7,3},{8,12},{10,14},{12... | collective-permute-start | bytes 786440 | tf_op jit(solution)/shard_map/gather_inner/ppermute | solution.py:23
  63.7 11.8 %collective-permute-start.16 = (bf16[4,128,256]{2,1,0:T(8,128)(2,1)S(1)}, bf16[4,128,256]{2,1,0:T(8,128)(2,1)S(1)}, u32[]{:S(2)}, u32[]{:S(2)}) collective-permute-start(bf16[4,128,256]{2,1,0:T(8,128)(2,1)S(1)} %inner_sum.1.rest_0_), channel_id=1, source_target_pairs={{0,6},{2,0},{4,2},{6,4},{1,7},{3,1},{5,3},{7,5},{8,14},{10,8},{12,... | collective-permute-start | bytes 786440 | tf_op jit(solution)/shard_map/gather_inner/ppermute | solution.py:23
  64.0 12.0 %collective-permute-start.19 = (bf16[4,128,256]{2,1,0:T(8,128)(2,1)S(1)}, bf16[4,128,256]{2,1,0:T(8,128)(2,1)S(1)}, u32[]{:S(2)}, u32[]{:S(2)}) collective-permute-start(bf16[4,128,256]{2,1,0:T(8,128)(2,1)S(1)} %inner_sum.1.rest_0_), channel_id=1, source_target_pairs={{0,1},{1,0},{2,3},{3,2},{4,5},{5,4},{6,7},{7,6},{8,9},{9,8},{10,11... | collective-permute-start | bytes 786440 | tf_op jit(solution)/shard_map/gather_inner/ppermute | solution.py:23
  68.7 7.3 %collective-permute-start.22 = (bf16[4,128,256]{2,1,0:T(8,128)(2,1)S(1)}, bf16[4,128,256]{2,1,0:T(8,128)(2,1)S(1)}, u32[]{:S(2)}, u32[]{:S(2)}) collective-permute-start(bf16[4,128,256]{2,1,0:T(8,128)(2,1)S(1)} %collective-permute-done.18.rest_3_), channel_id=1, source_target_pairs={{0,1},{1,0},{2,3},{3,2},{4,5},{5,4},{6,7},{7,6},{8,9},{9,8},{10,11... | collective-permute-start | bytes 786440 | tf_op jit(solution)/shard_map/gather_inner/ppermute | solution.py:23
  75.5 1.5 %collective-permute-start.21 = (bf16[4,128,256]{2,1,0:T(8,128)(2,1)S(1)}, bf16[4,128,256]{2,1,0:T(8,128)(2,1)S(1)}, u32[]{:S(2)}, u32[]{:S(2)}) collective-permute-start(bf16[4,128,256]{2,1,0:T(8,128)(2,1)S(1)} %collective-permute-done.17.rest_2_), channel_id=1, source_target_pairs={{0,1},{1,0},{2,3},{3,2},{4,5},{5,4},{6,7},{7,6},{8,9},{9,8},{10,11... | collective-permute-start | bytes 786440 | tf_op jit(solution)/shard_map/gather_inner/ppermute | solution.py:23
  75.5 1.9 %collective-permute-start.20 = (bf16[4,128,256]{2,1,0:T(8,128)(2,1)S(1)}, bf16[4,128,256]{2,1,0:T(8,128)(2,1)S(1)}, u32[]{:S(2)}, u32[]{:S(2)}) collective-permute-start(bf16[4,128,256]{2,1,0:T(8,128)(2,1)S(1)} %collective-permute-done.16.rest_1_), channel_id=1, source_target_pairs={{0,1},{1,0},{2,3},{3,2},{4,5},{5,4},{6,7},{7,6},{8,9},{9,8},{10,11... | collective-permute-start | bytes 786440 | tf_op jit(solution)/shard_map/gather_inner/ppermute | solution.py:23
  79.7 10.5 %collective-permute-start.23 = (bf16[8,128,256]{2,1,0:T(8,128)(2,1)S(1)}, bf16[8,128,256]{2,1,0:T(8,128)(2,1)S(1)}, u32[]{:S(2)}, u32[]{:S(2)}) collective-permute-start(bf16[8,128,256]{2,1,0:T(8,128)(2,1)S(1)} %get-tuple-element.40), channel_id=1, source_target_pairs={{0,8},{1,33},{2,10},{3,35},{4,12},{5,37},{6,14},{7,39},{8,16},{9,4... | collective-permute-start | bytes 1572872 | tf_op jit(solution)/shard_map/reduce_outer/ppermute | solution.py:34
  79.8 10.4 %collective-permute-start.24 = (bf16[8,128,256]{2,1,0:T(8,128)(2,1)S(1)}, bf16[8,128,256]{2,1,0:T(8,128)(2,1)S(1)}, u32[]{:S(2)}, u32[]{:S(2)}) collective-permute-start(bf16[8,128,256]{2,1,0:T(8,128)(2,1)S(1)} %get-tuple-element.41), channel_id=1, source_target_pairs={{0,24},{1,97},{2,26},{3,99},{4,28},{5,101},{6,30},{7,103},{8,0},{9... | collective-permute-start | bytes 1572872 | tf_op jit(solution)/shard_map/reduce_outer/ppermute | solution.py:34
  90.5 16.1 %collective-permute-start.25 = (bf16[16,128,256]{2,1,0:T(8,128)(2,1)S(1)}, bf16[16,128,256]{2,1,0:T(8,128)(2,1)S(1)}, u32[]{:S(2)}, u32[]{:S(2)}) collective-permute-start(bf16[16,128,256]{2,1,0:T(8,128)(2,1)S(1)} %get-tuple-element.42), channel_id=1, source_target_pairs={{0,8},{1,33},{2,10},{3,35},{4,12},{5,37},{6,14},{7,39},{8,16},{9,4... | collective-permute-start | bytes 3145736 | tf_op jit(solution)/shard_map/reduce_outer/ppermute | solution.py:34
  90.6 16.0 %collective-permute-start.26 = (bf16[16,128,256]{2,1,0:T(8,128)(2,1)S(1)}, bf16[16,128,256]{2,1,0:T(8,128)(2,1)S(1)}, u32[]{:S(2)}, u32[]{:S(2)}) collective-permute-start(bf16[16,128,256]{2,1,0:T(8,128)(2,1)S(1)} %get-tuple-element.43), channel_id=1, source_target_pairs={{0,24},{1,97},{2,26},{3,99},{4,28},{5,101},{6,30},{7,103},{8,0},{9... | collective-permute-start | bytes 3145736 | tf_op jit(solution)/shard_map/reduce_outer/ppermute | solution.py:34
  106.9 10.5 %collective-permute-start.27 = (bf16[4,128,256]{2,1,0:T(8,128)(2,1)S(1)}, bf16[4,128,256]{2,1,0:T(8,128)(2,1)S(1)}, u32[]{:S(2)}, u32[]{:S(2)}) collective-permute-start(bf16[4,128,256]{2,1,0:T(8,128)(2,1)S(1)} %get-tuple-element.45), channel_id=1, source_target_pairs={{0,32},{1,9},{2,34},{3,11},{4,36},{5,13},{6,38},{7,15},{8,40},{9,1... | collective-permute-start | bytes 786440 | tf_op jit(solution)/shard_map/reduce_outer/ppermute | solution.py:34
  108.1 9.3 %collective-permute-start.28 = (bf16[4,128,256]{2,1,0:T(8,128)(2,1)S(1)}, bf16[4,128,256]{2,1,0:T(8,128)(2,1)S(1)}, u32[]{:S(2)}, u32[]{:S(2)}) collective-permute-start(bf16[4,128,256]{2,1,0:T(8,128)(2,1)S(1)} %get-tuple-element.46), channel_id=1, source_target_pairs={{0,64},{1,17},{2,66},{3,19},{4,68},{5,21},{6,70},{7,23},{8,72},{9,... | collective-permute-start | bytes 786440 | tf_op jit(solution)/shard_map/reduce_outer/ppermute | solution.py:34
  108.9 9.4 %collective-permute-start.29 = (bf16[4,128,256]{2,1,0:T(8,128)(2,1)S(1)}, bf16[4,128,256]{2,1,0:T(8,128)(2,1)S(1)}, u32[]{:S(2)}, u32[]{:S(2)}) collective-permute-start(bf16[4,128,256]{2,1,0:T(8,128)(2,1)S(1)} %get-tuple-element.47), channel_id=1, source_target_pairs={{0,96},{1,25},{2,98},{3,27},{4,100},{5,29},{6,102},{7,31},{8,104},... | collective-permute-start | bytes 786440 | tf_op jit(solution)/shard_map/reduce_outer/ppermute | solution.py:34
  118.9 1.3 collective-permute-start.30
  120.2 4.3 %collective-permute-start.33 = (f32[128,128]{1,0:T(8,128)S(1)}, f32[128,128]{1,0:T(8,128)S(1)}, u32[]{:S(2)}, u32[]{:S(2)}) collective-permute-start(f32[128,128]{1,0:T(8,128)S(1)} %add.91), channel_id=1, source_target_pairs={{0,6},{2,0},{4,2},{6,4},{1,7},{3,1},{5,3},{7,5},{8,14},{10,8},{12,... | collective-permute-start | bytes 196616 | tf_op jit(solution)/shard_map/reduce_gram/ppermute | solution.py:23
  122.1 6.5 %collective-permute-start.32 = (f32[128,128]{1,0:T(8,128)S(1)}, f32[128,128]{1,0:T(8,128)S(1)}, u32[]{:S(2)}, u32[]{:S(2)}) collective-permute-start(f32[128,128]{1,0:T(8,128)S(1)} %add.91), channel_id=1, source_target_pairs={{0,2},{2,4},{4,6},{6,0},{1,3},{3,5},{5,7},{7,1},{8,10},{10,12},{12... | collective-permute-start | bytes 196616 | tf_op jit(solution)/shard_map/reduce_gram/ppermute | solution.py:23
  122.3 6.3 %collective-permute-start.31 = (f32[128,128]{1,0:T(8,128)S(1)}, f32[128,128]{1,0:T(8,128)S(1)}, u32[]{:S(2)}, u32[]{:S(2)}) collective-permute-start(f32[128,128]{1,0:T(8,128)S(1)} %add.91), channel_id=1, source_target_pairs={{0,4},{2,6},{4,0},{6,2},{1,5},{3,7},{5,1},{7,3},{8,12},{10,14},{12... | collective-permute-start | bytes 196616 | tf_op jit(solution)/shard_map/reduce_gram/ppermute | solution.py:23
  128.6 5.6 %collective-permute-start.36 = (f32[128,128]{1,0:T(8,128)S(1)}, f32[128,128]{1,0:T(8,128)S(1)}, u32[]{:S(2)}, u32[]{:S(2)}) collective-permute-start(f32[128,128]{1,0:T(8,128)S(1)} %add_add_fusion.2), channel_id=1, source_target_pairs={{0,24},{8,0},{16,8},{24,16},{1,25},{9,1},{17,9},{25,17},{2,26},{10... | collective-permute-start | bytes 196616 | tf_op jit(solution)/shard_map/reduce_gram/ppermute | solution.py:23
  132.0 6.2 %collective-permute-start.35 = (f32[128,128]{1,0:T(8,128)S(1)}, f32[128,128]{1,0:T(8,128)S(1)}, u32[]{:S(2)}, u32[]{:S(2)}) collective-permute-start(f32[128,128]{1,0:T(8,128)S(1)} %add_add_fusion.2), channel_id=1, source_target_pairs={{0,8},{8,16},{16,24},{24,0},{1,9},{9,17},{17,25},{25,1},{2,10},{10... | collective-permute-start | bytes 196616 | tf_op jit(solution)/shard_map/reduce_gram/ppermute | solution.py:23
  132.0 6.2 %collective-permute-start.34 = (f32[128,128]{1,0:T(8,128)S(1)}, f32[128,128]{1,0:T(8,128)S(1)}, u32[]{:S(2)}, u32[]{:S(2)}) collective-permute-start(f32[128,128]{1,0:T(8,128)S(1)} %add_add_fusion.2), channel_id=1, source_target_pairs={{0,16},{8,24},{16,0},{24,8},{1,17},{9,25},{17,1},{25,9},{2,18},{10... | collective-permute-start | bytes 196616 | tf_op jit(solution)/shard_map/reduce_gram/ppermute | solution.py:23
  138.2 5.2 %collective-permute-start.39 = (f32[128,128]{1,0:T(8,128)S(1)}, f32[128,128]{1,0:T(8,128)S(1)}, u32[]{:S(2)}, u32[]{:S(2)}) collective-permute-start(f32[128,128]{1,0:T(8,128)S(1)} %add_add_fusion.1), channel_id=1, source_target_pairs={{0,96},{32,0},{64,32},{96,64},{1,97},{33,1},{65,33},{97,65},{2,98}... | collective-permute-start | bytes 196616 | tf_op jit(solution)/shard_map/reduce_gram/ppermute | solution.py:23
  140.9 6.2 %collective-permute-start.38 = (f32[128,128]{1,0:T(8,128)S(1)}, f32[128,128]{1,0:T(8,128)S(1)}, u32[]{:S(2)}, u32[]{:S(2)}) collective-permute-start(f32[128,128]{1,0:T(8,128)S(1)} %add_add_fusion.1), channel_id=1, source_target_pairs={{0,32},{32,64},{64,96},{96,0},{1,33},{33,65},{65,97},{97,1},{2,34}... | collective-permute-start | bytes 196616 | tf_op jit(solution)/shard_map/reduce_gram/ppermute | solution.py:23
  140.9 6.2 %collective-permute-start.37 = (f32[128,128]{1,0:T(8,128)S(1)}, f32[128,128]{1,0:T(8,128)S(1)}, u32[]{:S(2)}, u32[]{:S(2)}) collective-permute-start(f32[128,128]{1,0:T(8,128)S(1)} %add_add_fusion.1), channel_id=1, source_target_pairs={{0,64},{32,96},{64,0},{96,32},{1,65},{33,97},{65,1},{97,33},{2,66}... | collective-permute-start | bytes 196616 | tf_op jit(solution)/shard_map/reduce_gram/ppermute | solution.py:23

commit v10 on v9

--- a/solution.py
+++ b/solution.py
@@ -256,7 +256,7 @@
 
 
 def backward_near_kernel(counts, near, tiles, *rest):
-    pieces, (total, held, sems) = rest[:8], rest[8:]
+    pieces, (total, right, left, held, sems) = rest[:8], rest[8:]
     copies = load_pieces(pieces, held, sems)
     total[...] = jnp.zeros_like(total)
     for one in copies:
@@ -266,14 +266,17 @@
         total[col] += dot(held[row], tiles[slot])
 
     listed(counts[0], near, 32, body)
+    right[...] = total[pl.ds(24, 8)].astype(BF16)
+    left[...] = total[pl.ds(48, 8)].astype(BF16)
 
 
 def backward_near(counts, near, tiles, pieces):
+    part = jax.ShapeDtypeStruct((8, RANK, SIDE), BF16)
     return pl.pallas_call(
         backward_near_kernel,
-        out_shape=jax.ShapeDtypeStruct((65, RANK, SIDE), F32),
+        out_shape=(jax.ShapeDtypeStruct((65, RANK, SIDE), F32), part, part),
         in_specs=scalars(2) + whole(1) + anywhere(8),
-        out_specs=whole(1)[0],
+        out_specs=tuple(whole(3)),
         scratch_shapes=[
             pltpu.VMEM((33, RANK, SIDE), BF16),
             pltpu.SemaphoreType.DMA((8,)),
@@ -326,15 +329,12 @@
 
 
 def relay_kernel(total, a, b, right, left):
-    low, high = pl.ds(0, 8), pl.ds(8, 8)
-    right[low] = (total[pl.ds(16, 8)] + a[...].astype(F32)).astype(BF16)
-    right[high] = total[pl.ds(24, 8)].astype(BF16)
-    left[low] = total[pl.ds(48, 8)].astype(BF16)
-    left[high] = (total[pl.ds(56, 8)] + b[...].astype(F32)).astype(BF16)
+    right[...] = (total[pl.ds(16, 8)] + a[...].astype(F32)).astype(BF16)
+    left[...] = (total[pl.ds(56, 8)] + b[...].astype(F32)).astype(BF16)
 
 
 def relay_sum(total, came):
-    part = jax.ShapeDtypeStruct((16, RANK, SIDE), BF16)
+    part = jax.ShapeDtypeStruct((8, RANK, SIDE), BF16)
     return pl.pallas_call(
         relay_kernel,
         out_shape=(part, part),
@@ -345,10 +345,12 @@
     )(total, *came)
 
 
-def middle_kernel(total, a, b, keep, *aways):
+def middle_kernel(total, *rest):
+    halves, (keep, *aways) = (rest[:2], rest[2:4]), rest[4:]
     for d in range(4):
-        at = pl.ds(4 * d, 4)
-        one = total[at] + (a[at].astype(F32) + b[at].astype(F32))
+        a, b = halves[d // 2]
+        at = pl.ds(4 * (d % 2), 4)
+        one = total[pl.ds(4 * d, 4)] + (a[at].astype(F32) + b[at].astype(F32))
         if d == 0:
             keep[...] = one
         else:
@@ -360,7 +362,7 @@
     keep, *aways = pl.pallas_call(
         middle_kernel,
         out_shape=(jax.ShapeDtypeStruct((4, RANK, SIDE), F32),) + (part,) * 3,
-        in_specs=whole(3),
+        in_specs=whole(5),
         out_specs=tuple(whole(4)),
         compiler_params=limits(6),
         name="middle_sum",
@@ -522,10 +524,12 @@
     aways = backward_far(counts, far_list, held, mine + theirs)
 
     with jax.named_scope("reduce_outer"):
-        came = (cross(aways[0], far_axes, 1), cross(aways[1], far_axes, -1))
-        total = backward_near(counts, near_list, held, mine + theirs)
-        right, left = relay_sum(total, came)
-        came = (cross(right, far_axes, 1), cross(left, far_axes, -1))
+        over = (cross(aways[0], far_axes, 1), cross(aways[1], far_axes, -1))
+        total, right_high, left_low = backward_near(counts, near_list, held, mine + theirs)
+        right_high, left_low = cross(right_high, far_axes, 1), cross(left_low, far_axes, -1)
+        right_low, left_high = relay_sum(total, over)
+        right_low, left_high = cross(right_low, far_axes, 1), cross(left_high, far_axes, -1)
+        came = (right_low, left_low, right_high, left_high)
         keep, aways = middle_sum(total, came)
         came = [cross(one, near_axes, d) for d, one in zip((1, 2, 3), aways)]
         outer, gram = outer_sum(keep, came)

time: 153 us -> 146 us (0.954)
  waiting for transfers between devices: 73.4 us -> 67.7 us
  Pallas kernels: 25 us -> 22.8 us
    ppermute x16 -> x18, waiting for transfers between devices: 34.9 us -> 31.5 us  [cross(): return lax.ppermute(array, AXES, pairs)]
    ppermute x24, waiting for transfers between devices: 38.6 us -> 36.2 us  [send(): lax.ppermute(array, axis, [(i, (i + step) % size) for i in range(size)])]
    ppermute x16 -> x18, starting transfers between devices: 25.5 us -> 27.7 us  [cross(): return lax.ppermute(array, AXES, pairs)]
  transfers between devices with their start and end apart: 40 -> 42, of which waited for: 22 -> 25; matrix products, arithmetic and copies ran while one was open for 1% -> 1% of each run, Pallas kernels for 9% -> 9%
where the time goes in v10:
time: 146 us
  waiting for transfers between devices  67.7 us (46%)
  starting transfers between devices  52.5 us (36%)
  Pallas kernels  22.8 us (16%)
  between operations  1.59 us (1%)
    ppermute x24, waiting for transfers between devices, send(): lax.ppermute(array, axis, [(i, (i + step) % size) for i in range(size)])  36.2 us
    ppermute x18, waiting for transfers between devices, cross(): return lax.ppermute(array, AXES, pairs)  31.5 us
    ppermute x18, starting transfers between devices, cross(): return lax.ppermute(array, AXES, pairs)  27.7 us
    ppermute x24, starting transfers between devices, send(): lax.ppermute(array, axis, [(i, (i + step) % size) for i in range(size)])  24.8 us
    pallas_call x1, Pallas kernels, finish(): pl.pallas_call(kernel, out_shape=(jax.ShapeDtypeStruct((4 * SIDE, RANK),...  5.51 us
    pallas_call x1, Pallas kernels, plan_tiles(): pl.pallas_call(plan_kernel, out_shape=(jax.ShapeDtypeStruct(tiles.shape,...  4.72 us
    pallas_call x1, Pallas kernels, forward_near(): pl.pallas_call(forward_near_kernel, out_shape=jax.ShapeDtypeStruct((33, S...  3.75 us
    pallas_call x1, Pallas kernels, backward_near(): pl.pallas_call(backward_near_kernel, out_shape=(jax.ShapeDtypeStruct((65,...  3.52 us
  transfers between devices with their start and end apart: 42, of which 25 were waited for; matrix products, arithmetic and copies ran while one was open for 1% of the time, Pallas kernels for 9%

profile of v10, /device:TPU:0, one launch (start us, length us, event | category | flops | bytes accessed | tf_op | source)
XLA Modules:
  0.0 145.7 jit_solution(9018046500351875844)
XLA Ops:
  0.6 2.9 %collective-permute-start = (bf16[1024,128]{1,0:T(8,128)(2,1)}, bf16[1024,128]{1,0:T(8,128)(2,1)S(1)}, u32[]{:S(2)}, u32[]{:S(2)}) collective-permute-start(bf16[1024,128]{1,0:T(8,128)(2,1)} %param.4), channel_id=1, source_target_pairs={{0,96},{1,25},{2,98},{3,27},{4,100},{5,29},{6,102},{7,31},{8,104},... | collective-permute-start | bytes 786440 | tf_op jit(solution)/shard_map/gather_basis/ppermute | solution.py:34
  3.5 0.8 collective-permute-start.1
  4.3 0.9 collective-permute-start.2
  5.2 0.8 fusion.10
  6.7 4.7 %plan_tiles.1 = (bf16[160,256,256]{2,1,0:T(8,128)(2,1)S(1)}, s32[2]{0:T(128)S(1)}, s32[192]{0:T(256)S(1)}, s32[192]{0:T(256)S(1)}) custom-call(s32[1]{0:T(128)S(6)} %copy.8.count, s32[160]{0:T(256)S(1)} %get-tuple-element.59.row_at, s32[160]{0:T(256)S(1)} %get-tuple-element.58.col_at, bf16[160,256,256]{2,1,0:T(8,128)(2,1)} %tiles.1), custom_call_target="tpu_custom_call" | custom-call | bytes 41943040 | tf_op jit(solution)/shard_map/gather_basis/plan_tiles/pallas_call | solution.py:127
  11.4 0.3 collective-permute-done.1
  11.7 2.7 %collective-permute-done.2 = bf16[1024,128]{1,0:T(8,128)(2,1)S(1)} collective-permute-done((bf16[1024,128]{1,0:T(8,128)(2,1)}, bf16[1024,128]{1,0:T(8,128)(2,1)S(1)}, u32[]{:S(2)}, u32[]{:S(2)}) %collective-permute-start.2) | collective-permute-done | bytes 262176 | tf_op jit(solution)/shard_map/gather_basis/ppermute | solution.py:34
  14.5 3.1 %collective-permute-start.5 = (bf16[8,256,128]{2,1,0:T(8,128)(2,1)S(1)}, bf16[8,256,128]{2,1,0:T(8,128)(2,1)S(1)}, u32[]{:S(2)}, u32[]{:S(2)}) collective-permute-start(bf16[8,256,128]{2,1,0:T(8,128)(2,1)S(1)} %bitcast.4), channel_id=1, source_target_pairs={{0,24},{1,97},{2,26},{3,99},{4,28},{5,101},{6,30},{7,103},{8,0},{9... | collective-permute-start | bytes 1572872 | tf_op jit(solution)/shard_map/gather_basis/ppermute | solution.py:34
  17.7 0.8 collective-permute-start.8
  18.4 2.6 %collective-permute-start.7 = (bf16[8,256,128]{2,1,0:T(8,128)(2,1)S(1)}, bf16[8,256,128]{2,1,0:T(8,128)(2,1)S(1)}, u32[]{:S(2)}, u32[]{:S(2)}) collective-permute-start(bf16[8,256,128]{2,1,0:T(8,128)(2,1)S(1)} %bitcast.8), channel_id=1, source_target_pairs={{0,24},{1,97},{2,26},{3,99},{4,28},{5,101},{6,30},{7,103},{8,0},{9... | collective-permute-start | bytes 1572872 | tf_op jit(solution)/shard_map/gather_basis/ppermute | solution.py:34
  21.0 3.3 %collective-permute-done.5.rest_3_ = bf16[8,256,128]{2,1,0:T(8,128)(2,1)S(1)} collective-permute-done((bf16[8,256,128]{2,1,0:T(8,128)(2,1)S(1)}, bf16[8,256,128]{2,1,0:T(8,128)(2,1)S(1)}, u32[]{:S(2)}, u32[]{:S(2)}) %collective-permute-start.5) | collective-permute-done | bytes 524320 | tf_op jit(solution)/shard_map/gather_basis/ppermute | solution.py:34
  24.3 3.7 %collective-permute-start.6 = (bf16[8,256,128]{2,1,0:T(8,128)(2,1)S(1)}, bf16[8,256,128]{2,1,0:T(8,128)(2,1)S(1)}, u32[]{:S(2)}, u32[]{:S(2)}) collective-permute-start(bf16[8,256,128]{2,1,0:T(8,128)(2,1)S(1)} %collective-permute-done.5.rest_3_), channel_id=1, source_target_pairs={{0,24},{1,97},{2,26},{3,99},{4,28},{5,101},{6,30},{7,103},{8,0},{9... | collective-permute-start | bytes 1572872 | tf_op jit(solution)/shard_map/gather_basis/ppermute | solution.py:34
  28.1 5.6 %collective-permute-done.8.rest_5_ = bf16[8,256,128]{2,1,0:T(8,128)(2,1)S(1)} collective-permute-done((bf16[8,256,128]{2,1,0:T(8,128)(2,1)S(1)}, bf16[8,256,128]{2,1,0:T(8,128)(2,1)S(1)}, u32[]{:S(2)}, u32[]{:S(2)}) %collective-permute-start.8) | collective-permute-done | bytes 524320 | tf_op jit(solution)/shard_map/gather_basis/ppermute | solution.py:34
  33.7 3.7 %forward_near.1.before = f32[33,256,128]{2,1,0:T(8,128)S(1)} custom-call(s32[2]{0:T(128)S(1)} %get-tuple-element.29.counts, s32[192]{0:T(256)S(1)} %get-tuple-element.30.near, bf16[160,256,256]{2,1,0:T(8,128)(2,1)S(1)} %get-tuple-element.32.tiles, bf16[8,256,128]{2,1,0:T(8,128)(2,1)S(1)} %bitcast.9, bf16[8,256,128]{2,1,0:T(8,128)(2,1)S(1)} %bitcast.6, ...), custom_call_target="tpu_custom_call" | custom-call | flops 2013265920 | bytes 1048576 | tf_op jit(solution)/shard_map/forward_near/pallas_call | solution.py:180
  37.4 1.8 %collective-permute-done.4.a = bf16[8,256,128]{2,1,0:T(8,128)(2,1)S(1)} collective-permute-done((bf16[8,256,128]{2,1,0:T(8,128)(2,1)S(1)}, bf16[8,256,128]{2,1,0:T(8,128)(2,1)S(1)}, u32[]{:S(2)}, u32[]{:S(2)}) %collective-permute-start.4) | collective-permute-done | bytes 524320 | tf_op jit(solution)/shard_map/gather_basis/ppermute | solution.py:34
  39.3 1.5 %forward_far.1 = (f32[33,256,128]{2,1,0:T(8,128)S(1)}, f32[4,256,128]{2,1,0:T(8,128)S(1)}, f32[4,256,128]{2,1,0:T(8,128)S(1)}, f32[4,256,128]{2,1,0:T(8,128)S(1)}, f32[4,256,128]{2,1,0:T(8,128)S(1)}) custom-call(s32[2]{0:T(128)S(1)} %get-tuple-element.29.counts, s32[192]{0:T(256)S(1)} %get-tuple-element.33.far, ...), custom_call_target="tpu_custom_call", output_to_operand_aliasing={{0}: (5, {})} | custom-call | tf_op jit(solution)/shard_map/forward_far/pallas_call | solution.py:210
  40.9 0.5 collective-permute-start.12
  41.5 0.4 collective-permute-start.9
  41.9 0.9 collective-permute-done.14.came
  43.1 4.1 %collective-permute-start.15 = (f16[1040,128]{1,0:T(8,128)(2,1)S(1)}, f16[1040,128]{1,0:T(8,128)(2,1)S(1)}, u32[]{:S(2)}, u32[]{:S(2)}) collective-permute-start(f16[1040,128]{1,0:T(8,128)(2,1)S(1)} %convert_element_type.22), channel_id=1, source_target_pairs={{0,6},{2,0},{4,2},{6,4},{1,7},{3,1},{5,3},{7,5},{8,14},{10,8},{12,... | collective-permute-start | bytes 798728 | tf_op jit(solution)/shard_map/reduce_inner/ppermute | solution.py:23
  47.5 0.2 core_sum.3
  47.8 1.9 %collective-permute-start.11 = (f16[1040,128]{1,0:T(8,128)(2,1)S(1)}, f16[1040,128]{1,0:T(8,128)(2,1)S(1)}, u32[]{:S(2)}, u32[]{:S(2)}) collective-permute-start(f16[1040,128]{1,0:T(8,128)(2,1)S(1)} %convert_element_type.18), channel_id=1, source_target_pairs={{0,4},{2,6},{4,0},{6,2},{1,5},{3,7},{5,1},{7,3},{8,12},{10,14},{12... | collective-permute-start | bytes 798728 | tf_op jit(solution)/shard_map/reduce_inner/ppermute | solution.py:23
  49.7 9.1 %collective-permute-done.15 = f16[1040,128]{1,0:T(8,128)(2,1)S(1)} collective-permute-done((f16[1040,128]{1,0:T(8,128)(2,1)S(1)}, f16[1040,128]{1,0:T(8,128)(2,1)S(1)}, u32[]{:S(2)}, u32[]{:S(2)}) %collective-permute-start.15) | collective-permute-done | bytes 266272 | tf_op jit(solution)/shard_map/reduce_inner/ppermute | solution.py:23
  58.9 3.7 %collective-permute-done.13 = f16[1040,128]{1,0:T(8,128)(2,1)S(1)} collective-permute-done((f16[1040,128]{1,0:T(8,128)(2,1)S(1)}, f16[1040,128]{1,0:T(8,128)(2,1)S(1)}, u32[]{:S(2)}, u32[]{:S(2)}) %collective-permute-start.13) | collective-permute-done | bytes 266272 | tf_op jit(solution)/shard_map/reduce_inner/ppermute | solution.py:23
  62.7 0.3 inner_sum.1.rest_0_
  63.0 0.6 collective-permute-start.17
  63.6 1.4 collective-permute-start.18
  65.1 7.2 %collective-permute-done.16.rest_1_ = bf16[4,128,256]{2,1,0:T(8,128)(2,1)S(1)} collective-permute-done((bf16[4,128,256]{2,1,0:T(8,128)(2,1)S(1)}, bf16[4,128,256]{2,1,0:T(8,128)(2,1)S(1)}, u32[]{:S(2)}, u32[]{:S(2)}) %collective-permute-start.16) | collective-permute-done | bytes 262176 | tf_op jit(solution)/shard_map/gather_inner/ppermute | solution.py:23
  72.3 1.6 %collective-permute-done.17.rest_2_ = bf16[4,128,256]{2,1,0:T(8,128)(2,1)S(1)} collective-permute-done((bf16[4,128,256]{2,1,0:T(8,128)(2,1)S(1)}, bf16[4,128,256]{2,1,0:T(8,128)(2,1)S(1)}, u32[]{:S(2)}, u32[]{:S(2)}) %collective-permute-start.17) | collective-permute-done | bytes 262176 | tf_op jit(solution)/shard_map/gather_inner/ppermute | solution.py:23
  73.9 3.5 %collective-permute-done.18.rest_3_ = bf16[4,128,256]{2,1,0:T(8,128)(2,1)S(1)} collective-permute-done((bf16[4,128,256]{2,1,0:T(8,128)(2,1)S(1)}, bf16[4,128,256]{2,1,0:T(8,128)(2,1)S(1)}, u32[]{:S(2)}, u32[]{:S(2)}) %collective-permute-start.18) | collective-permute-done | bytes 262176 | tf_op jit(solution)/shard_map/gather_inner/ppermute | solution.py:23
  77.4 1.5 %collective-permute-done.22.rest_7_ = bf16[4,128,256]{2,1,0:T(8,128)(2,1)S(1)} collective-permute-done((bf16[4,128,256]{2,1,0:T(8,128)(2,1)S(1)}, bf16[4,128,256]{2,1,0:T(8,128)(2,1)S(1)}, u32[]{:S(2)}, u32[]{:S(2)}) %collective-permute-start.22) | collective-permute-done | bytes 262176 | tf_op jit(solution)/shard_map/gather_inner/ppermute | solution.py:23
  78.9 1.7 %backward_far.1 = (bf16[8,128,256]{2,1,0:T(8,128)(2,1)S(1)}, bf16[8,128,256]{2,1,0:T(8,128)(2,1)S(1)}) custom-call(s32[2]{0:T(128)S(1)} %get-tuple-element.29.counts, s32[192]{0:T(256)S(1)} %get-tuple-element.33.far, bf16[160,256,256]{2,1,0:T(8,128)(2,1)S(1)} %get-tuple-element.32.tiles, bf16[4,128,256]{2,1,0:T(8,128)(2,1)S(1)} %inner_sum.1.rest_0_, ...), custom_call_target="tpu_custom_call" | custom-call | tf_op jit(solution)/shard_map/backward_far/pallas_call | solution.py:243
  80.8 3.2 %collective-permute-start.24 = (bf16[8,128,256]{2,1,0:T(8,128)(2,1)S(1)}, bf16[8,128,256]{2,1,0:T(8,128)(2,1)S(1)}, u32[]{:S(2)}, u32[]{:S(2)}) collective-permute-start(bf16[8,128,256]{2,1,0:T(8,128)(2,1)S(1)} %get-tuple-element.45), channel_id=1, source_target_pairs={{0,24},{1,97},{2,26},{3,99},{4,28},{5,101},{6,30},{7,103},{8,0},{9... | collective-permute-start | bytes 1572872 | tf_op jit(solution)/shard_map/reduce_outer/ppermute | solution.py:34
  84.0 3.5 %backward_near.1 = (f32[65,128,256]{2,1,0:T(8,128)S(1)}, bf16[8,128,256]{2,1,0:T(8,128)(2,1)S(1)}, bf16[8,128,256]{2,1,0:T(8,128)(2,1)S(1)}) custom-call(s32[2]{0:T(128)S(1)} %get-tuple-element.29.counts, s32[192]{0:T(256)S(1)} %get-tuple-element.30.near, bf16[160,256,256]{2,1,0:T(8,128)(2,1)S(1)} %get-tuple-element.32.tiles, ...), custom_call_target="tpu_custom_call" | custom-call | flops 2013265920 | bytes 1048576 | tf_op jit(solution)/shard_map/reduce_outer/backward_near/pallas_call | solution.py:275
  87.6 2.0 %collective-permute-start.27 = (bf16[8,128,256]{2,1,0:T(8,128)(2,1)S(1)}, bf16[8,128,256]{2,1,0:T(8,128)(2,1)S(1)}, u32[]{:S(2)}, u32[]{:S(2)}) collective-permute-start(bf16[8,128,256]{2,1,0:T(8,128)(2,1)S(1)} %get-tuple-element.48), channel_id=1, source_target_pairs={{0,8},{1,33},{2,10},{3,35},{4,12},{5,37},{6,14},{7,39},{8,16},{9,4... | collective-permute-start | bytes 1572872 | tf_op jit(solution)/shard_map/reduce_outer/ppermute | solution.py:34
  89.6 1.5 %collective-permute-done.23.a = bf16[8,128,256]{2,1,0:T(8,128)(2,1)S(1)} collective-permute-done((bf16[8,128,256]{2,1,0:T(8,128)(2,1)S(1)}, bf16[8,128,256]{2,1,0:T(8,128)(2,1)S(1)}, u32[]{:S(2)}, u32[]{:S(2)}) %collective-permute-start.23) | collective-permute-done | bytes 524320 | tf_op jit(solution)/shard_map/reduce_outer/ppermute | solution.py:34
  91.1 0.2 relay_sum.1
  91.4 3.3 %collective-permute-start.28 = (bf16[8,128,256]{2,1,0:T(8,128)(2,1)S(1)}, bf16[8,128,256]{2,1,0:T(8,128)(2,1)S(1)}, u32[]{:S(2)}, u32[]{:S(2)}) collective-permute-start(bf16[8,128,256]{2,1,0:T(8,128)(2,1)S(1)} %get-tuple-element.49), channel_id=1, source_target_pairs={{0,24},{1,97},{2,26},{3,99},{4,28},{5,101},{6,30},{7,103},{8,0},{9... | collective-permute-start | bytes 1572872 | tf_op jit(solution)/shard_map/reduce_outer/ppermute | solution.py:34
  94.7 2.0 %collective-permute-done.26.rest_1_ = bf16[8,128,256]{2,1,0:T(8,128)(2,1)S(1)} collective-permute-done((bf16[8,128,256]{2,1,0:T(8,128)(2,1)S(1)}, bf16[8,128,256]{2,1,0:T(8,128)(2,1)S(1)}, u32[]{:S(2)}, u32[]{:S(2)}) %collective-permute-start.26) | collective-permute-done | bytes 524320 | tf_op jit(solution)/shard_map/reduce_outer/ppermute | solution.py:34
  96.8 1.3 collective-permute-done.27.rest_2_
  98.1 5.6 %collective-permute-done.25.rest_0_ = bf16[8,128,256]{2,1,0:T(8,128)(2,1)S(1)} collective-permute-done((bf16[8,128,256]{2,1,0:T(8,128)(2,1)S(1)}, bf16[8,128,256]{2,1,0:T(8,128)(2,1)S(1)}, u32[]{:S(2)}, u32[]{:S(2)}) %collective-permute-start.25) | collective-permute-done | bytes 524320 | tf_op jit(solution)/shard_map/reduce_outer/ppermute | solution.py:34
  103.7 0.3 middle_sum.1
  104.0 0.8 collective-permute-start.29
  104.8 1.2 collective-permute-start.30
  106.1 2.1 %collective-permute-start.31 = (bf16[4,128,256]{2,1,0:T(8,128)(2,1)S(1)}, bf16[4,128,256]{2,1,0:T(8,128)(2,1)S(1)}, u32[]{:S(2)}, u32[]{:S(2)}) collective-permute-start(bf16[4,128,256]{2,1,0:T(8,128)(2,1)S(1)} %get-tuple-element.53), channel_id=1, source_target_pairs={{0,96},{1,25},{2,98},{3,27},{4,100},{5,29},{6,102},{7,31},{8,104},... | collective-permute-start | bytes 786440 | tf_op jit(solution)/shard_map/reduce_outer/ppermute | solution.py:34
  108.2 6.3 %collective-permute-done.29.a = bf16[4,128,256]{2,1,0:T(8,128)(2,1)S(1)} collective-permute-done((bf16[4,128,256]{2,1,0:T(8,128)(2,1)S(1)}, bf16[4,128,256]{2,1,0:T(8,128)(2,1)S(1)}, u32[]{:S(2)}, u32[]{:S(2)}) %collective-permute-start.29) | collective-permute-done | bytes 262176 | tf_op jit(solution)/shard_map/reduce_outer/ppermute | solution.py:34
  114.5 0.9 collective-permute-done.31.c
  115.4 0.6 outer_sum.1
  116.1 1.2 collective-permute-done.32
  117.3 1.0 collective-permute-start.33
  118.3 0.7 collective-permute-start.34
  119.0 2.6 %collective-permute-start.35 = (f32[128,128]{1,0:T(8,128)S(1)}, f32[128,128]{1,0:T(8,128)S(1)}, u32[]{:S(2)}, u32[]{:S(2)}) collective-permute-start(f32[128,128]{1,0:T(8,128)S(1)} %add.91), channel_id=1, source_target_pairs={{0,6},{2,0},{4,2},{6,4},{1,7},{3,1},{5,3},{7,5},{8,14},{10,8},{12,... | collective-permute-start | bytes 196616 | tf_op jit(solution)/shard_map/reduce_gram/ppermute | solution.py:23
  121.6 2.2 %collective-permute-done.33 = f32[128,128]{1,0:T(8,128)S(1)} collective-permute-done((f32[128,128]{1,0:T(8,128)S(1)}, f32[128,128]{1,0:T(8,128)S(1)}, u32[]{:S(2)}, u32[]{:S(2)}) %collective-permute-start.33) | collective-permute-done | bytes 65568 | tf_op jit(solution)/shard_map/reduce_gram/ppermute | solution.py:23
  123.8 0.7 collective-permute-done.34
  124.5 1.7 %collective-permute-start.36 = (f32[128,128]{1,0:T(8,128)S(1)}, f32[128,128]{1,0:T(8,128)S(1)}, u32[]{:S(2)}, u32[]{:S(2)}) collective-permute-start(f32[128,128]{1,0:T(8,128)S(1)} %add_add_fusion.2), channel_id=1, source_target_pairs={{0,16},{8,24},{16,0},{24,8},{1,17},{9,25},{17,1},{25,9},{2,18},{10... | collective-permute-start | bytes 196616 | tf_op jit(solution)/shard_map/reduce_gram/ppermute | solution.py:23
  126.2 1.2 collective-permute-start.37
  127.4 2.1 %collective-permute-start.38 = (f32[128,128]{1,0:T(8,128)S(1)}, f32[128,128]{1,0:T(8,128)S(1)}, u32[]{:S(2)}, u32[]{:S(2)}) collective-permute-start(f32[128,128]{1,0:T(8,128)S(1)} %add_add_fusion.2), channel_id=1, source_target_pairs={{0,24},{8,0},{16,8},{24,16},{1,25},{9,1},{17,9},{25,17},{2,26},{10... | collective-permute-start | bytes 196616 | tf_op jit(solution)/shard_map/reduce_gram/ppermute | solution.py:23
  129.5 1.4 collective-permute-done.36
  130.9 0.8 collective-permute-done.37
  131.7 3.0 %collective-permute-start.39 = (f32[128,128]{1,0:T(8,128)S(1)}, f32[128,128]{1,0:T(8,128)S(1)}, u32[]{:S(2)}, u32[]{:S(2)}) collective-permute-start(f32[128,128]{1,0:T(8,128)S(1)} %add_add_fusion.1), channel_id=1, source_target_pairs={{0,64},{32,96},{64,0},{96,32},{1,65},{33,97},{65,1},{97,33},{2,66}... | collective-permute-start | bytes 196616 | tf_op jit(solution)/shard_map/reduce_gram/ppermute | solution.py:23
  134.7 0.5 collective-permute-start.40
  135.3 2.7 %collective-permute-start.41 = (f32[128,128]{1,0:T(8,128)S(1)}, f32[128,128]{1,0:T(8,128)S(1)}, u32[]{:S(2)}, u32[]{:S(2)}) collective-permute-start(f32[128,128]{1,0:T(8,128)S(1)} %add_add_fusion.1), channel_id=1, source_target_pairs={{0,96},{32,0},{64,32},{96,64},{1,97},{33,1},{65,33},{97,65},{2,98}... | collective-permute-start | bytes 196616 | tf_op jit(solution)/shard_map/reduce_gram/ppermute | solution.py:23
  138.0 2.2 %collective-permute-done.40 = f32[128,128]{1,0:T(8,128)S(1)} collective-permute-done((f32[128,128]{1,0:T(8,128)S(1)}, f32[128,128]{1,0:T(8,128)S(1)}, u32[]{:S(2)}, u32[]{:S(2)}) %collective-permute-start.40) | collective-permute-done | bytes 65568 | tf_op jit(solution)/shard_map/reduce_gram/ppermute | solution.py:23
  140.2 5.5 %finish.1 = (f32[1024,128]{1,0:T(8,128)}, f32[128,128]{1,0:T(8,128)}) custom-call(f32[128,128]{1,0:T(8,128)S(1)} %add_add_fusion.refs_0_, f32[4,128,256]{2,1,0:T(8,128)S(1)} %get-tuple-element.55.refs_1_), custom_call_target="tpu_custom_call" | custom-call | tf_op jit(solution)/shard_map/finish/pallas_call | solution.py:468
  (49 shorter events, 1.7 us)
Async XLA Ops:
  0.6 10.8 %collective-permute-start = (bf16[1024,128]{1,0:T(8,128)(2,1)}, bf16[1024,128]{1,0:T(8,128)(2,1)S(1)}, u32[]{:S(2)}, u32[]{:S(2)}) collective-permute-start(bf16[1024,128]{1,0:T(8,128)(2,1)} %param.4), channel_id=1, source_target_pairs={{0,96},{1,25},{2,98},{3,27},{4,100},{5,29},{6,102},{7,31},{8,104},... | collective-permute-start | bytes 786440 | tf_op jit(solution)/shard_map/gather_basis/ppermute | solution.py:34
  3.5 8.2 %collective-permute-start.1 = (bf16[1024,128]{1,0:T(8,128)(2,1)}, bf16[1024,128]{1,0:T(8,128)(2,1)S(1)}, u32[]{:S(2)}, u32[]{:S(2)}) collective-permute-start(bf16[1024,128]{1,0:T(8,128)(2,1)} %param.4), channel_id=1, source_target_pairs={{0,64},{1,17},{2,66},{3,19},{4,68},{5,21},{6,70},{7,23},{8,72},{9,... | collective-permute-start | bytes 786440 | tf_op jit(solution)/shard_map/gather_basis/ppermute | solution.py:34
  4.3 10.1 %collective-permute-start.2 = (bf16[1024,128]{1,0:T(8,128)(2,1)}, bf16[1024,128]{1,0:T(8,128)(2,1)S(1)}, u32[]{:S(2)}, u32[]{:S(2)}) collective-permute-start(bf16[1024,128]{1,0:T(8,128)(2,1)} %param.4), channel_id=1, source_target_pairs={{0,32},{1,9},{2,34},{3,11},{4,36},{5,13},{6,38},{7,15},{8,40},{9,1... | collective-permute-start | bytes 786440 | tf_op jit(solution)/shard_map/gather_basis/ppermute | solution.py:34
  6.7 10.9 %copy-start = (bf16[1024,128]{1,0:T(8,128)(2,1)S(1)}, bf16[1024,128]{1,0:T(8,128)(2,1)}, u32[]{:S(2)}) copy-start(bf16[1024,128]{1,0:T(8,128)(2,1)} %param.4) | copy-start | bytes 786436
  14.5 9.8 %collective-permute-start.5 = (bf16[8,256,128]{2,1,0:T(8,128)(2,1)S(1)}, bf16[8,256,128]{2,1,0:T(8,128)(2,1)S(1)}, u32[]{:S(2)}, u32[]{:S(2)}) collective-permute-start(bf16[8,256,128]{2,1,0:T(8,128)(2,1)S(1)} %bitcast.4), channel_id=1, source_target_pairs={{0,24},{1,97},{2,26},{3,99},{4,28},{5,101},{6,30},{7,103},{8,0},{9... | collective-permute-start | bytes 1572872 | tf_op jit(solution)/shard_map/gather_basis/ppermute | solution.py:34
  17.6 10.5 %collective-permute-start.3 = (bf16[8,256,128]{2,1,0:T(8,128)(2,1)S(1)}, bf16[8,256,128]{2,1,0:T(8,128)(2,1)S(1)}, u32[]{:S(2)}, u32[]{:S(2)}) collective-permute-start(bf16[8,256,128]{2,1,0:T(8,128)(2,1)S(1)} %bitcast.7), channel_id=1, source_target_pairs={{0,8},{1,33},{2,10},{3,35},{4,12},{5,37},{6,14},{7,39},{8,16},{9,4... | collective-permute-start | bytes 1572872 | tf_op jit(solution)/shard_map/gather_basis/ppermute | solution.py:34
  17.7 16.0 %collective-permute-start.8 = (bf16[8,256,128]{2,1,0:T(8,128)(2,1)S(1)}, bf16[8,256,128]{2,1,0:T(8,128)(2,1)S(1)}, u32[]{:S(2)}, u32[]{:S(2)}) collective-permute-start(bf16[8,256,128]{2,1,0:T(8,128)(2,1)S(1)} %bitcast.5), channel_id=1, source_target_pairs={{0,8},{1,33},{2,10},{3,35},{4,12},{5,37},{6,14},{7,39},{8,16},{9,4... | collective-permute-start | bytes 1572872 | tf_op jit(solution)/shard_map/gather_basis/ppermute | solution.py:34
  18.4 15.2 %collective-permute-start.7 = (bf16[8,256,128]{2,1,0:T(8,128)(2,1)S(1)}, bf16[8,256,128]{2,1,0:T(8,128)(2,1)S(1)}, u32[]{:S(2)}, u32[]{:S(2)}) collective-permute-start(bf16[8,256,128]{2,1,0:T(8,128)(2,1)S(1)} %bitcast.8), channel_id=1, source_target_pairs={{0,24},{1,97},{2,26},{3,99},{4,28},{5,101},{6,30},{7,103},{8,0},{9... | collective-permute-start | bytes 1572872 | tf_op jit(solution)/shard_map/gather_basis/ppermute | solution.py:34
  24.3 13.2 %collective-permute-start.6 = (bf16[8,256,128]{2,1,0:T(8,128)(2,1)S(1)}, bf16[8,256,128]{2,1,0:T(8,128)(2,1)S(1)}, u32[]{:S(2)}, u32[]{:S(2)}) collective-permute-start(bf16[8,256,128]{2,1,0:T(8,128)(2,1)S(1)} %collective-permute-done.5.rest_3_), channel_id=1, source_target_pairs={{0,24},{1,97},{2,26},{3,99},{4,28},{5,101},{6,30},{7,103},{8,0},{9... | collective-permute-start | bytes 1572872 | tf_op jit(solution)/shard_map/gather_basis/ppermute | solution.py:34
  28.1 11.2 %collective-permute-start.4 = (bf16[8,256,128]{2,1,0:T(8,128)(2,1)S(1)}, bf16[8,256,128]{2,1,0:T(8,128)(2,1)S(1)}, u32[]{:S(2)}, u32[]{:S(2)}) collective-permute-start(bf16[8,256,128]{2,1,0:T(8,128)(2,1)S(1)} %collective-permute-done.3.rest_4_), channel_id=1, source_target_pairs={{0,8},{1,33},{2,10},{3,35},{4,12},{5,37},{6,14},{7,39},{8,16},{9,4... | collective-permute-start | bytes 1572872 | tf_op jit(solution)/shard_map/gather_basis/ppermute | solution.py:34
  40.8 2.0 %collective-permute-start.14 = (f32[4,256,128]{2,1,0:T(8,128)S(1)}, f32[4,256,128]{2,1,0:T(8,128)S(1)}, u32[]{:S(2)}, u32[]{:S(2)}) collective-permute-start(f32[4,256,128]{2,1,0:T(8,128)S(1)} %get-tuple-element.42), channel_id=1, source_target_pairs={{0,1},{1,0},{2,3},{3,2},{4,5},{5,4},{6,7},{7,6},{8,9},{9,8},{10,11... | collective-permute-start | bytes 1572872 | tf_op jit(solution)/shard_map/reduce_inner/ppermute | solution.py:23
  40.9 6.3 %collective-permute-start.12 = (f32[4,256,128]{2,1,0:T(8,128)S(1)}, f32[4,256,128]{2,1,0:T(8,128)S(1)}, u32[]{:S(2)}, u32[]{:S(2)}) collective-permute-start(f32[4,256,128]{2,1,0:T(8,128)S(1)} %get-tuple-element.41), channel_id=1, source_target_pairs={{0,1},{1,0},{2,3},{3,2},{4,5},{5,4},{6,7},{7,6},{8,9},{9,8},{10,11... | collective-permute-start | bytes 1572872 | tf_op jit(solution)/shard_map/reduce_inner/ppermute | solution.py:23
  41.4 6.1 %collective-permute-start.10 = (f32[4,256,128]{2,1,0:T(8,128)S(1)}, f32[4,256,128]{2,1,0:T(8,128)S(1)}, u32[]{:S(2)}, u32[]{:S(2)}) collective-permute-start(f32[4,256,128]{2,1,0:T(8,128)S(1)} %get-tuple-element.40), channel_id=1, source_target_pairs={{0,1},{1,0},{2,3},{3,2},{4,5},{5,4},{6,7},{7,6},{8,9},{9,8},{10,11... | collective-permute-start | bytes 1572872 | tf_op jit(solution)/shard_map/reduce_inner/ppermute | solution.py:23
  41.5 21.2 %collective-permute-start.9 = (f32[4,256,128]{2,1,0:T(8,128)S(1)}, f32[4,256,128]{2,1,0:T(8,128)S(1)}, u32[]{:S(2)}, u32[]{:S(2)}) collective-permute-start(f32[4,256,128]{2,1,0:T(8,128)S(1)} %get-tuple-element.39), channel_id=1, source_target_pairs={{0,1},{1,0},{2,3},{3,2},{4,5},{5,4},{6,7},{7,6},{8,9},{9,8},{10,11... | collective-permute-start | bytes 1572872 | tf_op jit(solution)/shard_map/reduce_inner/ppermute | solution.py:23
  43.1 15.8 %collective-permute-start.15 = (f16[1040,128]{1,0:T(8,128)(2,1)S(1)}, f16[1040,128]{1,0:T(8,128)(2,1)S(1)}, u32[]{:S(2)}, u32[]{:S(2)}) collective-permute-start(f16[1040,128]{1,0:T(8,128)(2,1)S(1)} %convert_element_type.22), channel_id=1, source_target_pairs={{0,6},{2,0},{4,2},{6,4},{1,7},{3,1},{5,3},{7,5},{8,14},{10,8},{12,... | collective-permute-start | bytes 798728 | tf_op jit(solution)/shard_map/reduce_inner/ppermute | solution.py:23
  47.5 15.1 %collective-permute-start.13 = (f16[1040,128]{1,0:T(8,128)(2,1)S(1)}, f16[1040,128]{1,0:T(8,128)(2,1)S(1)}, u32[]{:S(2)}, u32[]{:S(2)}) collective-permute-start(f16[1040,128]{1,0:T(8,128)(2,1)S(1)} %convert_element_type.20), channel_id=1, source_target_pairs={{0,2},{2,4},{4,6},{6,0},{1,3},{3,5},{5,7},{7,1},{8,10},{10,12},{12... | collective-permute-start | bytes 798728 | tf_op jit(solution)/shard_map/reduce_inner/ppermute | solution.py:23
  47.8 14.8 %collective-permute-start.11 = (f16[1040,128]{1,0:T(8,128)(2,1)S(1)}, f16[1040,128]{1,0:T(8,128)(2,1)S(1)}, u32[]{:S(2)}, u32[]{:S(2)}) collective-permute-start(f16[1040,128]{1,0:T(8,128)(2,1)S(1)} %convert_element_type.18), channel_id=1, source_target_pairs={{0,4},{2,6},{4,0},{6,2},{1,5},{3,7},{5,1},{7,3},{8,12},{10,14},{12... | collective-permute-start | bytes 798728 | tf_op jit(solution)/shard_map/reduce_inner/ppermute | solution.py:23
  63.0 9.3 %collective-permute-start.16 = (bf16[4,128,256]{2,1,0:T(8,128)(2,1)S(1)}, bf16[4,128,256]{2,1,0:T(8,128)(2,1)S(1)}, u32[]{:S(2)}, u32[]{:S(2)}) collective-permute-start(bf16[4,128,256]{2,1,0:T(8,128)(2,1)S(1)} %inner_sum.1.rest_0_), channel_id=1, source_target_pairs={{0,6},{2,0},{4,2},{6,4},{1,7},{3,1},{5,3},{7,5},{8,14},{10,8},{12,... | collective-permute-start | bytes 786440 | tf_op jit(solution)/shard_map/gather_inner/ppermute | solution.py:23
  63.0 10.9 %collective-permute-start.17 = (bf16[4,128,256]{2,1,0:T(8,128)(2,1)S(1)}, bf16[4,128,256]{2,1,0:T(8,128)(2,1)S(1)}, u32[]{:S(2)}, u32[]{:S(2)}) collective-permute-start(bf16[4,128,256]{2,1,0:T(8,128)(2,1)S(1)} %inner_sum.1.rest_0_), channel_id=1, source_target_pairs={{0,4},{2,6},{4,0},{6,2},{1,5},{3,7},{5,1},{7,3},{8,12},{10,14},{12... | collective-permute-start | bytes 786440 | tf_op jit(solution)/shard_map/gather_inner/ppermute | solution.py:23
  63.6 13.7 %collective-permute-start.18 = (bf16[4,128,256]{2,1,0:T(8,128)(2,1)S(1)}, bf16[4,128,256]{2,1,0:T(8,128)(2,1)S(1)}, u32[]{:S(2)}, u32[]{:S(2)}) collective-permute-start(bf16[4,128,256]{2,1,0:T(8,128)(2,1)S(1)} %inner_sum.1.rest_0_), channel_id=1, source_target_pairs={{0,2},{2,4},{4,6},{6,0},{1,3},{3,5},{5,7},{7,1},{8,10},{10,12},{12... | collective-permute-start | bytes 786440 | tf_op jit(solution)/shard_map/gather_inner/ppermute | solution.py:23
  65.1 12.4 %collective-permute-start.19 = (bf16[4,128,256]{2,1,0:T(8,128)(2,1)S(1)}, bf16[4,128,256]{2,1,0:T(8,128)(2,1)S(1)}, u32[]{:S(2)}, u32[]{:S(2)}) collective-permute-start(bf16[4,128,256]{2,1,0:T(8,128)(2,1)S(1)} %inner_sum.1.rest_0_), channel_id=1, source_target_pairs={{0,1},{1,0},{2,3},{3,2},{4,5},{5,4},{6,7},{7,6},{8,9},{9,8},{10,11... | collective-permute-start | bytes 786440 | tf_op jit(solution)/shard_map/gather_inner/ppermute | solution.py:23
  72.3 5.1 %collective-permute-start.20 = (bf16[4,128,256]{2,1,0:T(8,128)(2,1)S(1)}, bf16[4,128,256]{2,1,0:T(8,128)(2,1)S(1)}, u32[]{:S(2)}, u32[]{:S(2)}) collective-permute-start(bf16[4,128,256]{2,1,0:T(8,128)(2,1)S(1)} %collective-permute-done.16.rest_1_), channel_id=1, source_target_pairs={{0,1},{1,0},{2,3},{3,2},{4,5},{5,4},{6,7},{7,6},{8,9},{9,8},{10,11... | collective-permute-start | bytes 786440 | tf_op jit(solution)/shard_map/gather_inner/ppermute | solution.py:23
  73.9 3.5 %collective-permute-start.21 = (bf16[4,128,256]{2,1,0:T(8,128)(2,1)S(1)}, bf16[4,128,256]{2,1,0:T(8,128)(2,1)S(1)}, u32[]{:S(2)}, u32[]{:S(2)}) collective-permute-start(bf16[4,128,256]{2,1,0:T(8,128)(2,1)S(1)} %collective-permute-done.17.rest_2_), channel_id=1, source_target_pairs={{0,1},{1,0},{2,3},{3,2},{4,5},{5,4},{6,7},{7,6},{8,9},{9,8},{10,11... | collective-permute-start | bytes 786440 | tf_op jit(solution)/shard_map/gather_inner/ppermute | solution.py:23
  77.4 1.5 %collective-permute-start.22 = (bf16[4,128,256]{2,1,0:T(8,128)(2,1)S(1)}, bf16[4,128,256]{2,1,0:T(8,128)(2,1)S(1)}, u32[]{:S(2)}, u32[]{:S(2)}) collective-permute-start(bf16[4,128,256]{2,1,0:T(8,128)(2,1)S(1)} %collective-permute-done.18.rest_3_), channel_id=1, source_target_pairs={{0,1},{1,0},{2,3},{3,2},{4,5},{5,4},{6,7},{7,6},{8,9},{9,8},{10,11... | collective-permute-start | bytes 786440 | tf_op jit(solution)/shard_map/gather_inner/ppermute | solution.py:23
  80.7 10.5 %collective-permute-start.23 = (bf16[8,128,256]{2,1,0:T(8,128)(2,1)S(1)}, bf16[8,128,256]{2,1,0:T(8,128)(2,1)S(1)}, u32[]{:S(2)}, u32[]{:S(2)}) collective-permute-start(bf16[8,128,256]{2,1,0:T(8,128)(2,1)S(1)} %get-tuple-element.44), channel_id=1, source_target_pairs={{0,8},{1,33},{2,10},{3,35},{4,12},{5,37},{6,14},{7,39},{8,16},{9,4... | collective-permute-start | bytes 1572872 | tf_op jit(solution)/shard_map/reduce_outer/ppermute | solution.py:34
  80.8 10.4 %collective-permute-start.24 = (bf16[8,128,256]{2,1,0:T(8,128)(2,1)S(1)}, bf16[8,128,256]{2,1,0:T(8,128)(2,1)S(1)}, u32[]{:S(2)}, u32[]{:S(2)}) collective-permute-start(bf16[8,128,256]{2,1,0:T(8,128)(2,1)S(1)} %get-tuple-element.45), channel_id=1, source_target_pairs={{0,24},{1,97},{2,26},{3,99},{4,28},{5,101},{6,30},{7,103},{8,0},{9... | collective-permute-start | bytes 1572872 | tf_op jit(solution)/shard_map/reduce_outer/ppermute | solution.py:34
  87.5 9.2 %collective-permute-start.26 = (bf16[8,128,256]{2,1,0:T(8,128)(2,1)S(1)}, bf16[8,128,256]{2,1,0:T(8,128)(2,1)S(1)}, u32[]{:S(2)}, u32[]{:S(2)}) collective-permute-start(bf16[8,128,256]{2,1,0:T(8,128)(2,1)S(1)} %get-tuple-element.47), channel_id=1, source_target_pairs={{0,24},{1,97},{2,26},{3,99},{4,28},{5,101},{6,30},{7,103},{8,0},{9... | collective-permute-start | bytes 1572872 | tf_op jit(solution)/shard_map/reduce_outer/ppermute | solution.py:34
  87.6 10.5 %collective-permute-start.27 = (bf16[8,128,256]{2,1,0:T(8,128)(2,1)S(1)}, bf16[8,128,256]{2,1,0:T(8,128)(2,1)S(1)}, u32[]{:S(2)}, u32[]{:S(2)}) collective-permute-start(bf16[8,128,256]{2,1,0:T(8,128)(2,1)S(1)} %get-tuple-element.48), channel_id=1, source_target_pairs={{0,8},{1,33},{2,10},{3,35},{4,12},{5,37},{6,14},{7,39},{8,16},{9,4... | collective-permute-start | bytes 1572872 | tf_op jit(solution)/shard_map/reduce_outer/ppermute | solution.py:34
  91.4 12.3 %collective-permute-start.25 = (bf16[8,128,256]{2,1,0:T(8,128)(2,1)S(1)}, bf16[8,128,256]{2,1,0:T(8,128)(2,1)S(1)}, u32[]{:S(2)}, u32[]{:S(2)}) collective-permute-start(bf16[8,128,256]{2,1,0:T(8,128)(2,1)S(1)} %get-tuple-element.46), channel_id=1, source_target_pairs={{0,8},{1,33},{2,10},{3,35},{4,12},{5,37},{6,14},{7,39},{8,16},{9,4... | collective-permute-start | bytes 1572872 | tf_op jit(solution)/shard_map/reduce_outer/ppermute | solution.py:34
  91.4 12.2 %collective-permute-start.28 = (bf16[8,128,256]{2,1,0:T(8,128)(2,1)S(1)}, bf16[8,128,256]{2,1,0:T(8,128)(2,1)S(1)}, u32[]{:S(2)}, u32[]{:S(2)}) collective-permute-start(bf16[8,128,256]{2,1,0:T(8,128)(2,1)S(1)} %get-tuple-element.49), channel_id=1, source_target_pairs={{0,24},{1,97},{2,26},{3,99},{4,28},{5,101},{6,30},{7,103},{8,0},{9... | collective-permute-start | bytes 1572872 | tf_op jit(solution)/shard_map/reduce_outer/ppermute | solution.py:34
  104.0 10.5 %collective-permute-start.29 = (bf16[4,128,256]{2,1,0:T(8,128)(2,1)S(1)}, bf16[4,128,256]{2,1,0:T(8,128)(2,1)S(1)}, u32[]{:S(2)}, u32[]{:S(2)}) collective-permute-start(bf16[4,128,256]{2,1,0:T(8,128)(2,1)S(1)} %get-tuple-element.51), channel_id=1, source_target_pairs={{0,32},{1,9},{2,34},{3,11},{4,36},{5,13},{6,38},{7,15},{8,40},{9,1... | collective-permute-start | bytes 786440 | tf_op jit(solution)/shard_map/reduce_outer/ppermute | solution.py:34
  104.8 9.6 %collective-permute-start.30 = (bf16[4,128,256]{2,1,0:T(8,128)(2,1)S(1)}, bf16[4,128,256]{2,1,0:T(8,128)(2,1)S(1)}, u32[]{:S(2)}, u32[]{:S(2)}) collective-permute-start(bf16[4,128,256]{2,1,0:T(8,128)(2,1)S(1)} %get-tuple-element.52), channel_id=1, source_target_pairs={{0,64},{1,17},{2,66},{3,19},{4,68},{5,21},{6,70},{7,23},{8,72},{9,... | collective-permute-start | bytes 786440 | tf_op jit(solution)/shard_map/reduce_outer/ppermute | solution.py:34
  106.1 9.3 %collective-permute-start.31 = (bf16[4,128,256]{2,1,0:T(8,128)(2,1)S(1)}, bf16[4,128,256]{2,1,0:T(8,128)(2,1)S(1)}, u32[]{:S(2)}, u32[]{:S(2)}) collective-permute-start(bf16[4,128,256]{2,1,0:T(8,128)(2,1)S(1)} %get-tuple-element.53), channel_id=1, source_target_pairs={{0,96},{1,25},{2,98},{3,27},{4,100},{5,29},{6,102},{7,31},{8,104},... | collective-permute-start | bytes 786440 | tf_op jit(solution)/shard_map/reduce_outer/ppermute | solution.py:34
  116.0 1.3 collective-permute-start.32
  117.3 6.4 %collective-permute-start.33 = (f32[128,128]{1,0:T(8,128)S(1)}, f32[128,128]{1,0:T(8,128)S(1)}, u32[]{:S(2)}, u32[]{:S(2)}) collective-permute-start(f32[128,128]{1,0:T(8,128)S(1)} %add.91), channel_id=1, source_target_pairs={{0,4},{2,6},{4,0},{6,2},{1,5},{3,7},{5,1},{7,3},{8,12},{10,14},{12... | collective-permute-start | bytes 196616 | tf_op jit(solution)/shard_map/reduce_gram/ppermute | solution.py:23
  118.3 6.2 %collective-permute-start.34 = (f32[128,128]{1,0:T(8,128)S(1)}, f32[128,128]{1,0:T(8,128)S(1)}, u32[]{:S(2)}, u32[]{:S(2)}) collective-permute-start(f32[128,128]{1,0:T(8,128)S(1)} %add.91), channel_id=1, source_target_pairs={{0,2},{2,4},{4,6},{6,0},{1,3},{3,5},{5,7},{7,1},{8,10},{10,12},{12... | collective-permute-start | bytes 196616 | tf_op jit(solution)/shard_map/reduce_gram/ppermute | solution.py:23
  119.0 5.5 %collective-permute-start.35 = (f32[128,128]{1,0:T(8,128)S(1)}, f32[128,128]{1,0:T(8,128)S(1)}, u32[]{:S(2)}, u32[]{:S(2)}) collective-permute-start(f32[128,128]{1,0:T(8,128)S(1)} %add.91), channel_id=1, source_target_pairs={{0,6},{2,0},{4,2},{6,4},{1,7},{3,1},{5,3},{7,5},{8,14},{10,8},{12,... | collective-permute-start | bytes 196616 | tf_op jit(solution)/shard_map/reduce_gram/ppermute | solution.py:23
  124.5 6.4 %collective-permute-start.36 = (f32[128,128]{1,0:T(8,128)S(1)}, f32[128,128]{1,0:T(8,128)S(1)}, u32[]{:S(2)}, u32[]{:S(2)}) collective-permute-start(f32[128,128]{1,0:T(8,128)S(1)} %add_add_fusion.2), channel_id=1, source_target_pairs={{0,16},{8,24},{16,0},{24,8},{1,17},{9,25},{17,1},{25,9},{2,18},{10... | collective-permute-start | bytes 196616 | tf_op jit(solution)/shard_map/reduce_gram/ppermute | solution.py:23
  126.2 5.5 %collective-permute-start.37 = (f32[128,128]{1,0:T(8,128)S(1)}, f32[128,128]{1,0:T(8,128)S(1)}, u32[]{:S(2)}, u32[]{:S(2)}) collective-permute-start(f32[128,128]{1,0:T(8,128)S(1)} %add_add_fusion.2), channel_id=1, source_target_pairs={{0,8},{8,16},{16,24},{24,0},{1,9},{9,17},{17,25},{25,1},{2,10},{10... | collective-permute-start | bytes 196616 | tf_op jit(solution)/shard_map/reduce_gram/ppermute | solution.py:23
  127.4 4.3 %collective-permute-start.38 = (f32[128,128]{1,0:T(8,128)S(1)}, f32[128,128]{1,0:T(8,128)S(1)}, u32[]{:S(2)}, u32[]{:S(2)}) collective-permute-start(f32[128,128]{1,0:T(8,128)S(1)} %add_add_fusion.2), channel_id=1, source_target_pairs={{0,24},{8,0},{16,8},{24,16},{1,25},{9,1},{17,9},{25,17},{2,26},{10... | collective-permute-start | bytes 196616 | tf_op jit(solution)/shard_map/reduce_gram/ppermute | solution.py:23
  131.7 6.3 %collective-permute-start.39 = (f32[128,128]{1,0:T(8,128)S(1)}, f32[128,128]{1,0:T(8,128)S(1)}, u32[]{:S(2)}, u32[]{:S(2)}) collective-permute-start(f32[128,128]{1,0:T(8,128)S(1)} %add_add_fusion.1), channel_id=1, source_target_pairs={{0,64},{32,96},{64,0},{96,32},{1,65},{33,97},{65,1},{97,33},{2,66}... | collective-permute-start | bytes 196616 | tf_op jit(solution)/shard_map/reduce_gram/ppermute | solution.py:23
  134.7 5.5 %collective-permute-start.40 = (f32[128,128]{1,0:T(8,128)S(1)}, f32[128,128]{1,0:T(8,128)S(1)}, u32[]{:S(2)}, u32[]{:S(2)}) collective-permute-start(f32[128,128]{1,0:T(8,128)S(1)} %add_add_fusion.1), channel_id=1, source_target_pairs={{0,32},{32,64},{64,96},{96,0},{1,33},{33,65},{65,97},{97,1},{2,34}... | collective-permute-start | bytes 196616 | tf_op jit(solution)/shard_map/reduce_gram/ppermute | solution.py:23
  135.3 4.9 %collective-permute-start.41 = (f32[128,128]{1,0:T(8,128)S(1)}, f32[128,128]{1,0:T(8,128)S(1)}, u32[]{:S(2)}, u32[]{:S(2)}) collective-permute-start(f32[128,128]{1,0:T(8,128)S(1)} %add_add_fusion.1), channel_id=1, source_target_pairs={{0,96},{32,0},{64,32},{96,64},{1,97},{33,1},{65,33},{97,65},{2,98}... | collective-permute-start | bytes 196616 | tf_op jit(solution)/shard_map/reduce_gram/ppermute | solution.py:23

commit v11 on v10

--- a/solution.py
+++ b/solution.py
@@ -12,6 +12,7 @@
 SIDE = 256
 RANK = 128
 CHUNK = 32
+EARLY = 3
 EXTRA = 16
 SPARE = 32 * 256 + 64 * 65536
 F32 = jnp.float32
@@ -61,8 +62,8 @@
     return copies
 
 
-def hold_copies(count, tiles, held, sems):
-    chunks = (count[0] + CHUNK - 1) // CHUNK
+def hold_copies(count, tiles, held, sems, first, last):
+    end = jnp.clip((count[0] + CHUNK - 1) // CHUNK, first, last)
 
     def copy(i):
         at = pl.ds(i * CHUNK, CHUNK)
@@ -76,13 +77,19 @@
         copy(i).wait()
         return 0
 
-    return (lambda: lax.fori_loop(0, chunks, start, 0)), (
-        lambda: lax.fori_loop(0, chunks, wait, 0)
+    return (lambda: lax.fori_loop(first, end, start, 0)), (
+        lambda: lax.fori_loop(first, end, wait, 0)
     )
 
 
+def rest_kernel(count, tiles, before, held, sems):
+    start, wait = hold_copies(count, tiles, held, sems, EARLY, sems.shape[0])
+    start()
+    wait()
+
+
 def plan_kernel(count, row_at, col_at, tiles, held, counts, near, far, sems):
-    start, wait = hold_copies(count, tiles, held, sems)
+    start, wait = hold_copies(count, tiles, held, sems, 0, EARLY)
     start()
 
     def place(slot, ends):
@@ -137,6 +144,18 @@
         name="plan_tiles",
         **hold_parameters(tiles),
     )(count, row_at, col_at, tiles)
+
+
+def hold_rest(count, tiles, held):
+    return pl.pallas_call(
+        rest_kernel,
+        out_shape=jax.ShapeDtypeStruct(tiles.shape, tiles.dtype),
+        in_specs=scalars(1) + anywhere(1) + whole(1),
+        out_specs=whole(1)[0],
+        input_output_aliases={2: 0},
+        name="hold_rest",
+        **hold_parameters(tiles),
+    )(count, tiles, held)
 
 
 def listed(total, entries, chunk, body):
@@ -258,7 +277,8 @@
 def backward_near_kernel(counts, near, tiles, *rest):
     pieces, (total, right, left, held, sems) = rest[:8], rest[8:]
     copies = load_pieces(pieces, held, sems)
-    total[...] = jnp.zeros_like(total)
+    total[pl.ds(0, 32)] = jnp.zeros((32, RANK, SIDE), F32)
+    total[pl.ds(48, 17)] = jnp.zeros((17, RANK, SIDE), F32)
     for one in copies:
         one.wait()
 
@@ -505,6 +525,7 @@
         left_low, right_high = cross(low, far_axes, -1), cross(high, far_axes, 1)
         over = (cross(right_low, far_axes, 1), cross(left_high, far_axes, -1))
 
+    held = hold_rest(tile_count, tiles, held)
     keep = forward_near(
         counts, near_list, held, (low, high, left_low, left_high, right_low, right_high)
     )

time: 146 us -> 153 us (1.048)
  starting transfers between devices: 52.5 us -> 64.1 us
  Pallas kernels: 22.8 us -> 20.3 us
  waiting for transfers between devices: 67.7 us -> 65.7 us
    ppermute x24, starting transfers between devices: 24.8 us -> 34 us  [send(): lax.ppermute(array, axis, [(i, (i + step) % size) for i in range(size)])]
    ppermute x18, starting transfers between devices: 27.7 us -> 30.1 us  [cross(): return lax.ppermute(array, AXES, pairs)]
  transfers between devices with their start and end apart: 42 -> 42, of which waited for: 25 -> 27; matrix products, arithmetic and copies ran while one was open for 1% -> 1% of each run, Pallas kernels for 9% -> 7%
where the time goes in v11:
time: 153 us
  waiting for transfers between devices  65.7 us (43%)
  starting transfers between devices  64.1 us (42%)
  Pallas kernels  20.3 us (13%)
  between operations  1.57 us (1%)
    ppermute x24, waiting for transfers between devices, send(): lax.ppermute(array, axis, [(i, (i + step) % size) for i in range(size)])  35.7 us
    ppermute x24, starting transfers between devices, send(): lax.ppermute(array, axis, [(i, (i + step) % size) for i in range(size)])  34 us
    ppermute x18, starting transfers between devices, cross(): return lax.ppermute(array, AXES, pairs)  30.1 us
    ppermute x18, waiting for transfers between devices, cross(): return lax.ppermute(array, AXES, pairs)  30.1 us
    pallas_call x1, Pallas kernels, finish(): pl.pallas_call(kernel, out_shape=(jax.ShapeDtypeStruct((4 * SIDE, RANK),...  5.51 us
    pallas_call x1, Pallas kernels, plan_tiles(): pl.pallas_call(plan_kernel, out_shape=(jax.ShapeDtypeStruct(tiles.shape,...  4.72 us
  transfers between devices with their start and end apart: 42, of which 27 were waited for; matrix products, arithmetic and copies ran while one was open for 1% of the time, Pallas kernels for 7%

profile of v11, /device:TPU:0, one launch (start us, length us, event | category | flops | bytes accessed | tf_op | source)
XLA Modules:
  0.0 152.9 jit_solution(3124514124902545686)
XLA Ops:
  0.6 3.2 %collective-permute-start.1 = (bf16[1024,128]{1,0:T(8,128)(2,1)}, bf16[1024,128]{1,0:T(8,128)(2,1)S(1)}, u32[]{:S(2)}, u32[]{:S(2)}) collective-permute-start(bf16[1024,128]{1,0:T(8,128)(2,1)} %param.4), channel_id=1, source_target_pairs={{0,64},{1,17},{2,66},{3,19},{4,68},{5,21},{6,70},{7,23},{8,72},{9,... | collective-permute-start | bytes 786440 | tf_op jit(solution)/shard_map/gather_basis/ppermute | solution.py:35
  3.8 1.1 collective-permute-start
  5.0 0.9 collective-permute-start.2
  5.9 0.8 fusion.10
  7.3 4.7 %plan_tiles.1 = (bf16[160,256,256]{2,1,0:T(8,128)(2,1)S(1)}, s32[2]{0:T(128)S(1)}, s32[192]{0:T(256)S(1)}, s32[192]{0:T(256)S(1)}) custom-call(s32[1]{0:T(128)S(6)} %copy.10.count, s32[160]{0:T(256)S(1)} %get-tuple-element.59.row_at, s32[160]{0:T(256)S(1)} %get-tuple-element.58.col_at, bf16[160,256,256]{2,1,0:T(8,128)(2,1)} %tiles.3), custom_call_target="tpu_custom_call" | custom-call | bytes 41943040 | tf_op jit(solution)/shard_map/gather_basis/plan_tiles/pallas_call | solution.py:134
  12.1 0.7 collective-permute-done.2
  12.8 3.6 %collective-permute-start.5 = (bf16[8,256,128]{2,1,0:T(8,128)(2,1)S(1)}, bf16[8,256,128]{2,1,0:T(8,128)(2,1)S(1)}, u32[]{:S(2)}, u32[]{:S(2)}) collective-permute-start(bf16[8,256,128]{2,1,0:T(8,128)(2,1)S(1)} %bitcast.4), channel_id=1, source_target_pairs={{0,24},{1,97},{2,26},{3,99},{4,28},{5,101},{6,30},{7,103},{8,0},{9... | collective-permute-start | bytes 1572872 | tf_op jit(solution)/shard_map/gather_basis/ppermute | solution.py:35
  16.6 3.2 %collective-permute-start.7 = (bf16[8,256,128]{2,1,0:T(8,128)(2,1)S(1)}, bf16[8,256,128]{2,1,0:T(8,128)(2,1)S(1)}, u32[]{:S(2)}, u32[]{:S(2)}) collective-permute-start(bf16[8,256,128]{2,1,0:T(8,128)(2,1)S(1)} %bitcast.8), channel_id=1, source_target_pairs={{0,24},{1,97},{2,26},{3,99},{4,28},{5,101},{6,30},{7,103},{8,0},{9... | collective-permute-start | bytes 1572872 | tf_op jit(solution)/shard_map/gather_basis/ppermute | solution.py:35
  19.8 3.3 %collective-permute-done.5.rest_3_ = bf16[8,256,128]{2,1,0:T(8,128)(2,1)S(1)} collective-permute-done((bf16[8,256,128]{2,1,0:T(8,128)(2,1)S(1)}, bf16[8,256,128]{2,1,0:T(8,128)(2,1)S(1)}, u32[]{:S(2)}, u32[]{:S(2)}) %collective-permute-start.5) | collective-permute-done | bytes 524320 | tf_op jit(solution)/shard_map/gather_basis/ppermute | solution.py:35
  23.1 3.7 %collective-permute-start.6 = (bf16[8,256,128]{2,1,0:T(8,128)(2,1)S(1)}, bf16[8,256,128]{2,1,0:T(8,128)(2,1)S(1)}, u32[]{:S(2)}, u32[]{:S(2)}) collective-permute-start(bf16[8,256,128]{2,1,0:T(8,128)(2,1)S(1)} %collective-permute-done.5.rest_3_), channel_id=1, source_target_pairs={{0,24},{1,97},{2,26},{3,99},{4,28},{5,101},{6,30},{7,103},{8,0},{9... | collective-permute-start | bytes 1572872 | tf_op jit(solution)/shard_map/gather_basis/ppermute | solution.py:35
  26.9 5.6 %collective-permute-done.8.rest_5_ = bf16[8,256,128]{2,1,0:T(8,128)(2,1)S(1)} collective-permute-done((bf16[8,256,128]{2,1,0:T(8,128)(2,1)S(1)}, bf16[8,256,128]{2,1,0:T(8,128)(2,1)S(1)}, u32[]{:S(2)}, u32[]{:S(2)}) %collective-permute-start.8) | collective-permute-done | bytes 524320 | tf_op jit(solution)/shard_map/gather_basis/ppermute | solution.py:35
  32.5 2.4 %forward_near.1.before = f32[33,256,128]{2,1,0:T(8,128)S(1)} custom-call(s32[2]{0:T(128)S(1)} %get-tuple-element.29.counts, s32[192]{0:T(256)S(1)} %get-tuple-element.30.near, bf16[160,256,256]{2,1,0:T(8,128)(2,1)S(1)} %hold_rest.1.tiles, bf16[8,256,128]{2,1,0:T(8,128)(2,1)S(1)} %bitcast.9, bf16[8,256,128]{2,1,0:T(8,128)(2,1)S(1)} %bitcast.6, ...), custom_call_target="tpu_custom_call" | custom-call | flops 2013265920 | bytes 1048576 | tf_op jit(solution)/shard_map/forward_near/pallas_call | solution.py:199
  35.0 3.2 %collective-permute-done.4.a = bf16[8,256,128]{2,1,0:T(8,128)(2,1)S(1)} collective-permute-done((bf16[8,256,128]{2,1,0:T(8,128)(2,1)S(1)}, bf16[8,256,128]{2,1,0:T(8,128)(2,1)S(1)}, u32[]{:S(2)}, u32[]{:S(2)}) %collective-permute-start.4) | collective-permute-done | bytes 524320 | tf_op jit(solution)/shard_map/gather_basis/ppermute | solution.py:35
  38.1 1.5 %forward_far.1 = (f32[33,256,128]{2,1,0:T(8,128)S(1)}, f32[4,256,128]{2,1,0:T(8,128)S(1)}, f32[4,256,128]{2,1,0:T(8,128)S(1)}, f32[4,256,128]{2,1,0:T(8,128)S(1)}, f32[4,256,128]{2,1,0:T(8,128)S(1)}) custom-call(s32[2]{0:T(128)S(1)} %get-tuple-element.29.counts, s32[192]{0:T(256)S(1)} %get-tuple-element.33.far, ...), custom_call_target="tpu_custom_call", output_to_operand_aliasing={{0}: (5, {})} | custom-call | tf_op jit(solution)/shard_map/forward_far/pallas_call | solution.py:229
  39.8 0.5 collective-permute-start.12
  40.3 0.4 collective-permute-start.9
  40.8 0.9 collective-permute-done.10.came
  41.9 4.2 %collective-permute-start.11 = (f16[1040,128]{1,0:T(8,128)(2,1)S(1)}, f16[1040,128]{1,0:T(8,128)(2,1)S(1)}, u32[]{:S(2)}, u32[]{:S(2)}) collective-permute-start(f16[1040,128]{1,0:T(8,128)(2,1)S(1)} %convert_element_type.18), channel_id=1, source_target_pairs={{0,4},{2,6},{4,0},{6,2},{1,5},{3,7},{5,1},{7,3},{8,12},{10,14},{12... | collective-permute-start | bytes 798728 | tf_op jit(solution)/shard_map/reduce_inner/ppermute | solution.py:24
  46.4 1.1 collective-permute-start.13
  47.7 2.3 %collective-permute-start.15 = (f16[1040,128]{1,0:T(8,128)(2,1)S(1)}, f16[1040,128]{1,0:T(8,128)(2,1)S(1)}, u32[]{:S(2)}, u32[]{:S(2)}) collective-permute-start(f16[1040,128]{1,0:T(8,128)(2,1)S(1)} %convert_element_type.22), channel_id=1, source_target_pairs={{0,6},{2,0},{4,2},{6,4},{1,7},{3,1},{5,3},{7,5},{8,14},{10,8},{12,... | collective-permute-start | bytes 798728 | tf_op jit(solution)/shard_map/reduce_inner/ppermute | solution.py:24
  50.0 3.3 %collective-permute-done.11 = f16[1040,128]{1,0:T(8,128)(2,1)S(1)} collective-permute-done((f16[1040,128]{1,0:T(8,128)(2,1)S(1)}, f16[1040,128]{1,0:T(8,128)(2,1)S(1)}, u32[]{:S(2)}, u32[]{:S(2)}) %collective-permute-start.11) | collective-permute-done | bytes 266272 | tf_op jit(solution)/shard_map/reduce_inner/ppermute | solution.py:24
  53.4 5.1 %collective-permute-done.13 = f16[1040,128]{1,0:T(8,128)(2,1)S(1)} collective-permute-done((f16[1040,128]{1,0:T(8,128)(2,1)S(1)}, f16[1040,128]{1,0:T(8,128)(2,1)S(1)}, u32[]{:S(2)}, u32[]{:S(2)}) %collective-permute-start.13) | collective-permute-done | bytes 266272 | tf_op jit(solution)/shard_map/reduce_inner/ppermute | solution.py:24
  58.5 0.7 collective-permute-done.15
  59.3 0.3 inner_sum.1.rest_0_
  59.6 1.1 collective-permute-start.18
  60.7 3.0 %collective-permute-start.17 = (bf16[4,128,256]{2,1,0:T(8,128)(2,1)S(1)}, bf16[4,128,256]{2,1,0:T(8,128)(2,1)S(1)}, u32[]{:S(2)}, u32[]{:S(2)}) collective-permute-start(bf16[4,128,256]{2,1,0:T(8,128)(2,1)S(1)} %inner_sum.1.rest_0_), channel_id=1, source_target_pairs={{0,4},{2,6},{4,0},{6,2},{1,5},{3,7},{5,1},{7,3},{8,12},{10,14},{12... | collective-permute-start | bytes 786440 | tf_op jit(solution)/shard_map/gather_inner/ppermute | solution.py:24
  63.8 1.0 collective-permute-start.16
  64.7 4.1 %collective-permute-done.18.rest_3_ = bf16[4,128,256]{2,1,0:T(8,128)(2,1)S(1)} collective-permute-done((bf16[4,128,256]{2,1,0:T(8,128)(2,1)S(1)}, bf16[4,128,256]{2,1,0:T(8,128)(2,1)S(1)}, u32[]{:S(2)}, u32[]{:S(2)}) %collective-permute-start.18) | collective-permute-done | bytes 262176 | tf_op jit(solution)/shard_map/gather_inner/ppermute | solution.py:24
  68.8 6.8 %collective-permute-done.17.rest_2_ = bf16[4,128,256]{2,1,0:T(8,128)(2,1)S(1)} collective-permute-done((bf16[4,128,256]{2,1,0:T(8,128)(2,1)S(1)}, bf16[4,128,256]{2,1,0:T(8,128)(2,1)S(1)}, u32[]{:S(2)}, u32[]{:S(2)}) %collective-permute-start.17) | collective-permute-done | bytes 262176 | tf_op jit(solution)/shard_map/gather_inner/ppermute | solution.py:24
  75.6 0.5 collective-permute-start.20
  76.1 1.0 collective-permute-done.21.rest_6_
  77.1 0.4 collective-permute-done.20.rest_5_
  77.5 1.7 %backward_far.1 = (bf16[8,128,256]{2,1,0:T(8,128)(2,1)S(1)}, bf16[8,128,256]{2,1,0:T(8,128)(2,1)S(1)}) custom-call(s32[2]{0:T(128)S(1)} %get-tuple-element.29.counts, s32[192]{0:T(256)S(1)} %get-tuple-element.33.far, bf16[160,256,256]{2,1,0:T(8,128)(2,1)S(1)} %hold_rest.1.tiles, bf16[4,128,256]{2,1,0:T(8,128)(2,1)S(1)} %inner_sum.1.rest_0_, ...), custom_call_target="tpu_custom_call" | custom-call | tf_op jit(solution)/shard_map/backward_far/pallas_call | solution.py:262
  79.3 3.2 %collective-permute-start.24 = (bf16[8,128,256]{2,1,0:T(8,128)(2,1)S(1)}, bf16[8,128,256]{2,1,0:T(8,128)(2,1)S(1)}, u32[]{:S(2)}, u32[]{:S(2)}) collective-permute-start(bf16[8,128,256]{2,1,0:T(8,128)(2,1)S(1)} %get-tuple-element.45), channel_id=1, source_target_pairs={{0,24},{1,97},{2,26},{3,99},{4,28},{5,101},{6,30},{7,103},{8,0},{9... | collective-permute-start | bytes 1572872 | tf_op jit(solution)/shard_map/reduce_outer/ppermute | solution.py:35
  82.5 2.3 %backward_near.1 = (f32[65,128,256]{2,1,0:T(8,128)S(1)}, bf16[8,128,256]{2,1,0:T(8,128)(2,1)S(1)}, bf16[8,128,256]{2,1,0:T(8,128)(2,1)S(1)}) custom-call(s32[2]{0:T(128)S(1)} %get-tuple-element.29.counts, s32[192]{0:T(256)S(1)} %get-tuple-element.30.near, bf16[160,256,256]{2,1,0:T(8,128)(2,1)S(1)} %hold_rest.1.tiles, ...), custom_call_target="tpu_custom_call" | custom-call | flops 2013265920 | bytes 1048576 | tf_op jit(solution)/shard_map/reduce_outer/backward_near/pallas_call | solution.py:295
  84.9 1.1 collective-permute-start.26
  86.0 1.0 collective-permute-start.27
  87.0 2.7 %collective-permute-done.23.a = bf16[8,128,256]{2,1,0:T(8,128)(2,1)S(1)} collective-permute-done((bf16[8,128,256]{2,1,0:T(8,128)(2,1)S(1)}, bf16[8,128,256]{2,1,0:T(8,128)(2,1)S(1)}, u32[]{:S(2)}, u32[]{:S(2)}) %collective-permute-start.23) | collective-permute-done | bytes 524320 | tf_op jit(solution)/shard_map/reduce_outer/ppermute | solution.py:35
  89.7 0.2 relay_sum.1
  90.0 3.3 %collective-permute-start.28 = (bf16[8,128,256]{2,1,0:T(8,128)(2,1)S(1)}, bf16[8,128,256]{2,1,0:T(8,128)(2,1)S(1)}, u32[]{:S(2)}, u32[]{:S(2)}) collective-permute-start(bf16[8,128,256]{2,1,0:T(8,128)(2,1)S(1)} %get-tuple-element.49), channel_id=1, source_target_pairs={{0,24},{1,97},{2,26},{3,99},{4,28},{5,101},{6,30},{7,103},{8,0},{9... | collective-permute-start | bytes 1572872 | tf_op jit(solution)/shard_map/reduce_outer/ppermute | solution.py:35
  93.3 1.6 %collective-permute-done.26.rest_1_ = bf16[8,128,256]{2,1,0:T(8,128)(2,1)S(1)} collective-permute-done((bf16[8,128,256]{2,1,0:T(8,128)(2,1)S(1)}, bf16[8,128,256]{2,1,0:T(8,128)(2,1)S(1)}, u32[]{:S(2)}, u32[]{:S(2)}) %collective-permute-start.26) | collective-permute-done | bytes 524320 | tf_op jit(solution)/shard_map/reduce_outer/ppermute | solution.py:35
  94.9 1.5 %collective-permute-done.27.rest_2_ = bf16[8,128,256]{2,1,0:T(8,128)(2,1)S(1)} collective-permute-done((bf16[8,128,256]{2,1,0:T(8,128)(2,1)S(1)}, bf16[8,128,256]{2,1,0:T(8,128)(2,1)S(1)}, u32[]{:S(2)}, u32[]{:S(2)}) %collective-permute-start.27) | collective-permute-done | bytes 524320 | tf_op jit(solution)/shard_map/reduce_outer/ppermute | solution.py:35
  96.4 5.6 %collective-permute-done.25.rest_0_ = bf16[8,128,256]{2,1,0:T(8,128)(2,1)S(1)} collective-permute-done((bf16[8,128,256]{2,1,0:T(8,128)(2,1)S(1)}, bf16[8,128,256]{2,1,0:T(8,128)(2,1)S(1)}, u32[]{:S(2)}, u32[]{:S(2)}) %collective-permute-start.25) | collective-permute-done | bytes 524320 | tf_op jit(solution)/shard_map/reduce_outer/ppermute | solution.py:35
  102.0 0.3 middle_sum.1
  102.4 0.4 collective-permute-start.29
  102.8 3.4 %collective-permute-start.30 = (bf16[4,128,256]{2,1,0:T(8,128)(2,1)S(1)}, bf16[4,128,256]{2,1,0:T(8,128)(2,1)S(1)}, u32[]{:S(2)}, u32[]{:S(2)}) collective-permute-start(bf16[4,128,256]{2,1,0:T(8,128)(2,1)S(1)} %get-tuple-element.52), channel_id=1, source_target_pairs={{0,64},{1,17},{2,66},{3,19},{4,68},{5,21},{6,70},{7,23},{8,72},{9,... | collective-permute-start | bytes 786440 | tf_op jit(solution)/shard_map/reduce_outer/ppermute | solution.py:35
  106.1 1.7 %collective-permute-start.31 = (bf16[4,128,256]{2,1,0:T(8,128)(2,1)S(1)}, bf16[4,128,256]{2,1,0:T(8,128)(2,1)S(1)}, u32[]{:S(2)}, u32[]{:S(2)}) collective-permute-start(bf16[4,128,256]{2,1,0:T(8,128)(2,1)S(1)} %get-tuple-element.53), channel_id=1, source_target_pairs={{0,96},{1,25},{2,98},{3,27},{4,100},{5,29},{6,102},{7,31},{8,104},... | collective-permute-start | bytes 786440 | tf_op jit(solution)/shard_map/reduce_outer/ppermute | solution.py:35
  107.9 2.1 %collective-permute-done.29.a = bf16[4,128,256]{2,1,0:T(8,128)(2,1)S(1)} collective-permute-done((bf16[4,128,256]{2,1,0:T(8,128)(2,1)S(1)}, bf16[4,128,256]{2,1,0:T(8,128)(2,1)S(1)}, u32[]{:S(2)}, u32[]{:S(2)}) %collective-permute-start.29) | collective-permute-done | bytes 262176 | tf_op jit(solution)/shard_map/reduce_outer/ppermute | solution.py:35
  110.0 3.3 %collective-permute-done.30.b = bf16[4,128,256]{2,1,0:T(8,128)(2,1)S(1)} collective-permute-done((bf16[4,128,256]{2,1,0:T(8,128)(2,1)S(1)}, bf16[4,128,256]{2,1,0:T(8,128)(2,1)S(1)}, u32[]{:S(2)}, u32[]{:S(2)}) %collective-permute-start.30) | collective-permute-done | bytes 262176 | tf_op jit(solution)/shard_map/reduce_outer/ppermute | solution.py:35
  113.3 0.4 collective-permute-done.31.c
  113.7 0.6 outer_sum.1
  114.4 1.2 collective-permute-done.32
  115.6 2.5 %collective-permute-start.35 = (f32[128,128]{1,0:T(8,128)S(1)}, f32[128,128]{1,0:T(8,128)S(1)}, u32[]{:S(2)}, u32[]{:S(2)}) collective-permute-start(f32[128,128]{1,0:T(8,128)S(1)} %add.91), channel_id=1, source_target_pairs={{0,6},{2,0},{4,2},{6,4},{1,7},{3,1},{5,3},{7,5},{8,14},{10,8},{12,... | collective-permute-start | bytes 196616 | tf_op jit(solution)/shard_map/reduce_gram/ppermute | solution.py:24
  118.1 8.8 %collective-permute-start.33 = (f32[128,128]{1,0:T(8,128)S(1)}, f32[128,128]{1,0:T(8,128)S(1)}, u32[]{:S(2)}, u32[]{:S(2)}) collective-permute-start(f32[128,128]{1,0:T(8,128)S(1)} %add.91), channel_id=1, source_target_pairs={{0,4},{2,6},{4,0},{6,2},{1,5},{3,7},{5,1},{7,3},{8,12},{10,14},{12... | collective-permute-start | bytes 196616 | tf_op jit(solution)/shard_map/reduce_gram/ppermute | solution.py:24
  126.9 0.8 collective-permute-done.34
  127.7 2.5 %collective-permute-done.33 = f32[128,128]{1,0:T(8,128)S(1)} collective-permute-done((f32[128,128]{1,0:T(8,128)S(1)}, f32[128,128]{1,0:T(8,128)S(1)}, u32[]{:S(2)}, u32[]{:S(2)}) %collective-permute-start.33) | collective-permute-done | bytes 65568 | tf_op jit(solution)/shard_map/reduce_gram/ppermute | solution.py:24
  130.3 2.0 %collective-permute-start.37 = (f32[128,128]{1,0:T(8,128)S(1)}, f32[128,128]{1,0:T(8,128)S(1)}, u32[]{:S(2)}, u32[]{:S(2)}) collective-permute-start(f32[128,128]{1,0:T(8,128)S(1)} %add_add_fusion.2), channel_id=1, source_target_pairs={{0,8},{8,16},{16,24},{24,0},{1,9},{9,17},{17,25},{25,1},{2,10},{10... | collective-permute-start | bytes 196616 | tf_op jit(solution)/shard_map/reduce_gram/ppermute | solution.py:24
  132.3 2.6 %collective-permute-done.38 = f32[128,128]{1,0:T(8,128)S(1)} collective-permute-done((f32[128,128]{1,0:T(8,128)S(1)}, f32[128,128]{1,0:T(8,128)S(1)}, u32[]{:S(2)}, u32[]{:S(2)}) %collective-permute-start.38) | collective-permute-done | bytes 65568 | tf_op jit(solution)/shard_map/reduce_gram/ppermute | solution.py:24
  134.8 1.1 collective-permute-done.37
  135.9 2.1 %collective-permute-done.36 = f32[128,128]{1,0:T(8,128)S(1)} collective-permute-done((f32[128,128]{1,0:T(8,128)S(1)}, f32[128,128]{1,0:T(8,128)S(1)}, u32[]{:S(2)}, u32[]{:S(2)}) %collective-permute-start.36) | collective-permute-done | bytes 65568 | tf_op jit(solution)/shard_map/reduce_gram/ppermute | solution.py:24
  138.1 3.1 %collective-permute-start.41 = (f32[128,128]{1,0:T(8,128)S(1)}, f32[128,128]{1,0:T(8,128)S(1)}, u32[]{:S(2)}, u32[]{:S(2)}) collective-permute-start(f32[128,128]{1,0:T(8,128)S(1)} %add_add_fusion.1), channel_id=1, source_target_pairs={{0,96},{32,0},{64,32},{96,64},{1,97},{33,1},{65,33},{97,65},{2,98}... | collective-permute-start | bytes 196616 | tf_op jit(solution)/shard_map/reduce_gram/ppermute | solution.py:24
  141.2 3.1 %collective-permute-start.39 = (f32[128,128]{1,0:T(8,128)S(1)}, f32[128,128]{1,0:T(8,128)S(1)}, u32[]{:S(2)}, u32[]{:S(2)}) collective-permute-start(f32[128,128]{1,0:T(8,128)S(1)} %add_add_fusion.1), channel_id=1, source_target_pairs={{0,64},{32,96},{64,0},{96,32},{1,65},{33,97},{65,1},{97,33},{2,66}... | collective-permute-start | bytes 196616 | tf_op jit(solution)/shard_map/reduce_gram/ppermute | solution.py:24
  144.3 3.1 %collective-permute-done.40 = f32[128,128]{1,0:T(8,128)S(1)} collective-permute-done((f32[128,128]{1,0:T(8,128)S(1)}, f32[128,128]{1,0:T(8,128)S(1)}, u32[]{:S(2)}, u32[]{:S(2)}) %collective-permute-start.40) | collective-permute-done | bytes 65568 | tf_op jit(solution)/shard_map/reduce_gram/ppermute | solution.py:24
  147.4 5.5 %finish.1 = (f32[1024,128]{1,0:T(8,128)}, f32[128,128]{1,0:T(8,128)}) custom-call(f32[128,128]{1,0:T(8,128)S(1)} %add_add_fusion.refs_0_, f32[4,128,256]{2,1,0:T(8,128)S(1)} %get-tuple-element.55.refs_1_), custom_call_target="tpu_custom_call" | custom-call | tf_op jit(solution)/shard_map/finish/pallas_call | solution.py:488
  (50 shorter events, 1.8 us)
Async XLA Ops:
  0.6 15.8 %copy-start = (bf16[1024,128]{1,0:T(8,128)(2,1)S(1)}, bf16[1024,128]{1,0:T(8,128)(2,1)}, u32[]{:S(2)}) copy-start(bf16[1024,128]{1,0:T(8,128)(2,1)} %param.4) | copy-start | bytes 786436
  0.6 11.4 %collective-permute-start.1 = (bf16[1024,128]{1,0:T(8,128)(2,1)}, bf16[1024,128]{1,0:T(8,128)(2,1)S(1)}, u32[]{:S(2)}, u32[]{:S(2)}) collective-permute-start(bf16[1024,128]{1,0:T(8,128)(2,1)} %param.4), channel_id=1, source_target_pairs={{0,64},{1,17},{2,66},{3,19},{4,68},{5,21},{6,70},{7,23},{8,72},{9,... | collective-permute-start | bytes 786440 | tf_op jit(solution)/shard_map/gather_basis/ppermute | solution.py:35
  3.8 8.2 %collective-permute-start = (bf16[1024,128]{1,0:T(8,128)(2,1)}, bf16[1024,128]{1,0:T(8,128)(2,1)S(1)}, u32[]{:S(2)}, u32[]{:S(2)}) collective-permute-start(bf16[1024,128]{1,0:T(8,128)(2,1)} %param.4), channel_id=1, source_target_pairs={{0,96},{1,25},{2,98},{3,27},{4,100},{5,29},{6,102},{7,31},{8,104},... | collective-permute-start | bytes 786440 | tf_op jit(solution)/shard_map/gather_basis/ppermute | solution.py:35
  5.0 7.8 %collective-permute-start.2 = (bf16[1024,128]{1,0:T(8,128)(2,1)}, bf16[1024,128]{1,0:T(8,128)(2,1)S(1)}, u32[]{:S(2)}, u32[]{:S(2)}) collective-permute-start(bf16[1024,128]{1,0:T(8,128)(2,1)} %param.4), channel_id=1, source_target_pairs={{0,32},{1,9},{2,34},{3,11},{4,36},{5,13},{6,38},{7,15},{8,40},{9,1... | collective-permute-start | bytes 786440 | tf_op jit(solution)/shard_map/gather_basis/ppermute | solution.py:35
  12.8 10.3 %collective-permute-start.5 = (bf16[8,256,128]{2,1,0:T(8,128)(2,1)S(1)}, bf16[8,256,128]{2,1,0:T(8,128)(2,1)S(1)}, u32[]{:S(2)}, u32[]{:S(2)}) collective-permute-start(bf16[8,256,128]{2,1,0:T(8,128)(2,1)S(1)} %bitcast.4), channel_id=1, source_target_pairs={{0,24},{1,97},{2,26},{3,99},{4,28},{5,101},{6,30},{7,103},{8,0},{9... | collective-permute-start | bytes 1572872 | tf_op jit(solution)/shard_map/gather_basis/ppermute | solution.py:35
  16.4 10.5 %collective-permute-start.3 = (bf16[8,256,128]{2,1,0:T(8,128)(2,1)S(1)}, bf16[8,256,128]{2,1,0:T(8,128)(2,1)S(1)}, u32[]{:S(2)}, u32[]{:S(2)}) collective-permute-start(bf16[8,256,128]{2,1,0:T(8,128)(2,1)S(1)} %bitcast.7), channel_id=1, source_target_pairs={{0,8},{1,33},{2,10},{3,35},{4,12},{5,37},{6,14},{7,39},{8,16},{9,4... | collective-permute-start | bytes 1572872 | tf_op jit(solution)/shard_map/gather_basis/ppermute | solution.py:35
  16.5 16.0 %collective-permute-start.8 = (bf16[8,256,128]{2,1,0:T(8,128)(2,1)S(1)}, bf16[8,256,128]{2,1,0:T(8,128)(2,1)S(1)}, u32[]{:S(2)}, u32[]{:S(2)}) collective-permute-start(bf16[8,256,128]{2,1,0:T(8,128)(2,1)S(1)} %bitcast.5), channel_id=1, source_target_pairs={{0,8},{1,33},{2,10},{3,35},{4,12},{5,37},{6,14},{7,39},{8,16},{9,4... | collective-permute-start | bytes 1572872 | tf_op jit(solution)/shard_map/gather_basis/ppermute | solution.py:35
  16.6 15.9 %collective-permute-start.7 = (bf16[8,256,128]{2,1,0:T(8,128)(2,1)S(1)}, bf16[8,256,128]{2,1,0:T(8,128)(2,1)S(1)}, u32[]{:S(2)}, u32[]{:S(2)}) collective-permute-start(bf16[8,256,128]{2,1,0:T(8,128)(2,1)S(1)} %bitcast.8), channel_id=1, source_target_pairs={{0,24},{1,97},{2,26},{3,99},{4,28},{5,101},{6,30},{7,103},{8,0},{9... | collective-permute-start | bytes 1572872 | tf_op jit(solution)/shard_map/gather_basis/ppermute | solution.py:35
  23.1 11.9 %collective-permute-start.6 = (bf16[8,256,128]{2,1,0:T(8,128)(2,1)S(1)}, bf16[8,256,128]{2,1,0:T(8,128)(2,1)S(1)}, u32[]{:S(2)}, u32[]{:S(2)}) collective-permute-start(bf16[8,256,128]{2,1,0:T(8,128)(2,1)S(1)} %collective-permute-done.5.rest_3_), channel_id=1, source_target_pairs={{0,24},{1,97},{2,26},{3,99},{4,28},{5,101},{6,30},{7,103},{8,0},{9... | collective-permute-start | bytes 1572872 | tf_op jit(solution)/shard_map/gather_basis/ppermute | solution.py:35
  26.9 11.2 %collective-permute-start.4 = (bf16[8,256,128]{2,1,0:T(8,128)(2,1)S(1)}, bf16[8,256,128]{2,1,0:T(8,128)(2,1)S(1)}, u32[]{:S(2)}, u32[]{:S(2)}) collective-permute-start(bf16[8,256,128]{2,1,0:T(8,128)(2,1)S(1)} %collective-permute-done.3.rest_4_), channel_id=1, source_target_pairs={{0,8},{1,33},{2,10},{3,35},{4,12},{5,37},{6,14},{7,39},{8,16},{9,4... | collective-permute-start | bytes 1572872 | tf_op jit(solution)/shard_map/gather_basis/ppermute | solution.py:35
  39.7 2.0 %collective-permute-start.10 = (f32[4,256,128]{2,1,0:T(8,128)S(1)}, f32[4,256,128]{2,1,0:T(8,128)S(1)}, u32[]{:S(2)}, u32[]{:S(2)}) collective-permute-start(f32[4,256,128]{2,1,0:T(8,128)S(1)} %get-tuple-element.40), channel_id=1, source_target_pairs={{0,1},{1,0},{2,3},{3,2},{4,5},{5,4},{6,7},{7,6},{8,9},{9,8},{10,11... | collective-permute-start | bytes 1572872 | tf_op jit(solution)/shard_map/reduce_inner/ppermute | solution.py:24
  39.8 6.4 %collective-permute-start.12 = (f32[4,256,128]{2,1,0:T(8,128)S(1)}, f32[4,256,128]{2,1,0:T(8,128)S(1)}, u32[]{:S(2)}, u32[]{:S(2)}) collective-permute-start(f32[4,256,128]{2,1,0:T(8,128)S(1)} %get-tuple-element.41), channel_id=1, source_target_pairs={{0,1},{1,0},{2,3},{3,2},{4,5},{5,4},{6,7},{7,6},{8,9},{9,8},{10,11... | collective-permute-start | bytes 1572872 | tf_op jit(solution)/shard_map/reduce_inner/ppermute | solution.py:24
  40.3 7.2 %collective-permute-start.14 = (f32[4,256,128]{2,1,0:T(8,128)S(1)}, f32[4,256,128]{2,1,0:T(8,128)S(1)}, u32[]{:S(2)}, u32[]{:S(2)}) collective-permute-start(f32[4,256,128]{2,1,0:T(8,128)S(1)} %get-tuple-element.42), channel_id=1, source_target_pairs={{0,1},{1,0},{2,3},{3,2},{4,5},{5,4},{6,7},{7,6},{8,9},{9,8},{10,11... | collective-permute-start | bytes 1572872 | tf_op jit(solution)/shard_map/reduce_inner/ppermute | solution.py:24
  40.3 19.0 %collective-permute-start.9 = (f32[4,256,128]{2,1,0:T(8,128)S(1)}, f32[4,256,128]{2,1,0:T(8,128)S(1)}, u32[]{:S(2)}, u32[]{:S(2)}) collective-permute-start(f32[4,256,128]{2,1,0:T(8,128)S(1)} %get-tuple-element.39), channel_id=1, source_target_pairs={{0,1},{1,0},{2,3},{3,2},{4,5},{5,4},{6,7},{7,6},{8,9},{9,8},{10,11... | collective-permute-start | bytes 1572872 | tf_op jit(solution)/shard_map/reduce_inner/ppermute | solution.py:24
  41.9 11.4 %collective-permute-start.11 = (f16[1040,128]{1,0:T(8,128)(2,1)S(1)}, f16[1040,128]{1,0:T(8,128)(2,1)S(1)}, u32[]{:S(2)}, u32[]{:S(2)}) collective-permute-start(f16[1040,128]{1,0:T(8,128)(2,1)S(1)} %convert_element_type.18), channel_id=1, source_target_pairs={{0,4},{2,6},{4,0},{6,2},{1,5},{3,7},{5,1},{7,3},{8,12},{10,14},{12... | collective-permute-start | bytes 798728 | tf_op jit(solution)/shard_map/reduce_inner/ppermute | solution.py:24
  46.4 12.1 %collective-permute-start.13 = (f16[1040,128]{1,0:T(8,128)(2,1)S(1)}, f16[1040,128]{1,0:T(8,128)(2,1)S(1)}, u32[]{:S(2)}, u32[]{:S(2)}) collective-permute-start(f16[1040,128]{1,0:T(8,128)(2,1)S(1)} %convert_element_type.20), channel_id=1, source_target_pairs={{0,2},{2,4},{4,6},{6,0},{1,3},{3,5},{5,7},{7,1},{8,10},{10,12},{12... | collective-permute-start | bytes 798728 | tf_op jit(solution)/shard_map/reduce_inner/ppermute | solution.py:24
  47.7 11.6 %collective-permute-start.15 = (f16[1040,128]{1,0:T(8,128)(2,1)S(1)}, f16[1040,128]{1,0:T(8,128)(2,1)S(1)}, u32[]{:S(2)}, u32[]{:S(2)}) collective-permute-start(f16[1040,128]{1,0:T(8,128)(2,1)S(1)} %convert_element_type.22), channel_id=1, source_target_pairs={{0,6},{2,0},{4,2},{6,4},{1,7},{3,1},{5,3},{7,5},{8,14},{10,8},{12,... | collective-permute-start | bytes 798728 | tf_op jit(solution)/shard_map/reduce_inner/ppermute | solution.py:24
  59.6 9.2 %collective-permute-start.18 = (bf16[4,128,256]{2,1,0:T(8,128)(2,1)S(1)}, bf16[4,128,256]{2,1,0:T(8,128)(2,1)S(1)}, u32[]{:S(2)}, u32[]{:S(2)}) collective-permute-start(bf16[4,128,256]{2,1,0:T(8,128)(2,1)S(1)} %inner_sum.1.rest_0_), channel_id=1, source_target_pairs={{0,2},{2,4},{4,6},{6,0},{1,3},{3,5},{5,7},{7,1},{8,10},{10,12},{12... | collective-permute-start | bytes 786440 | tf_op jit(solution)/shard_map/gather_inner/ppermute | solution.py:24
  60.7 14.8 %collective-permute-start.17 = (bf16[4,128,256]{2,1,0:T(8,128)(2,1)S(1)}, bf16[4,128,256]{2,1,0:T(8,128)(2,1)S(1)}, u32[]{:S(2)}, u32[]{:S(2)}) collective-permute-start(bf16[4,128,256]{2,1,0:T(8,128)(2,1)S(1)} %inner_sum.1.rest_0_), channel_id=1, source_target_pairs={{0,4},{2,6},{4,0},{6,2},{1,5},{3,7},{5,1},{7,3},{8,12},{10,14},{12... | collective-permute-start | bytes 786440 | tf_op jit(solution)/shard_map/gather_inner/ppermute | solution.py:24
  63.8 11.8 %collective-permute-start.16 = (bf16[4,128,256]{2,1,0:T(8,128)(2,1)S(1)}, bf16[4,128,256]{2,1,0:T(8,128)(2,1)S(1)}, u32[]{:S(2)}, u32[]{:S(2)}) collective-permute-start(bf16[4,128,256]{2,1,0:T(8,128)(2,1)S(1)} %inner_sum.1.rest_0_), channel_id=1, source_target_pairs={{0,6},{2,0},{4,2},{6,4},{1,7},{3,1},{5,3},{7,5},{8,14},{10,8},{12,... | collective-permute-start | bytes 786440 | tf_op jit(solution)/shard_map/gather_inner/ppermute | solution.py:24
  64.7 11.4 %collective-permute-start.19 = (bf16[4,128,256]{2,1,0:T(8,128)(2,1)S(1)}, bf16[4,128,256]{2,1,0:T(8,128)(2,1)S(1)}, u32[]{:S(2)}, u32[]{:S(2)}) collective-permute-start(bf16[4,128,256]{2,1,0:T(8,128)(2,1)S(1)} %inner_sum.1.rest_0_), channel_id=1, source_target_pairs={{0,1},{1,0},{2,3},{3,2},{4,5},{5,4},{6,7},{7,6},{8,9},{9,8},{10,11... | collective-permute-start | bytes 786440 | tf_op jit(solution)/shard_map/gather_inner/ppermute | solution.py:24
  68.8 7.3 %collective-permute-start.22 = (bf16[4,128,256]{2,1,0:T(8,128)(2,1)S(1)}, bf16[4,128,256]{2,1,0:T(8,128)(2,1)S(1)}, u32[]{:S(2)}, u32[]{:S(2)}) collective-permute-start(bf16[4,128,256]{2,1,0:T(8,128)(2,1)S(1)} %collective-permute-done.18.rest_3_), channel_id=1, source_target_pairs={{0,1},{1,0},{2,3},{3,2},{4,5},{5,4},{6,7},{7,6},{8,9},{9,8},{10,11... | collective-permute-start | bytes 786440 | tf_op jit(solution)/shard_map/gather_inner/ppermute | solution.py:24
  75.6 1.5 %collective-permute-start.21 = (bf16[4,128,256]{2,1,0:T(8,128)(2,1)S(1)}, bf16[4,128,256]{2,1,0:T(8,128)(2,1)S(1)}, u32[]{:S(2)}, u32[]{:S(2)}) collective-permute-start(bf16[4,128,256]{2,1,0:T(8,128)(2,1)S(1)} %collective-permute-done.17.rest_2_), channel_id=1, source_target_pairs={{0,1},{1,0},{2,3},{3,2},{4,5},{5,4},{6,7},{7,6},{8,9},{9,8},{10,11... | collective-permute-start | bytes 786440 | tf_op jit(solution)/shard_map/gather_inner/ppermute | solution.py:24
  75.6 1.9 %collective-permute-start.20 = (bf16[4,128,256]{2,1,0:T(8,128)(2,1)S(1)}, bf16[4,128,256]{2,1,0:T(8,128)(2,1)S(1)}, u32[]{:S(2)}, u32[]{:S(2)}) collective-permute-start(bf16[4,128,256]{2,1,0:T(8,128)(2,1)S(1)} %collective-permute-done.16.rest_1_), channel_id=1, source_target_pairs={{0,1},{1,0},{2,3},{3,2},{4,5},{5,4},{6,7},{7,6},{8,9},{9,8},{10,11... | collective-permute-start | bytes 786440 | tf_op jit(solution)/shard_map/gather_inner/ppermute | solution.py:24
  79.2 10.5 %collective-permute-start.23 = (bf16[8,128,256]{2,1,0:T(8,128)(2,1)S(1)}, bf16[8,128,256]{2,1,0:T(8,128)(2,1)S(1)}, u32[]{:S(2)}, u32[]{:S(2)}) collective-permute-start(bf16[8,128,256]{2,1,0:T(8,128)(2,1)S(1)} %get-tuple-element.44), channel_id=1, source_target_pairs={{0,8},{1,33},{2,10},{3,35},{4,12},{5,37},{6,14},{7,39},{8,16},{9,4... | collective-permute-start | bytes 1572872 | tf_op jit(solution)/shard_map/reduce_outer/ppermute | solution.py:35
  79.3 10.4 %collective-permute-start.24 = (bf16[8,128,256]{2,1,0:T(8,128)(2,1)S(1)}, bf16[8,128,256]{2,1,0:T(8,128)(2,1)S(1)}, u32[]{:S(2)}, u32[]{:S(2)}) collective-permute-start(bf16[8,128,256]{2,1,0:T(8,128)(2,1)S(1)} %get-tuple-element.45), channel_id=1, source_target_pairs={{0,24},{1,97},{2,26},{3,99},{4,28},{5,101},{6,30},{7,103},{8,0},{9... | collective-permute-start | bytes 1572872 | tf_op jit(solution)/shard_map/reduce_outer/ppermute | solution.py:35
  84.9 10.0 %collective-permute-start.26 = (bf16[8,128,256]{2,1,0:T(8,128)(2,1)S(1)}, bf16[8,128,256]{2,1,0:T(8,128)(2,1)S(1)}, u32[]{:S(2)}, u32[]{:S(2)}) collective-permute-start(bf16[8,128,256]{2,1,0:T(8,128)(2,1)S(1)} %get-tuple-element.47), channel_id=1, source_target_pairs={{0,24},{1,97},{2,26},{3,99},{4,28},{5,101},{6,30},{7,103},{8,0},{9... | collective-permute-start | bytes 1572872 | tf_op jit(solution)/shard_map/reduce_outer/ppermute | solution.py:35
  86.0 10.4 %collective-permute-start.27 = (bf16[8,128,256]{2,1,0:T(8,128)(2,1)S(1)}, bf16[8,128,256]{2,1,0:T(8,128)(2,1)S(1)}, u32[]{:S(2)}, u32[]{:S(2)}) collective-permute-start(bf16[8,128,256]{2,1,0:T(8,128)(2,1)S(1)} %get-tuple-element.48), channel_id=1, source_target_pairs={{0,8},{1,33},{2,10},{3,35},{4,12},{5,37},{6,14},{7,39},{8,16},{9,4... | collective-permute-start | bytes 1572872 | tf_op jit(solution)/shard_map/reduce_outer/ppermute | solution.py:35
  89.9 12.1 %collective-permute-start.25 = (bf16[8,128,256]{2,1,0:T(8,128)(2,1)S(1)}, bf16[8,128,256]{2,1,0:T(8,128)(2,1)S(1)}, u32[]{:S(2)}, u32[]{:S(2)}) collective-permute-start(bf16[8,128,256]{2,1,0:T(8,128)(2,1)S(1)} %get-tuple-element.46), channel_id=1, source_target_pairs={{0,8},{1,33},{2,10},{3,35},{4,12},{5,37},{6,14},{7,39},{8,16},{9,4... | collective-permute-start | bytes 1572872 | tf_op jit(solution)/shard_map/reduce_outer/ppermute | solution.py:35
  90.0 12.0 %collective-permute-start.28 = (bf16[8,128,256]{2,1,0:T(8,128)(2,1)S(1)}, bf16[8,128,256]{2,1,0:T(8,128)(2,1)S(1)}, u32[]{:S(2)}, u32[]{:S(2)}) collective-permute-start(bf16[8,128,256]{2,1,0:T(8,128)(2,1)S(1)} %get-tuple-element.49), channel_id=1, source_target_pairs={{0,24},{1,97},{2,26},{3,99},{4,28},{5,101},{6,30},{7,103},{8,0},{9... | collective-permute-start | bytes 1572872 | tf_op jit(solution)/shard_map/reduce_outer/ppermute | solution.py:35
  102.4 7.7 %collective-permute-start.29 = (bf16[4,128,256]{2,1,0:T(8,128)(2,1)S(1)}, bf16[4,128,256]{2,1,0:T(8,128)(2,1)S(1)}, u32[]{:S(2)}, u32[]{:S(2)}) collective-permute-start(bf16[4,128,256]{2,1,0:T(8,128)(2,1)S(1)} %get-tuple-element.51), channel_id=1, source_target_pairs={{0,32},{1,9},{2,34},{3,11},{4,36},{5,13},{6,38},{7,15},{8,40},{9,1... | collective-permute-start | bytes 786440 | tf_op jit(solution)/shard_map/reduce_outer/ppermute | solution.py:35
  102.8 10.5 %collective-permute-start.30 = (bf16[4,128,256]{2,1,0:T(8,128)(2,1)S(1)}, bf16[4,128,256]{2,1,0:T(8,128)(2,1)S(1)}, u32[]{:S(2)}, u32[]{:S(2)}) collective-permute-start(bf16[4,128,256]{2,1,0:T(8,128)(2,1)S(1)} %get-tuple-element.52), channel_id=1, source_target_pairs={{0,64},{1,17},{2,66},{3,19},{4,68},{5,21},{6,70},{7,23},{8,72},{9,... | collective-permute-start | bytes 786440 | tf_op jit(solution)/shard_map/reduce_outer/ppermute | solution.py:35
  106.1 7.5 %collective-permute-start.31 = (bf16[4,128,256]{2,1,0:T(8,128)(2,1)S(1)}, bf16[4,128,256]{2,1,0:T(8,128)(2,1)S(1)}, u32[]{:S(2)}, u32[]{:S(2)}) collective-permute-start(bf16[4,128,256]{2,1,0:T(8,128)(2,1)S(1)} %get-tuple-element.53), channel_id=1, source_target_pairs={{0,96},{1,25},{2,98},{3,27},{4,100},{5,29},{6,102},{7,31},{8,104},... | collective-permute-start | bytes 786440 | tf_op jit(solution)/shard_map/reduce_outer/ppermute | solution.py:35
  114.3 1.3 collective-permute-start.32
  115.6 11.3 %collective-permute-start.35 = (f32[128,128]{1,0:T(8,128)S(1)}, f32[128,128]{1,0:T(8,128)S(1)}, u32[]{:S(2)}, u32[]{:S(2)}) collective-permute-start(f32[128,128]{1,0:T(8,128)S(1)} %add.91), channel_id=1, source_target_pairs={{0,6},{2,0},{4,2},{6,4},{1,7},{3,1},{5,3},{7,5},{8,14},{10,8},{12,... | collective-permute-start | bytes 196616 | tf_op jit(solution)/shard_map/reduce_gram/ppermute | solution.py:24
  118.1 9.6 %collective-permute-start.34 = (f32[128,128]{1,0:T(8,128)S(1)}, f32[128,128]{1,0:T(8,128)S(1)}, u32[]{:S(2)}, u32[]{:S(2)}) collective-permute-start(f32[128,128]{1,0:T(8,128)S(1)} %add.91), channel_id=1, source_target_pairs={{0,2},{2,4},{4,6},{6,0},{1,3},{3,5},{5,7},{7,1},{8,10},{10,12},{12... | collective-permute-start | bytes 196616 | tf_op jit(solution)/shard_map/reduce_gram/ppermute | solution.py:24
  118.1 12.0 %collective-permute-start.33 = (f32[128,128]{1,0:T(8,128)S(1)}, f32[128,128]{1,0:T(8,128)S(1)}, u32[]{:S(2)}, u32[]{:S(2)}) collective-permute-start(f32[128,128]{1,0:T(8,128)S(1)} %add.91), channel_id=1, source_target_pairs={{0,4},{2,6},{4,0},{6,2},{1,5},{3,7},{5,1},{7,3},{8,12},{10,14},{12... | collective-permute-start | bytes 196616 | tf_op jit(solution)/shard_map/reduce_gram/ppermute | solution.py:24
  130.2 4.7 %collective-permute-start.38 = (f32[128,128]{1,0:T(8,128)S(1)}, f32[128,128]{1,0:T(8,128)S(1)}, u32[]{:S(2)}, u32[]{:S(2)}) collective-permute-start(f32[128,128]{1,0:T(8,128)S(1)} %add_add_fusion.2), channel_id=1, source_target_pairs={{0,24},{8,0},{16,8},{24,16},{1,25},{9,1},{17,9},{25,17},{2,26},{10... | collective-permute-start | bytes 196616 | tf_op jit(solution)/shard_map/reduce_gram/ppermute | solution.py:24
  130.3 5.7 %collective-permute-start.37 = (f32[128,128]{1,0:T(8,128)S(1)}, f32[128,128]{1,0:T(8,128)S(1)}, u32[]{:S(2)}, u32[]{:S(2)}) collective-permute-start(f32[128,128]{1,0:T(8,128)S(1)} %add_add_fusion.2), channel_id=1, source_target_pairs={{0,8},{8,16},{16,24},{24,0},{1,9},{9,17},{17,25},{25,1},{2,10},{10... | collective-permute-start | bytes 196616 | tf_op jit(solution)/shard_map/reduce_gram/ppermute | solution.py:24
  132.3 5.8 %collective-permute-start.36 = (f32[128,128]{1,0:T(8,128)S(1)}, f32[128,128]{1,0:T(8,128)S(1)}, u32[]{:S(2)}, u32[]{:S(2)}) collective-permute-start(f32[128,128]{1,0:T(8,128)S(1)} %add_add_fusion.2), channel_id=1, source_target_pairs={{0,16},{8,24},{16,0},{24,8},{1,17},{9,25},{17,1},{25,9},{2,18},{10... | collective-permute-start | bytes 196616 | tf_op jit(solution)/shard_map/reduce_gram/ppermute | solution.py:24
  138.1 6.2 %collective-permute-start.41 = (f32[128,128]{1,0:T(8,128)S(1)}, f32[128,128]{1,0:T(8,128)S(1)}, u32[]{:S(2)}, u32[]{:S(2)}) collective-permute-start(f32[128,128]{1,0:T(8,128)S(1)} %add_add_fusion.1), channel_id=1, source_target_pairs={{0,96},{32,0},{64,32},{96,64},{1,97},{33,1},{65,33},{97,65},{2,98}... | collective-permute-start | bytes 196616 | tf_op jit(solution)/shard_map/reduce_gram/ppermute | solution.py:24
  141.2 6.2 %collective-permute-start.40 = (f32[128,128]{1,0:T(8,128)S(1)}, f32[128,128]{1,0:T(8,128)S(1)}, u32[]{:S(2)}, u32[]{:S(2)}) collective-permute-start(f32[128,128]{1,0:T(8,128)S(1)} %add_add_fusion.1), channel_id=1, source_target_pairs={{0,32},{32,64},{64,96},{96,0},{1,33},{33,65},{65,97},{97,1},{2,34}... | collective-permute-start | bytes 196616 | tf_op jit(solution)/shard_map/reduce_gram/ppermute | solution.py:24
  141.2 6.2 %collective-permute-start.39 = (f32[128,128]{1,0:T(8,128)S(1)}, f32[128,128]{1,0:T(8,128)S(1)}, u32[]{:S(2)}, u32[]{:S(2)}) collective-permute-start(f32[128,128]{1,0:T(8,128)S(1)} %add_add_fusion.1), channel_id=1, source_target_pairs={{0,64},{32,96},{64,0},{96,32},{1,65},{33,97},{65,1},{97,33},{2,66}... | collective-permute-start | bytes 196616 | tf_op jit(solution)/shard_map/reduce_gram/ppermute | solution.py:24

commit v12 on v11

--- a/solution.py
+++ b/solution.py
@@ -212,10 +212,9 @@
 
 
 def forward_far_kernel(counts, far, tiles, a, b, before, total, *rest):
-    *aways, held, sems = rest
-    copies = load_pieces([a, b], held, sems)
-    for one in copies:
-        one.wait()
+    *aways, held = rest
+    held[pl.ds(0, 8)] = a[...]
+    held[pl.ds(8, 8)] = b[...]
 
     def body(slot, row, col):
         total[row] += dot(tiles[slot], held[jnp.minimum(col - 32, 16)])
@@ -230,12 +229,9 @@
         forward_far_kernel,
         out_shape=(jax.ShapeDtypeStruct((33, SIDE, RANK), F32),)
         + (jax.ShapeDtypeStruct((4, SIDE, RANK), F32),) * 4,
-        in_specs=scalars(2) + whole(1) + anywhere(2) + whole(1),
+        in_specs=scalars(2) + whole(4),
         out_specs=tuple(whole(5)),
-        scratch_shapes=[
-            pltpu.VMEM((17, SIDE, RANK), BF16),
-            pltpu.SemaphoreType.DMA((2,)),
-        ],
+        scratch_shapes=[pltpu.VMEM((17, SIDE, RANK), BF16)],
         input_output_aliases={5: 0},
         compiler_params=limits(4),
         name="forward_far",
@@ -243,11 +239,10 @@
 
 
 def backward_far_kernel(counts, far, tiles, *rest):
-    pieces, (a, b, held, total, sems) = rest[:8], rest[8:]
-    copies = load_pieces(pieces, held, sems)
+    pieces, (a, b, held, total) = rest[:8], rest[8:]
     total[...] = jnp.zeros_like(total)
-    for one in copies:
-        one.wait()
+    for i, piece in enumerate(pieces):
+        held[pl.ds(4 * i, 4)] = piece[...]
 
     def body(slot, row, col):
         total[jnp.minimum(col - 32, 16)] += dot(held[row], tiles[slot])
@@ -262,12 +257,11 @@
     return pl.pallas_call(
         backward_far_kernel,
         out_shape=(part, part),
-        in_specs=scalars(2) + whole(1) + anywhere(8),
+        in_specs=scalars(2) + whole(9),
         out_specs=tuple(whole(2)),
         scratch_shapes=[
             pltpu.VMEM((33, RANK, SIDE), BF16),
             pltpu.VMEM((17, RANK, SIDE), F32),
-            pltpu.SemaphoreType.DMA((8,)),
         ],
         compiler_params=limits(8),
         name="backward_far",

time: 153 us -> 149 us (0.974)
  starting transfers between devices: 64.1 us -> 59.8 us
  Pallas kernels: 20.3 us -> 22.5 us
    ppermute x24, starting transfers between devices: 34 us -> 30.5 us  [send(): lax.ppermute(array, axis, [(i, (i + step) % size) for i in range(size)])]
  transfers between devices with their start and end apart: 42 -> 42, of which waited for: 27 -> 27; matrix products, arithmetic and copies ran while one was open for 1% -> 1% of each run, Pallas kernels for 7% -> 8%
where the time goes in v12:
time: 149 us; the launch traced here: 150 us
  waiting for transfers between devices  64.9 us (44%)
  starting transfers between devices  59.8 us (40%)
  Pallas kernels  22.5 us (15%)
  between operations  1.57 us (1%)
    ppermute x24, waiting for transfers between devices, send(): lax.ppermute(array, axis, [(i, (i + step) % size) for i in range(size)])  36.3 us
    ppermute x24, starting transfers between devices, send(): lax.ppermute(array, axis, [(i, (i + step) % size) for i in range(size)])  30.5 us
    ppermute x18, starting transfers between devices, cross(): return lax.ppermute(array, AXES, pairs)  29.2 us
    ppermute x18, waiting for transfers between devices, cross(): return lax.ppermute(array, AXES, pairs)  28.7 us
    pallas_call x1, Pallas kernels, finish(): pl.pallas_call(kernel, out_shape=(jax.ShapeDtypeStruct((4 * SIDE, RANK),...  5.51 us
    pallas_call x1, Pallas kernels, plan_tiles(): pl.pallas_call(plan_kernel, out_shape=(jax.ShapeDtypeStruct(tiles.shape,...  4.72 us
    pallas_call x1, Pallas kernels, forward_near(): pl.pallas_call(forward_near_kernel, out_shape=jax.ShapeDtypeStruct((33, S...  3.75 us
    pallas_call x1, Pallas kernels, backward_near(): pl.pallas_call(backward_near_kernel, out_shape=(jax.ShapeDtypeStruct((65,...  3.38 us
  transfers between devices with their start and end apart: 42, of which 27 were waited for; matrix products, arithmetic and copies ran while one was open for 1% of the time, Pallas kernels for 8%

profile of v12, /device:TPU:0, one launch (start us, length us, event | category | flops | bytes accessed | tf_op | source)
XLA Modules:
  0.0 150.0 jit_solution(14435902053974901651)
XLA Ops:
  0.6 3.2 %collective-permute-start.1 = (bf16[1024,128]{1,0:T(8,128)(2,1)}, bf16[1024,128]{1,0:T(8,128)(2,1)S(1)}, u32[]{:S(2)}, u32[]{:S(2)}) collective-permute-start(bf16[1024,128]{1,0:T(8,128)(2,1)} %param.4), channel_id=1, source_target_pairs={{0,64},{1,17},{2,66},{3,19},{4,68},{5,21},{6,70},{7,23},{8,72},{9,... | collective-permute-start | bytes 786440 | tf_op jit(solution)/shard_map/gather_basis/ppermute | solution.py:35
  3.8 1.1 collective-permute-start
  5.0 0.9 collective-permute-start.2
  5.9 0.8 fusion.10
  7.3 4.7 %plan_tiles.1 = (bf16[160,256,256]{2,1,0:T(8,128)(2,1)S(1)}, s32[2]{0:T(128)S(1)}, s32[192]{0:T(256)S(1)}, s32[192]{0:T(256)S(1)}) custom-call(s32[1]{0:T(128)S(6)} %copy.10.count, s32[160]{0:T(256)S(1)} %get-tuple-element.59.row_at, s32[160]{0:T(256)S(1)} %get-tuple-element.58.col_at, bf16[160,256,256]{2,1,0:T(8,128)(2,1)} %tiles.3), custom_call_target="tpu_custom_call" | custom-call | bytes 41943040 | tf_op jit(solution)/shard_map/gather_basis/plan_tiles/pallas_call | solution.py:134
  12.1 0.7 collective-permute-done.2
  12.8 3.1 %collective-permute-start.5 = (bf16[8,256,128]{2,1,0:T(8,128)(2,1)S(1)}, bf16[8,256,128]{2,1,0:T(8,128)(2,1)S(1)}, u32[]{:S(2)}, u32[]{:S(2)}) collective-permute-start(bf16[8,256,128]{2,1,0:T(8,128)(2,1)S(1)} %bitcast.4), channel_id=1, source_target_pairs={{0,24},{1,97},{2,26},{3,99},{4,28},{5,101},{6,30},{7,103},{8,0},{9... | collective-permute-start | bytes 1572872 | tf_op jit(solution)/shard_map/gather_basis/ppermute | solution.py:35
  16.0 0.7 collective-permute-start.8
  16.7 2.7 %collective-permute-start.7 = (bf16[8,256,128]{2,1,0:T(8,128)(2,1)S(1)}, bf16[8,256,128]{2,1,0:T(8,128)(2,1)S(1)}, u32[]{:S(2)}, u32[]{:S(2)}) collective-permute-start(bf16[8,256,128]{2,1,0:T(8,128)(2,1)S(1)} %bitcast.8), channel_id=1, source_target_pairs={{0,24},{1,97},{2,26},{3,99},{4,28},{5,101},{6,30},{7,103},{8,0},{9... | collective-permute-start | bytes 1572872 | tf_op jit(solution)/shard_map/gather_basis/ppermute | solution.py:35
  19.3 3.3 %collective-permute-done.5.rest_3_ = bf16[8,256,128]{2,1,0:T(8,128)(2,1)S(1)} collective-permute-done((bf16[8,256,128]{2,1,0:T(8,128)(2,1)S(1)}, bf16[8,256,128]{2,1,0:T(8,128)(2,1)S(1)}, u32[]{:S(2)}, u32[]{:S(2)}) %collective-permute-start.5) | collective-permute-done | bytes 524320 | tf_op jit(solution)/shard_map/gather_basis/ppermute | solution.py:35
  22.6 3.7 %collective-permute-start.6 = (bf16[8,256,128]{2,1,0:T(8,128)(2,1)S(1)}, bf16[8,256,128]{2,1,0:T(8,128)(2,1)S(1)}, u32[]{:S(2)}, u32[]{:S(2)}) collective-permute-start(bf16[8,256,128]{2,1,0:T(8,128)(2,1)S(1)} %collective-permute-done.5.rest_3_), channel_id=1, source_target_pairs={{0,24},{1,97},{2,26},{3,99},{4,28},{5,101},{6,30},{7,103},{8,0},{9... | collective-permute-start | bytes 1572872 | tf_op jit(solution)/shard_map/gather_basis/ppermute | solution.py:35
  26.4 5.6 %collective-permute-done.8.rest_5_ = bf16[8,256,128]{2,1,0:T(8,128)(2,1)S(1)} collective-permute-done((bf16[8,256,128]{2,1,0:T(8,128)(2,1)S(1)}, bf16[8,256,128]{2,1,0:T(8,128)(2,1)S(1)}, u32[]{:S(2)}, u32[]{:S(2)}) %collective-permute-start.8) | collective-permute-done | bytes 524320 | tf_op jit(solution)/shard_map/gather_basis/ppermute | solution.py:35
  32.0 3.7 %forward_near.1.before = f32[33,256,128]{2,1,0:T(8,128)S(1)} custom-call(s32[2]{0:T(128)S(1)} %get-tuple-element.29.counts, s32[192]{0:T(256)S(1)} %get-tuple-element.30.near, bf16[160,256,256]{2,1,0:T(8,128)(2,1)S(1)} %hold_rest.1.tiles, bf16[8,256,128]{2,1,0:T(8,128)(2,1)S(1)} %bitcast.9, bf16[8,256,128]{2,1,0:T(8,128)(2,1)S(1)} %bitcast.6, ...), custom_call_target="tpu_custom_call" | custom-call | flops 2013265920 | bytes 1048576 | tf_op jit(solution)/shard_map/forward_near/pallas_call | solution.py:199
  35.8 1.8 %collective-permute-done.4.a = bf16[8,256,128]{2,1,0:T(8,128)(2,1)S(1)} collective-permute-done((bf16[8,256,128]{2,1,0:T(8,128)(2,1)S(1)}, bf16[8,256,128]{2,1,0:T(8,128)(2,1)S(1)}, u32[]{:S(2)}, u32[]{:S(2)}) %collective-permute-start.4) | collective-permute-done | bytes 524320 | tf_op jit(solution)/shard_map/gather_basis/ppermute | solution.py:35
  37.6 1.5 forward_far.1
  39.2 0.5 collective-permute-start.12
  39.8 0.4 collective-permute-start.9
  40.2 0.9 collective-permute-done.10.came
  41.4 4.0 %collective-permute-start.11 = (f16[1040,128]{1,0:T(8,128)(2,1)S(1)}, f16[1040,128]{1,0:T(8,128)(2,1)S(1)}, u32[]{:S(2)}, u32[]{:S(2)}) collective-permute-start(f16[1040,128]{1,0:T(8,128)(2,1)S(1)} %convert_element_type.18), channel_id=1, source_target_pairs={{0,4},{2,6},{4,0},{6,2},{1,5},{3,7},{5,1},{7,3},{8,12},{10,14},{12... | collective-permute-start | bytes 798728 | tf_op jit(solution)/shard_map/reduce_inner/ppermute | solution.py:24
  45.6 1.6 %collective-permute-start.13 = (f16[1040,128]{1,0:T(8,128)(2,1)S(1)}, f16[1040,128]{1,0:T(8,128)(2,1)S(1)}, u32[]{:S(2)}, u32[]{:S(2)}) collective-permute-start(f16[1040,128]{1,0:T(8,128)(2,1)S(1)} %convert_element_type.20), channel_id=1, source_target_pairs={{0,2},{2,4},{4,6},{6,0},{1,3},{3,5},{5,7},{7,1},{8,10},{10,12},{12... | collective-permute-start | bytes 798728 | tf_op jit(solution)/shard_map/reduce_inner/ppermute | solution.py:24
  47.4 1.8 %collective-permute-start.15 = (f16[1040,128]{1,0:T(8,128)(2,1)S(1)}, f16[1040,128]{1,0:T(8,128)(2,1)S(1)}, u32[]{:S(2)}, u32[]{:S(2)}) collective-permute-start(f16[1040,128]{1,0:T(8,128)(2,1)S(1)} %convert_element_type.22), channel_id=1, source_target_pairs={{0,6},{2,0},{4,2},{6,4},{1,7},{3,1},{5,3},{7,5},{8,14},{10,8},{12,... | collective-permute-start | bytes 798728 | tf_op jit(solution)/shard_map/reduce_inner/ppermute | solution.py:24
  49.2 3.3 %collective-permute-done.11 = f16[1040,128]{1,0:T(8,128)(2,1)S(1)} collective-permute-done((f16[1040,128]{1,0:T(8,128)(2,1)S(1)}, f16[1040,128]{1,0:T(8,128)(2,1)S(1)}, u32[]{:S(2)}, u32[]{:S(2)}) %collective-permute-start.11) | collective-permute-done | bytes 266272 | tf_op jit(solution)/shard_map/reduce_inner/ppermute | solution.py:24
  52.6 5.1 %collective-permute-done.13 = f16[1040,128]{1,0:T(8,128)(2,1)S(1)} collective-permute-done((f16[1040,128]{1,0:T(8,128)(2,1)S(1)}, f16[1040,128]{1,0:T(8,128)(2,1)S(1)}, u32[]{:S(2)}, u32[]{:S(2)}) %collective-permute-start.13) | collective-permute-done | bytes 266272 | tf_op jit(solution)/shard_map/reduce_inner/ppermute | solution.py:24
  57.8 1.2 collective-permute-done.15
  59.3 1.3 collective-permute-start.18
  60.6 2.8 %collective-permute-start.17 = (bf16[4,128,256]{2,1,0:T(8,128)(2,1)S(1)}, bf16[4,128,256]{2,1,0:T(8,128)(2,1)S(1)}, u32[]{:S(2)}, u32[]{:S(2)}) collective-permute-start(bf16[4,128,256]{2,1,0:T(8,128)(2,1)S(1)} %inner_sum.1.rest_0_), channel_id=1, source_target_pairs={{0,4},{2,6},{4,0},{6,2},{1,5},{3,7},{5,1},{7,3},{8,12},{10,14},{12... | collective-permute-start | bytes 786440 | tf_op jit(solution)/shard_map/gather_inner/ppermute | solution.py:24
  63.5 0.6 collective-permute-start.16
  64.0 4.5 %collective-permute-done.18.rest_3_ = bf16[4,128,256]{2,1,0:T(8,128)(2,1)S(1)} collective-permute-done((bf16[4,128,256]{2,1,0:T(8,128)(2,1)S(1)}, bf16[4,128,256]{2,1,0:T(8,128)(2,1)S(1)}, u32[]{:S(2)}, u32[]{:S(2)}) %collective-permute-start.18) | collective-permute-done | bytes 262176 | tf_op jit(solution)/shard_map/gather_inner/ppermute | solution.py:24
  68.5 6.8 %collective-permute-done.17.rest_2_ = bf16[4,128,256]{2,1,0:T(8,128)(2,1)S(1)} collective-permute-done((bf16[4,128,256]{2,1,0:T(8,128)(2,1)S(1)}, bf16[4,128,256]{2,1,0:T(8,128)(2,1)S(1)}, u32[]{:S(2)}, u32[]{:S(2)}) %collective-permute-start.17) | collective-permute-done | bytes 262176 | tf_op jit(solution)/shard_map/gather_inner/ppermute | solution.py:24
  75.3 0.5 collective-permute-start.20
  75.8 1.0 collective-permute-done.21.rest_6_
  76.8 0.4 collective-permute-done.20.rest_5_
  77.2 1.6 %backward_far.1 = (bf16[8,128,256]{2,1,0:T(8,128)(2,1)S(1)}, bf16[8,128,256]{2,1,0:T(8,128)(2,1)S(1)}) custom-call(s32[2]{0:T(128)S(1)} %get-tuple-element.29.counts, s32[192]{0:T(256)S(1)} %get-tuple-element.33.far, bf16[160,256,256]{2,1,0:T(8,128)(2,1)S(1)} %hold_rest.1.tiles, bf16[4,128,256]{2,1,0:T(8,128)(2,1)S(1)} %inner_sum.1.rest_0_, ...), custom_call_target="tpu_custom_call" | custom-call | tf_op jit(solution)/shard_map/backward_far/pallas_call | solution.py:257
  78.9 3.2 %collective-permute-start.24 = (bf16[8,128,256]{2,1,0:T(8,128)(2,1)S(1)}, bf16[8,128,256]{2,1,0:T(8,128)(2,1)S(1)}, u32[]{:S(2)}, u32[]{:S(2)}) collective-permute-start(bf16[8,128,256]{2,1,0:T(8,128)(2,1)S(1)} %get-tuple-element.45), channel_id=1, source_target_pairs={{0,24},{1,97},{2,26},{3,99},{4,28},{5,101},{6,30},{7,103},{8,0},{9... | collective-permute-start | bytes 1572872 | tf_op jit(solution)/shard_map/reduce_outer/ppermute | solution.py:35
  82.2 3.4 %backward_near.1 = (f32[65,128,256]{2,1,0:T(8,128)S(1)}, bf16[8,128,256]{2,1,0:T(8,128)(2,1)S(1)}, bf16[8,128,256]{2,1,0:T(8,128)(2,1)S(1)}) custom-call(s32[2]{0:T(128)S(1)} %get-tuple-element.29.counts, s32[192]{0:T(256)S(1)} %get-tuple-element.30.near, bf16[160,256,256]{2,1,0:T(8,128)(2,1)S(1)} %hold_rest.1.tiles, ...), custom_call_target="tpu_custom_call" | custom-call | flops 2013265920 | bytes 1048576 | tf_op jit(solution)/shard_map/reduce_outer/backward_near/pallas_call | solution.py:289
  85.6 2.0 %collective-permute-start.27 = (bf16[8,128,256]{2,1,0:T(8,128)(2,1)S(1)}, bf16[8,128,256]{2,1,0:T(8,128)(2,1)S(1)}, u32[]{:S(2)}, u32[]{:S(2)}) collective-permute-start(bf16[8,128,256]{2,1,0:T(8,128)(2,1)S(1)} %get-tuple-element.48), channel_id=1, source_target_pairs={{0,8},{1,33},{2,10},{3,35},{4,12},{5,37},{6,14},{7,39},{8,16},{9,4... | collective-permute-start | bytes 1572872 | tf_op jit(solution)/shard_map/reduce_outer/ppermute | solution.py:35
  87.6 1.7 %collective-permute-done.23.a = bf16[8,128,256]{2,1,0:T(8,128)(2,1)S(1)} collective-permute-done((bf16[8,128,256]{2,1,0:T(8,128)(2,1)S(1)}, bf16[8,128,256]{2,1,0:T(8,128)(2,1)S(1)}, u32[]{:S(2)}, u32[]{:S(2)}) %collective-permute-start.23) | collective-permute-done | bytes 524320 | tf_op jit(solution)/shard_map/reduce_outer/ppermute | solution.py:35
  89.6 3.3 %collective-permute-start.28 = (bf16[8,128,256]{2,1,0:T(8,128)(2,1)S(1)}, bf16[8,128,256]{2,1,0:T(8,128)(2,1)S(1)}, u32[]{:S(2)}, u32[]{:S(2)}) collective-permute-start(bf16[8,128,256]{2,1,0:T(8,128)(2,1)S(1)} %get-tuple-element.49), channel_id=1, source_target_pairs={{0,24},{1,97},{2,26},{3,99},{4,28},{5,101},{6,30},{7,103},{8,0},{9... | collective-permute-start | bytes 1572872 | tf_op jit(solution)/shard_map/reduce_outer/ppermute | solution.py:35
  92.9 1.9 %collective-permute-done.26.rest_1_ = bf16[8,128,256]{2,1,0:T(8,128)(2,1)S(1)} collective-permute-done((bf16[8,128,256]{2,1,0:T(8,128)(2,1)S(1)}, bf16[8,128,256]{2,1,0:T(8,128)(2,1)S(1)}, u32[]{:S(2)}, u32[]{:S(2)}) %collective-permute-start.26) | collective-permute-done | bytes 524320 | tf_op jit(solution)/shard_map/reduce_outer/ppermute | solution.py:35
  94.8 1.3 collective-permute-done.27.rest_2_
  96.1 5.6 %collective-permute-done.25.rest_0_ = bf16[8,128,256]{2,1,0:T(8,128)(2,1)S(1)} collective-permute-done((bf16[8,128,256]{2,1,0:T(8,128)(2,1)S(1)}, bf16[8,128,256]{2,1,0:T(8,128)(2,1)S(1)}, u32[]{:S(2)}, u32[]{:S(2)}) %collective-permute-start.25) | collective-permute-done | bytes 524320 | tf_op jit(solution)/shard_map/reduce_outer/ppermute | solution.py:35
  101.7 0.3 middle_sum.1
  102.0 2.3 %collective-permute-start.29 = (bf16[4,128,256]{2,1,0:T(8,128)(2,1)S(1)}, bf16[4,128,256]{2,1,0:T(8,128)(2,1)S(1)}, u32[]{:S(2)}, u32[]{:S(2)}) collective-permute-start(bf16[4,128,256]{2,1,0:T(8,128)(2,1)S(1)} %get-tuple-element.51), channel_id=1, source_target_pairs={{0,32},{1,9},{2,34},{3,11},{4,36},{5,13},{6,38},{7,15},{8,40},{9,1... | collective-permute-start | bytes 786440 | tf_op jit(solution)/shard_map/reduce_outer/ppermute | solution.py:35
  104.4 2.3 %collective-permute-start.30 = (bf16[4,128,256]{2,1,0:T(8,128)(2,1)S(1)}, bf16[4,128,256]{2,1,0:T(8,128)(2,1)S(1)}, u32[]{:S(2)}, u32[]{:S(2)}) collective-permute-start(bf16[4,128,256]{2,1,0:T(8,128)(2,1)S(1)} %get-tuple-element.52), channel_id=1, source_target_pairs={{0,64},{1,17},{2,66},{3,19},{4,68},{5,21},{6,70},{7,23},{8,72},{9,... | collective-permute-start | bytes 786440 | tf_op jit(solution)/shard_map/reduce_outer/ppermute | solution.py:35
  106.7 0.5 collective-permute-start.31
  107.1 2.6 %collective-permute-done.29.a = bf16[4,128,256]{2,1,0:T(8,128)(2,1)S(1)} collective-permute-done((bf16[4,128,256]{2,1,0:T(8,128)(2,1)S(1)}, bf16[4,128,256]{2,1,0:T(8,128)(2,1)S(1)}, u32[]{:S(2)}, u32[]{:S(2)}) %collective-permute-start.29) | collective-permute-done | bytes 262176 | tf_op jit(solution)/shard_map/reduce_outer/ppermute | solution.py:35
  109.7 4.1 %collective-permute-done.30.b = bf16[4,128,256]{2,1,0:T(8,128)(2,1)S(1)} collective-permute-done((bf16[4,128,256]{2,1,0:T(8,128)(2,1)S(1)}, bf16[4,128,256]{2,1,0:T(8,128)(2,1)S(1)}, u32[]{:S(2)}, u32[]{:S(2)}) %collective-permute-start.30) | collective-permute-done | bytes 262176 | tf_op jit(solution)/shard_map/reduce_outer/ppermute | solution.py:35
  113.8 0.6 outer_sum.1
  114.5 1.2 collective-permute-done.32
  115.8 5.0 %collective-permute-start.35 = (f32[128,128]{1,0:T(8,128)S(1)}, f32[128,128]{1,0:T(8,128)S(1)}, u32[]{:S(2)}, u32[]{:S(2)}) collective-permute-start(f32[128,128]{1,0:T(8,128)S(1)} %add.91), channel_id=1, source_target_pairs={{0,6},{2,0},{4,2},{6,4},{1,7},{3,1},{5,3},{7,5},{8,14},{10,8},{12,... | collective-permute-start | bytes 196616 | tf_op jit(solution)/shard_map/reduce_gram/ppermute | solution.py:24
  120.8 1.5 %collective-permute-start.33 = (f32[128,128]{1,0:T(8,128)S(1)}, f32[128,128]{1,0:T(8,128)S(1)}, u32[]{:S(2)}, u32[]{:S(2)}) collective-permute-start(f32[128,128]{1,0:T(8,128)S(1)} %add.91), channel_id=1, source_target_pairs={{0,4},{2,6},{4,0},{6,2},{1,5},{3,7},{5,1},{7,3},{8,12},{10,14},{12... | collective-permute-start | bytes 196616 | tf_op jit(solution)/shard_map/reduce_gram/ppermute | solution.py:24
  122.3 0.4 collective-permute-done.35
  122.7 4.6 %collective-permute-done.34 = f32[128,128]{1,0:T(8,128)S(1)} collective-permute-done((f32[128,128]{1,0:T(8,128)S(1)}, f32[128,128]{1,0:T(8,128)S(1)}, u32[]{:S(2)}, u32[]{:S(2)}) %collective-permute-start.34) | collective-permute-done | bytes 65568 | tf_op jit(solution)/shard_map/reduce_gram/ppermute | solution.py:24
  127.4 2.6 %collective-permute-start.37 = (f32[128,128]{1,0:T(8,128)S(1)}, f32[128,128]{1,0:T(8,128)S(1)}, u32[]{:S(2)}, u32[]{:S(2)}) collective-permute-start(f32[128,128]{1,0:T(8,128)S(1)} %add_add_fusion.2), channel_id=1, source_target_pairs={{0,8},{8,16},{16,24},{24,0},{1,9},{9,17},{17,25},{25,1},{2,10},{10... | collective-permute-start | bytes 196616 | tf_op jit(solution)/shard_map/reduce_gram/ppermute | solution.py:24
  129.9 2.0 %collective-permute-start.36 = (f32[128,128]{1,0:T(8,128)S(1)}, f32[128,128]{1,0:T(8,128)S(1)}, u32[]{:S(2)}, u32[]{:S(2)}) collective-permute-start(f32[128,128]{1,0:T(8,128)S(1)} %add_add_fusion.2), channel_id=1, source_target_pairs={{0,16},{8,24},{16,0},{24,8},{1,17},{9,25},{17,1},{25,9},{2,18},{10... | collective-permute-start | bytes 196616 | tf_op jit(solution)/shard_map/reduce_gram/ppermute | solution.py:24
  131.9 0.5 collective-permute-done.38
  132.4 0.5 collective-permute-done.37
  132.9 2.8 %collective-permute-done.36 = f32[128,128]{1,0:T(8,128)S(1)} collective-permute-done((f32[128,128]{1,0:T(8,128)S(1)}, f32[128,128]{1,0:T(8,128)S(1)}, u32[]{:S(2)}, u32[]{:S(2)}) %collective-permute-start.36) | collective-permute-done | bytes 65568 | tf_op jit(solution)/shard_map/reduce_gram/ppermute | solution.py:24
  135.7 2.5 %collective-permute-start.41 = (f32[128,128]{1,0:T(8,128)S(1)}, f32[128,128]{1,0:T(8,128)S(1)}, u32[]{:S(2)}, u32[]{:S(2)}) collective-permute-start(f32[128,128]{1,0:T(8,128)S(1)} %add_add_fusion.1), channel_id=1, source_target_pairs={{0,96},{32,0},{64,32},{96,64},{1,97},{33,1},{65,33},{97,65},{2,98}... | collective-permute-start | bytes 196616 | tf_op jit(solution)/shard_map/reduce_gram/ppermute | solution.py:24
  138.3 0.4 collective-permute-start.40
  138.6 2.7 %collective-permute-start.39 = (f32[128,128]{1,0:T(8,128)S(1)}, f32[128,128]{1,0:T(8,128)S(1)}, u32[]{:S(2)}, u32[]{:S(2)}) collective-permute-start(f32[128,128]{1,0:T(8,128)S(1)} %add_add_fusion.1), channel_id=1, source_target_pairs={{0,64},{32,96},{64,0},{96,32},{1,65},{33,97},{65,1},{97,33},{2,66}... | collective-permute-start | bytes 196616 | tf_op jit(solution)/shard_map/reduce_gram/ppermute | solution.py:24
  141.4 2.4 %collective-permute-done.40 = f32[128,128]{1,0:T(8,128)S(1)} collective-permute-done((f32[128,128]{1,0:T(8,128)S(1)}, f32[128,128]{1,0:T(8,128)S(1)}, u32[]{:S(2)}, u32[]{:S(2)}) %collective-permute-start.40) | collective-permute-done | bytes 65568 | tf_op jit(solution)/shard_map/reduce_gram/ppermute | solution.py:24
  143.7 0.7 collective-permute-done.39
  144.5 5.5 %finish.1 = (f32[1024,128]{1,0:T(8,128)}, f32[128,128]{1,0:T(8,128)}) custom-call(f32[128,128]{1,0:T(8,128)S(1)} %add_add_fusion.refs_0_, f32[4,128,256]{2,1,0:T(8,128)S(1)} %get-tuple-element.55.refs_1_), custom_call_target="tpu_custom_call" | custom-call | tf_op jit(solution)/shard_map/finish/pallas_call | solution.py:482
  (50 shorter events, 2.3 us)
Async XLA Ops:
  0.6 15.3 %copy-start = (bf16[1024,128]{1,0:T(8,128)(2,1)S(1)}, bf16[1024,128]{1,0:T(8,128)(2,1)}, u32[]{:S(2)}) copy-start(bf16[1024,128]{1,0:T(8,128)(2,1)} %param.4) | copy-start | bytes 786436
  0.6 11.4 %collective-permute-start.1 = (bf16[1024,128]{1,0:T(8,128)(2,1)}, bf16[1024,128]{1,0:T(8,128)(2,1)S(1)}, u32[]{:S(2)}, u32[]{:S(2)}) collective-permute-start(bf16[1024,128]{1,0:T(8,128)(2,1)} %param.4), channel_id=1, source_target_pairs={{0,64},{1,17},{2,66},{3,19},{4,68},{5,21},{6,70},{7,23},{8,72},{9,... | collective-permute-start | bytes 786440 | tf_op jit(solution)/shard_map/gather_basis/ppermute | solution.py:35
  3.8 8.2 %collective-permute-start = (bf16[1024,128]{1,0:T(8,128)(2,1)}, bf16[1024,128]{1,0:T(8,128)(2,1)S(1)}, u32[]{:S(2)}, u32[]{:S(2)}) collective-permute-start(bf16[1024,128]{1,0:T(8,128)(2,1)} %param.4), channel_id=1, source_target_pairs={{0,96},{1,25},{2,98},{3,27},{4,100},{5,29},{6,102},{7,31},{8,104},... | collective-permute-start | bytes 786440 | tf_op jit(solution)/shard_map/gather_basis/ppermute | solution.py:35
  5.0 7.8 %collective-permute-start.2 = (bf16[1024,128]{1,0:T(8,128)(2,1)}, bf16[1024,128]{1,0:T(8,128)(2,1)S(1)}, u32[]{:S(2)}, u32[]{:S(2)}) collective-permute-start(bf16[1024,128]{1,0:T(8,128)(2,1)} %param.4), channel_id=1, source_target_pairs={{0,32},{1,9},{2,34},{3,11},{4,36},{5,13},{6,38},{7,15},{8,40},{9,1... | collective-permute-start | bytes 786440 | tf_op jit(solution)/shard_map/gather_basis/ppermute | solution.py:35
  12.8 9.8 %collective-permute-start.5 = (bf16[8,256,128]{2,1,0:T(8,128)(2,1)S(1)}, bf16[8,256,128]{2,1,0:T(8,128)(2,1)S(1)}, u32[]{:S(2)}, u32[]{:S(2)}) collective-permute-start(bf16[8,256,128]{2,1,0:T(8,128)(2,1)S(1)} %bitcast.4), channel_id=1, source_target_pairs={{0,24},{1,97},{2,26},{3,99},{4,28},{5,101},{6,30},{7,103},{8,0},{9... | collective-permute-start | bytes 1572872 | tf_op jit(solution)/shard_map/gather_basis/ppermute | solution.py:35
  15.9 10.5 %collective-permute-start.3 = (bf16[8,256,128]{2,1,0:T(8,128)(2,1)S(1)}, bf16[8,256,128]{2,1,0:T(8,128)(2,1)S(1)}, u32[]{:S(2)}, u32[]{:S(2)}) collective-permute-start(bf16[8,256,128]{2,1,0:T(8,128)(2,1)S(1)} %bitcast.7), channel_id=1, source_target_pairs={{0,8},{1,33},{2,10},{3,35},{4,12},{5,37},{6,14},{7,39},{8,16},{9,4... | collective-permute-start | bytes 1572872 | tf_op jit(solution)/shard_map/gather_basis/ppermute | solution.py:35
  16.0 16.0 %collective-permute-start.8 = (bf16[8,256,128]{2,1,0:T(8,128)(2,1)S(1)}, bf16[8,256,128]{2,1,0:T(8,128)(2,1)S(1)}, u32[]{:S(2)}, u32[]{:S(2)}) collective-permute-start(bf16[8,256,128]{2,1,0:T(8,128)(2,1)S(1)} %bitcast.5), channel_id=1, source_target_pairs={{0,8},{1,33},{2,10},{3,35},{4,12},{5,37},{6,14},{7,39},{8,16},{9,4... | collective-permute-start | bytes 1572872 | tf_op jit(solution)/shard_map/gather_basis/ppermute | solution.py:35
  16.7 15.3 %collective-permute-start.7 = (bf16[8,256,128]{2,1,0:T(8,128)(2,1)S(1)}, bf16[8,256,128]{2,1,0:T(8,128)(2,1)S(1)}, u32[]{:S(2)}, u32[]{:S(2)}) collective-permute-start(bf16[8,256,128]{2,1,0:T(8,128)(2,1)S(1)} %bitcast.8), channel_id=1, source_target_pairs={{0,24},{1,97},{2,26},{3,99},{4,28},{5,101},{6,30},{7,103},{8,0},{9... | collective-permute-start | bytes 1572872 | tf_op jit(solution)/shard_map/gather_basis/ppermute | solution.py:35
  22.6 13.2 %collective-permute-start.6 = (bf16[8,256,128]{2,1,0:T(8,128)(2,1)S(1)}, bf16[8,256,128]{2,1,0:T(8,128)(2,1)S(1)}, u32[]{:S(2)}, u32[]{:S(2)}) collective-permute-start(bf16[8,256,128]{2,1,0:T(8,128)(2,1)S(1)} %collective-permute-done.5.rest_3_), channel_id=1, source_target_pairs={{0,24},{1,97},{2,26},{3,99},{4,28},{5,101},{6,30},{7,103},{8,0},{9... | collective-permute-start | bytes 1572872 | tf_op jit(solution)/shard_map/gather_basis/ppermute | solution.py:35
  26.4 11.2 %collective-permute-start.4 = (bf16[8,256,128]{2,1,0:T(8,128)(2,1)S(1)}, bf16[8,256,128]{2,1,0:T(8,128)(2,1)S(1)}, u32[]{:S(2)}, u32[]{:S(2)}) collective-permute-start(bf16[8,256,128]{2,1,0:T(8,128)(2,1)S(1)} %collective-permute-done.3.rest_4_), channel_id=1, source_target_pairs={{0,8},{1,33},{2,10},{3,35},{4,12},{5,37},{6,14},{7,39},{8,16},{9,4... | collective-permute-start | bytes 1572872 | tf_op jit(solution)/shard_map/gather_basis/ppermute | solution.py:35
  39.1 2.0 %collective-permute-start.10 = (f32[4,256,128]{2,1,0:T(8,128)S(1)}, f32[4,256,128]{2,1,0:T(8,128)S(1)}, u32[]{:S(2)}, u32[]{:S(2)}) collective-permute-start(f32[4,256,128]{2,1,0:T(8,128)S(1)} %get-tuple-element.40), channel_id=1, source_target_pairs={{0,1},{1,0},{2,3},{3,2},{4,5},{5,4},{6,7},{7,6},{8,9},{9,8},{10,11... | collective-permute-start | bytes 1572872 | tf_op jit(solution)/shard_map/reduce_inner/ppermute | solution.py:24
  39.2 6.1 %collective-permute-start.12 = (f32[4,256,128]{2,1,0:T(8,128)S(1)}, f32[4,256,128]{2,1,0:T(8,128)S(1)}, u32[]{:S(2)}, u32[]{:S(2)}) collective-permute-start(f32[4,256,128]{2,1,0:T(8,128)S(1)} %get-tuple-element.41), channel_id=1, source_target_pairs={{0,1},{1,0},{2,3},{3,2},{4,5},{5,4},{6,7},{7,6},{8,9},{9,8},{10,11... | collective-permute-start | bytes 1572872 | tf_op jit(solution)/shard_map/reduce_inner/ppermute | solution.py:24
  39.7 7.5 %collective-permute-start.14 = (f32[4,256,128]{2,1,0:T(8,128)S(1)}, f32[4,256,128]{2,1,0:T(8,128)S(1)}, u32[]{:S(2)}, u32[]{:S(2)}) collective-permute-start(f32[4,256,128]{2,1,0:T(8,128)S(1)} %get-tuple-element.42), channel_id=1, source_target_pairs={{0,1},{1,0},{2,3},{3,2},{4,5},{5,4},{6,7},{7,6},{8,9},{9,8},{10,11... | collective-permute-start | bytes 1572872 | tf_op jit(solution)/shard_map/reduce_inner/ppermute | solution.py:24
  39.8 19.2 %collective-permute-start.9 = (f32[4,256,128]{2,1,0:T(8,128)S(1)}, f32[4,256,128]{2,1,0:T(8,128)S(1)}, u32[]{:S(2)}, u32[]{:S(2)}) collective-permute-start(f32[4,256,128]{2,1,0:T(8,128)S(1)} %get-tuple-element.39), channel_id=1, source_target_pairs={{0,1},{1,0},{2,3},{3,2},{4,5},{5,4},{6,7},{7,6},{8,9},{9,8},{10,11... | collective-permute-start | bytes 1572872 | tf_op jit(solution)/shard_map/reduce_inner/ppermute | solution.py:24
  41.4 11.2 %collective-permute-start.11 = (f16[1040,128]{1,0:T(8,128)(2,1)S(1)}, f16[1040,128]{1,0:T(8,128)(2,1)S(1)}, u32[]{:S(2)}, u32[]{:S(2)}) collective-permute-start(f16[1040,128]{1,0:T(8,128)(2,1)S(1)} %convert_element_type.18), channel_id=1, source_target_pairs={{0,4},{2,6},{4,0},{6,2},{1,5},{3,7},{5,1},{7,3},{8,12},{10,14},{12... | collective-permute-start | bytes 798728 | tf_op jit(solution)/shard_map/reduce_inner/ppermute | solution.py:24
  45.6 12.1 %collective-permute-start.13 = (f16[1040,128]{1,0:T(8,128)(2,1)S(1)}, f16[1040,128]{1,0:T(8,128)(2,1)S(1)}, u32[]{:S(2)}, u32[]{:S(2)}) collective-permute-start(f16[1040,128]{1,0:T(8,128)(2,1)S(1)} %convert_element_type.20), channel_id=1, source_target_pairs={{0,2},{2,4},{4,6},{6,0},{1,3},{3,5},{5,7},{7,1},{8,10},{10,12},{12... | collective-permute-start | bytes 798728 | tf_op jit(solution)/shard_map/reduce_inner/ppermute | solution.py:24
  47.4 11.6 %collective-permute-start.15 = (f16[1040,128]{1,0:T(8,128)(2,1)S(1)}, f16[1040,128]{1,0:T(8,128)(2,1)S(1)}, u32[]{:S(2)}, u32[]{:S(2)}) collective-permute-start(f16[1040,128]{1,0:T(8,128)(2,1)S(1)} %convert_element_type.22), channel_id=1, source_target_pairs={{0,6},{2,0},{4,2},{6,4},{1,7},{3,1},{5,3},{7,5},{8,14},{10,8},{12,... | collective-permute-start | bytes 798728 | tf_op jit(solution)/shard_map/reduce_inner/ppermute | solution.py:24
  59.3 9.2 %collective-permute-start.18 = (bf16[4,128,256]{2,1,0:T(8,128)(2,1)S(1)}, bf16[4,128,256]{2,1,0:T(8,128)(2,1)S(1)}, u32[]{:S(2)}, u32[]{:S(2)}) collective-permute-start(bf16[4,128,256]{2,1,0:T(8,128)(2,1)S(1)} %inner_sum.1.rest_0_), channel_id=1, source_target_pairs={{0,2},{2,4},{4,6},{6,0},{1,3},{3,5},{5,7},{7,1},{8,10},{10,12},{12... | collective-permute-start | bytes 786440 | tf_op jit(solution)/shard_map/gather_inner/ppermute | solution.py:24
  60.6 14.7 %collective-permute-start.17 = (bf16[4,128,256]{2,1,0:T(8,128)(2,1)S(1)}, bf16[4,128,256]{2,1,0:T(8,128)(2,1)S(1)}, u32[]{:S(2)}, u32[]{:S(2)}) collective-permute-start(bf16[4,128,256]{2,1,0:T(8,128)(2,1)S(1)} %inner_sum.1.rest_0_), channel_id=1, source_target_pairs={{0,4},{2,6},{4,0},{6,2},{1,5},{3,7},{5,1},{7,3},{8,12},{10,14},{12... | collective-permute-start | bytes 786440 | tf_op jit(solution)/shard_map/gather_inner/ppermute | solution.py:24
  63.5 11.8 %collective-permute-start.16 = (bf16[4,128,256]{2,1,0:T(8,128)(2,1)S(1)}, bf16[4,128,256]{2,1,0:T(8,128)(2,1)S(1)}, u32[]{:S(2)}, u32[]{:S(2)}) collective-permute-start(bf16[4,128,256]{2,1,0:T(8,128)(2,1)S(1)} %inner_sum.1.rest_0_), channel_id=1, source_target_pairs={{0,6},{2,0},{4,2},{6,4},{1,7},{3,1},{5,3},{7,5},{8,14},{10,8},{12,... | collective-permute-start | bytes 786440 | tf_op jit(solution)/shard_map/gather_inner/ppermute | solution.py:24
  64.0 11.8 %collective-permute-start.19 = (bf16[4,128,256]{2,1,0:T(8,128)(2,1)S(1)}, bf16[4,128,256]{2,1,0:T(8,128)(2,1)S(1)}, u32[]{:S(2)}, u32[]{:S(2)}) collective-permute-start(bf16[4,128,256]{2,1,0:T(8,128)(2,1)S(1)} %inner_sum.1.rest_0_), channel_id=1, source_target_pairs={{0,1},{1,0},{2,3},{3,2},{4,5},{5,4},{6,7},{7,6},{8,9},{9,8},{10,11... | collective-permute-start | bytes 786440 | tf_op jit(solution)/shard_map/gather_inner/ppermute | solution.py:24
  68.5 7.3 %collective-permute-start.22 = (bf16[4,128,256]{2,1,0:T(8,128)(2,1)S(1)}, bf16[4,128,256]{2,1,0:T(8,128)(2,1)S(1)}, u32[]{:S(2)}, u32[]{:S(2)}) collective-permute-start(bf16[4,128,256]{2,1,0:T(8,128)(2,1)S(1)} %collective-permute-done.18.rest_3_), channel_id=1, source_target_pairs={{0,1},{1,0},{2,3},{3,2},{4,5},{5,4},{6,7},{7,6},{8,9},{9,8},{10,11... | collective-permute-start | bytes 786440 | tf_op jit(solution)/shard_map/gather_inner/ppermute | solution.py:24
  75.3 1.5 %collective-permute-start.21 = (bf16[4,128,256]{2,1,0:T(8,128)(2,1)S(1)}, bf16[4,128,256]{2,1,0:T(8,128)(2,1)S(1)}, u32[]{:S(2)}, u32[]{:S(2)}) collective-permute-start(bf16[4,128,256]{2,1,0:T(8,128)(2,1)S(1)} %collective-permute-done.17.rest_2_), channel_id=1, source_target_pairs={{0,1},{1,0},{2,3},{3,2},{4,5},{5,4},{6,7},{7,6},{8,9},{9,8},{10,11... | collective-permute-start | bytes 786440 | tf_op jit(solution)/shard_map/gather_inner/ppermute | solution.py:24
  75.3 1.9 %collective-permute-start.20 = (bf16[4,128,256]{2,1,0:T(8,128)(2,1)S(1)}, bf16[4,128,256]{2,1,0:T(8,128)(2,1)S(1)}, u32[]{:S(2)}, u32[]{:S(2)}) collective-permute-start(bf16[4,128,256]{2,1,0:T(8,128)(2,1)S(1)} %collective-permute-done.16.rest_1_), channel_id=1, source_target_pairs={{0,1},{1,0},{2,3},{3,2},{4,5},{5,4},{6,7},{7,6},{8,9},{9,8},{10,11... | collective-permute-start | bytes 786440 | tf_op jit(solution)/shard_map/gather_inner/ppermute | solution.py:24
  78.8 10.5 %collective-permute-start.23 = (bf16[8,128,256]{2,1,0:T(8,128)(2,1)S(1)}, bf16[8,128,256]{2,1,0:T(8,128)(2,1)S(1)}, u32[]{:S(2)}, u32[]{:S(2)}) collective-permute-start(bf16[8,128,256]{2,1,0:T(8,128)(2,1)S(1)} %get-tuple-element.44), channel_id=1, source_target_pairs={{0,8},{1,33},{2,10},{3,35},{4,12},{5,37},{6,14},{7,39},{8,16},{9,4... | collective-permute-start | bytes 1572872 | tf_op jit(solution)/shard_map/reduce_outer/ppermute | solution.py:35
  78.9 10.4 %collective-permute-start.24 = (bf16[8,128,256]{2,1,0:T(8,128)(2,1)S(1)}, bf16[8,128,256]{2,1,0:T(8,128)(2,1)S(1)}, u32[]{:S(2)}, u32[]{:S(2)}) collective-permute-start(bf16[8,128,256]{2,1,0:T(8,128)(2,1)S(1)} %get-tuple-element.45), channel_id=1, source_target_pairs={{0,24},{1,97},{2,26},{3,99},{4,28},{5,101},{6,30},{7,103},{8,0},{9... | collective-permute-start | bytes 1572872 | tf_op jit(solution)/shard_map/reduce_outer/ppermute | solution.py:35
  85.5 9.2 %collective-permute-start.26 = (bf16[8,128,256]{2,1,0:T(8,128)(2,1)S(1)}, bf16[8,128,256]{2,1,0:T(8,128)(2,1)S(1)}, u32[]{:S(2)}, u32[]{:S(2)}) collective-permute-start(bf16[8,128,256]{2,1,0:T(8,128)(2,1)S(1)} %get-tuple-element.47), channel_id=1, source_target_pairs={{0,24},{1,97},{2,26},{3,99},{4,28},{5,101},{6,30},{7,103},{8,0},{9... | collective-permute-start | bytes 1572872 | tf_op jit(solution)/shard_map/reduce_outer/ppermute | solution.py:35
  85.6 10.5 %collective-permute-start.27 = (bf16[8,128,256]{2,1,0:T(8,128)(2,1)S(1)}, bf16[8,128,256]{2,1,0:T(8,128)(2,1)S(1)}, u32[]{:S(2)}, u32[]{:S(2)}) collective-permute-start(bf16[8,128,256]{2,1,0:T(8,128)(2,1)S(1)} %get-tuple-element.48), channel_id=1, source_target_pairs={{0,8},{1,33},{2,10},{3,35},{4,12},{5,37},{6,14},{7,39},{8,16},{9,4... | collective-permute-start | bytes 1572872 | tf_op jit(solution)/shard_map/reduce_outer/ppermute | solution.py:35
  89.5 12.2 %collective-permute-start.25 = (bf16[8,128,256]{2,1,0:T(8,128)(2,1)S(1)}, bf16[8,128,256]{2,1,0:T(8,128)(2,1)S(1)}, u32[]{:S(2)}, u32[]{:S(2)}) collective-permute-start(bf16[8,128,256]{2,1,0:T(8,128)(2,1)S(1)} %get-tuple-element.46), channel_id=1, source_target_pairs={{0,8},{1,33},{2,10},{3,35},{4,12},{5,37},{6,14},{7,39},{8,16},{9,4... | collective-permute-start | bytes 1572872 | tf_op jit(solution)/shard_map/reduce_outer/ppermute | solution.py:35
  89.6 12.1 %collective-permute-start.28 = (bf16[8,128,256]{2,1,0:T(8,128)(2,1)S(1)}, bf16[8,128,256]{2,1,0:T(8,128)(2,1)S(1)}, u32[]{:S(2)}, u32[]{:S(2)}) collective-permute-start(bf16[8,128,256]{2,1,0:T(8,128)(2,1)S(1)} %get-tuple-element.49), channel_id=1, source_target_pairs={{0,24},{1,97},{2,26},{3,99},{4,28},{5,101},{6,30},{7,103},{8,0},{9... | collective-permute-start | bytes 1572872 | tf_op jit(solution)/shard_map/reduce_outer/ppermute | solution.py:35
  102.0 7.7 %collective-permute-start.29 = (bf16[4,128,256]{2,1,0:T(8,128)(2,1)S(1)}, bf16[4,128,256]{2,1,0:T(8,128)(2,1)S(1)}, u32[]{:S(2)}, u32[]{:S(2)}) collective-permute-start(bf16[4,128,256]{2,1,0:T(8,128)(2,1)S(1)} %get-tuple-element.51), channel_id=1, source_target_pairs={{0,32},{1,9},{2,34},{3,11},{4,36},{5,13},{6,38},{7,15},{8,40},{9,1... | collective-permute-start | bytes 786440 | tf_op jit(solution)/shard_map/reduce_outer/ppermute | solution.py:35
  104.4 9.5 %collective-permute-start.30 = (bf16[4,128,256]{2,1,0:T(8,128)(2,1)S(1)}, bf16[4,128,256]{2,1,0:T(8,128)(2,1)S(1)}, u32[]{:S(2)}, u32[]{:S(2)}) collective-permute-start(bf16[4,128,256]{2,1,0:T(8,128)(2,1)S(1)} %get-tuple-element.52), channel_id=1, source_target_pairs={{0,64},{1,17},{2,66},{3,19},{4,68},{5,21},{6,70},{7,23},{8,72},{9,... | collective-permute-start | bytes 786440 | tf_op jit(solution)/shard_map/reduce_outer/ppermute | solution.py:35
  106.7 7.2 %collective-permute-start.31 = (bf16[4,128,256]{2,1,0:T(8,128)(2,1)S(1)}, bf16[4,128,256]{2,1,0:T(8,128)(2,1)S(1)}, u32[]{:S(2)}, u32[]{:S(2)}) collective-permute-start(bf16[4,128,256]{2,1,0:T(8,128)(2,1)S(1)} %get-tuple-element.53), channel_id=1, source_target_pairs={{0,96},{1,25},{2,98},{3,27},{4,100},{5,29},{6,102},{7,31},{8,104},... | collective-permute-start | bytes 786440 | tf_op jit(solution)/shard_map/reduce_outer/ppermute | solution.py:35
  114.4 1.3 collective-permute-start.32
  115.8 6.9 %collective-permute-start.35 = (f32[128,128]{1,0:T(8,128)S(1)}, f32[128,128]{1,0:T(8,128)S(1)}, u32[]{:S(2)}, u32[]{:S(2)}) collective-permute-start(f32[128,128]{1,0:T(8,128)S(1)} %add.91), channel_id=1, source_target_pairs={{0,6},{2,0},{4,2},{6,4},{1,7},{3,1},{5,3},{7,5},{8,14},{10,8},{12,... | collective-permute-start | bytes 196616 | tf_op jit(solution)/shard_map/reduce_gram/ppermute | solution.py:24
  120.8 6.5 %collective-permute-start.34 = (f32[128,128]{1,0:T(8,128)S(1)}, f32[128,128]{1,0:T(8,128)S(1)}, u32[]{:S(2)}, u32[]{:S(2)}) collective-permute-start(f32[128,128]{1,0:T(8,128)S(1)} %add.91), channel_id=1, source_target_pairs={{0,2},{2,4},{4,6},{6,0},{1,3},{3,5},{5,7},{7,1},{8,10},{10,12},{12... | collective-permute-start | bytes 196616 | tf_op jit(solution)/shard_map/reduce_gram/ppermute | solution.py:24
  120.8 6.5 %collective-permute-start.33 = (f32[128,128]{1,0:T(8,128)S(1)}, f32[128,128]{1,0:T(8,128)S(1)}, u32[]{:S(2)}, u32[]{:S(2)}) collective-permute-start(f32[128,128]{1,0:T(8,128)S(1)} %add.91), channel_id=1, source_target_pairs={{0,4},{2,6},{4,0},{6,2},{1,5},{3,7},{5,1},{7,3},{8,12},{10,14},{12... | collective-permute-start | bytes 196616 | tf_op jit(solution)/shard_map/reduce_gram/ppermute | solution.py:24
  127.3 5.1 %collective-permute-start.38 = (f32[128,128]{1,0:T(8,128)S(1)}, f32[128,128]{1,0:T(8,128)S(1)}, u32[]{:S(2)}, u32[]{:S(2)}) collective-permute-start(f32[128,128]{1,0:T(8,128)S(1)} %add_add_fusion.2), channel_id=1, source_target_pairs={{0,24},{8,0},{16,8},{24,16},{1,25},{9,1},{17,9},{25,17},{2,26},{10... | collective-permute-start | bytes 196616 | tf_op jit(solution)/shard_map/reduce_gram/ppermute | solution.py:24
  127.4 5.5 %collective-permute-start.37 = (f32[128,128]{1,0:T(8,128)S(1)}, f32[128,128]{1,0:T(8,128)S(1)}, u32[]{:S(2)}, u32[]{:S(2)}) collective-permute-start(f32[128,128]{1,0:T(8,128)S(1)} %add_add_fusion.2), channel_id=1, source_target_pairs={{0,8},{8,16},{16,24},{24,0},{1,9},{9,17},{17,25},{25,1},{2,10},{10... | collective-permute-start | bytes 196616 | tf_op jit(solution)/shard_map/reduce_gram/ppermute | solution.py:24
  129.9 5.8 %collective-permute-start.36 = (f32[128,128]{1,0:T(8,128)S(1)}, f32[128,128]{1,0:T(8,128)S(1)}, u32[]{:S(2)}, u32[]{:S(2)}) collective-permute-start(f32[128,128]{1,0:T(8,128)S(1)} %add_add_fusion.2), channel_id=1, source_target_pairs={{0,16},{8,24},{16,0},{24,8},{1,17},{9,25},{17,1},{25,9},{2,18},{10... | collective-permute-start | bytes 196616 | tf_op jit(solution)/shard_map/reduce_gram/ppermute | solution.py:24
  135.7 5.6 %collective-permute-start.41 = (f32[128,128]{1,0:T(8,128)S(1)}, f32[128,128]{1,0:T(8,128)S(1)}, u32[]{:S(2)}, u32[]{:S(2)}) collective-permute-start(f32[128,128]{1,0:T(8,128)S(1)} %add_add_fusion.1), channel_id=1, source_target_pairs={{0,96},{32,0},{64,32},{96,64},{1,97},{33,1},{65,33},{97,65},{2,98}... | collective-permute-start | bytes 196616 | tf_op jit(solution)/shard_map/reduce_gram/ppermute | solution.py:24
  138.3 5.5 %collective-permute-start.40 = (f32[128,128]{1,0:T(8,128)S(1)}, f32[128,128]{1,0:T(8,128)S(1)}, u32[]{:S(2)}, u32[]{:S(2)}) collective-permute-start(f32[128,128]{1,0:T(8,128)S(1)} %add_add_fusion.1), channel_id=1, source_target_pairs={{0,32},{32,64},{64,96},{96,0},{1,33},{33,65},{65,97},{97,1},{2,34}... | collective-permute-start | bytes 196616 | tf_op jit(solution)/shard_map/reduce_gram/ppermute | solution.py:24
  138.6 5.8 %collective-permute-start.39 = (f32[128,128]{1,0:T(8,128)S(1)}, f32[128,128]{1,0:T(8,128)S(1)}, u32[]{:S(2)}, u32[]{:S(2)}) collective-permute-start(f32[128,128]{1,0:T(8,128)S(1)} %add_add_fusion.1), channel_id=1, source_target_pairs={{0,64},{32,96},{64,0},{96,32},{1,65},{33,97},{65,1},{97,33},{2,66}... | collective-permute-start | bytes 196616 | tf_op jit(solution)/shard_map/reduce_gram/ppermute | solution.py:24
